TPU v7x, 128 devices: a whole 4x4x4 slice. The times are simulated.
128 devices in a mesh: row: 32 (over z, x, core), col: 4 (over y).
Axes of the slice: x: 4, y: 4, z: 4, core: 2. Of those that a mesh axis runs over, the one named last changes fastest.
Arguments:
- doc_taps: bfloat16 [98304, 2, 5120], P(('row', 'col')), may hold values from -24 to 24
- w_down: bfloat16 [5120, 512], replicated, may hold values from -0.078125 to 0.078125
- owner_of: int32 [4, 24576], P('col'), may hold values from 0 to 31, as said below
- adj_values: bfloat16 [128, 24, 128, 128], P(('row', 'col')), as said below
- adj_index: int32 [128, 24], P(('row', 'col')), may hold values from 0 to 23, as said below
- w_msg: bfloat16 [512, 512], replicated, may hold values from -0.25 to 0.25
- gate_scale: float32 [512], replicated, may hold values from 0.5 to 1.5
- cotangent: bfloat16 [98304, 512], P(('row', 'col')), may hold values from -0.078125 to 0.078125
Outputs:
- side_out: bfloat16 [98304, 512], P(('row', 'col'))
- grad_down: float32 [5120, 512], P('row')
- grad_msg: float32 [512, 512], P('row')
- grad_gate: float32 [512], P('row')
Inputs may be any that keep to these rules, and one draw needn't show every extreme that they name: `owner_of`: each row owner receives exactly 768 documents of each column group; one device sends at most 72 documents to one owner, and 72 is reached in every column group. `adj_index`: entry e of a device lies in its block row e // 4; the first entry of each block row is the diagonal block of the row group. Within a row group the adjacency is symmetric: summed block (I, J) is the transpose of summed block (J, I). `adj_values`: blocks of the same pair in transposed positions are transposes of each other; diagonal blocks are symmetric.
All inputs are finite; a program needn't handle non-finite values.
Results may differ from a plain program's by a relative error of at most 0.0072.
Values may be sent and summed in bfloat16 or wider, within the bound.
No kernel may reach another device: no remote copies, remote signals or barrier semaphores. Data moves between devices by JAX's collectives and lax.ppermute only.
A program may use at most 128 MiB of HBM per device.

v0:
```python
import jax
import jax.numpy as jnp
from jax import lax
from jax.sharding import PartitionSpec as P


def merge_blocks(values, index, per_row):
    entries = values.shape[0]
    block_size = values.shape[1]
    row_blocks = entries // per_row
    grouped_index = index.reshape(row_blocks, per_row)
    same = grouped_index[:, :, None] == grouped_index[:, None, :]
    earlier = jnp.arange(per_row)[None, :] < jnp.arange(per_row)[:, None]
    first = jnp.logical_not(jnp.any(same & earlier[None], axis=2))
    grouped_vals = values.reshape(row_blocks, per_row, block_size, block_size).astype(jnp.float32)
    summed = jnp.einsum(
        "rkj,rjab->rkab", same.astype(jnp.float32), grouped_vals, precision=lax.Precision.HIGHEST
    )
    merged = jnp.where(first[:, :, None, None], summed, 0.0).astype(jnp.bfloat16)
    return merged


def block_product(merged, index, operand):
    row_blocks, per_row, block_size, _ = merged.shape
    width = operand.shape[1]
    picked = operand.reshape(-1, block_size, width)[index]
    picked = picked.reshape(row_blocks, per_row, block_size, width)
    return jnp.einsum("rkab,rkbh->rah", merged, picked, preferred_element_type=jnp.float32).reshape(
        row_blocks * block_size, width
    )


def contract_rows(left_mat, right_mat):
    return lax.dot_general(
        left_mat, right_mat, (((0,), (0,)), ((), ())), preferred_element_type=jnp.float32
    )


def shards(doc_taps, w_down, owner_of, adj_values, adj_index, w_msg, gate_scale, cotangent):
    doc_count = doc_taps.shape[0]
    row_size = lax.axis_size("row")
    col_size = lax.axis_size("col")
    capacity = 3 * doc_count // row_size
    side_width = w_down.shape[1]
    block_size = adj_values.shape[2]
    row_blocks = doc_count // block_size
    per_row = adj_values.shape[1] // row_blocks
    group_blocks = col_size * row_blocks
    my_row = lax.axis_index("row")
    pooled = (jnp.sum(doc_taps, axis=1, dtype=jnp.float32) / doc_taps.shape[1]).astype(jnp.bfloat16)
    side = jnp.dot(pooled, w_down, preferred_element_type=jnp.float32).astype(jnp.bfloat16)
    owners = owner_of[0]
    my_dest = lax.dynamic_slice_in_dim(owners, my_row * doc_count, doc_count)
    targets = jnp.arange(row_size, dtype=jnp.int32)
    dest_hits = (my_dest[:, None] == targets[None, :]).astype(jnp.int32)
    dest_rank = jnp.sum(dest_hits * (jnp.cumsum(dest_hits, axis=0) - 1), axis=1)
    send_slot = my_dest * capacity + dest_rank
    members = (owners == my_row).astype(jnp.int32).reshape(row_size, doc_count)
    member_rank = jnp.cumsum(members, axis=1) - 1
    flat_members = members.reshape(-1)
    position = jnp.cumsum(flat_members) - 1
    sources = (targets[:, None] * capacity + member_rank).reshape(-1)
    landing = jnp.where(flat_members > 0, position, doc_count)
    pos_to_slot = jnp.zeros((doc_count,), jnp.int32).at[landing].set(sources, mode="drop")
    outgoing = jnp.zeros((row_size * capacity, side_width), jnp.bfloat16).at[send_slot].set(side)
    incoming = lax.all_to_all(outgoing, "row", split_axis=0, concat_axis=0, tiled=True)
    owned = incoming[pos_to_slot]
    gathered = lax.all_gather(owned, "col", axis=0, tiled=True)
    block_index = adj_index[0]
    merged = merge_blocks(adj_values[0], block_index, per_row)
    aggregate = block_product(merged, block_index, gathered).astype(jnp.bfloat16)
    message = jnp.dot(aggregate, w_msg, preferred_element_type=jnp.float32)
    squash = jax.nn.sigmoid(message)
    activated = message * squash
    side_out = (owned.astype(jnp.float32) + gate_scale * activated).astype(jnp.bfloat16)
    upstream = cotangent.astype(jnp.float32)
    message_grad = (upstream * gate_scale * squash * (1.0 + message * (1.0 - squash))).astype(
        jnp.bfloat16
    )
    gate_part = jnp.sum(upstream * activated, axis=0)
    msg_part = contract_rows(aggregate, message_grad)
    aggregate_grad = lax.dot_general(
        message_grad, w_msg, (((1,), (1,)), ((), ())), preferred_element_type=jnp.float32
    ).astype(jnp.bfloat16)
    grad_blocks = aggregate_grad.reshape(row_blocks, block_size, side_width)
    contrib = jnp.einsum("rkab,rah->rkbh", merged, grad_blocks, preferred_element_type=jnp.float32)
    contrib = contrib.reshape(row_blocks * per_row, block_size * side_width)
    one_hot = (block_index[None, :] == jnp.arange(group_blocks, dtype=jnp.int32)[:, None]).astype(
        jnp.float32
    )
    partial_terms = jnp.dot(one_hot, contrib, precision=lax.Precision.HIGHEST)
    partial_terms = partial_terms.reshape(group_blocks * block_size, side_width)
    returned = lax.psum_scatter(partial_terms, "col", scatter_dimension=0, tiled=True)
    owned_grad = (upstream + returned).astype(jnp.bfloat16)
    back_out = (
        jnp.zeros((row_size * capacity, side_width), jnp.bfloat16).at[pos_to_slot].set(owned_grad)
    )
    back_in = lax.all_to_all(back_out, "row", split_axis=0, concat_axis=0, tiled=True)
    side_grad = back_in[send_slot]
    down_part = contract_rows(pooled, side_grad)
    down_share, msg_share, gate_share = (
        lax.psum_scatter(down_part, ("row", "col"), scatter_dimension=0, tiled=True),
        lax.psum_scatter(msg_part, ("row", "col"), scatter_dimension=0, tiled=True),
        lax.psum_scatter(gate_part, ("row", "col"), scatter_dimension=0, tiled=True),
    )
    grad_down, grad_msg, grad_gate = (
        lax.all_gather(down_share, "col", axis=0, tiled=True),
        lax.all_gather(msg_share, "col", axis=0, tiled=True),
        lax.all_gather(gate_share, "col", axis=0, tiled=True),
    )
    return (side_out, grad_down, grad_msg, grad_gate)


def solution(mesh):
    placed = (
        P(("row", "col"), None, None),
        P(),
        P("col", None),
        P(("row", "col"), None, None, None),
        P(("row", "col"), None),
        P(),
        P(),
        P(("row", "col"), None),
    )
    return jax.shard_map(
        shards,
        mesh=mesh,
        in_specs=placed,
        out_specs=(P(("row", "col"), None), P("row", None), P("row", None), P("row")),
        check_vma=False,
    )
```

profile of v0, /device:TPU:0, one launch (start us, length us, event | category | flops | bytes accessed | tf_op | source)
XLA Modules:
  0.0 1174.4 jit_solution(1805247026903506426)
XLA Ops:
  7.2 0.8 dynamic-slice_reduce_fusion
  8.0 1.7 reduce-window.26
  9.7 0.3 slice_reduce_fusion.1
  10.0 0.1 fusion.16
  10.1 0.7 fusion.23
  10.8 49.7 %convert_reduce_fusion = f32[768,5120]{1,0:T(8,128)} fusion(bf16[768,2,5120]{2,1,0:T(2,128)(2,1)} %param.8), kind=kLoop, calls=%fused_computation.6 | loop fusion | flops 11796480 | bytes 31457280 | tf_op jit(solution)/shard_map/reduce_sum | solution.py:50
  60.5 11.2 fusion.8
  71.7 7.2 scatter_custom_fusion
  79.0 8.4 all-to-all-start
  87.3 0.2 all-gather.4.cloned.1.call-start
  87.6 0.5 broadcast.245
  88.1 1.6 fusion.29
  89.6 0.1 copy.26
  89.7 0.2 reduce-window.30
  90.0 0.3 reduce-window.31
  90.3 0.1 slice.31
  90.4 0.1 slice_reduce_fusion.2
  90.5 0.1 add_bitcast_fusion.1
  90.6 0.1 pad_slice_fusion
  90.7 0.1 copy.27
  90.8 0.8 compare_select_fusion
  91.6 0.1 add.103
  91.7 0.9 reshape.245
  92.6 1.7 reduce-window.42
  94.4 0.3 slice_reduce_fusion
  94.7 0.1 add_add_fusion.1
  94.8 0.1 copy.29
  94.9 90.4 %scatter_custom_fusion.1 = s32[768]{0:T(1024)S(1)} fusion(s32[24576]{0:T(1024)} %bitcast.97, s32[24576]{0:T(1024)S(1)} %add.105, s32[]{:T(128)} %constant.15.clone.1), kind=kCustom, calls=%fused_computation.62 | custom fusion | bytes 3584 | tf_op jit(solution)/shard_map/scatter | solution.py:64
  185.3 3.3 gather_fusion
  188.7 0.0 reduce-scatter.3.cloned.1.call-start
  188.7 0.7 reduce.18
  189.4 0.1 eq.83
  189.5 0.3 fusion.18
  189.8 0.8 select_convert_fusion
  190.6 0.6 copy.32
  191.2 38.9 %all-gather.4.cloned.1.call-done = bf16[3072,512]{1,0:T(8,128)(2,1)} async-done(((bf16[768,512]{1,0:T(8,128)(2,1)}), bf16[3072,512]{1,0:T(8,128)(2,1)}) %all-gather.4.cloned.1.call-update) | async-done | bytes 3145744 | tf_op jit(solution)/shard_map/all_gather | solution.py:68
  230.0 4.4 gather_fusion.1
  234.5 2.7 bitcast_convert_fusion
  237.2 2.3 fusion.6
  239.5 0.6 convolution_convert_fusion
  240.1 0.3 copy-done.6
  240.4 1.0 fusion.30
  241.3 3.6 copy.37
  245.0 5.0 fusion.19
  250.0 6.9 reshape.243
  256.9 64.3 %reduce-scatter.3.cloned.1.call-done = f32[768,512]{1,0:T(8,128)} async-done(((f32[3072,512]{1,0:T(8,128)}), f32[768,512]{1,0:T(8,128)}) %reduce-scatter.3.cloned.1.call-update) | async-done | bytes 1572880 | tf_op jit(solution)/shard_map/reduce_scatter | solution.py:93
  321.2 8.5 scatter_custom_fusion.2
  329.7 7.4 all-to-all-start.1
  337.1 2.7 fusion.31
  339.9 30.3 %all-to-all-done.1 = bf16[32,72,512]{2,1,0:T(8,128)(2,1)S(1)} async-done(((bf16[32,72,512]{2,1,0:T(8,128)(2,1)}), bf16[32,72,512]{2,1,0:T(8,128)(2,1)S(1)}, u32[]{:S(2)}, u32[]{:S(2)}) %all-to-all-start.1) | async-done | bytes 2359328 | tf_op jit(solution)/shard_map/all_to_all | solution.py:98
  370.2 2.7 gather_fusion.2
  372.9 12.6 %fusion = f32[5120,512]{1,0:T(8,128)} fusion(bf16[768,512]{1,0:T(8,128)(2,1)S(1)} %gather_fusion.2, f32[768,5120]{1,0:T(8,128)} %convert_reduce_fusion), kind=kOutput, calls=%fused_computation.8 | convolution fusion | flops 4034396160 | bytes 27000832 | tf_op jit(solution)/shard_map/dot_general | solution.py:34
  385.5 0.6 copy-done.11
  386.1 0.6 dynamic-slice.1
  387.3 63.1 %all-reduce.4 = f32[512]{0:T(512)S(1)} all-reduce(f32[512]{0:T(512)S(1)} %get-tuple-element.6), channel_id=6, replica_groups=mesh['row'=32,'col'=4] {'row','col'}, use_global_device_ids=true, to_apply=%region_17.18.clone | all-reduce | flops 512 | bytes 4096
  450.4 0.2 dynamic-slice_dynamic-update-slice_fusion
  450.5 10.5 all-reduce.2
  461.0 36.1 %all-reduce.7.cloned.1.call-done = f32[512,512]{1,0:T(8,128)} async-done(((f32[512,512]{1,0:T(8,128)}), f32[512,512]{1,0:T(8,128)}) %all-reduce.7.cloned.1.call-update) | async-done | bytes 1048592
  497.1 0.7 dynamic-slice_bitcast_fusion
  497.8 12.0 %all-gather.1 = f32[4,4,512]{2,1,0:T(4,128)S(1)} all-gather(f32[1,4,512]{2,1,0:T(4,128)S(1)} %dynamic-slice_bitcast_fusion), channel_id=1, replica_groups=mesh['row'=32,'col'=4] {'col'}, dimensions={0}, use_global_device_ids=true | all-gather | bytes 40960 | tf_op jit(solution)/shard_map/all_gather | solution.py:108
  509.8 0.6 reshape.301
  510.4 644.1 %reduce-scatter.5.cloned.1.call-done = f32[40,512]{1,0:T(8,128)} async-done(((f32[5120,512]{1,0:T(8,128)}), f32[40,512]{1,0:T(8,128)}) %reduce-scatter.5.cloned.1.call-update) | async-done | bytes 81936 | tf_op jit(solution)/shard_map/reduce_scatter | solution.py:102
  1154.5 12.6 %all_gather.13 = f32[160,512]{1,0:T(8,128)S(1)} all-gather(f32[40,512]{1,0:T(8,128)} %reduce-scatter.5.cloned.1.call-done), channel_id=1, replica_groups=mesh['row'=32,'col'=4] {'col'}, dimensions={0}, use_global_device_ids=true | all-gather | bytes 409600 | tf_op jit(solution)/shard_map/all_gather | solution.py:107
  1167.1 0.7 copy.44
  (49 shorter events, 0.4 us)
Async XLA Ops:
  7.2 182.6 %copy-start = (bf16[1,24,128,128]{3,2,1,0:T(8,128)(2,1)S(1)}, bf16[1,24,128,128]{3,2,1,0:T(8,128)(2,1)}, u32[]{:S(2)}) copy-start(bf16[1,24,128,128]{3,2,1,0:T(8,128)(2,1)} %param.11) | copy-start | bytes 2359300
  79.0 9.1 copy-start.7
  79.0 106.3 %all-to-all-start = ((bf16[32,72,512]{2,1,0:T(8,128)(2,1)}), bf16[32,72,512]{2,1,0:T(8,128)(2,1)S(1)}, u32[]{:S(2)}, u32[]{:S(2)}) async-start(bf16[32,72,512]{2,1,0:T(8,128)(2,1)} %bitcast.89), calls=%async_computation | async-start | bytes 4718592 | tf_op jit(solution)/shard_map/all_to_all | solution.py:66
  87.3 142.7 %all-gather.4.cloned.1.call-start = ((), (), s32[]{:S(2)}) async-start(), calls=%async_computation.6 | async-start | bytes 3932160 | tf_op jit(solution)/shard_map/all_gather | solution.py:68
  185.3 3.4 copy-start.8
  188.7 132.5 %reduce-scatter.3.cloned.1.call-start = ((), (), s32[]{:S(2)}) async-start(), calls=%async_computation.4 | async-start | bytes 7864320 | tf_op jit(solution)/shard_map/reduce_scatter | solution.py:93
  234.5 2.7 copy-start.4
  234.5 2.7 copy-start.5
  234.5 2.7 copy-start.9
  234.5 2.7 copy-start.10
  237.2 2.3 copy-start.2
  239.5 0.9 copy-start.6
  329.7 7.4 copy-start.3
  329.7 40.5 %all-to-all-start.1 = ((bf16[32,72,512]{2,1,0:T(8,128)(2,1)}), bf16[32,72,512]{2,1,0:T(8,128)(2,1)S(1)}, u32[]{:S(2)}, u32[]{:S(2)}) async-start(bf16[32,72,512]{2,1,0:T(8,128)(2,1)} %bitcast.90), calls=%async_computation.2 | async-start | bytes 4718592 | tf_op jit(solution)/shard_map/all_to_all | solution.py:98
  337.1 160.0 %all-reduce.7.cloned.1.call-start = ((), (), s32[]{:S(2)}) async-start(), calls=%async_computation.7 | async-start | bytes 2097152
  339.9 814.7 %reduce-scatter.5.cloned.1.call-start = ((), (), s32[]{:S(2)}) async-start(), calls=%async_computation.5 | async-start | bytes 10567680 | tf_op jit(solution)/shard_map/reduce_scatter | solution.py:102
  385.4 0.7 copy-start.11
  385.4 782.4 %copy-start.1 = (bf16[1,24,128,128]{3,2,1,0:T(8,128)(2,1)S(1)}, bf16[1,24,128,128]{3,2,1,0:T(8,128)(2,1)}, u32[]{:S(2)}) copy-start(bf16[1,24,128,128]{3,2,1,0:T(8,128)(2,1)} %param.11) | copy-start | bytes 2359300
Sparse Core Ops, SparseCore 0:
  188.8 41.1 all-gather.3
  257.0 64.1 reduce-scatter.2
  342.7 154.3 all-reduce.6
  499.4 655.0 reduce-scatter.4
where the time goes:
time: 1180 us; the launch traced here: 1170 us
  waiting for transfers between devices  814 us (69%)
  local copies, waits for them, and re-layouts  126 us (11%)
  blocking collectives  98.1 us (8%)
  other arithmetic  66.7 us (6%)
  matrix products  38.7 us (3%)
  starting transfers between devices  16.1 us (1%)
  between operations  14.8 us (1%)
    reduce_scatter x1, waiting for transfers between devices, shards(): lax.psum_scatter(down_part, ('row', 'col'), scatter_dimension=0, tiled=True)  644 us
    scatter x1, local copies, waits for them, and re-layouts, shards(): jnp.zeros((doc_count,), jnp.int32).at[landing].set(sources, mode='drop')  90.4 us
    unnamed x2, blocking collectives  73.5 us
    reduce_scatter x1, waiting for transfers between devices, shards(): lax.psum_scatter(partial_terms, 'col', scatter_dimension=0, tiled=True)  64.3 us
    reduce_sum x1, other arithmetic, shards(): jnp.sum(doc_taps, axis=1, dtype=jnp.float32) / doc_taps.shape[1]  49.7 us
    all_gather x1, waiting for transfers between devices, shards(): gathered = lax.all_gather(owned, 'col', axis=0, tiled=True)  38.9 us
    unnamed x5, waiting for transfers between devices  36.1 us
    all_to_all x1, waiting for transfers between devices, shards(): lax.all_to_all(back_out, 'row', split_axis=0, concat_axis=0, tiled=True)  30.3 us
  transfers between devices with their start and end apart: 6, of which 5 were waited for; matrix products, arithmetic and copies ran while one was open for 10% of the time, Pallas kernels for 0%

commit v1 on v0

v1 whole, which is shorter than its diff:
```python
import jax
import jax.numpy as jnp
import numpy as np
from jax import lax
from jax.experimental import pallas as pl
from jax.experimental.pallas import tpu as pltpu
from jax.sharding import Mesh
from jax.sharding import PartitionSpec as P

ROWS = ("z", "x", "core")
BF16 = jnp.bfloat16
F32 = jnp.float32
SLOTS = 72


def iota(shape, dim):
    return lax.broadcasted_iota(jnp.int32, shape, dim)


def one_hot(mask):
    return jnp.where(mask, 1.0, 0.0).astype(BF16)


def params(mib):
    return pltpu.CompilerParams(vmem_limit_bytes=mib * 1024 * 1024)


def cost(flops, moved, special=0):
    return pl.CostEstimate(flops=int(flops), bytes_accessed=int(moved), transcendentals=int(special))


def whole(*shape):
    return pl.BlockSpec(shape, lambda i: (0,) * len(shape))


def pool_tiles(pick, x_ref, pooled_ref):
    tiles = x_ref.shape[1] // 16
    for group in range(x_ref.shape[0] // 16):
        docs = pl.ds(group * 16, 16)
        block = jnp.concatenate(
            [x_ref[docs, t * 16:(t + 1) * 16, :].reshape(256, 128) for t in range(tiles)], axis=1
        )
        mean = jnp.dot(pick[...], block, preferred_element_type=F32).astype(BF16)
        for j in range(8):
            for t in range(tiles):
                at = (t * 8 + j) * 128
                pooled_ref[docs, at:at + 128] = mean[j * 16:(j + 1) * 16, t * 128:(t + 1) * 128]


def pack_rows(slot, side, out_ref):
    docs = side.shape[0]
    step = out_ref.shape[0] // 6
    for part in range(6):
        rows = iota((step, docs), 0) + part * step
        chosen = one_hot(rows == slot)
        out_ref[part * step:(part + 1) * step, :] = jnp.dot(
            chosen, side, preferred_element_type=F32
        ).astype(BF16)


def pool_kernel(owner_ref, x_ref, w_ref, pooled_ref, out_ref, slot_ref, pick, side):
    at = pl.program_id(0)
    step = x_ref.shape[0]
    docs = side.shape[0]

    @pl.when(at == 0)
    def _():
        out_row, in_row = iota((128, 256), 0), iota((128, 256), 1)
        same_doc = out_row % 16 == in_row // 16
        same_tile = out_row // 16 == (in_row % 16) // 2
        pick[...] = jnp.where(same_doc & same_tile, 0.5, 0.0).astype(BF16)

    pool_tiles(pick, x_ref, pooled_ref)
    side[pl.ds(pl.multiple_of(at * step, step), step), :] = jnp.dot(
        pooled_ref[...], w_ref[...], preferred_element_type=F32
    ).astype(BF16)

    @pl.when(at == pl.num_programs(0) - 1)
    def _():
        first = pl.multiple_of(lax.axis_index(ROWS) * docs, 128)
        dest = owner_ref[:, pl.ds(first, docs)]
        hit = iota((32, docs), 0) == dest
        earlier = one_hot(iota((docs, docs), 0) < iota((docs, docs), 1))
        before = jnp.dot(one_hot(hit), earlier, preferred_element_type=F32)
        rank = jnp.sum(jnp.where(hit, before, 0.0), axis=0, keepdims=True)
        slot = dest * SLOTS + rank.astype(jnp.int32)
        slot_ref[...] = slot
        pack_rows(slot, side[...], out_ref)


def pool_and_pack(owner_of, doc_taps, w_down, wide, slots):
    docs, tokens, depth = doc_taps.shape
    tiles = depth // 128
    taps = doc_taps.reshape(docs, tokens, tiles, 128).transpose(0, 2, 1, 3)
    taps = taps.reshape(docs, tokens * tiles, 128)
    step = 128
    return pl.pallas_call(
        pool_kernel,
        grid=(docs // step,),
        in_specs=[
            whole(*owner_of.shape),
            pl.BlockSpec((step, tokens * tiles, 128), lambda i: (i, 0, 0)),
            whole(depth, wide),
        ],
        out_specs=[
            pl.BlockSpec((step, depth), lambda i: (i, 0)),
            whole(slots, wide),
            whole(1, docs),
        ],
        out_shape=[
            jax.ShapeDtypeStruct((docs, depth), BF16),
            jax.ShapeDtypeStruct((slots, wide), BF16),
            jax.ShapeDtypeStruct((1, docs), jnp.int32),
        ],
        scratch_shapes=[pltpu.VMEM((128, 256), BF16), pltpu.VMEM((docs, wide), BF16)],
        compiler_params=params(56),
        cost_estimate=cost(6e9, 28e6),
    )(owner_of, taps, w_down)


def project_kernel(slot_ref, pooled_ref, w_ref, out_ref, total):
    at = pl.program_id(0)
    term = jnp.dot(pooled_ref[...], w_ref[...], preferred_element_type=F32)

    @pl.when(at == 0)
    def _():
        total[...] = term

    @pl.when(at > 0)
    def _():
        total[...] += term

    @pl.when(at == pl.num_programs(0) - 1)
    def _():
        pack_rows(slot_ref[...], total[...].astype(BF16), out_ref)


def project_and_pack(slot, pooled, w_down, wide, chunk, slots):
    docs, depth = pooled.shape
    step = depth // 5
    return pl.pallas_call(
        project_kernel,
        grid=(5,),
        in_specs=[
            whole(1, docs),
            pl.BlockSpec((docs, step), lambda i: (0, i)),
            pl.BlockSpec((step, wide), lambda i: (i, chunk)),
        ],
        out_specs=whole(slots, wide),
        out_shape=jax.ShapeDtypeStruct((slots, wide), BF16),
        scratch_shapes=[pltpu.VMEM((docs, wide), F32)],
        compiler_params=params(24),
        cost_estimate=cost(3e9, 12e6),
    )(slot, pooled, w_down)


def turn_kernel(pooled_ref, mine_ref, theirs_ref):
    turned = pooled_ref[...].T
    rows = mine_ref.shape[2]
    cols = mine_ref.shape[0]
    core = lax.axis_index("core")
    for this in range(2):
        @pl.when(core == this)
        def _():
            for out_ref, which in ((mine_ref, this), (theirs_ref, 1 - this)):
                for chip in range(mine_ref.shape[1]):
                    for col in range(cols):
                        at = ((chip * 2 + which) * cols + col) * rows
                        out_ref[col, chip] = turned[at:at + rows, :]


def turn(pooled, chips, cols):
    docs, depth = pooled.shape
    rows = depth // (2 * chips * cols)
    pair = 4 * cols * rows
    out = jax.ShapeDtypeStruct((cols, chips, rows, docs), BF16)
    return pl.pallas_call(
        turn_kernel,
        grid=(chips // 2,),
        in_specs=[pl.BlockSpec((docs, pair), lambda i: (0, i))],
        out_specs=[pl.BlockSpec((cols, 2, rows, docs), lambda i: (0, i, 0, 0))] * 2,
        out_shape=[out, out],
        compiler_params=params(24),
        cost_estimate=cost(1e9, 16e6),
    )(pooled)


def take_kernel(place_ref, table_ref, out_ref):
    step, depth = out_ref.shape[0], table_ref.shape[0]
    if place_ref.shape[0] == 1:
        mask = iota((step, depth), 0) + pl.program_id(0) * step == place_ref[...]
    else:
        mask = iota((step, depth), 1) == place_ref[...]
    out_ref[...] = jnp.dot(one_hot(mask), table_ref[...], preferred_element_type=F32).astype(BF16)


def take(place, table, count):
    depth, width = table.shape
    step = count // 3
    if place.shape[0] == 1:
        place_spec = whole(1, depth)
    else:
        place_spec = pl.BlockSpec((step, 1), lambda i: (i, 0))
    return pl.pallas_call(
        take_kernel,
        grid=(3,),
        in_specs=[place_spec, whole(depth, width)],
        out_specs=pl.BlockSpec((step, width), lambda i: (i, 0)),
        out_shape=jax.ShapeDtypeStruct((count, width), BF16),
        compiler_params=params(20),
        cost_estimate=cost(2 * count * depth * width, 2e6),
    )(place, table)


def gather_col(part):
    up = [(c, (c + 1) % 4) for c in range(4)]
    down = [(c, (c + 3) % 4) for c in range(4)]
    half = part.shape[0] // 2
    before = lax.ppermute(part, "col", up)
    after = lax.ppermute(part, "col", down)
    low = lax.ppermute(before[:half], "col", up)
    high = lax.ppermute(after[half:], "col", down)
    return part, after, low, high, before


def stage(parts, table):
    at = 0
    for part in parts:
        table[at:at + part.shape[0], :] = part[...]
        at += part.shape[0]


def block_row(index_ref, values_ref, table, row, per_row):
    total = None
    for k in range(per_row):
        entry = row * per_row + k
        at = pl.multiple_of(index_ref[entry] * 128, 128)
        term = jnp.dot(values_ref[entry], table[pl.ds(at, 128), :], preferred_element_type=F32)
        total = term if total is None else total + term
    return total


def product_kernel(index_ref, values_ref, *refs):
    parts, (out_ref, table) = refs[:5], refs[5:]
    stage(parts, table)
    rows = out_ref.shape[0] // 128
    per_row = values_ref.shape[0] // rows
    for row in range(rows):
        out_ref[row * 128:(row + 1) * 128, :] = block_row(
            index_ref, values_ref, table, row, per_row
        ).astype(BF16)


def product(index, values, parts):
    nodes, width = parts[0].shape
    vmem = pl.BlockSpec(memory_space=pltpu.VMEM)
    return pl.pallas_call(
        product_kernel,
        in_specs=[pl.BlockSpec(memory_space=pltpu.SMEM)] + [vmem] * 6,
        out_specs=vmem,
        out_shape=jax.ShapeDtypeStruct((nodes, width), BF16),
        scratch_shapes=[pltpu.VMEM((4 * nodes, width), BF16)],
        compiler_params=params(16),
        cost_estimate=cost(2e8, 3e6),
    )(index, values, *parts)


def layer_kernel(index_ref, values_ref, *refs):
    parts = refs[:5]
    (first_ref, owned_ref, cot_ref, w_ref, wt_ref, gate_ref) = refs[5:11]
    (side_out_ref, agg_ref, mgrad_ref, agrad0_ref, agrad1_ref, gpart_ref, table) = refs[11:]
    at = pl.program_id(0)

    @pl.when(at == 0)
    def _():
        stage(parts, table)

    step = cot_ref.shape[0]
    wide = first_ref.shape[1]
    nodes = step * pl.num_programs(0)
    per_row = values_ref.shape[0] * 128 // nodes
    rows = step // 128
    agg_ref[:, :wide] = first_ref[...]
    for row in range(rows):
        agg_ref[row * 128:(row + 1) * 128, wide:] = block_row(
            index_ref, values_ref, table, at * rows + row, per_row
        ).astype(BF16)
    message = jnp.dot(agg_ref[...], w_ref[...], preferred_element_type=F32)
    squash = jax.nn.sigmoid(message)
    activated = message * squash
    gate = gate_ref[...]
    upstream = cot_ref[...].astype(F32)
    owned = jnp.concatenate(
        [owned_ref[...], parts[0][pl.ds(pl.multiple_of(at * step, step), step), :]], axis=1
    )
    side_out_ref[...] = (owned.astype(F32) + gate * activated).astype(BF16)
    mgrad = (upstream * gate * squash * (1.0 + message * (1.0 - squash))).astype(BF16)
    mgrad_ref[...] = mgrad
    agrad = jnp.dot(mgrad, wt_ref[...], preferred_element_type=F32).astype(BF16)
    agrad0_ref[...] = agrad[:, :wide]
    agrad1_ref[...] = agrad[:, wide:]
    part = jnp.sum(upstream * activated, axis=0, keepdims=True)

    @pl.when(at == 0)
    def _():
        gpart_ref[...] = part

    @pl.when(at > 0)
    def _():
        gpart_ref[...] += part


def layer(index, values, parts, first, owned, cotangent, w_msg, gate):
    nodes, width = cotangent.shape
    wide = width // 2
    step = 256
    rows = lambda size: pl.BlockSpec((step, size), lambda i: (i, 0))
    shape = lambda size: jax.ShapeDtypeStruct((nodes, size), BF16)
    return pl.pallas_call(
        layer_kernel,
        grid=(nodes // step,),
        in_specs=[pl.BlockSpec(memory_space=pltpu.SMEM), whole(*values.shape)]
        + [whole(*part.shape) for part in parts]
        + [rows(wide), rows(wide), rows(width), whole(width, width), whole(width, width),
           whole(1, width)],
        out_specs=[rows(width), rows(width), rows(width), rows(wide), rows(wide), whole(1, width)],
        out_shape=[shape(width), shape(width), shape(width), shape(wide), shape(wide),
                   jax.ShapeDtypeStruct((1, width), F32)],
        scratch_shapes=[pltpu.VMEM((4 * nodes, wide), BF16)],
        compiler_params=params(32),
        cost_estimate=cost(12e8, 8e6, nodes * width),
    )(index, values, *parts, first, owned, cotangent, w_msg, w_msg.T, gate)


def back_kernel(index_ref, values_ref, *refs):
    parts = refs[:5]
    cot_ref, place_ref, out_ref, table, grad = refs[5:]
    nodes = cot_ref.shape[0]
    per_row = values_ref.shape[0] * 128 // nodes

    @pl.when(pl.program_id(0) == 0)
    def _():
        stage(parts, table)
        for row in range(nodes // 128):
            at = slice(row * 128, (row + 1) * 128)
            total = block_row(index_ref, values_ref, table, row, per_row)
            grad[at, :] = (cot_ref[at, :].astype(F32) + total).astype(BF16)

    mask = iota((out_ref.shape[0], nodes), 1) == place_ref[...]
    out_ref[...] = jnp.dot(one_hot(mask), grad[...], preferred_element_type=F32).astype(BF16)


def back(index, values, parts, cotangent, chunk, place, slots):
    nodes, wide = parts[0].shape
    step = slots // 6
    return pl.pallas_call(
        back_kernel,
        grid=(6,),
        in_specs=[pl.BlockSpec(memory_space=pltpu.SMEM), whole(*values.shape)]
        + [whole(*part.shape) for part in parts]
        + [pl.BlockSpec((nodes, wide), lambda i: (0, chunk)),
           pl.BlockSpec((step, 1), lambda i: (i, 0))],
        out_specs=pl.BlockSpec((step, wide), lambda i: (i, 0)),
        out_shape=jax.ShapeDtypeStruct((slots, wide), BF16),
        scratch_shapes=[pltpu.VMEM((4 * nodes, wide), BF16), pltpu.VMEM((nodes, wide), BF16)],
        compiler_params=params(24),
        cost_estimate=cost(2 * slots * nodes * wide, 5e6),
    )(index, values, *parts, cotangent, place)


def relay(rows):
    slots, width = rows.shape
    size = lax.axis_size(ROWS)
    moved = lax.all_to_all(
        rows.reshape(size, slots // size, width), ROWS, split_axis=0, concat_axis=0, tiled=True
    )
    return moved.reshape(slots, width)


def col_pieces(part):
    return [lax.ppermute(part, "col", [(c, c ^ step) for c in range(4)]) for step in (1, 2, 3)]


def shards(doc_taps, w_down, owner_of, adj_values, adj_index, w_msg, gate_scale, cotangent):
    docs = doc_taps.shape[0]
    depth, width = w_down.shape
    wide = width // 2
    row_size, cols = lax.axis_size(ROWS), lax.axis_size("col")
    my_row, my_col = lax.axis_index(ROWS), lax.axis_index("col")
    slots = row_size * SLOTS
    chips = row_size // 2
    share = depth // row_size
    piece = share // cols
    values = adj_values[0]
    blocks = docs // 128
    index = (adj_index[0] // blocks - my_col) % cols * blocks + adj_index[0] % blocks
    gate = gate_scale.reshape(1, width)

    pooled, packed, slot = pool_and_pack(owner_of, doc_taps, w_down, wide, slots)
    incoming0 = relay(packed)
    incoming1 = relay(project_and_pack(slot, pooled, w_down, wide, 1, slots))

    owners = owner_of[0]
    counts = jnp.sum((owners.reshape(row_size, docs) == my_row).astype(jnp.int32), axis=1)
    lower = jnp.arange(row_size)[None, :] < jnp.arange(row_size)[:, None]
    starts = jnp.sum(jnp.where(lower, counts[None, :], 0), axis=1)
    in_slot = jnp.arange(SLOTS, dtype=jnp.int32)[None, :]
    position = jnp.where(in_slot < counts[:, None], starts[:, None] + in_slot, -1).reshape(slots)
    pos_row, pos_col = position.reshape(1, slots), position.reshape(slots, 1)

    owned0 = take(pos_row, incoming0, docs)
    parts0 = gather_col(owned0)
    owned1 = take(pos_row, incoming1, docs)
    parts1 = gather_col(owned1)
    first = product(index, values, parts0)
    side_out, aggregate, message_grad, agrad0, agrad1, gate_part = layer(
        index, values, parts1, first, owned0, cotangent, w_msg, gate
    )

    mine, theirs = turn(pooled, chips, cols)
    mine = mine.reshape(depth // 2, docs)
    swap = [(0, 1), (1, 0)]
    other = lax.ppermute(theirs.reshape(depth // 2, docs), "core", swap)

    msg_part = lax.dot_general(
        aggregate, message_grad, (((0,), (0,)), ((), ())), preferred_element_type=F32
    )
    msg_share = width // row_size
    gate_rows = jnp.pad(
        gate_part.reshape(row_size, 1, msg_share), ((0, 0), (0, 7), (0, width - msg_share))
    )
    small = jnp.concatenate([msg_part.reshape(row_size, msg_share, width), gate_rows], axis=1)
    small = lax.all_to_all(small, ROWS, split_axis=0, concat_axis=0, tiled=True)

    slot_col = slot.reshape(docs, 1)
    downs = []
    for chunk, agrad in enumerate((agrad0, agrad1)):
        gparts = gather_col(agrad)
        back_in = relay(back(index, values, gparts, cotangent, chunk, pos_col, slots))
        side_grad = take(slot_col, back_in, docs)
        other_grad = lax.ppermute(side_grad, "core", swap)
        down_part = jnp.dot(mine, side_grad, preferred_element_type=F32) + jnp.dot(
            other, other_grad, preferred_element_type=F32
        )
        by_col = lax.all_to_all(
            down_part.astype(BF16).reshape(cols, chips * piece, wide),
            "col", split_axis=0, concat_axis=0, tiled=True,
        )
        by_col = jnp.sum(by_col.astype(F32), axis=0).astype(BF16)
        by_chip = lax.all_to_all(
            by_col.reshape(chips, piece, wide), ("z", "x"), split_axis=0, concat_axis=0, tiled=True
        )
        downs.append(jnp.sum(by_chip.astype(F32), axis=0))

    down = jnp.concatenate(downs, axis=1)
    found = [down] + col_pieces(down)
    rows = []
    for col in range(cols):
        row = found[0]
        for step in (1, 2, 3):
            row = jnp.where(my_col ^ step == col, found[step], row)
        rows.append(row)
    grad_down = jnp.concatenate(rows, axis=0)

    small_sum = jnp.sum(small, axis=0)
    near, far, cross = col_pieces(small_sum)
    small_sum = (small_sum + near) + (far + cross)
    grad_msg = small_sum[:msg_share]
    grad_gate = small_sum[msg_share, :msg_share]
    return side_out, grad_down, grad_msg, grad_gate


def solution(mesh):
    rows, cols = mesh.devices.shape
    z = 4
    x = rows // (2 * z)
    split = Mesh(mesh.devices.reshape(z, x, 2, cols), ("z", "x", "core", "col"))
    each = ROWS + ("col",)
    placed = (
        P(each, None, None),
        P(),
        P("col", None),
        P(each, None, None, None),
        P(each, None),
        P(),
        P(),
        P(each, None),
    )
    return jax.shard_map(
        shards,
        mesh=split,
        in_specs=placed,
        out_specs=(P(each, None), P(ROWS, None), P(ROWS, None), P(ROWS)),
        check_vma=False,
    )
```

time: 1180 us -> 286 us (0.24)
  waiting for transfers between devices: 814 us -> 91.8 us
  local copies, waits for them, and re-layouts: 126 us -> 27.4 us
  blocking collectives: 98.1 us -> 0 us
  starting transfers between devices: 16.1 us -> 88.3 us
  other arithmetic: 66.7 us -> 7.04 us
  Pallas kernels: 0 us -> 51.2 us
  matrix products: 38.7 us -> 17.5 us
  between operations: 14.8 us -> 1.1 us
    reduce_scatter x2 -> x0, waiting for transfers between devices: 708 us -> none  [the longest x1 644 us: shards(): lax.psum_scatter(down_part, ('row', 'col'), scatter_dimension=0, tiled=True)]
    scatter x2 -> x0, local copies, waits for them, and re-layouts: 97.6 us -> none  [the longest x1 90.4 us: shards(): jnp.zeros((doc_count,), jnp.int32).at[landing].set(sources, mode='drop')]
    unnamed x2 -> x0, blocking collectives: 73.5 us -> none
    pallas_call x0 -> x11, Pallas kernels: none -> 51.2 us  [the longest x1 16.5 us: pool_and_pack(): pl.pallas_call(pool_kernel, grid=(docs // step,), in_specs=[whole(*owner_...]
    reduce_sum x2 -> x7, other arithmetic: 49.8 us -> 3.81 us  [the longest x2 1.96 us: shards(): by_col = jnp.sum(by_col.astype(F32), axis=0).astype(BF16)]
    all_gather x1 -> x0, waiting for transfers between devices: 38.9 us -> none  [shards(): gathered = lax.all_gather(owned, 'col', axis=0, tiled=True)]
    ppermute x0 -> x25, starting transfers between devices: none -> 36.6 us  [the longest x4 12.6 us: gather_col(): high = lax.ppermute(after[half:], 'col', down)]
    unnamed x5 -> x0, waiting for transfers between devices: 36.1 us -> none
  transfers between devices with their start and end apart: 6 -> 34, of which waited for: 5 -> 16; matrix products, arithmetic and copies ran while one was open for 10% -> 12% of each run, Pallas kernels for 0% -> 12%
where the time goes in v1:
time: 286 us; the launch traced here: 284 us
  waiting for transfers between devices  91.8 us (32%)
  starting transfers between devices  88.3 us (31%)
  Pallas kernels  51.2 us (18%)
  local copies, waits for them, and re-layouts  27.4 us (10%)
  matrix products  17.5 us (6%)
  other arithmetic  7.04 us (2%)
    all_to_all x4, waiting for transfers between devices, relay(): lax.all_to_all(rows.reshape(size, slots // size, width), ROWS, split_axis...  27.8 us
    all_to_all x4, starting transfers between devices, relay(): lax.all_to_all(rows.reshape(size, slots // size, width), ROWS, split_axis...  27 us
    all_to_all x2, waiting for transfers between devices, shards(): lax.all_to_all(down_part.astype(BF16).reshape(cols, chips * piece, wide),...  22.6 us
    ppermute x4, waiting for transfers between devices, gather_col(): before = lax.ppermute(part, 'col', up)  18.9 us
    unnamed x49, local copies, waits for them, and re-layouts  18.1 us
    pallas_call x1, Pallas kernels, pool_and_pack(): pl.pallas_call(pool_kernel, grid=(docs // step,), in_specs=[whole(*owner_...  16.5 us
    ppermute x4, starting transfers between devices, gather_col(): high = lax.ppermute(after[half:], 'col', down)  12.6 us
    all_to_all x2, starting transfers between devices, shards(): lax.all_to_all(by_col.reshape(chips, piece, wide), ('z', 'x'), split_axis...  12.2 us
  transfers between devices with their start and end apart: 34, of which 16 were waited for; matrix products, arithmetic and copies ran while one was open for 12% of the time, Pallas kernels for 12%

profile of v1, /device:TPU:0, one launch (start us, length us, event | category | flops | bytes accessed | tf_op | source)
XLA Modules:
  0.0 284.4 jit_solution(5614834073059047157)
XLA Ops:
  0.6 16.5 %shard_map.111 = (bf16[768,5120]{1,0:T(8,128)(2,1)}, bf16[2304,256]{1,0:T(8,128)(2,1)}, s32[1,768]{1,0:T(1,128)}) custom-call(s32[1,24576]{1,0:T(1,128)} %owner_ref.1, bf16[768,80,128]{2,1,0:T(8,128)(2,1)} %bitcast.69, bf16[5120,512]{1,0:T(8,128)(2,1)} %w_ref.3), custom_call_target="tpu_custom_call" | custom-call | flops 6000000000 | bytes 28000000 | tf_op jit(solution)/shard_map/pallas_call | solution.py:97
  17.1 8.3 %all-to-all-start.1 = ((bf16[32,72,256]{2,1,0:T(8,128)(2,1)}), bf16[32,72,256]{2,1,0:T(8,128)(2,1)S(1)}, u32[]{:S(2)}, u32[]{:S(2)}) async-start(bf16[32,72,256]{2,1,0:T(8,128)(2,1)} %bitcast.67), calls=%async_computation.1 | async-start | bytes 2359296 | tf_op jit(solution)/shard_map/all_to_all | solution.py:374
  25.4 3.2 %copy-done = bf16[768,5120]{1,0:T(8,128)(2,1)S(1)} copy-done((bf16[768,5120]{1,0:T(8,128)(2,1)S(1)}, bf16[768,5120]{1,0:T(8,128)(2,1)}, u32[]{:S(2)}) %copy-start) | copy-done | bytes 7864344
  28.6 2.5 copy-done.5
  31.8 6.1 %shard_map.112 = bf16[2304,256]{1,0:T(8,128)(2,1)} custom-call(s32[1,768]{1,0:T(1,128)S(1)} %copy-done.18, bf16[768,5120]{1,0:T(8,128)(2,1)S(1)} %copy-done, bf16[5120,512]{1,0:T(8,128)(2,1)S(1)} %copy-done.5), custom_call_target="tpu_custom_call" | custom-call | flops 3000000000 | bytes 12000000 | tf_op jit(solution)/shard_map/pallas_call | solution.py:141
  37.9 6.5 %all-to-all-done.1 = bf16[32,72,256]{2,1,0:T(8,128)(2,1)S(1)} async-done(((bf16[32,72,256]{2,1,0:T(8,128)(2,1)}), bf16[32,72,256]{2,1,0:T(8,128)(2,1)S(1)}, u32[]{:S(2)}, u32[]{:S(2)}) %all-to-all-start.1) | async-done | bytes 1179680 | tf_op jit(solution)/shard_map/all_to_all | solution.py:374
  44.4 3.9 %all-to-all-start = ((bf16[32,72,256]{2,1,0:T(8,128)(2,1)}), bf16[32,72,256]{2,1,0:T(8,128)(2,1)S(1)}, u32[]{:S(2)}, u32[]{:S(2)}) async-start(bf16[32,72,256]{2,1,0:T(8,128)(2,1)} %bitcast.7), calls=%async_computation | async-start | bytes 2359296 | tf_op jit(solution)/shard_map/all_to_all | solution.py:374
  49.1 1.5 shard_map.114.refs_0_.refs_6_
  50.6 1.7 collective-permute-start.5
  52.2 1.7 collective-permute-start.4
  53.9 13.5 %all-to-all-done = bf16[32,72,256]{2,1,0:T(8,128)(2,1)S(1)} async-done(((bf16[32,72,256]{2,1,0:T(8,128)(2,1)}), bf16[32,72,256]{2,1,0:T(8,128)(2,1)S(1)}, u32[]{:S(2)}, u32[]{:S(2)}) %all-to-all-start) | async-done | bytes 1179680 | tf_op jit(solution)/shard_map/all_to_all | solution.py:374
  67.4 2.3 shard_map.113.refs_0_
  69.6 1.6 collective-permute-start.1
  71.2 1.7 collective-permute-start
  72.9 3.2 %copy-done.1 = bf16[768,5120]{1,0:T(8,128)(2,1)S(1)} copy-done((bf16[768,5120]{1,0:T(8,128)(2,1)S(1)}, bf16[768,5120]{1,0:T(8,128)(2,1)}, u32[]{:S(2)}) %copy-start.1) | copy-done | bytes 7864344
  76.1 5.7 %shard_map.117 = (bf16[4,16,40,768]{3,2,1,0:T(8,128)(2,1)S(1)}, bf16[4,16,40,768]{3,2,1,0:T(8,128)(2,1)}) custom-call(bf16[768,5120]{1,0:T(8,128)(2,1)S(1)} %copy-done.1), custom_call_target="tpu_custom_call" | custom-call | flops 1000000000 | bytes 16000000 | tf_op jit(solution)/shard_map/pallas_call | solution.py:177
  81.8 1.9 copy-done.2
  83.8 1.7 slice.42
  85.9 1.6 slice.43
  87.5 2.9 %collective-permute-start.7 = (bf16[384,256]{1,0:T(8,128)(2,1)}, bf16[384,256]{1,0:T(8,128)(2,1)}, u32[]{:S(2)}, u32[]{:S(2)}) collective-permute-start(bf16[384,256]{1,0:T(8,128)(2,1)} %slice.43), channel_id=1, source_target_pairs={{0,3},{1,0},{2,1},{3,2},{4,7},{5,4},{6,5},{7,6},{8,11},{9,8},{10,9... | collective-permute-start | bytes 589832 | tf_op jit(solution)/shard_map/ppermute | solution.py:222
  91.8 3.2 %collective-permute-start.3 = (bf16[384,256]{1,0:T(8,128)(2,1)}, bf16[384,256]{1,0:T(8,128)(2,1)}, u32[]{:S(2)}, u32[]{:S(2)}) collective-permute-start(bf16[384,256]{1,0:T(8,128)(2,1)} %slice.41), channel_id=1, source_target_pairs={{0,3},{1,0},{2,1},{3,2},{4,7},{5,4},{6,5},{7,6},{8,11},{9,8},{10,9... | collective-permute-start | bytes 589832 | tf_op jit(solution)/shard_map/ppermute | solution.py:222
  95.3 2.0 shard_map.115.refs_5_
  97.3 2.0 collective-permute-done.2.refs_2_
  99.4 4.8 %shard_map.116 = (bf16[768,512]{1,0:T(8,128)(2,1)}, bf16[768,512]{1,0:T(8,128)(2,1)S(1)}, bf16[768,512]{1,0:T(8,128)(2,1)S(1)}, bf16[768,256]{1,0:T(8,128)(2,1)S...) custom-call(s32[24]{0:T(128)S(1)} %fusion.4.index_ref, bf16[24,128,128]{2,1,0:T(8,128)(2,1)S(1)} %bitcast.55, ...), custom_call_target="tpu_custom_call" | custom-call | flops 1200000000 | bytes 8000000 | tf_op jit(solution)/shard_map/pallas_call | solution.py:319
  108.8 2.0 fusion.9
  110.8 1.4 select_maximum_fusion
  112.1 4.7 %all-to-all-start.8 = ((f32[32,24,512]{2,1,0:T(8,128)}), f32[32,24,512]{2,1,0:T(8,128)}, u32[]{:S(2)}, u32[]{:S(2)}) async-start(f32[32,24,512]{2,1,0:T(8,128)} %select_maximum_fusion), calls=%async_computation.8 | async-start | bytes 3145728 | tf_op jit(solution)/shard_map/all_to_all | solution.py:433
  116.8 1.3 collective-permute-start.9
  118.1 2.6 collective-permute-start.8
  120.7 9.3 %collective-permute-done.9.refs_4_ = bf16[768,256]{1,0:T(8,128)(2,1)S(1)} collective-permute-done((bf16[768,256]{1,0:T(8,128)(2,1)S(1)}, bf16[768,256]{1,0:T(8,128)(2,1)S(1)}, u32[]{:S(2)}, u32[]{:S(2)}) %collective-permute-start.9) | collective-permute-done | bytes 393248 | tf_op jit(solution)/shard_map/ppermute | solution.py:219
  131.4 3.2 %collective-permute-start.11 = (bf16[384,256]{1,0:T(8,128)(2,1)}, bf16[384,256]{1,0:T(8,128)(2,1)}, u32[]{:S(2)}, u32[]{:S(2)}) collective-permute-start(bf16[384,256]{1,0:T(8,128)(2,1)} %slice.45), channel_id=1, source_target_pairs={{0,3},{1,0},{2,1},{3,2},{4,7},{5,4},{6,5},{7,6},{8,11},{9,8},{10,9... | collective-permute-start | bytes 589832 | tf_op jit(solution)/shard_map/ppermute | solution.py:222
  134.6 1.1 select_n.149.refs_6_
  135.7 3.0 %collective-permute-done.10.refs_2_ = bf16[384,256]{1,0:T(8,128)(2,1)} collective-permute-done((bf16[384,256]{1,0:T(8,128)(2,1)}, bf16[384,256]{1,0:T(8,128)(2,1)}, u32[]{:S(2)}, u32[]{:S(2)}) %collective-permute-start.10) | collective-permute-done | bytes 196640 | tf_op jit(solution)/shard_map/ppermute | solution.py:221
  139.7 4.2 %shard_map.118 = bf16[2304,256]{1,0:T(8,128)(2,1)S(1)} custom-call(s32[24]{0:T(128)S(1)} %fusion.4.index_ref, bf16[24,128,128]{2,1,0:T(8,128)(2,1)S(1)} %bitcast.56, bf16[768,256]{1,0:T(8,128)(2,1)S(1)} %copy-done.17, bf16[768,256]{1,0:T(8,128)(2,1)S(1)} %collective-permute-done.8.refs_1_, bf16[384,256]{1,0:T(8,128)(2,1)} %collective-permute-done.10.refs_2_, ...), custom_call_target="tpu_custom_call" | custom-call | flops 905969664 | bytes 5000000 | tf_op jit(solution)/shard_map/pallas_call | solution.py:356
  143.9 1.0 copy-done.6
  145.0 7.7 %all-to-all-start.2 = ((bf16[32,72,256]{2,1,0:T(8,128)(2,1)}), bf16[32,72,256]{2,1,0:T(8,128)(2,1)}, u32[]{:S(2)}, u32[]{:S(2)}) async-start(bf16[32,72,256]{2,1,0:T(8,128)(2,1)} %bitcast.58), calls=%async_computation.2 | async-start | bytes 2359296 | tf_op jit(solution)/shard_map/all_to_all | solution.py:374
  153.0 3.4 %collective-permute-start.14 = (bf16[768,256]{1,0:T(8,128)(2,1)}, bf16[768,256]{1,0:T(8,128)(2,1)S(1)}, u32[]{:S(2)}, u32[]{:S(2)}) collective-permute-start(bf16[768,256]{1,0:T(8,128)(2,1)} %copy-done.13), channel_id=1, source_target_pairs={{0,3},{1,0},{2,1},{3,2},{4,7},{5,4},{6,5},{7,6},{8,11},{9,8},{10,9... | collective-permute-start | bytes 1179656 | tf_op jit(solution)/shard_map/ppermute | solution.py:220
  156.5 9.6 %collective-permute-done.15.refs_4_ = bf16[768,256]{1,0:T(8,128)(2,1)S(1)} collective-permute-done((bf16[768,256]{1,0:T(8,128)(2,1)}, bf16[768,256]{1,0:T(8,128)(2,1)S(1)}, u32[]{:S(2)}, u32[]{:S(2)}) %collective-permute-start.15) | collective-permute-done | bytes 393248 | tf_op jit(solution)/shard_map/ppermute | solution.py:219
  166.2 3.3 %collective-permute-start.17 = (bf16[384,256]{1,0:T(8,128)(2,1)S(1)}, bf16[384,256]{1,0:T(8,128)(2,1)S(1)}, u32[]{:S(2)}, u32[]{:S(2)}) collective-permute-start(bf16[384,256]{1,0:T(8,128)(2,1)S(1)} %slice.47), channel_id=1, source_target_pairs={{0,3},{1,0},{2,1},{3,2},{4,7},{5,4},{6,5},{7,6},{8,11},{9,8},{10,9... | collective-permute-start | bytes 589832 | tf_op jit(solution)/shard_map/ppermute | solution.py:222
  169.5 4.5 %collective-permute-done.16.refs_2_ = bf16[384,256]{1,0:T(8,128)(2,1)S(1)} collective-permute-done((bf16[384,256]{1,0:T(8,128)(2,1)S(1)}, bf16[384,256]{1,0:T(8,128)(2,1)S(1)}, u32[]{:S(2)}, u32[]{:S(2)}) %collective-permute-start.16) | collective-permute-done | bytes 196640 | tf_op jit(solution)/shard_map/ppermute | solution.py:221
  174.0 3.7 %shard_map.120 = bf16[2304,256]{1,0:T(8,128)(2,1)S(1)} custom-call(s32[24]{0:T(128)S(1)} %fusion.4.index_ref, bf16[24,128,128]{2,1,0:T(8,128)(2,1)S(1)} %bitcast.57, bf16[768,256]{1,0:T(8,128)(2,1)S(1)} %copy-done.14, bf16[768,256]{1,0:T(8,128)(2,1)S(1)} %collective-permute-done.14.refs_1_, bf16[384,256]{1,0:T(8,128)(2,1)S(1)} %collective-permute-done.16.refs_2_, ...), custom_call_target="tpu_custom_call" | custom-call | flops 905969664 | bytes 5000000 | tf_op jit(solution)/shard_map/pallas_call | solution.py:356
  177.7 1.0 copy-done.7
  178.7 7.1 %all-to-all-start.5 = ((bf16[32,72,256]{2,1,0:T(8,128)(2,1)}), bf16[32,72,256]{2,1,0:T(8,128)(2,1)S(1)}, u32[]{:S(2)}, u32[]{:S(2)}) async-start(bf16[32,72,256]{2,1,0:T(8,128)(2,1)} %bitcast.59), calls=%async_computation.5 | async-start | bytes 2359296 | tf_op jit(solution)/shard_map/all_to_all | solution.py:374
  186.0 2.9 %shard_map.119 = bf16[768,256]{1,0:T(8,128)(2,1)S(1)} custom-call(s32[768,1]{1,0:T(8,128)S(1)} %copy.25.place_ref, bf16[2304,256]{1,0:T(8,128)(2,1)} %bitcast.16.table_ref), custom_call_target="tpu_custom_call" | custom-call | flops 905969664 | bytes 2000000 | tf_op jit(solution)/shard_map/pallas_call | solution.py:204
  189.3 3.3 %fusion.7 = f32[2560,256]{1,0:T(8,128)S(1)} fusion(bf16[2560,768]{1,0:T(8,128)(2,1)} %bitcast.52, bf16[768,256]{1,0:T(8,128)(2,1)S(1)} %shard_map.119), kind=kOutput, calls=%fused_computation.31 | convolution fusion | flops 1006632960 | bytes 6946816 | tf_op jit(solution)/shard_map/dot_general | solution.py:442
  192.6 4.5 %fusion = bf16[2560,256]{1,0:T(8,128)(2,1)} fusion(f32[2560,256]{1,0:T(8,128)S(1)} %fusion.7, bf16[2560,768]{1,0:T(8,128)(2,1)} %collective-permute-done.12, bf16[768,256]{1,0:T(8,128)(2,1)S(1)} %collective-permute-done.13), kind=kOutput, calls=%fused_computation.2 | convolution fusion | flops 1007943680 | bytes 8257536 | tf_op jit(solution)/shard_map/dot_general | solution.py:442
  197.1 7.8 %all-to-all-done.5 = bf16[32,72,256]{2,1,0:T(8,128)(2,1)S(1)} async-done(((bf16[32,72,256]{2,1,0:T(8,128)(2,1)}), bf16[32,72,256]{2,1,0:T(8,128)(2,1)S(1)}, u32[]{:S(2)}, u32[]{:S(2)}) %all-to-all-start.5) | async-done | bytes 1179680 | tf_op jit(solution)/shard_map/all_to_all | solution.py:374
  204.9 4.3 %all-to-all-start.3 = ((bf16[4,640,256]{2,1,0:T(8,128)(2,1)}), bf16[4,640,256]{2,1,0:T(8,128)(2,1)S(1)}, u32[]{:S(2)}, u32[]{:S(2)}) async-start(bf16[4,640,256]{2,1,0:T(8,128)(2,1)} %bitcast.18), calls=%async_computation.3 | async-start | bytes 2621440 | tf_op jit(solution)/shard_map/all_to_all | solution.py:445
  209.2 1.6 shard_map.121
  210.9 3.3 %fusion.8 = f32[2560,256]{1,0:T(8,128)S(1)} fusion(bf16[2560,768]{1,0:T(8,128)(2,1)} %bitcast.53, bf16[768,256]{1,0:T(8,128)(2,1)S(1)} %shard_map.121), kind=kOutput, calls=%fused_computation.32 | convolution fusion | flops 1006632960 | bytes 6946816 | tf_op jit(solution)/shard_map/dot_general | solution.py:442
  214.2 4.5 %fusion.1 = bf16[2560,256]{1,0:T(8,128)(2,1)} fusion(f32[2560,256]{1,0:T(8,128)S(1)} %fusion.8, bf16[2560,768]{1,0:T(8,128)(2,1)} %collective-permute-done.12, bf16[768,256]{1,0:T(8,128)(2,1)S(1)} %collective-permute-done.18), kind=kOutput, calls=%fused_computation.3 | convolution fusion | flops 1007943680 | bytes 8257536 | tf_op jit(solution)/shard_map/dot_general | solution.py:442
  218.7 7.5 %all-to-all-done.3 = bf16[4,640,256]{2,1,0:T(8,128)(2,1)S(1)} async-done(((bf16[4,640,256]{2,1,0:T(8,128)(2,1)}), bf16[4,640,256]{2,1,0:T(8,128)(2,1)S(1)}, u32[]{:S(2)}, u32[]{:S(2)}) %all-to-all-start.3) | async-done | bytes 1310752 | tf_op jit(solution)/shard_map/all_to_all | solution.py:445
  226.2 3.5 %all-to-all-start.6 = ((bf16[4,640,256]{2,1,0:T(8,128)(2,1)}), bf16[4,640,256]{2,1,0:T(8,128)(2,1)S(1)}, u32[]{:S(2)}, u32[]{:S(2)}) async-start(bf16[4,640,256]{2,1,0:T(8,128)(2,1)} %bitcast.22), calls=%async_computation.6 | async-start | bytes 2621440 | tf_op jit(solution)/shard_map/all_to_all | solution.py:445
  230.7 15.1 %all-to-all-done.6 = bf16[4,640,256]{2,1,0:T(8,128)(2,1)S(1)} async-done(((bf16[4,640,256]{2,1,0:T(8,128)(2,1)}), bf16[4,640,256]{2,1,0:T(8,128)(2,1)S(1)}, u32[]{:S(2)}, u32[]{:S(2)}) %all-to-all-start.6) | async-done | bytes 1310752 | tf_op jit(solution)/shard_map/all_to_all | solution.py:445
  245.8 6.7 %all-to-all-start.4 = ((bf16[16,40,256]{2,1,0:T(8,128)(2,1)}), bf16[16,40,256]{2,1,0:T(8,128)(2,1)S(1)}, u32[]{:S(2)}, u32[]{:S(2)}) async-start(bf16[16,40,256]{2,1,0:T(8,128)(2,1)} %bitcast.19), calls=%async_computation.4 | async-start | bytes 655360 | tf_op jit(solution)/shard_map/all_to_all | solution.py:450
  252.5 1.5 reduce_sum.75
  254.7 2.1 collective-permute-start.23
  256.7 2.1 collective-permute-start.24
  259.8 1.8 all-to-all-done.4
  261.6 5.5 %all-to-all-start.7 = ((bf16[16,40,256]{2,1,0:T(8,128)(2,1)}), bf16[16,40,256]{2,1,0:T(8,128)(2,1)S(1)}, u32[]{:S(2)}, u32[]{:S(2)}) async-start(bf16[16,40,256]{2,1,0:T(8,128)(2,1)} %bitcast.23), calls=%async_computation.7 | async-start | bytes 655360 | tf_op jit(solution)/shard_map/all_to_all | solution.py:450
  267.1 8.9 %all-to-all-done.7 = bf16[16,40,256]{2,1,0:T(8,128)(2,1)S(1)} async-done(((bf16[16,40,256]{2,1,0:T(8,128)(2,1)}), bf16[16,40,256]{2,1,0:T(8,128)(2,1)S(1)}, u32[]{:S(2)}, u32[]{:S(2)}) %all-to-all-start.7) | async-done | bytes 327712 | tf_op jit(solution)/shard_map/all_to_all | solution.py:450
  276.1 1.2 collective-permute-start.19
  277.6 2.7 collective-permute-start.21
  281.9 1.5 collective-permute-done.20
  (102 shorter events, 17.3 us)
Async XLA Ops:
  17.1 27.3 %all-to-all-start.1 = ((bf16[32,72,256]{2,1,0:T(8,128)(2,1)}), bf16[32,72,256]{2,1,0:T(8,128)(2,1)S(1)}, u32[]{:S(2)}, u32[]{:S(2)}) async-start(bf16[32,72,256]{2,1,0:T(8,128)(2,1)} %bitcast.67), calls=%async_computation.1 | async-start | bytes 2359296 | tf_op jit(solution)/shard_map/all_to_all | solution.py:374
  25.4 3.2 %copy-start = (bf16[768,5120]{1,0:T(8,128)(2,1)S(1)}, bf16[768,5120]{1,0:T(8,128)(2,1)}, u32[]{:S(2)}) copy-start(bf16[768,5120]{1,0:T(8,128)(2,1)} %get-tuple-element.16.pooled_ref) | copy-start | bytes 23592964
  28.6 2.5 copy-start.5
  31.1 0.7 copy-start.18
  31.8 16.6 %copy-start.22 = (s32[1,24576]{1,0:T(1,128)S(1)}, s32[1,24576]{1,0:T(1,128)}, u32[]{:S(2)}) copy-start(s32[1,24576]{1,0:T(1,128)} %owner_ref.1) | copy-start | bytes 294916
  44.4 23.0 %all-to-all-start = ((bf16[32,72,256]{2,1,0:T(8,128)(2,1)}), bf16[32,72,256]{2,1,0:T(8,128)(2,1)S(1)}, u32[]{:S(2)}, u32[]{:S(2)}) async-start(bf16[32,72,256]{2,1,0:T(8,128)(2,1)} %bitcast.7), calls=%async_computation | async-start | bytes 2359296 | tf_op jit(solution)/shard_map/all_to_all | solution.py:374
  49.0 20.6 %copy-start.21 = (s32[32,72]{1,0:T(8,128)}, s32[32,72]{1,0:T(8,128)S(1)}, u32[]{:S(2)}) copy-start(s32[32,72]{1,0:T(8,128)S(1)} %add_select_fusion) | copy-start | bytes 27652
  50.6 33.2 %collective-permute-start.5 = (bf16[768,256]{1,0:T(8,128)(2,1)S(1)}, bf16[768,256]{1,0:T(8,128)(2,1)}, u32[]{:S(2)}, u32[]{:S(2)}) collective-permute-start(bf16[768,256]{1,0:T(8,128)(2,1)S(1)} %shard_map.114.refs_0_.refs_6_), channel_id=1, source_target_pairs={{0,1},{1,2},{2,3},{3,0},{4,5},{5,6},{6,7},{7,4},{8,9},{9,10},{10,1... | collective-permute-start | bytes 1179656 | tf_op jit(solution)/shard_map/ppermute | solution.py:219
  52.2 33.6 %collective-permute-start.4 = (bf16[768,256]{1,0:T(8,128)(2,1)S(1)}, bf16[768,256]{1,0:T(8,128)(2,1)}, u32[]{:S(2)}, u32[]{:S(2)}) collective-permute-start(bf16[768,256]{1,0:T(8,128)(2,1)S(1)} %shard_map.114.refs_0_.refs_6_), channel_id=1, source_target_pairs={{0,3},{1,0},{2,1},{3,2},{4,7},{5,4},{6,5},{7,6},{8,11},{9,8},{10,9... | collective-permute-start | bytes 1179656 | tf_op jit(solution)/shard_map/ppermute | solution.py:220
  67.4 27.7 %copy-start.23 = (s32[1,24]{1,0:T(1,128)S(1)}, s32[1,24]{1,0:T(1,128)}, u32[]{:S(2)}) copy-start(s32[1,24]{1,0:T(1,128)} %param.12) | copy-start | bytes 292
  67.4 27.7 %copy-start.8 = (bf16[512,512]{1,0:T(8,128)(2,1)S(1)}, bf16[512,512]{1,0:T(8,128)(2,1)}, u32[]{:S(2)}) copy-start(bf16[512,512]{1,0:T(8,128)(2,1)} %refs_8_.1) | copy-start | bytes 1572868
  69.6 20.7 %collective-permute-start.1 = (bf16[768,256]{1,0:T(8,128)(2,1)}, bf16[768,256]{1,0:T(8,128)(2,1)S(1)}, u32[]{:S(2)}, u32[]{:S(2)}) collective-permute-start(bf16[768,256]{1,0:T(8,128)(2,1)} %shard_map.113.refs_0_), channel_id=1, source_target_pairs={{0,1},{1,2},{2,3},{3,0},{4,5},{5,6},{6,7},{7,4},{8,9},{9,10},{10,1... | collective-permute-start | bytes 1179656 | tf_op jit(solution)/shard_map/ppermute | solution.py:219
  71.2 19.8 %collective-permute-start = (bf16[768,256]{1,0:T(8,128)(2,1)}, bf16[768,256]{1,0:T(8,128)(2,1)S(1)}, u32[]{:S(2)}, u32[]{:S(2)}) collective-permute-start(bf16[768,256]{1,0:T(8,128)(2,1)} %shard_map.113.refs_0_), channel_id=1, source_target_pairs={{0,3},{1,0},{2,1},{3,2},{4,7},{5,4},{6,5},{7,6},{8,11},{9,8},{10,9... | collective-permute-start | bytes 1179656 | tf_op jit(solution)/shard_map/ppermute | solution.py:220
  72.9 3.2 %copy-start.1 = (bf16[768,5120]{1,0:T(8,128)(2,1)S(1)}, bf16[768,5120]{1,0:T(8,128)(2,1)}, u32[]{:S(2)}) copy-start(bf16[768,5120]{1,0:T(8,128)(2,1)} %get-tuple-element.16.pooled_ref) | copy-start | bytes 23592964
  81.8 1.9 copy-start.2
  83.7 11.6 %copy-start.3 = (bf16[1,24,128,128]{3,2,1,0:T(8,128)(2,1)S(1)}, bf16[1,24,128,128]{3,2,1,0:T(8,128)(2,1)}, u32[]{:S(2)}) copy-start(bf16[1,24,128,128]{3,2,1,0:T(8,128)(2,1)} %param.11) | copy-start | bytes 2359300
  83.7 108.8 %collective-permute-start.12 = (bf16[2560,768]{1,0:T(8,128)(2,1)}, bf16[2560,768]{1,0:T(8,128)(2,1)}, u32[]{:S(2)}, u32[]{:S(2)}) collective-permute-start(bf16[2560,768]{1,0:T(8,128)(2,1)} %bitcast.17), channel_id=1, source_target_pairs={{0,4},{4,0},{1,5},{5,1},{2,6},{6,2},{3,7},{7,3},{8,12},{12,8},{9,1... | collective-permute-start | bytes 11796488 | tf_op jit(solution)/shard_map/ppermute | solution.py:423
  83.7 15.6 %copy-start.4 = (bf16[768,512]{1,0:T(8,128)(2,1)S(1)}, bf16[768,512]{1,0:T(8,128)(2,1)}, u32[]{:S(2)}) copy-start(bf16[768,512]{1,0:T(8,128)(2,1)} %refs_5_.3) | copy-start | bytes 2359300
  83.8 15.6 %copy-start.20 = (f32[512]{0:T(512)S(1)}, f32[512]{0:T(512)}, u32[]{:S(2)}) copy-start(f32[512]{0:T(512)} %param.14) | copy-start | bytes 6148
  85.5 9.8 %collective-permute-start.6 = (bf16[384,256]{1,0:T(8,128)(2,1)}, bf16[384,256]{1,0:T(8,128)(2,1)}, u32[]{:S(2)}, u32[]{:S(2)}) collective-permute-start(bf16[384,256]{1,0:T(8,128)(2,1)} %slice.42), channel_id=1, source_target_pairs={{0,1},{1,2},{2,3},{3,0},{4,5},{5,6},{6,7},{7,4},{8,9},{9,10},{10,1... | collective-permute-start | bytes 589832 | tf_op jit(solution)/shard_map/ppermute | solution.py:221
  87.5 7.8 %collective-permute-start.7 = (bf16[384,256]{1,0:T(8,128)(2,1)}, bf16[384,256]{1,0:T(8,128)(2,1)}, u32[]{:S(2)}, u32[]{:S(2)}) collective-permute-start(bf16[384,256]{1,0:T(8,128)(2,1)} %slice.43), channel_id=1, source_target_pairs={{0,3},{1,0},{2,1},{3,2},{4,7},{5,4},{6,5},{7,6},{8,11},{9,8},{10,9... | collective-permute-start | bytes 589832 | tf_op jit(solution)/shard_map/ppermute | solution.py:222
  91.1 8.2 %collective-permute-start.2 = (bf16[384,256]{1,0:T(8,128)(2,1)}, bf16[384,256]{1,0:T(8,128)(2,1)}, u32[]{:S(2)}, u32[]{:S(2)}) collective-permute-start(bf16[384,256]{1,0:T(8,128)(2,1)} %slice.40), channel_id=1, source_target_pairs={{0,1},{1,2},{2,3},{3,0},{4,5},{5,6},{6,7},{7,4},{8,9},{9,10},{10,1... | collective-permute-start | bytes 589832 | tf_op jit(solution)/shard_map/ppermute | solution.py:221
  91.1 4.0 %copy-start.9 = (bf16[768,256]{1,0:T(8,128)(2,1)}, bf16[768,256]{1,0:T(8,128)(2,1)S(1)}, u32[]{:S(2)}) copy-start(bf16[768,256]{1,0:T(8,128)(2,1)S(1)} %collective-permute-done.refs_1_) | copy-start | bytes 1179652
  91.8 7.6 %collective-permute-start.3 = (bf16[384,256]{1,0:T(8,128)(2,1)}, bf16[384,256]{1,0:T(8,128)(2,1)}, u32[]{:S(2)}, u32[]{:S(2)}) collective-permute-start(bf16[384,256]{1,0:T(8,128)(2,1)} %slice.41), channel_id=1, source_target_pairs={{0,3},{1,0},{2,1},{3,2},{4,7},{5,4},{6,5},{7,6},{8,11},{9,8},{10,9... | collective-permute-start | bytes 589832 | tf_op jit(solution)/shard_map/ppermute | solution.py:222
  95.3 4.1 %copy-start.10 = (bf16[768,256]{1,0:T(8,128)(2,1)S(1)}, bf16[768,256]{1,0:T(8,128)(2,1)}, u32[]{:S(2)}) copy-start(bf16[768,256]{1,0:T(8,128)(2,1)} %copy-done.9) | copy-start | bytes 1179652
  104.2 0.9 copy-start.11
  105.1 0.9 copy-start.12
  106.0 0.7 copy-start.13
  106.8 0.8 copy-start.15
  110.8 6.1 %copy-start.16 = (bf16[768,256]{1,0:T(8,128)(2,1)S(1)}, bf16[768,256]{1,0:T(8,128)(2,1)}, u32[]{:S(2)}) copy-start(bf16[768,256]{1,0:T(8,128)(2,1)} %copy-done.15) | copy-start | bytes 1179652
  112.1 32.8 %all-to-all-start.8 = ((f32[32,24,512]{2,1,0:T(8,128)}), f32[32,24,512]{2,1,0:T(8,128)}, u32[]{:S(2)}, u32[]{:S(2)}) async-start(f32[32,24,512]{2,1,0:T(8,128)} %select_maximum_fusion), calls=%async_computation.8 | async-start | bytes 3145728 | tf_op jit(solution)/shard_map/all_to_all | solution.py:433
  116.8 13.2 %collective-permute-start.9 = (bf16[768,256]{1,0:T(8,128)(2,1)S(1)}, bf16[768,256]{1,0:T(8,128)(2,1)S(1)}, u32[]{:S(2)}, u32[]{:S(2)}) collective-permute-start(bf16[768,256]{1,0:T(8,128)(2,1)S(1)} %copy-done.16), channel_id=1, source_target_pairs={{0,1},{1,2},{2,3},{3,0},{4,5},{5,6},{6,7},{7,4},{8,9},{9,10},{10,1... | collective-permute-start | bytes 1179656 | tf_op jit(solution)/shard_map/ppermute | solution.py:219
  118.1 12.6 %collective-permute-start.8 = (bf16[768,256]{1,0:T(8,128)(2,1)S(1)}, bf16[768,256]{1,0:T(8,128)(2,1)S(1)}, u32[]{:S(2)}, u32[]{:S(2)}) collective-permute-start(bf16[768,256]{1,0:T(8,128)(2,1)S(1)} %copy-done.16), channel_id=1, source_target_pairs={{0,3},{1,0},{2,1},{3,2},{4,7},{5,4},{6,5},{7,6},{8,11},{9,8},{10,9... | collective-permute-start | bytes 1179656 | tf_op jit(solution)/shard_map/ppermute | solution.py:220
  130.7 8.0 %collective-permute-start.10 = (bf16[384,256]{1,0:T(8,128)(2,1)}, bf16[384,256]{1,0:T(8,128)(2,1)}, u32[]{:S(2)}, u32[]{:S(2)}) collective-permute-start(bf16[384,256]{1,0:T(8,128)(2,1)} %slice.44), channel_id=1, source_target_pairs={{0,1},{1,2},{2,3},{3,0},{4,5},{5,6},{6,7},{7,4},{8,9},{9,10},{10,1... | collective-permute-start | bytes 589832 | tf_op jit(solution)/shard_map/ppermute | solution.py:221
  131.4 7.3 %collective-permute-start.11 = (bf16[384,256]{1,0:T(8,128)(2,1)}, bf16[384,256]{1,0:T(8,128)(2,1)}, u32[]{:S(2)}, u32[]{:S(2)}) collective-permute-start(bf16[384,256]{1,0:T(8,128)(2,1)} %slice.45), channel_id=1, source_target_pairs={{0,3},{1,0},{2,1},{3,2},{4,7},{5,4},{6,5},{7,6},{8,11},{9,8},{10,9... | collective-permute-start | bytes 589832 | tf_op jit(solution)/shard_map/ppermute | solution.py:222
  138.7 1.0 copy-start.17
  143.9 1.0 copy-start.6
  145.0 29.0 %copy-start.14 = (bf16[768,256]{1,0:T(8,128)(2,1)S(1)}, bf16[768,256]{1,0:T(8,128)(2,1)}, u32[]{:S(2)}) copy-start(bf16[768,256]{1,0:T(8,128)(2,1)} %copy-done.13) | copy-start | bytes 1179652
  145.0 33.8 %all-to-all-start.2 = ((bf16[32,72,256]{2,1,0:T(8,128)(2,1)}), bf16[32,72,256]{2,1,0:T(8,128)(2,1)}, u32[]{:S(2)}, u32[]{:S(2)}) async-start(bf16[32,72,256]{2,1,0:T(8,128)(2,1)} %bitcast.58), calls=%async_computation.2 | async-start | bytes 2359296 | tf_op jit(solution)/shard_map/all_to_all | solution.py:374
  152.6 13.4 %collective-permute-start.15 = (bf16[768,256]{1,0:T(8,128)(2,1)}, bf16[768,256]{1,0:T(8,128)(2,1)S(1)}, u32[]{:S(2)}, u32[]{:S(2)}) collective-permute-start(bf16[768,256]{1,0:T(8,128)(2,1)} %copy-done.13), channel_id=1, source_target_pairs={{0,1},{1,2},{2,3},{3,0},{4,5},{5,6},{6,7},{7,4},{8,9},{9,10},{10,1... | collective-permute-start | bytes 1179656 | tf_op jit(solution)/shard_map/ppermute | solution.py:219
  153.0 13.1 %collective-permute-start.14 = (bf16[768,256]{1,0:T(8,128)(2,1)}, bf16[768,256]{1,0:T(8,128)(2,1)S(1)}, u32[]{:S(2)}, u32[]{:S(2)}) collective-permute-start(bf16[768,256]{1,0:T(8,128)(2,1)} %copy-done.13), channel_id=1, source_target_pairs={{0,3},{1,0},{2,1},{3,2},{4,7},{5,4},{6,5},{7,6},{8,11},{9,8},{10,9... | collective-permute-start | bytes 1179656 | tf_op jit(solution)/shard_map/ppermute | solution.py:220
  166.1 7.9 %collective-permute-start.16 = (bf16[384,256]{1,0:T(8,128)(2,1)S(1)}, bf16[384,256]{1,0:T(8,128)(2,1)S(1)}, u32[]{:S(2)}, u32[]{:S(2)}) collective-permute-start(bf16[384,256]{1,0:T(8,128)(2,1)S(1)} %slice.46), channel_id=1, source_target_pairs={{0,1},{1,2},{2,3},{3,0},{4,5},{5,6},{6,7},{7,4},{8,9},{9,10},{10,1... | collective-permute-start | bytes 589832 | tf_op jit(solution)/shard_map/ppermute | solution.py:221
  166.2 19.6 %copy-start.19 = (s32[1,768]{1,0:T(1,128)S(1)}, s32[1,768]{1,0:T(1,128)}, u32[]{:S(2)}) copy-start(s32[1,768]{1,0:T(1,128)} %get-tuple-element.15.slot_ref) | copy-start | bytes 9220
  166.2 7.8 %collective-permute-start.17 = (bf16[384,256]{1,0:T(8,128)(2,1)S(1)}, bf16[384,256]{1,0:T(8,128)(2,1)S(1)}, u32[]{:S(2)}, u32[]{:S(2)}) collective-permute-start(bf16[384,256]{1,0:T(8,128)(2,1)S(1)} %slice.47), channel_id=1, source_target_pairs={{0,3},{1,0},{2,1},{3,2},{4,7},{5,4},{6,5},{7,6},{8,11},{9,8},{10,9... | collective-permute-start | bytes 589832 | tf_op jit(solution)/shard_map/ppermute | solution.py:222
  177.7 1.0 copy-start.7
  178.7 26.1 %all-to-all-start.5 = ((bf16[32,72,256]{2,1,0:T(8,128)(2,1)}), bf16[32,72,256]{2,1,0:T(8,128)(2,1)S(1)}, u32[]{:S(2)}, u32[]{:S(2)}) async-start(bf16[32,72,256]{2,1,0:T(8,128)(2,1)} %bitcast.59), calls=%async_computation.5 | async-start | bytes 2359296 | tf_op jit(solution)/shard_map/all_to_all | solution.py:374
  188.9 3.7 %collective-permute-start.13 = (bf16[768,256]{1,0:T(8,128)(2,1)S(1)}, bf16[768,256]{1,0:T(8,128)(2,1)S(1)}, u32[]{:S(2)}, u32[]{:S(2)}) collective-permute-start(bf16[768,256]{1,0:T(8,128)(2,1)S(1)} %shard_map.119), channel_id=1, source_target_pairs={{0,4},{4,0},{1,5},{5,1},{2,6},{6,2},{3,7},{7,3},{8,12},{12,8},{9,1... | collective-permute-start | bytes 1179656 | tf_op jit(solution)/shard_map/ppermute | solution.py:441
  204.9 21.3 %all-to-all-start.3 = ((bf16[4,640,256]{2,1,0:T(8,128)(2,1)}), bf16[4,640,256]{2,1,0:T(8,128)(2,1)S(1)}, u32[]{:S(2)}, u32[]{:S(2)}) async-start(bf16[4,640,256]{2,1,0:T(8,128)(2,1)} %bitcast.18), calls=%async_computation.3 | async-start | bytes 2621440 | tf_op jit(solution)/shard_map/all_to_all | solution.py:445
  210.8 3.4 %collective-permute-start.18 = (bf16[768,256]{1,0:T(8,128)(2,1)S(1)}, bf16[768,256]{1,0:T(8,128)(2,1)S(1)}, u32[]{:S(2)}, u32[]{:S(2)}) collective-permute-start(bf16[768,256]{1,0:T(8,128)(2,1)S(1)} %shard_map.121), channel_id=1, source_target_pairs={{0,4},{4,0},{1,5},{5,1},{2,6},{6,2},{3,7},{7,3},{8,12},{12,8},{9,1... | collective-permute-start | bytes 1179656 | tf_op jit(solution)/shard_map/ppermute | solution.py:441
  226.2 19.6 %all-to-all-start.6 = ((bf16[4,640,256]{2,1,0:T(8,128)(2,1)}), bf16[4,640,256]{2,1,0:T(8,128)(2,1)S(1)}, u32[]{:S(2)}, u32[]{:S(2)}) async-start(bf16[4,640,256]{2,1,0:T(8,128)(2,1)} %bitcast.22), calls=%async_computation.6 | async-start | bytes 2621440 | tf_op jit(solution)/shard_map/all_to_all | solution.py:445
  245.8 15.8 %all-to-all-start.4 = ((bf16[16,40,256]{2,1,0:T(8,128)(2,1)}), bf16[16,40,256]{2,1,0:T(8,128)(2,1)S(1)}, u32[]{:S(2)}, u32[]{:S(2)}) async-start(bf16[16,40,256]{2,1,0:T(8,128)(2,1)} %bitcast.19), calls=%async_computation.4 | async-start | bytes 655360 | tf_op jit(solution)/shard_map/all_to_all | solution.py:450
  254.0 13.0 %collective-permute-start.22 = (f32[24,512]{1,0:T(8,128)S(1)}, f32[24,512]{1,0:T(8,128)S(1)}, u32[]{:S(2)}, u32[]{:S(2)}) collective-permute-start(f32[24,512]{1,0:T(8,128)S(1)} %reduce_sum.75), channel_id=1, source_target_pairs={{0,1},{1,0},{2,3},{3,2},{4,5},{5,4},{6,7},{7,6},{8,9},{9,8},{10,11... | collective-permute-start | bytes 147464 | tf_op jit(solution)/shard_map/ppermute | solution.py:381
  254.7 12.4 %collective-permute-start.23 = (f32[24,512]{1,0:T(8,128)S(1)}, f32[24,512]{1,0:T(8,128)S(1)}, u32[]{:S(2)}, u32[]{:S(2)}) collective-permute-start(f32[24,512]{1,0:T(8,128)S(1)} %reduce_sum.75), channel_id=1, source_target_pairs={{0,2},{1,3},{2,0},{3,1},{4,6},{5,7},{6,4},{7,5},{8,10},{9,11},{10,... | collective-permute-start | bytes 147464 | tf_op jit(solution)/shard_map/ppermute | solution.py:381
  256.7 10.3 %collective-permute-start.24 = (f32[24,512]{1,0:T(8,128)S(1)}, f32[24,512]{1,0:T(8,128)S(1)}, u32[]{:S(2)}, u32[]{:S(2)}) collective-permute-start(f32[24,512]{1,0:T(8,128)S(1)} %reduce_sum.75), channel_id=1, source_target_pairs={{0,3},{1,2},{2,1},{3,0},{4,7},{5,6},{6,5},{7,4},{8,11},{9,10},{10,... | collective-permute-start | bytes 147464 | tf_op jit(solution)/shard_map/ppermute | solution.py:381
  261.6 14.5 %all-to-all-start.7 = ((bf16[16,40,256]{2,1,0:T(8,128)(2,1)}), bf16[16,40,256]{2,1,0:T(8,128)(2,1)S(1)}, u32[]{:S(2)}, u32[]{:S(2)}) async-start(bf16[16,40,256]{2,1,0:T(8,128)(2,1)} %bitcast.23), calls=%async_computation.7 | async-start | bytes 655360 | tf_op jit(solution)/shard_map/all_to_all | solution.py:450
  276.1 5.7 %collective-permute-start.19 = (f32[40,512]{1,0:T(8,128)S(1)}, f32[40,512]{1,0:T(8,128)S(1)}, u32[]{:S(2)}, u32[]{:S(2)}) collective-permute-start(f32[40,512]{1,0:T(8,128)S(1)} %pad_maximum_fusion.1), channel_id=1, source_target_pairs={{0,3},{1,2},{2,1},{3,0},{4,7},{5,6},{6,5},{7,4},{8,11},{9,10},{10,... | collective-permute-start | bytes 245768 | tf_op jit(solution)/shard_map/ppermute | solution.py:381
  277.4 5.9 %collective-permute-start.20 = (f32[40,512]{1,0:T(8,128)S(1)}, f32[40,512]{1,0:T(8,128)S(1)}, u32[]{:S(2)}, u32[]{:S(2)}) collective-permute-start(f32[40,512]{1,0:T(8,128)S(1)} %pad_maximum_fusion.1), channel_id=1, source_target_pairs={{0,2},{1,3},{2,0},{3,1},{4,6},{5,7},{6,4},{7,5},{8,10},{9,11},{10,... | collective-permute-start | bytes 245768 | tf_op jit(solution)/shard_map/ppermute | solution.py:381
  277.6 6.0 %collective-permute-start.21 = (f32[40,512]{1,0:T(8,128)S(1)}, f32[40,512]{1,0:T(8,128)S(1)}, u32[]{:S(2)}, u32[]{:S(2)}) collective-permute-start(f32[40,512]{1,0:T(8,128)S(1)} %pad_maximum_fusion.1), channel_id=1, source_target_pairs={{0,1},{1,0},{2,3},{3,2},{4,5},{5,4},{6,7},{7,6},{8,9},{9,8},{10,11... | collective-permute-start | bytes 245768 | tf_op jit(solution)/shard_map/ppermute | solution.py:381

commit v2 on v1

v2 whole, which is shorter than its diff:
```python
import functools

import jax
import jax.numpy as jnp
import numpy as np
from jax import lax
from jax.experimental import pallas as pl
from jax.experimental.pallas import tpu as pltpu
from jax.sharding import Mesh
from jax.sharding import PartitionSpec as P

ROWS = ("z", "x", "core")
BF16 = jnp.bfloat16
F32 = jnp.float32
SLOTS = 72


def iota(shape, dim):
    return lax.broadcasted_iota(jnp.int32, shape, dim)


def one_hot(mask):
    return jnp.where(mask, 1.0, 0.0).astype(BF16)


def params(mib=60):
    return pltpu.CompilerParams(vmem_limit_bytes=mib * 1024 * 1024)


def cost(flops, moved, special=0):
    return pl.CostEstimate(flops=int(flops), bytes_accessed=int(moved), transcendentals=int(special))


def whole(*shape):
    return pl.BlockSpec(shape, lambda i: (0,) * len(shape))


def bf16(*shape):
    return jax.ShapeDtypeStruct(shape, BF16)


def pool_tiles(pick, x_ref, pooled_ref):
    tiles = x_ref.shape[1] // 16
    for group in range(x_ref.shape[0] // 16):
        docs = pl.ds(group * 16, 16)
        block = jnp.concatenate(
            [x_ref[docs, t * 16:(t + 1) * 16, :].reshape(256, 128) for t in range(tiles)], axis=1
        )
        mean = jnp.dot(pick[...], block, preferred_element_type=F32).astype(BF16)
        for j in range(8):
            for t in range(tiles):
                at = (t * 8 + j) * 128
                pooled_ref[docs, at:at + 128] = mean[j * 16:(j + 1) * 16, t * 128:(t + 1) * 128]


def project_block(x_ref, w_hbm, first, pick, pooled, side, w_ref, w_sem):
    at = pl.program_id(0)
    step = x_ref.shape[0]
    load = pltpu.make_async_copy(w_hbm.at[:, pl.ds(first, w_ref.shape[1])], w_ref, w_sem)

    @pl.when(at == 0)
    def _():
        load.start()
        out_row, in_row = iota((128, 256), 0), iota((128, 256), 1)
        same_doc = out_row % 16 == in_row // 16
        same_tile = out_row // 16 == (in_row % 16) // 2
        pick[...] = jnp.where(same_doc & same_tile, 0.5, 0.0).astype(BF16)

    pool_tiles(pick, x_ref, pooled)

    @pl.when(at == 0)
    def _():
        load.wait()

    side[pl.ds(pl.multiple_of(at * step, step), step), :] = jnp.dot(
        pooled[...], w_ref[...], preferred_element_type=F32
    ).astype(BF16)


def pool_kernel(owner_ref, x_ref, w_hbm, out_ref, slot_ref,
                pick, pooled, side, w_ref, w_sem, chosen):
    at = pl.program_id(0)
    docs = side.shape[0]
    share = out_ref.shape[0] // 6

    @pl.when(at == 0)
    def _():
        first = pl.multiple_of(lax.axis_index(ROWS) * docs, 128)
        dest = owner_ref[:, pl.ds(first, docs)]
        hit = iota((32, docs), 0) == dest
        earlier = one_hot(iota((docs, docs), 0) < iota((docs, docs), 1))
        before = jnp.dot(one_hot(hit), earlier, preferred_element_type=F32)
        rank = jnp.sum(jnp.where(hit, before, 0.0), axis=0, keepdims=True)
        slot_ref[...] = dest * SLOTS + rank.astype(jnp.int32)

    project_block(x_ref, w_hbm, 0, pick, pooled, side, w_ref, w_sem)
    rows = iota((share, docs), 0) + at * share
    chosen[pl.ds(pl.multiple_of(at * share, 16), share), :] = one_hot(rows == slot_ref[...])

    @pl.when(at == pl.num_programs(0) - 1)
    def _():
        for part in range(6):
            rows = slice(part * share, (part + 1) * share)
            out_ref[rows, :] = jnp.dot(
                chosen[rows, :], side[...], preferred_element_type=F32
            ).astype(BF16)


def turn_kernel(slot_ref, x_ref, w_hbm, out_ref, mine_ref, theirs_ref,
                pick, pooled, side, w_ref, w_sem):
    first = w_hbm.shape[1] - w_ref.shape[1]
    project_block(x_ref, w_hbm, first, pick, pooled, side, w_ref, w_sem)
    rows = mine_ref.shape[1]
    core = lax.axis_index("core")
    for pair in range(mine_ref.shape[0] // 2):
        turned = pooled[:, pair * 4 * rows:(pair + 1) * 4 * rows].T
        for this in range(2):
            @pl.when(core == this)
            def _():
                for turned_ref, which in ((mine_ref, this), (theirs_ref, 1 - this)):
                    for chip in range(2):
                        at = (chip * 2 + which) * rows
                        turned_ref[pair * 2 + chip] = turned[at:at + rows, :]

    @pl.when(pl.program_id(0) == pl.num_programs(0) - 1)
    def _():
        step = out_ref.shape[0] // 6
        for part in range(6):
            rows = iota((step, side.shape[0]), 0) + part * step
            out_ref[part * step:(part + 1) * step, :] = jnp.dot(
                one_hot(rows == slot_ref[...]), side[...], preferred_element_type=F32
            ).astype(BF16)


def taps_by_tile(doc_taps):
    docs, tokens, depth = doc_taps.shape
    tiles = depth // 128
    taps = doc_taps.reshape(docs, tokens, tiles, 128).transpose(0, 2, 1, 3)
    return taps.reshape(docs, tokens * tiles, 128)


def pool_scratch(step, docs, depth, wide):
    return [
        pltpu.VMEM((128, 256), BF16),
        pltpu.VMEM((step, depth), BF16),
        pltpu.VMEM((docs, wide), BF16),
        pltpu.VMEM((depth, wide), BF16),
        pltpu.SemaphoreType.DMA,
    ]


def pool_and_pack(owner_of, taps, w_down, wide, slots):
    docs, rows, _ = taps.shape
    step = docs // 6
    return pl.pallas_call(
        pool_kernel,
        grid=(6,),
        in_specs=[
            whole(*owner_of.shape),
            pl.BlockSpec((step, rows, 128), lambda i: (i, 0, 0)),
            pl.BlockSpec(memory_space=pl.ANY),
        ],
        out_specs=[whole(slots, wide), whole(1, docs)],
        out_shape=[bf16(slots, wide), jax.ShapeDtypeStruct((1, docs), jnp.int32)],
        scratch_shapes=pool_scratch(step, docs, w_down.shape[0], wide)
        + [pltpu.VMEM((slots, docs), BF16)],
        compiler_params=params(),
        cost_estimate=cost(6e9, 20e6),
    )(owner_of, taps, w_down)


def pool_and_turn(slot, taps, w_down, wide, slots, chips):
    docs, rows, _ = taps.shape
    depth = w_down.shape[0]
    step = docs // 6
    turned = pl.BlockSpec((chips, depth // (2 * chips), step), lambda i: (0, 0, i))
    shape = bf16(chips, depth // (2 * chips), docs)
    return pl.pallas_call(
        turn_kernel,
        grid=(6,),
        in_specs=[
            whole(1, docs),
            pl.BlockSpec((step, rows, 128), lambda i: (i, 0, 0)),
            pl.BlockSpec(memory_space=pl.ANY),
        ],
        out_specs=[whole(slots, wide), turned, turned],
        out_shape=[bf16(slots, wide), shape, shape],
        scratch_shapes=pool_scratch(step, docs, depth, wide),
        compiler_params=params(),
        cost_estimate=cost(6e9, 28e6),
    )(slot, taps, w_down)


def take_kernel(waited, place_ref, table_ref, *out_refs):
    at = pl.program_id(0)
    out_refs = out_refs[waited:]
    depth = table_ref.shape[0]
    step = out_refs[0].shape[0]
    if place_ref.shape[0] == 1:
        mask = iota((step, depth), 0) + at * step == place_ref[...]
    else:
        mask = iota((step, depth), 1) == place_ref[...]
    rows = jnp.dot(one_hot(mask), table_ref[...], preferred_element_type=F32).astype(BF16)
    if len(out_refs) == 1:
        out_refs[0][...] = rows
    else:
        for i, out_ref in enumerate(out_refs):
            @pl.when(at == i)
            def _():
                out_ref[...] = rows


def take(place, table, count, halves=False, after=()):
    depth, width = table.shape
    step = count // 2
    if place.shape[0] == 1:
        place_spec = whole(1, depth)
    else:
        place_spec = pl.BlockSpec((step, 1), lambda i: (i, 0))
    if halves:
        out_specs, out_shape = [whole(step, width)] * 2, [bf16(step, width)] * 2
    else:
        out_specs, out_shape = pl.BlockSpec((step, width), lambda i: (i, 0)), bf16(count, width)
    return pl.pallas_call(
        functools.partial(take_kernel, len(after)),
        grid=(2,),
        in_specs=[place_spec, whole(depth, width)]
        + [pl.BlockSpec(memory_space=pl.ANY) for _ in after],
        out_specs=out_specs,
        out_shape=out_shape,
        compiler_params=params(24),
        cost_estimate=cost(2 * count * depth * width, 2e6),
    )(place, table, *after)


def shift(part, by):
    return lax.ppermute(part, "col", [(c, (c + by) % 4) for c in range(4)])


def gather_ring(low, high):
    before_low, after_high = shift(low, 1), shift(high, 3)
    before_high, after_low = shift(high, 1), shift(low, 3)
    far_low, far_high = shift(before_low, 1), shift(after_high, 3)
    return low, high, after_low, after_high, far_low, far_high, before_low, before_high


def stage(parts, table):
    at = 0
    for part in parts:
        table[at:at + part.shape[0], :] = part[...]
        at += part.shape[0]


def block_row(index_ref, values_ref, table, row, per_row):
    total = None
    for k in range(per_row):
        entry = row * per_row + k
        at = pl.multiple_of(index_ref[entry] * 128, 128)
        term = jnp.dot(values_ref[entry], table[pl.ds(at, 128), :], preferred_element_type=F32)
        total = term if total is None else total + term
    return total


def product_kernel(index_ref, values_ref, *refs):
    parts, (out_ref, table) = refs[:-2], refs[-2:]
    stage(parts, table)
    rows = out_ref.shape[0] // 128
    per_row = values_ref.shape[0] // rows
    for row in range(rows):
        out_ref[row * 128:(row + 1) * 128, :] = block_row(
            index_ref, values_ref, table, row, per_row
        ).astype(BF16)


def product(index, values, parts, nodes):
    width = parts[0].shape[1]
    vmem = pl.BlockSpec(memory_space=pltpu.VMEM)
    return pl.pallas_call(
        product_kernel,
        in_specs=[pl.BlockSpec(memory_space=pltpu.SMEM), vmem] + [vmem] * len(parts),
        out_specs=vmem,
        out_shape=bf16(nodes, width),
        scratch_shapes=[pltpu.VMEM((4 * nodes, width), BF16)],
        compiler_params=params(),
        cost_estimate=cost(2e8, 3e6),
    )(index, values, *parts)


def layer_kernel(index_ref, values_ref, *refs):
    parts = refs[:8]
    (first_ref, low_in_ref, high_in_ref, cot_ref, w_ref, wt_ref, gate_ref) = refs[8:15]
    (side_out_ref, agg_ref, mgrad_ref, low_ref, high_ref, next_low_ref, next_high_ref,
     gpart_ref, table) = refs[15:]
    at = pl.program_id(0)

    @pl.when(at == 0)
    def _():
        stage(parts, table)

    step = cot_ref.shape[0]
    wide = first_ref.shape[1]
    lead = low_ref.shape[1]
    nodes = step * pl.num_programs(0)
    per_row = values_ref.shape[0] * 128 // nodes
    rows = step // 128
    agg_ref[:, :wide] = first_ref[...]
    for row in range(rows):
        agg_ref[row * 128:(row + 1) * 128, wide:] = block_row(
            index_ref, values_ref, table, at * rows + row, per_row
        ).astype(BF16)
    gate = gate_ref[...]
    part = None
    for third in range(rows):
        here = slice(third * 128, (third + 1) * 128)
        message = jnp.dot(agg_ref[here, :], w_ref[...], preferred_element_type=F32)
        squash = jax.nn.sigmoid(message)
        activated = message * squash
        upstream = cot_ref[here, :].astype(F32)
        at_row = pl.multiple_of(at * step + third * 128, 128)
        lead_in = jnp.where(at == 0, low_in_ref[here, :], high_in_ref[here, :])
        owned = jnp.concatenate([lead_in, table[pl.ds(at_row, 128), :]], axis=1)
        side_out_ref[here, :] = (owned.astype(F32) + gate * activated).astype(BF16)
        mgrad_ref[here, :] = (
            upstream * gate * squash * (1.0 + message * (1.0 - squash))
        ).astype(BF16)
        term = jnp.sum(upstream * activated, axis=0, keepdims=True)
        part = term if part is None else part + term
    agrad = jnp.dot(mgrad_ref[...], wt_ref[...], preferred_element_type=F32).astype(BF16)

    @pl.when(at == 0)
    def _():
        low_ref[...] = agrad[:, :lead]
        next_low_ref[...] = agrad[:, lead:]
        gpart_ref[...] = part

    @pl.when(at == 1)
    def _():
        high_ref[...] = agrad[:, :lead]
        next_high_ref[...] = agrad[:, lead:]
        gpart_ref[...] += part


def layer(index, values, parts, first, owned, cotangent, w_msg, gate, lead):
    nodes, width = cotangent.shape
    wide = first.shape[1]
    step = nodes // 2
    rows = lambda size: pl.BlockSpec((step, size), lambda i: (i, 0))
    return pl.pallas_call(
        layer_kernel,
        grid=(2,),
        in_specs=[pl.BlockSpec(memory_space=pltpu.SMEM), whole(*values.shape)]
        + [whole(*part.shape) for part in parts]
        + [rows(wide), whole(step, wide), whole(step, wide), rows(width), whole(width, width), whole(width, width),
           whole(1, width)],
        out_specs=[rows(width), rows(width), rows(width), whole(step, lead), whole(step, lead),
                   whole(step, width - lead), whole(step, width - lead), whole(1, width)],
        out_shape=[bf16(nodes, width), bf16(nodes, width), bf16(nodes, width), bf16(step, lead),
                   bf16(step, lead), bf16(step, width - lead), bf16(step, width - lead),
                   jax.ShapeDtypeStruct((1, width), F32)],
        scratch_shapes=[pltpu.VMEM((4 * nodes, width - wide), BF16)],
        compiler_params=params(),
        cost_estimate=cost(12e8, 8e6, nodes * width),
    )(index, values, *parts, first, *owned, cotangent, w_msg, w_msg.T, gate)


def back_kernel(first, index_ref, values_ref, *refs):
    parts, (cot_ref, place_ref), (out_ref, table, grad) = refs[:8], refs[8:10], refs[-3:]
    nodes = cot_ref.shape[0]
    per_row = values_ref.shape[0] * 128 // nodes

    @pl.when(pl.program_id(0) == 0)
    def _():
        stage(parts, table)
        for row in range(nodes // 128):
            at = slice(row * 128, (row + 1) * 128)
            total = block_row(index_ref, values_ref, table, row, per_row)
            upstream = cot_ref[at, first:first + total.shape[1]].astype(F32)
            grad[at, :] = (upstream + total).astype(BF16)

    mask = iota((out_ref.shape[0], nodes), 1) == place_ref[...]
    out_ref[...] = jnp.dot(one_hot(mask), grad[...], preferred_element_type=F32).astype(BF16)


def back(index, values, parts, cotangent, first, place, slots, after=()):
    nodes = cotangent.shape[0]
    wide = parts[0].shape[1]
    step = slots // 4
    return pl.pallas_call(
        functools.partial(back_kernel, first),
        grid=(4,),
        in_specs=[pl.BlockSpec(memory_space=pltpu.SMEM), whole(*values.shape)]
        + [whole(*part.shape) for part in parts]
        + [whole(*cotangent.shape), pl.BlockSpec((step, 1), lambda i: (i, 0))]
        + [pl.BlockSpec(memory_space=pl.ANY) for _ in after],
        out_specs=pl.BlockSpec((step, wide), lambda i: (i, 0)),
        out_shape=bf16(slots, wide),
        scratch_shapes=[pltpu.VMEM((4 * nodes, wide), BF16), pltpu.VMEM((nodes, wide), BF16)],
        compiler_params=params(),
        cost_estimate=cost(2 * slots * nodes * wide, 5e6),
    )(index, values, *parts, cotangent, place, *after)


def small_kernel(agg_ref, mgrad_ref, gate_ref, after_ref, mine_ref, theirs_ref):
    msg = lax.dot_general(
        agg_ref[...], mgrad_ref[...], (((0,), (0,)), ((), ())), preferred_element_type=F32
    )
    chips, rows, width = mine_ref.shape
    share = width // (2 * chips)
    tail = jnp.concatenate([gate_ref[...], jnp.zeros((rows - share - 1, width), F32)], axis=0)
    core = lax.axis_index("core")
    for this in range(2):
        @pl.when(core == this)
        def _():
            for out_ref, which in ((mine_ref, this), (theirs_ref, 1 - this)):
                for chip in range(chips):
                    at = (chip * 2 + which) * share
                    out_ref[chip, :share, :] = msg[at:at + share, :]
                    out_ref[chip, share:, :] = tail


def small_sums(aggregate, message_grad, gate_part, chips, after):
    width = aggregate.shape[1]
    vmem = pl.BlockSpec(memory_space=pltpu.VMEM)
    out = jax.ShapeDtypeStruct((chips, 24, width), F32)
    return pl.pallas_call(
        small_kernel,
        in_specs=[vmem] * 3 + [pl.BlockSpec(memory_space=pl.ANY)],
        out_specs=[vmem] * 2,
        out_shape=[out, out],
        compiler_params=params(),
        cost_estimate=cost(4e8, 4e6),
    )(aggregate, message_grad, gate_part, after)


def down_rows(mine_ref, other_ref, grad_ref, other_grad_ref):
    docs = mine_ref.shape[2]
    rows = mine_ref.shape[0] * mine_ref.shape[1]
    return jnp.dot(
        mine_ref[...].reshape(rows, docs), grad_ref[...], preferred_element_type=F32
    ) + jnp.dot(
        other_ref[...].reshape(rows, docs), other_grad_ref[...], preferred_element_type=F32
    )


def tiles_of(array):
    return [array[:, at:at + 128] for at in range(0, array.shape[1], 128)]


def two_terms(row):
    high = row.astype(BF16).astype(F32)
    return [high, row - high, jnp.zeros((6, 128), F32)]


def down_by_col_kernel(mine_ref, other_ref, grad_ref, other_grad_ref, small_ref,
                       other_small_ref, *out_refs):
    total = down_rows(mine_ref, other_ref, grad_ref, other_grad_ref)
    small = small_ref[...] + other_small_ref[...]
    chips = small.shape[0]
    msg = (small.shape[1] - 8) // 4
    piece = total.shape[0] // (4 * chips)
    blocks = []
    for chip in range(chips):
        for col in range(4):
            at = (chip * 4 + col) * piece
            gate = small[chip, 4 * msg:4 * msg + 1, col * 128:(col + 1) * 128]
            cells = (
                tiles_of(total[at:at + piece, :])
                + tiles_of(small[chip, col * msg:(col + 1) * msg, :])
                + two_terms(gate)
            )
            blocks.append(jnp.concatenate(cells, axis=0).astype(BF16))
    my_col = lax.axis_index("col")
    for first in range(4):
        @pl.when(my_col == first)
        def _():
            for k, out_ref in enumerate(out_refs):
                for chip in range(chips):
                    out_ref[chip] = blocks[chip * 4 + (first + k) % 4]


def lead_kernel(*refs):
    total = sum([ref[...].astype(F32) for ref in refs[1:4]], refs[0][...].astype(F32))
    out_ref = refs[4]
    at = total.shape[1] - 8
    for chip in range(total.shape[0]):
        gate = total[chip, at:at + 1, :] + total[chip, at + 1:at + 2, :]
        cells = [total[chip, :at, :]] + two_terms(gate)
        out_ref[chip] = jnp.concatenate(cells, axis=0).astype(BF16)


def lead_sum(pieces):
    vmem = pl.BlockSpec(memory_space=pltpu.VMEM)
    return pl.pallas_call(
        lead_kernel,
        in_specs=[vmem] * 4,
        out_specs=vmem,
        out_shape=bf16(*pieces[0].shape),
        compiler_params=params(24),
        cost_estimate=cost(1e6, 1e6),
    )(*pieces)


def down_by_chip_kernel(mine_ref, other_ref, grad_ref, other_grad_ref, led_ref, out_ref):
    total = down_rows(mine_ref, other_ref, grad_ref, other_grad_ref)
    chips, share, _ = mine_ref.shape
    led = out_ref.shape[1] - led_ref.shape[1]
    for chip in range(chips):
        cells = tiles_of(total[chip * share:(chip + 1) * share, :])
        out_ref[chip, :led, :] = jnp.concatenate(cells, axis=0).astype(BF16)
        out_ref[chip, led:, :] = led_ref[chip]


def down_specs(mine, grad):
    chips, share, docs = mine.shape
    rows = pl.BlockSpec((chips // 4, share, docs), lambda i: (i, 0, 0))
    return [rows, rows, whole(*grad.shape), whole(*grad.shape)]


def down_by_col(mine, other, grad, other_grad, small, other_small, cols):
    chips, share, docs = mine.shape
    rows = share // cols * grad.shape[1] // 128 + 24
    by_chip = pl.BlockSpec((chips // 4,) + small.shape[1:], lambda i: (i, 0, 0))
    return pl.pallas_call(
        down_by_col_kernel,
        grid=(4,),
        in_specs=down_specs(mine, grad) + [by_chip, by_chip],
        out_specs=[pl.BlockSpec((chips // 4, rows, 128), lambda i: (i, 0, 0))] * cols,
        out_shape=[bf16(chips, rows, 128)] * cols,
        compiler_params=params(),
        cost_estimate=cost(2e9, 10e6),
    )(mine, other, grad, other_grad, small, other_small)


def down_by_chip(mine, other, grad, other_grad, led):
    chips, share, docs = mine.shape
    rows = share * grad.shape[1] // 128 + led.shape[1]
    by_chip = lambda size: pl.BlockSpec((chips // 4, size, 128), lambda i: (i, 0, 0))
    return pl.pallas_call(
        down_by_chip_kernel,
        grid=(4,),
        in_specs=down_specs(mine, grad) + [by_chip(led.shape[1])],
        out_specs=by_chip(rows),
        out_shape=bf16(chips, rows, 128),
        compiler_params=params(),
        cost_estimate=cost(2e9, 12e6),
    )(mine, other, grad, other_grad, led)


def fold_kernel(parts_ref, out_ref):
    total = jnp.sum(parts_ref[...].astype(F32), axis=0)
    at = total.shape[0] - 8
    gate = total[at:at + 1, :] + total[at + 1:at + 2, :]
    out_ref[...] = jnp.concatenate([total[:at, :]] + two_terms(gate), axis=0).astype(BF16)


def fold(parts):
    chips, rows, width = parts.shape
    vmem = pl.BlockSpec(memory_space=pltpu.VMEM)
    return pl.pallas_call(
        fold_kernel,
        in_specs=[vmem],
        out_specs=vmem,
        out_shape=bf16(rows, width),
        compiler_params=params(24),
        cost_estimate=cost(1e6, 2e6),
    )(parts)


def finish_kernel(lead, *refs):
    found, (down_ref, msg_ref, gate_ref) = refs[:4], refs[4:]
    share, width = down_ref.shape
    msg = msg_ref.shape[0]
    piece = share // 4
    my_col = lax.axis_index("col")
    own, near, far, cross = (ref[...].astype(F32) for ref in found)
    total = (own + near) + (far + cross)
    at = 0
    for lane in range(lead, width, 128):
        down_ref[:, lane:lane + 128] = total[at:at + share, :]
        at += share

    def from_col(col):
        step = my_col ^ col
        part = own[at:, :]
        for i, other in enumerate((near, far, cross)):
            part = jnp.where(step == i + 1, other[at:, :], part)
        return part

    for col in range(4):
        part = from_col(col)
        row = 0
        for lane in range(0, lead, 128):
            down_ref[col * piece:(col + 1) * piece, lane:lane + 128] = part[row:row + piece, :]
            row += piece
        for lane in range(0, width, 128):
            msg_ref[col * msg // 4:(col + 1) * msg // 4, lane:lane + 128] = (
                part[row:row + msg // 4, :]
            )
            row += msg // 4
    first = lax.axis_index(ROWS) * msg
    gate = from_col(first // 128)[-8:, :]
    spread = jnp.broadcast_to(gate[0:1, :] + gate[1:2, :], (8, 128))
    gate_ref[...] = pltpu.roll(spread, (128 - first % 128) % 128, 1)[:1, :msg]


def finish(found, share, msg, width, lead):
    vmem = pl.BlockSpec(memory_space=pltpu.VMEM)
    shape = lambda *dims: jax.ShapeDtypeStruct(dims, F32)
    return pl.pallas_call(
        functools.partial(finish_kernel, lead),
        in_specs=[vmem] * 4,
        out_specs=[vmem] * 3,
        out_shape=[shape(share, width), shape(msg, width), shape(1, msg)],
        compiler_params=params(24),
        cost_estimate=cost(1e6, 1e6),
    )(*found)


def relay(rows):
    slots, width = rows.shape
    size = lax.axis_size(ROWS)
    moved = lax.all_to_all(
        rows.reshape(size, slots // size, width), ROWS, split_axis=0, concat_axis=0, tiled=True
    )
    return moved.reshape(slots, width)


def shards(doc_taps, w_down, owner_of, adj_values, adj_index, w_msg, gate_scale, cotangent):
    docs = doc_taps.shape[0]
    depth, width = w_down.shape
    wide = width // 2
    lead = width // 4
    row_size, cols = lax.axis_size(ROWS), lax.axis_size("col")
    my_row, my_col = lax.axis_index(ROWS), lax.axis_index("col")
    slots = row_size * SLOTS
    chips = row_size // 2
    values = adj_values[0]
    blocks = docs // 128
    index = (adj_index[0] // blocks - my_col) % cols * blocks + adj_index[0] % blocks
    gate = gate_scale.reshape(1, width)
    swap = lambda array: lax.ppermute(array, "core", [(0, 1), (1, 0)])

    taps = taps_by_tile(doc_taps)
    packed0, slot = pool_and_pack(owner_of, taps, w_down, wide, slots)
    incoming0 = relay(packed0)
    packed1, mine, theirs = pool_and_turn(slot, taps, w_down, width - wide, slots, chips)
    other = swap(theirs)
    incoming1 = relay(packed1)

    owners = owner_of[0]
    counts = jnp.sum((owners.reshape(row_size, docs) == my_row).astype(jnp.int32), axis=1)
    lower = jnp.arange(row_size)[None, :] < jnp.arange(row_size)[:, None]
    starts = jnp.sum(jnp.where(lower, counts[None, :], 0), axis=1)
    in_slot = jnp.arange(SLOTS, dtype=jnp.int32)[None, :]
    position = jnp.where(in_slot < counts[:, None], starts[:, None] + in_slot, -1).reshape(slots)
    pos_row, pos_col = position.reshape(1, slots), position.reshape(slots, 1)

    owned0 = take(pos_row, incoming0, docs, halves=True)
    parts0 = gather_ring(*owned0)
    owned1 = take(pos_row, incoming1, docs, halves=True, after=parts0[4:6])
    first = product(index, values, parts0, docs)
    side_out, aggregate, message_grad, low, high, next_low, next_high, gate_part = layer(
        index, values, gather_ring(*owned1), first, owned0, cotangent, w_msg, gate, lead
    )

    slot_col = slot.reshape(docs, 1)
    next_parts = gather_ring(next_low, next_high)
    packed_back0 = back(index, values, gather_ring(low, high), cotangent, 0, pos_col, slots,
                        after=(next_parts[2], next_parts[7]))
    returned0 = relay(packed_back0)
    packed_back1 = back(index, values, next_parts, cotangent, lead, pos_col, slots)
    returned1 = relay(packed_back1)

    small, other_small = small_sums(aggregate, message_grad, gate_part, chips, packed_back0)
    other_small = swap(other_small)
    grad0 = take(slot_col, returned0, docs)
    pieces = down_by_col(mine, other, grad0, swap(grad0), small, other_small, cols)
    led = lead_sum([pieces[0]] + [shift(pieces[k], k) for k in range(1, cols)])
    grad1 = take(slot_col, returned1, docs, after=(led,))
    down = down_by_chip(mine, other, grad1, swap(grad1), led)
    down = lax.all_to_all(down, ("z", "x"), split_axis=0, concat_axis=0, tiled=True)
    own = fold(down)
    found = [own] + [
        lax.ppermute(own, "col", [(c, c ^ step) for c in range(4)]) for step in (1, 2, 3)
    ]
    grad_down, grad_msg, grad_gate = finish(
        found, depth // row_size, width // row_size, width, lead
    )
    return side_out, grad_down, grad_msg, grad_gate.reshape(width // row_size)


def solution(mesh):
    rows, cols = mesh.devices.shape
    z = 4
    x = rows // (2 * z)
    split = Mesh(mesh.devices.reshape(z, x, 2, cols), ("z", "x", "core", "col"))
    each = ROWS + ("col",)
    placed = (
        P(each, None, None),
        P(),
        P("col", None),
        P(each, None, None, None),
        P(each, None),
        P(),
        P(),
        P(each, None),
    )
    return jax.shard_map(
        shards,
        mesh=split,
        in_specs=placed,
        out_specs=(P(each, None), P(ROWS, None), P(ROWS, None), P(ROWS)),
        check_vma=False,
    )
```

time: 286 us -> 259 us (0.906)
  waiting for transfers between devices: 91.8 us -> 50 us
  blocking collectives: 0 us -> 37.2 us
  Pallas kernels: 51.2 us -> 84.2 us
  local copies, waits for them, and re-layouts: 27.4 us -> 9.25 us
  matrix products: 17.5 us -> 0 us
  starting transfers between devices: 88.3 us -> 75 us
  other arithmetic: 7.04 us -> 1.11 us
    all_to_all x0 -> x1, blocking collectives: none -> 37.2 us  [shards(): lax.all_to_all(down, ('z', 'x'), split_axis=0, concat_axis=0, tiled=True)]
    all_to_all x5 -> x0, waiting for transfers between devices: 33.3 us -> none  [the longest x2 22.6 us: shards(): lax.all_to_all(down_part.astype(BF16).reshape(cols, chips * piece, wide),...]
    pallas_call x10 -> x15, Pallas kernels: 49.3 us -> 81.1 us  [the longest x1 20.2 us: pool_and_turn(): pl.pallas_call(turn_kernel, grid=(6,), in_specs=[whole(1, docs), pl.Block...]
    all_to_all x4, waiting for transfers between devices: 27.8 us -> 2.9 us  [relay(): lax.all_to_all(rows.reshape(size, slots // size, width), ROWS, split_axis...]
    all_to_all x5 -> x0, starting transfers between devices: 24.7 us -> none  [the longest x2 12.2 us: shards(): lax.all_to_all(by_col.reshape(chips, piece, wide), ('z', 'x'), split_axis...]
    dot_general x5 -> x0, matrix products: 17.5 us -> none  [the longest x2 8.92 us: shards(): jnp.dot(other, other_grad, preferred_element_type=F32)]
    ppermute x25 -> x34, waiting for transfers between devices: 30.7 us -> 47.1 us  [the longest x27 37 us: shift(): return lax.ppermute(part, 'col', [(c, (c + by) % 4) for c in range(4)])]
    unnamed x49 -> x77, local copies, waits for them, and re-layouts: 18.1 us -> 7.54 us
  transfers between devices with their start and end apart: 34 -> 38, of which waited for: 16 -> 18; matrix products, arithmetic and copies ran while one was open for 12% -> 1% of each run, Pallas kernels for 12% -> 22%
where the time goes in v2:
time: 259 us; the launch traced here: 258 us
  Pallas kernels  84.2 us (33%)
  starting transfers between devices  75 us (29%)
  waiting for transfers between devices  50 us (19%)
  blocking collectives  37.2 us (14%)
  local copies, waits for them, and re-layouts  9.25 us (4%)
    ppermute x27, starting transfers between devices, shift(): return lax.ppermute(part, 'col', [(c, (c + by) % 4) for c in range(4)])  38.9 us
    all_to_all x1, blocking collectives, shards(): lax.all_to_all(down, ('z', 'x'), split_axis=0, concat_axis=0, tiled=True)  37.2 us
    ppermute x27, waiting for transfers between devices, shift(): return lax.ppermute(part, 'col', [(c, (c + by) % 4) for c in range(4)])  37 us
    all_to_all x4, starting transfers between devices, relay(): lax.all_to_all(rows.reshape(size, slots // size, width), ROWS, split_axis...  30.3 us
    pallas_call x1, Pallas kernels, pool_and_turn(): pl.pallas_call(turn_kernel, grid=(6,), in_specs=[whole(1, docs), pl.Block...  20.2 us
    pallas_call x1, Pallas kernels, pool_and_pack(): pl.pallas_call(pool_kernel, grid=(6,), in_specs=[whole(*owner_of.shape),...  15.8 us
    pallas_call x2, Pallas kernels, back(): pl.pallas_call(functools.partial(back_kernel, first), grid=(4,), in_specs...  12.9 us
    pallas_call x1, Pallas kernels, down_by_chip(): pl.pallas_call(down_by_chip_kernel, grid=(4,), in_specs=down_specs(mine,...  8.37 us
  transfers between devices with their start and end apart: 38, of which 18 were waited for; matrix products, arithmetic and copies ran while one was open for 1% of the time, Pallas kernels for 22%

profile of v2, /device:TPU:0, one launch (start us, length us, event | category | flops | bytes accessed | tf_op | source)
XLA Modules:
  0.0 257.9 jit_solution(10937539563473915003)
XLA Ops:
  0.6 15.8 %shard_map.111 = (bf16[2304,256]{1,0:T(8,128)(2,1)}, s32[1,768]{1,0:T(1,128)}) custom-call(s32[1,24576]{1,0:T(1,128)} %owner_ref.1, bf16[768,80,128]{2,1,0:T(8,128)(2,1)} %bitcast.48, bf16[5120,512]{1,0:T(8,128)(2,1)} %w_hbm.3), custom_call_target="tpu_custom_call" | custom-call | flops 6000000000 | bytes 20000000 | tf_op jit(solution)/shard_map/pallas_call | solution.py:155
  16.5 8.3 %all-to-all-start.1 = ((bf16[32,72,256]{2,1,0:T(8,128)(2,1)}), bf16[32,72,256]{2,1,0:T(8,128)(2,1)S(1)}, u32[]{:S(2)}, u32[]{:S(2)}) async-start(bf16[32,72,256]{2,1,0:T(8,128)(2,1)} %bitcast.45), calls=%async_computation.1 | async-start | bytes 2359296 | tf_op jit(solution)/shard_map/all_to_all | solution.py:622
  24.7 20.2 %shard_map.112 = (bf16[2304,256]{1,0:T(8,128)(2,1)}, bf16[16,160,768]{2,1,0:T(8,128)(2,1)}, bf16[16,160,768]{2,1,0:T(8,128)(2,1)}) custom-call(s32[1,768]{1,0:T(1,128)} %get-tuple-element.30.slot_ref, bf16[768,80,128]{2,1,0:T(8,128)(2,1)} %bitcast.49, bf16[5120,512]{1,0:T(8,128)(2,1)} %w_hbm.3), custom_call_target="tpu_custom_call" | custom-call | flops 6000000000 | bytes 28000000 | tf_op jit(solution)/shard_map/pallas_call | solution.py:178
  44.9 8.2 %all-to-all-start = ((bf16[32,72,256]{2,1,0:T(8,128)(2,1)}), bf16[32,72,256]{2,1,0:T(8,128)(2,1)S(1)}, u32[]{:S(2)}, u32[]{:S(2)}) async-start(bf16[32,72,256]{2,1,0:T(8,128)(2,1)} %bitcast.44), calls=%async_computation | async-start | bytes 2359296 | tf_op jit(solution)/shard_map/all_to_all | solution.py:622
  54.3 1.3 shard_map.113
  55.6 1.6 collective-permute-start
  57.3 1.7 collective-permute-start.2
  58.9 5.1 %collective-permute-done.refs_6_ = bf16[384,256]{1,0:T(8,128)(2,1)S(1)} collective-permute-done((bf16[384,256]{1,0:T(8,128)(2,1)S(1)}, bf16[384,256]{1,0:T(8,128)(2,1)S(1)}, u32[]{:S(2)}, u32[]{:S(2)}) %collective-permute-start) | collective-permute-done | bytes 196640 | tf_op jit(solution)/shard_map/ppermute | solution.py:237
  64.3 2.9 %collective-permute-start.3 = (bf16[384,256]{1,0:T(8,128)(2,1)S(1)}, bf16[384,256]{1,0:T(8,128)(2,1)S(1)}, u32[]{:S(2)}, u32[]{:S(2)}) collective-permute-start(bf16[384,256]{1,0:T(8,128)(2,1)S(1)} %collective-permute-done.2.refs_3_), channel_id=1, source_target_pairs={{0,3},{1,0},{2,1},{3,2},{4,7},{5,4},{6,5},{7,6},{8,11},{9,8},{10,9... | collective-permute-start | bytes 589832 | tf_op jit(solution)/shard_map/ppermute | solution.py:237
  67.3 0.5 collective-permute-start.10
  67.8 1.5 collective-permute-start.11
  69.3 2.9 %all-to-all-done = bf16[32,72,256]{2,1,0:T(8,128)(2,1)S(1)} async-done(((bf16[32,72,256]{2,1,0:T(8,128)(2,1)}), bf16[32,72,256]{2,1,0:T(8,128)(2,1)S(1)}, u32[]{:S(2)}, u32[]{:S(2)}) %all-to-all-start) | async-done | bytes 1179680 | tf_op jit(solution)/shard_map/all_to_all | solution.py:622
  72.2 0.6 collective-permute-done.1.out_refs_0_.refs_4_
  72.8 1.3 shard_map.114
  74.2 1.0 collective-permute-start.6
  75.2 2.6 %collective-permute-start.5 = (bf16[384,256]{1,0:T(8,128)(2,1)S(1)}, bf16[384,256]{1,0:T(8,128)(2,1)S(1)}, u32[]{:S(2)}, u32[]{:S(2)}) collective-permute-start(bf16[384,256]{1,0:T(8,128)(2,1)S(1)} %get-tuple-element.36.refs_1_), channel_id=1, source_target_pairs={{0,3},{1,0},{2,1},{3,2},{4,7},{5,4},{6,5},{7,6},{8,11},{9,8},{10,9... | collective-permute-start | bytes 589832 | tf_op jit(solution)/shard_map/ppermute | solution.py:237
  77.8 1.0 copy.21
  78.8 1.9 collective-permute-start.4
  81.5 1.5 collective-permute-done.5.refs_3_
  83.1 3.7 %collective-permute-start.8 = (bf16[384,256]{1,0:T(8,128)(2,1)S(1)}, bf16[384,256]{1,0:T(8,128)(2,1)S(1)}, u32[]{:S(2)}, u32[]{:S(2)}) collective-permute-start(bf16[384,256]{1,0:T(8,128)(2,1)S(1)} %collective-permute-done.5.refs_3_), channel_id=1, source_target_pairs={{0,3},{1,0},{2,1},{3,2},{4,7},{5,4},{6,5},{7,6},{8,11},{9,8},{10,9... | collective-permute-start | bytes 589832 | tf_op jit(solution)/shard_map/ppermute | solution.py:237
  86.8 0.5 fusion.2.index_ref
  87.3 3.1 %shard_map.115.refs_8_ = bf16[768,256]{1,0:T(8,128)(2,1)} custom-call(s32[24]{0:T(128)} %fusion.2.index_ref, bf16[24,128,128]{2,1,0:T(8,128)(2,1)} %bitcast.37, bf16[384,256]{1,0:T(8,128)(2,1)} %copy-done.1, bf16[384,256]{1,0:T(8,128)(2,1)} %copy-done.2, bf16[384,256]{1,0:T(8,128)(2,1)} %copy-done.27, bf16[384,256]{1,0:T(8,128)(2,1)} %copy-done.26, ...), custom_call_target="tpu_custom_call" | custom-call | flops 200000000 | bytes 3000000 | tf_op jit(solution)/shard_map/pallas_call | solution.py:278
  90.6 0.6 copy-done.21
  91.4 5.9 %shard_map.116 = (bf16[768,512]{1,0:T(8,128)(2,1)}, bf16[768,512]{1,0:T(8,128)(2,1)}, bf16[768,512]{1,0:T(8,128)(2,1)}, bf16[384,128]{1,0:T(8,128)(2,1)}, bf16[3...) custom-call(s32[24]{0:T(128)} %fusion.2.index_ref, ...), custom_call_target="tpu_custom_call" | custom-call | flops 1200000000 | bytes 8000000 | tf_op jit(solution)/shard_map/pallas_call | solution.py:348
  97.3 3.0 %collective-permute-start.19 = (bf16[384,128]{1,0:T(8,128)(2,1)}, bf16[384,128]{1,0:T(8,128)(2,1)S(1)}, u32[]{:S(2)}, u32[]{:S(2)}) collective-permute-start(bf16[384,128]{1,0:T(8,128)(2,1)} %get-tuple-element.42.refs_0_), channel_id=1, source_target_pairs={{0,3},{1,0},{2,1},{3,2},{4,7},{5,4},{6,5},{7,6},{8,11},{9,8},{10,9... | collective-permute-start | bytes 294920 | tf_op jit(solution)/shard_map/ppermute | solution.py:237
  100.4 1.9 collective-permute-start.21
  102.4 1.3 collective-permute-done.19.refs_2_
  103.7 3.6 %collective-permute-start.13 = (bf16[384,384]{1,0:T(8,128)(2,1)}, bf16[384,384]{1,0:T(8,128)(2,1)S(1)}, u32[]{:S(2)}, u32[]{:S(2)}) collective-permute-start(bf16[384,384]{1,0:T(8,128)(2,1)} %get-tuple-element.40.refs_0_), channel_id=1, source_target_pairs={{0,3},{1,0},{2,1},{3,2},{4,7},{5,4},{6,5},{7,6},{8,11},{9,8},{10,9... | collective-permute-start | bytes 884744 | tf_op jit(solution)/shard_map/ppermute | solution.py:237
  107.5 0.8 collective-permute-start.22
  108.3 1.3 collective-permute-done.24.refs_7_
  109.6 1.1 collective-permute-start.23
  110.7 6.9 %collective-permute-done.22.refs_4_ = bf16[384,128]{1,0:T(8,128)(2,1)S(1)} collective-permute-done((bf16[384,128]{1,0:T(8,128)(2,1)S(1)}, bf16[384,128]{1,0:T(8,128)(2,1)S(1)}, u32[]{:S(2)}, u32[]{:S(2)}) %collective-permute-start.22) | collective-permute-done | bytes 98336 | tf_op jit(solution)/shard_map/ppermute | solution.py:237
  117.7 3.2 %collective-permute-start.14 = (bf16[384,384]{1,0:T(8,128)(2,1)}, bf16[384,384]{1,0:T(8,128)(2,1)S(1)}, u32[]{:S(2)}, u32[]{:S(2)}) collective-permute-start(bf16[384,384]{1,0:T(8,128)(2,1)} %get-tuple-element.41.refs_1_), channel_id=1, source_target_pairs={{0,3},{1,0},{2,1},{3,2},{4,7},{5,4},{6,5},{7,6},{8,11},{9,8},{10,9... | collective-permute-start | bytes 884744 | tf_op jit(solution)/shard_map/ppermute | solution.py:237
  120.9 1.4 select_n.51.refs_9_
  122.4 0.7 copy-done.11
  123.0 0.7 copy-done.12
  123.8 5.5 %shard_map.118.after_ref = bf16[2304,128]{1,0:T(8,128)(2,1)} custom-call(s32[24]{0:T(128)} %fusion.2.index_ref, bf16[24,128,128]{2,1,0:T(8,128)(2,1)} %bitcast.39, bf16[384,128]{1,0:T(8,128)(2,1)} %get-tuple-element.42.refs_0_, bf16[384,128]{1,0:T(8,128)(2,1)} %get-tuple-element.43.refs_1_, bf16[384,128]{1,0:T(8,128)(2,1)} %copy-done.30, ...), custom_call_target="tpu_custom_call" | custom-call | flops 452984832 | bytes 5000000 | tf_op jit(solution)/shard_map/pallas_call | solution.py:388
  129.2 6.6 %all-to-all-start.3 = ((bf16[32,72,128]{2,1,0:T(8,128)(2,1)}), bf16[32,72,128]{2,1,0:T(8,128)(2,1)S(1)}, u32[]{:S(2)}, u32[]{:S(2)}) async-start(bf16[32,72,128]{2,1,0:T(8,128)(2,1)} %bitcast.42), calls=%async_computation.3 | async-start | bytes 1179648 | tf_op jit(solution)/shard_map/all_to_all | solution.py:622
  136.0 3.2 %collective-permute-start.17 = (bf16[384,384]{1,0:T(8,128)(2,1)S(1)}, bf16[384,384]{1,0:T(8,128)(2,1)S(1)}, u32[]{:S(2)}, u32[]{:S(2)}) collective-permute-start(bf16[384,384]{1,0:T(8,128)(2,1)S(1)} %collective-permute-done.14.refs_3_), channel_id=1, source_target_pairs={{0,3},{1,0},{2,1},{3,2},{4,7},{5,4},{6,5},{7,6},{8,11},{9,8},{10,9... | collective-permute-start | bytes 884744 | tf_op jit(solution)/shard_map/ppermute | solution.py:237
  139.2 7.2 %collective-permute-done.16.refs_4_ = bf16[384,384]{1,0:T(8,128)(2,1)S(1)} collective-permute-done((bf16[384,384]{1,0:T(8,128)(2,1)S(1)}, bf16[384,384]{1,0:T(8,128)(2,1)S(1)}, u32[]{:S(2)}, u32[]{:S(2)}) %collective-permute-start.16) | collective-permute-done | bytes 294944 | tf_op jit(solution)/shard_map/ppermute | solution.py:237
  146.3 0.7 copy-done.17
  147.1 0.7 copy-done.18
  147.8 7.4 %shard_map.117 = bf16[2304,384]{1,0:T(8,128)(2,1)} custom-call(s32[24]{0:T(128)} %fusion.2.index_ref, bf16[24,128,128]{2,1,0:T(8,128)(2,1)} %bitcast.40, bf16[384,384]{1,0:T(8,128)(2,1)} %get-tuple-element.40.refs_0_, bf16[384,384]{1,0:T(8,128)(2,1)} %get-tuple-element.41.refs_1_, bf16[384,384]{1,0:T(8,128)(2,1)} %copy-done.11, bf16[384,384]{1,0:T(8,128)(2,1)} %copy-done.16, ...), custom_call_target="tpu_custom_call" | custom-call | flops 1358954496 | bytes 5000000 | tf_op jit(solution)/shard_map/pallas_call | solution.py:388
  155.2 7.3 %all-to-all-start.2 = ((bf16[32,72,384]{2,1,0:T(8,128)(2,1)}), bf16[32,72,384]{2,1,0:T(8,128)(2,1)S(1)}, u32[]{:S(2)}, u32[]{:S(2)}) async-start(bf16[32,72,384]{2,1,0:T(8,128)(2,1)} %bitcast.41), calls=%async_computation.2 | async-start | bytes 3538944 | tf_op jit(solution)/shard_map/all_to_all | solution.py:622
  162.5 3.2 %shard_map.120 = (f32[16,24,512]{2,1,0:T(8,128)}, f32[16,24,512]{2,1,0:T(8,128)}) custom-call(bf16[768,512]{1,0:T(8,128)(2,1)} %get-tuple-element.44.agg_ref, bf16[768,512]{1,0:T(8,128)(2,1)} %get-tuple-element.45.mgrad_ref, f32[1,512]{1,0:T(1,128)} %get-tuple-element.46.gate_ref, bf16[2304,128]{1,0:T(8,128)(2,1)} %shard_map.118.after_ref), custom_call_target="tpu_custom_call" | custom-call | flops 400000000 | bytes 4000000 | tf_op jit(solution)/shard_map/pallas_call | solution.py:425
  166.2 1.4 shard_map.119.grad_ref
  167.8 1.3 collective-permute-done.25.other_grad_ref
  169.1 0.7 copy-done.28
  170.1 7.1 %shard_map.121 = (bf16[16,64,128]{2,1,0:T(8,128)(2,1)}, bf16[16,64,128]{2,1,0:T(8,128)(2,1)}, bf16[16,64,128]{2,1,0:T(8,128)(2,1)}, bf16[16,64,128]{2,1,0:T(8,128)(2,1)}) custom-call(bf16[16,160,768]{2,1,0:T(8,128)(2,1)} %get-tuple-element.38.mine_ref, bf16[16,160,768]{2,1,0:T(8,128)(2,1)} %collective-permute-done.12.other_ref, bf16[768,128]{1,0:T(8,128)(2,1)} %copy-done.9, ...), custom_call_target="tpu_custom_call" | custom-call | flops 2000000000 | bytes 10000000 | tf_op jit(solution)/shard_map/pallas_call | solution.py:523
  177.3 3.7 %collective-permute-start.28 = (bf16[16,64,128]{2,1,0:T(8,128)(2,1)}, bf16[16,64,128]{2,1,0:T(8,128)(2,1)S(1)}, u32[]{:S(2)}, u32[]{:S(2)}) collective-permute-start(bf16[16,64,128]{2,1,0:T(8,128)(2,1)} %get-tuple-element.51), channel_id=1, source_target_pairs={{0,2},{1,3},{2,0},{3,1},{4,6},{5,7},{6,4},{7,5},{8,10},{9,11},{10,... | collective-permute-start | bytes 786440 | tf_op jit(solution)/shard_map/ppermute | solution.py:237
  180.9 6.4 %collective-permute-done.27.refs_1_ = bf16[16,64,128]{2,1,0:T(8,128)(2,1)S(1)} collective-permute-done((bf16[16,64,128]{2,1,0:T(8,128)(2,1)}, bf16[16,64,128]{2,1,0:T(8,128)(2,1)S(1)}, u32[]{:S(2)}, u32[]{:S(2)}) %collective-permute-start.27) | collective-permute-done | bytes 262176 | tf_op jit(solution)/shard_map/ppermute | solution.py:237
  187.3 5.8 %collective-permute-done.28.refs_2_ = bf16[16,64,128]{2,1,0:T(8,128)(2,1)S(1)} collective-permute-done((bf16[16,64,128]{2,1,0:T(8,128)(2,1)}, bf16[16,64,128]{2,1,0:T(8,128)(2,1)S(1)}, u32[]{:S(2)}, u32[]{:S(2)}) %collective-permute-start.28) | collective-permute-done | bytes 262176 | tf_op jit(solution)/shard_map/ppermute | solution.py:237
  193.3 0.9 copy-done.4
  194.4 2.3 shard_map.123.grad_ref
  196.8 2.0 collective-permute-done.30.other_grad_ref
  198.8 0.8 copy-done.14
  199.6 8.4 %shard_map.124 = bf16[16,544,128]{2,1,0:T(8,128)(2,1)} custom-call(bf16[16,160,768]{2,1,0:T(8,128)(2,1)} %get-tuple-element.38.mine_ref, bf16[16,160,768]{2,1,0:T(8,128)(2,1)} %collective-permute-done.12.other_ref, bf16[768,384]{1,0:T(8,128)(2,1)} %copy-done.3, bf16[768,384]{1,0:T(8,128)(2,1)} %copy-done.14, bf16[16,64,128]{2,1,0:T(8,128)(2,1)} %copy-done), custom_call_target="tpu_custom_call" | custom-call | flops 2000000000 | bytes 12000000 | tf_op jit(solution)/shard_map/pallas_call | solution.py:538
  208.0 37.2 %all_to_all.25.parts_ref = bf16[16,544,128]{2,1,0:T(8,128)(2,1)S(1)} all-to-all(bf16[16,544,128]{2,1,0:T(8,128)(2,1)} %shard_map.124), channel_id=1, replica_groups=mesh['z'=4,'x'=4,'core'=2,'col'=4] {'z','x'}, dimensions={0} | all-to-all | bytes 4456448 | tf_op jit(solution)/shard_map/all_to_all | solution.py:681
  245.8 3.8 %collective-permute-start.32 = (bf16[544,128]{1,0:T(8,128)(2,1)S(1)}, bf16[544,128]{1,0:T(8,128)(2,1)S(1)}, u32[]{:S(2)}, u32[]{:S(2)}) collective-permute-start(bf16[544,128]{1,0:T(8,128)(2,1)S(1)} %shard_map.125.refs_0_), channel_id=1, source_target_pairs={{0,2},{1,3},{2,0},{3,1},{4,6},{5,7},{6,4},{7,5},{8,10},{9,11},{10,... | collective-permute-start | bytes 417800 | tf_op jit(solution)/shard_map/ppermute | solution.py:684
  249.7 0.6 collective-permute-start.33
  250.3 1.5 collective-permute-done.31.refs_1_
  251.7 3.6 %collective-permute-done.32.refs_2_ = bf16[544,128]{1,0:T(8,128)(2,1)S(1)} collective-permute-done((bf16[544,128]{1,0:T(8,128)(2,1)S(1)}, bf16[544,128]{1,0:T(8,128)(2,1)S(1)}, u32[]{:S(2)}, u32[]{:S(2)}) %collective-permute-start.32) | collective-permute-done | bytes 139296 | tf_op jit(solution)/shard_map/ppermute | solution.py:684
  255.3 1.7 collective-permute-done.33.refs_3_
  257.1 0.9 shard_map.126
  (115 shorter events, 5.1 us)
Async XLA Ops:
  16.5 28.5 %all-to-all-start.1 = ((bf16[32,72,256]{2,1,0:T(8,128)(2,1)}), bf16[32,72,256]{2,1,0:T(8,128)(2,1)S(1)}, u32[]{:S(2)}, u32[]{:S(2)}) async-start(bf16[32,72,256]{2,1,0:T(8,128)(2,1)} %bitcast.45), calls=%async_computation.1 | async-start | bytes 2359296 | tf_op jit(solution)/shard_map/all_to_all | solution.py:622
  44.9 8.6 %copy-start.29 = (s32[1,24576]{1,0:T(1,128)S(1)}, s32[1,24576]{1,0:T(1,128)}, u32[]{:S(2)}) copy-start(s32[1,24576]{1,0:T(1,128)} %owner_ref.1) | copy-start | bytes 294916
  44.9 27.2 %all-to-all-start = ((bf16[32,72,256]{2,1,0:T(8,128)(2,1)}), bf16[32,72,256]{2,1,0:T(8,128)(2,1)S(1)}, u32[]{:S(2)}, u32[]{:S(2)}) async-start(bf16[32,72,256]{2,1,0:T(8,128)(2,1)} %bitcast.44), calls=%async_computation | async-start | bytes 2359296 | tf_op jit(solution)/shard_map/all_to_all | solution.py:622
  53.2 115.9 %collective-permute-start.12 = (bf16[16,160,768]{2,1,0:T(8,128)(2,1)}, bf16[16,160,768]{2,1,0:T(8,128)(2,1)}, u32[]{:S(2)}, u32[]{:S(2)}) collective-permute-start(bf16[16,160,768]{2,1,0:T(8,128)(2,1)} %get-tuple-element.39), channel_id=1, source_target_pairs={{0,4},{4,0},{1,5},{5,1},{2,6},{6,2},{3,7},{7,3},{8,12},{12,8},{9,1... | collective-permute-start | bytes 11796488 | tf_op jit(solution)/shard_map/ppermute | solution.py:641
  55.6 31.7 %copy-start.1 = (bf16[384,256]{1,0:T(8,128)(2,1)}, bf16[384,256]{1,0:T(8,128)(2,1)S(1)}, u32[]{:S(2)}) copy-start(bf16[384,256]{1,0:T(8,128)(2,1)S(1)} %get-tuple-element.33.refs_0_.refs_9_) | copy-start | bytes 589828
  55.6 31.7 %copy-start.2 = (bf16[384,256]{1,0:T(8,128)(2,1)}, bf16[384,256]{1,0:T(8,128)(2,1)S(1)}, u32[]{:S(2)}) copy-start(bf16[384,256]{1,0:T(8,128)(2,1)S(1)} %get-tuple-element.34.refs_1_.refs_10_) | copy-start | bytes 589828
  55.6 22.2 %copy-start.10 = (bf16[512,512]{1,0:T(8,128)(2,1)S(1)}, bf16[512,512]{1,0:T(8,128)(2,1)}, u32[]{:S(2)}) copy-start(bf16[512,512]{1,0:T(8,128)(2,1)} %refs_12_.1) | copy-start | bytes 1572868
  55.6 31.1 %copy-start.37 = (s32[1,24]{1,0:T(1,128)S(1)}, s32[1,24]{1,0:T(1,128)}, u32[]{:S(2)}) copy-start(s32[1,24]{1,0:T(1,128)} %param.12) | copy-start | bytes 292
  55.6 8.4 %collective-permute-start = (bf16[384,256]{1,0:T(8,128)(2,1)S(1)}, bf16[384,256]{1,0:T(8,128)(2,1)S(1)}, u32[]{:S(2)}, u32[]{:S(2)}) collective-permute-start(bf16[384,256]{1,0:T(8,128)(2,1)S(1)} %get-tuple-element.33.refs_0_.refs_9_), channel_id=1, source_target_pairs={{0,1},{1,2},{2,3},{3,0},{4,5},{5,6},{6,7},{7,4},{8,9},{9,10},{10,1... | collective-permute-start | bytes 589832 | tf_op jit(solution)/shard_map/ppermute | solution.py:237
  57.3 7.0 %collective-permute-start.2 = (bf16[384,256]{1,0:T(8,128)(2,1)S(1)}, bf16[384,256]{1,0:T(8,128)(2,1)S(1)}, u32[]{:S(2)}, u32[]{:S(2)}) collective-permute-start(bf16[384,256]{1,0:T(8,128)(2,1)S(1)} %get-tuple-element.34.refs_1_.refs_10_), channel_id=1, source_target_pairs={{0,3},{1,0},{2,1},{3,2},{4,7},{5,4},{6,5},{7,6},{8,11},{9,8},{10,9... | collective-permute-start | bytes 589832 | tf_op jit(solution)/shard_map/ppermute | solution.py:237
  64.0 23.3 %copy-start.25 = (bf16[384,256]{1,0:T(8,128)(2,1)}, bf16[384,256]{1,0:T(8,128)(2,1)S(1)}, u32[]{:S(2)}) copy-start(bf16[384,256]{1,0:T(8,128)(2,1)S(1)} %collective-permute-done.refs_6_) | copy-start | bytes 589828
  64.0 8.8 %collective-permute-start.1 = (bf16[384,256]{1,0:T(8,128)(2,1)S(1)}, bf16[384,256]{1,0:T(8,128)(2,1)S(1)}, u32[]{:S(2)}, u32[]{:S(2)}) collective-permute-start(bf16[384,256]{1,0:T(8,128)(2,1)S(1)} %collective-permute-done.refs_6_), channel_id=1, source_target_pairs={{0,1},{1,2},{2,3},{3,0},{4,5},{5,6},{6,7},{7,4},{8,9},{9,10},{10,1... | collective-permute-start | bytes 589832 | tf_op jit(solution)/shard_map/ppermute | solution.py:237
  64.3 23.0 %copy-start.26 = (bf16[384,256]{1,0:T(8,128)(2,1)}, bf16[384,256]{1,0:T(8,128)(2,1)S(1)}, u32[]{:S(2)}) copy-start(bf16[384,256]{1,0:T(8,128)(2,1)S(1)} %collective-permute-done.2.refs_3_) | copy-start | bytes 589828
  64.3 8.5 %collective-permute-start.3 = (bf16[384,256]{1,0:T(8,128)(2,1)S(1)}, bf16[384,256]{1,0:T(8,128)(2,1)S(1)}, u32[]{:S(2)}, u32[]{:S(2)}) collective-permute-start(bf16[384,256]{1,0:T(8,128)(2,1)S(1)} %collective-permute-done.2.refs_3_), channel_id=1, source_target_pairs={{0,3},{1,0},{2,1},{3,2},{4,7},{5,4},{6,5},{7,6},{8,11},{9,8},{10,9... | collective-permute-start | bytes 589832 | tf_op jit(solution)/shard_map/ppermute | solution.py:237
  67.3 11.6 %collective-permute-start.10 = (bf16[384,256]{1,0:T(8,128)(2,1)S(1)}, bf16[384,256]{1,0:T(8,128)(2,1)S(1)}, u32[]{:S(2)}, u32[]{:S(2)}) collective-permute-start(bf16[384,256]{1,0:T(8,128)(2,1)S(1)} %get-tuple-element.33.refs_0_.refs_9_), channel_id=1, source_target_pairs={{0,3},{1,0},{2,1},{3,2},{4,7},{5,4},{6,5},{7,6},{8,11},{9,8},{10,9... | collective-permute-start | bytes 589832 | tf_op jit(solution)/shard_map/ppermute | solution.py:237
  67.8 13.0 %collective-permute-start.11 = (bf16[384,256]{1,0:T(8,128)(2,1)S(1)}, bf16[384,256]{1,0:T(8,128)(2,1)}, u32[]{:S(2)}, u32[]{:S(2)}) collective-permute-start(bf16[384,256]{1,0:T(8,128)(2,1)S(1)} %get-tuple-element.34.refs_1_.refs_10_), channel_id=1, source_target_pairs={{0,1},{1,2},{2,3},{3,0},{4,5},{5,6},{6,7},{7,4},{8,9},{9,10},{10,1... | collective-permute-start | bytes 589832 | tf_op jit(solution)/shard_map/ppermute | solution.py:237
  72.8 14.5 %copy-start.7 = (bf16[384,256]{1,0:T(8,128)(2,1)}, bf16[384,256]{1,0:T(8,128)(2,1)S(1)}, u32[]{:S(2)}) copy-start(bf16[384,256]{1,0:T(8,128)(2,1)S(1)} %collective-permute-done.1.out_refs_0_.refs_4_) | copy-start | bytes 589828
  72.8 14.5 %copy-start.8 = (bf16[384,256]{1,0:T(8,128)(2,1)}, bf16[384,256]{1,0:T(8,128)(2,1)S(1)}, u32[]{:S(2)}) copy-start(bf16[384,256]{1,0:T(8,128)(2,1)S(1)} %collective-permute-done.3.out_refs_1_.refs_5_) | copy-start | bytes 589828
  74.2 16.4 %copy-start.5 = (bf16[384,256]{1,0:T(8,128)(2,1)}, bf16[384,256]{1,0:T(8,128)(2,1)S(1)}, u32[]{:S(2)}) copy-start(bf16[384,256]{1,0:T(8,128)(2,1)S(1)} %get-tuple-element.35.refs_0_) | copy-start | bytes 589828
  74.2 16.4 %copy-start.6 = (bf16[384,256]{1,0:T(8,128)(2,1)}, bf16[384,256]{1,0:T(8,128)(2,1)S(1)}, u32[]{:S(2)}) copy-start(bf16[384,256]{1,0:T(8,128)(2,1)S(1)} %get-tuple-element.36.refs_1_) | copy-start | bytes 589828
  74.2 7.2 %collective-permute-start.6 = (bf16[384,256]{1,0:T(8,128)(2,1)S(1)}, bf16[384,256]{1,0:T(8,128)(2,1)S(1)}, u32[]{:S(2)}, u32[]{:S(2)}) collective-permute-start(bf16[384,256]{1,0:T(8,128)(2,1)S(1)} %get-tuple-element.35.refs_0_), channel_id=1, source_target_pairs={{0,1},{1,2},{2,3},{3,0},{4,5},{5,6},{6,7},{7,4},{8,9},{9,10},{10,1... | collective-permute-start | bytes 589832 | tf_op jit(solution)/shard_map/ppermute | solution.py:237
  75.2 7.8 %collective-permute-start.5 = (bf16[384,256]{1,0:T(8,128)(2,1)S(1)}, bf16[384,256]{1,0:T(8,128)(2,1)S(1)}, u32[]{:S(2)}, u32[]{:S(2)}) collective-permute-start(bf16[384,256]{1,0:T(8,128)(2,1)S(1)} %get-tuple-element.36.refs_1_), channel_id=1, source_target_pairs={{0,3},{1,0},{2,1},{3,2},{4,7},{5,4},{6,5},{7,6},{8,11},{9,8},{10,9... | collective-permute-start | bytes 589832 | tf_op jit(solution)/shard_map/ppermute | solution.py:237
  78.8 8.5 %copy-start.27 = (bf16[384,256]{1,0:T(8,128)(2,1)}, bf16[384,256]{1,0:T(8,128)(2,1)S(1)}, u32[]{:S(2)}) copy-start(bf16[384,256]{1,0:T(8,128)(2,1)S(1)} %collective-permute-done.10.refs_2_) | copy-start | bytes 589828
  78.8 11.6 %collective-permute-start.4 = (bf16[384,256]{1,0:T(8,128)(2,1)S(1)}, bf16[384,256]{1,0:T(8,128)(2,1)S(1)}, u32[]{:S(2)}, u32[]{:S(2)}) collective-permute-start(bf16[384,256]{1,0:T(8,128)(2,1)S(1)} %get-tuple-element.35.refs_0_), channel_id=1, source_target_pairs={{0,3},{1,0},{2,1},{3,2},{4,7},{5,4},{6,5},{7,6},{8,11},{9,8},{10,9... | collective-permute-start | bytes 589832 | tf_op jit(solution)/shard_map/ppermute | solution.py:237
  80.8 9.7 %collective-permute-start.9 = (bf16[384,256]{1,0:T(8,128)(2,1)S(1)}, bf16[384,256]{1,0:T(8,128)(2,1)S(1)}, u32[]{:S(2)}, u32[]{:S(2)}) collective-permute-start(bf16[384,256]{1,0:T(8,128)(2,1)S(1)} %get-tuple-element.36.refs_1_), channel_id=1, source_target_pairs={{0,1},{1,2},{2,3},{3,0},{4,5},{5,6},{6,7},{7,4},{8,9},{9,10},{10,1... | collective-permute-start | bytes 589832 | tf_op jit(solution)/shard_map/ppermute | solution.py:237
  81.4 9.2 %copy-start.19 = (bf16[384,256]{1,0:T(8,128)(2,1)}, bf16[384,256]{1,0:T(8,128)(2,1)S(1)}, u32[]{:S(2)}) copy-start(bf16[384,256]{1,0:T(8,128)(2,1)S(1)} %collective-permute-done.6.refs_6_) | copy-start | bytes 589828
  81.4 9.1 %collective-permute-start.7 = (bf16[384,256]{1,0:T(8,128)(2,1)S(1)}, bf16[384,256]{1,0:T(8,128)(2,1)S(1)}, u32[]{:S(2)}, u32[]{:S(2)}) collective-permute-start(bf16[384,256]{1,0:T(8,128)(2,1)S(1)} %collective-permute-done.6.refs_6_), channel_id=1, source_target_pairs={{0,1},{1,2},{2,3},{3,0},{4,5},{5,6},{6,7},{7,4},{8,9},{9,10},{10,1... | collective-permute-start | bytes 589832 | tf_op jit(solution)/shard_map/ppermute | solution.py:237
  83.1 7.5 %copy-start.20 = (bf16[384,256]{1,0:T(8,128)(2,1)}, bf16[384,256]{1,0:T(8,128)(2,1)S(1)}, u32[]{:S(2)}) copy-start(bf16[384,256]{1,0:T(8,128)(2,1)S(1)} %collective-permute-done.5.refs_3_) | copy-start | bytes 589828
  83.1 7.5 %collective-permute-start.8 = (bf16[384,256]{1,0:T(8,128)(2,1)S(1)}, bf16[384,256]{1,0:T(8,128)(2,1)S(1)}, u32[]{:S(2)}, u32[]{:S(2)}) collective-permute-start(bf16[384,256]{1,0:T(8,128)(2,1)S(1)} %collective-permute-done.5.refs_3_), channel_id=1, source_target_pairs={{0,3},{1,0},{2,1},{3,2},{4,7},{5,4},{6,5},{7,6},{8,11},{9,8},{10,9... | collective-permute-start | bytes 589832 | tf_op jit(solution)/shard_map/ppermute | solution.py:237
  97.3 6.4 %collective-permute-start.19 = (bf16[384,128]{1,0:T(8,128)(2,1)}, bf16[384,128]{1,0:T(8,128)(2,1)S(1)}, u32[]{:S(2)}, u32[]{:S(2)}) collective-permute-start(bf16[384,128]{1,0:T(8,128)(2,1)} %get-tuple-element.42.refs_0_), channel_id=1, source_target_pairs={{0,3},{1,0},{2,1},{3,2},{4,7},{5,4},{6,5},{7,6},{8,11},{9,8},{10,9... | collective-permute-start | bytes 294920 | tf_op jit(solution)/shard_map/ppermute | solution.py:237
  100.3 7.0 %collective-permute-start.20 = (bf16[384,128]{1,0:T(8,128)(2,1)}, bf16[384,128]{1,0:T(8,128)(2,1)S(1)}, u32[]{:S(2)}, u32[]{:S(2)}) collective-permute-start(bf16[384,128]{1,0:T(8,128)(2,1)} %get-tuple-element.43.refs_1_), channel_id=1, source_target_pairs={{0,3},{1,0},{2,1},{3,2},{4,7},{5,4},{6,5},{7,6},{8,11},{9,8},{10,9... | collective-permute-start | bytes 294920 | tf_op jit(solution)/shard_map/ppermute | solution.py:237
  100.4 7.1 %collective-permute-start.21 = (bf16[384,128]{1,0:T(8,128)(2,1)}, bf16[384,128]{1,0:T(8,128)(2,1)S(1)}, u32[]{:S(2)}, u32[]{:S(2)}) collective-permute-start(bf16[384,128]{1,0:T(8,128)(2,1)} %get-tuple-element.42.refs_0_), channel_id=1, source_target_pairs={{0,1},{1,2},{2,3},{3,0},{4,5},{5,6},{6,7},{7,4},{8,9},{9,10},{10,1... | collective-permute-start | bytes 294920 | tf_op jit(solution)/shard_map/ppermute | solution.py:237
  102.3 7.3 %collective-permute-start.24 = (bf16[384,128]{1,0:T(8,128)(2,1)}, bf16[384,128]{1,0:T(8,128)(2,1)S(1)}, u32[]{:S(2)}, u32[]{:S(2)}) collective-permute-start(bf16[384,128]{1,0:T(8,128)(2,1)} %get-tuple-element.43.refs_1_), channel_id=1, source_target_pairs={{0,1},{1,2},{2,3},{3,0},{4,5},{5,6},{6,7},{7,4},{8,9},{9,10},{10,1... | collective-permute-start | bytes 294920 | tf_op jit(solution)/shard_map/ppermute | solution.py:237
  103.7 18.6 %copy-start.30 = (bf16[384,128]{1,0:T(8,128)(2,1)}, bf16[384,128]{1,0:T(8,128)(2,1)S(1)}, u32[]{:S(2)}) copy-start(bf16[384,128]{1,0:T(8,128)(2,1)S(1)} %collective-permute-done.19.refs_2_) | copy-start | bytes 294916
  103.7 18.6 %collective-permute-start.13 = (bf16[384,384]{1,0:T(8,128)(2,1)}, bf16[384,384]{1,0:T(8,128)(2,1)S(1)}, u32[]{:S(2)}, u32[]{:S(2)}) collective-permute-start(bf16[384,384]{1,0:T(8,128)(2,1)} %get-tuple-element.40.refs_0_), channel_id=1, source_target_pairs={{0,3},{1,0},{2,1},{3,2},{4,7},{5,4},{6,5},{7,6},{8,11},{9,8},{10,9... | collective-permute-start | bytes 884744 | tf_op jit(solution)/shard_map/ppermute | solution.py:237
  107.3 15.0 %copy-start.31 = (bf16[384,128]{1,0:T(8,128)(2,1)}, bf16[384,128]{1,0:T(8,128)(2,1)S(1)}, u32[]{:S(2)}) copy-start(bf16[384,128]{1,0:T(8,128)(2,1)S(1)} %collective-permute-done.20.refs_3_) | copy-start | bytes 294916
  107.3 15.0 %collective-permute-start.18 = (bf16[384,384]{1,0:T(8,128)(2,1)}, bf16[384,384]{1,0:T(8,128)(2,1)S(1)}, u32[]{:S(2)}, u32[]{:S(2)}) collective-permute-start(bf16[384,384]{1,0:T(8,128)(2,1)} %get-tuple-element.41.refs_1_), channel_id=1, source_target_pairs={{0,1},{1,2},{2,3},{3,0},{4,5},{5,6},{6,7},{7,4},{8,9},{9,10},{10,1... | collective-permute-start | bytes 884744 | tf_op jit(solution)/shard_map/ppermute | solution.py:237
  107.5 14.9 %copy-start.32 = (bf16[384,128]{1,0:T(8,128)(2,1)}, bf16[384,128]{1,0:T(8,128)(2,1)S(1)}, u32[]{:S(2)}) copy-start(bf16[384,128]{1,0:T(8,128)(2,1)S(1)} %collective-permute-done.21.refs_6_) | copy-start | bytes 294916
  107.5 10.2 %collective-permute-start.22 = (bf16[384,128]{1,0:T(8,128)(2,1)S(1)}, bf16[384,128]{1,0:T(8,128)(2,1)S(1)}, u32[]{:S(2)}, u32[]{:S(2)}) collective-permute-start(bf16[384,128]{1,0:T(8,128)(2,1)S(1)} %collective-permute-done.21.refs_6_), channel_id=1, source_target_pairs={{0,1},{1,2},{2,3},{3,0},{4,5},{5,6},{6,7},{7,4},{8,9},{9,10},{10,1... | collective-permute-start | bytes 294920 | tf_op jit(solution)/shard_map/ppermute | solution.py:237
  109.6 12.8 %copy-start.33 = (bf16[384,128]{1,0:T(8,128)(2,1)}, bf16[384,128]{1,0:T(8,128)(2,1)S(1)}, u32[]{:S(2)}) copy-start(bf16[384,128]{1,0:T(8,128)(2,1)S(1)} %collective-permute-done.24.refs_7_) | copy-start | bytes 294916
  109.6 8.1 %collective-permute-start.23 = (bf16[384,128]{1,0:T(8,128)(2,1)S(1)}, bf16[384,128]{1,0:T(8,128)(2,1)S(1)}, u32[]{:S(2)}, u32[]{:S(2)}) collective-permute-start(bf16[384,128]{1,0:T(8,128)(2,1)S(1)} %collective-permute-done.20.refs_3_), channel_id=1, source_target_pairs={{0,3},{1,0},{2,1},{3,2},{4,7},{5,4},{6,5},{7,6},{8,11},{9,8},{10,9... | collective-permute-start | bytes 294920 | tf_op jit(solution)/shard_map/ppermute | solution.py:237
  117.7 4.7 %copy-start.34 = (bf16[384,128]{1,0:T(8,128)(2,1)}, bf16[384,128]{1,0:T(8,128)(2,1)S(1)}, u32[]{:S(2)}) copy-start(bf16[384,128]{1,0:T(8,128)(2,1)S(1)} %collective-permute-done.22.refs_4_) | copy-start | bytes 294916
  117.7 18.2 %collective-permute-start.15 = (bf16[384,384]{1,0:T(8,128)(2,1)}, bf16[384,384]{1,0:T(8,128)(2,1)S(1)}, u32[]{:S(2)}, u32[]{:S(2)}) collective-permute-start(bf16[384,384]{1,0:T(8,128)(2,1)} %get-tuple-element.40.refs_0_), channel_id=1, source_target_pairs={{0,1},{1,2},{2,3},{3,0},{4,5},{5,6},{6,7},{7,4},{8,9},{9,10},{10,1... | collective-permute-start | bytes 884744 | tf_op jit(solution)/shard_map/ppermute | solution.py:237
  117.7 4.7 %copy-start.35 = (bf16[384,128]{1,0:T(8,128)(2,1)}, bf16[384,128]{1,0:T(8,128)(2,1)S(1)}, u32[]{:S(2)}) copy-start(bf16[384,128]{1,0:T(8,128)(2,1)S(1)} %collective-permute-done.23.refs_5_) | copy-start | bytes 294916
  117.7 18.3 %collective-permute-start.14 = (bf16[384,384]{1,0:T(8,128)(2,1)}, bf16[384,384]{1,0:T(8,128)(2,1)S(1)}, u32[]{:S(2)}, u32[]{:S(2)}) collective-permute-start(bf16[384,384]{1,0:T(8,128)(2,1)} %get-tuple-element.41.refs_1_), channel_id=1, source_target_pairs={{0,3},{1,0},{2,1},{3,2},{4,7},{5,4},{6,5},{7,6},{8,11},{9,8},{10,9... | collective-permute-start | bytes 884744 | tf_op jit(solution)/shard_map/ppermute | solution.py:237
  129.2 25.9 %all-to-all-start.3 = ((bf16[32,72,128]{2,1,0:T(8,128)(2,1)}), bf16[32,72,128]{2,1,0:T(8,128)(2,1)S(1)}, u32[]{:S(2)}, u32[]{:S(2)}) async-start(bf16[32,72,128]{2,1,0:T(8,128)(2,1)} %bitcast.42), calls=%async_computation.3 | async-start | bytes 1179648 | tf_op jit(solution)/shard_map/all_to_all | solution.py:622
  135.8 10.5 %copy-start.15 = (bf16[384,384]{1,0:T(8,128)(2,1)}, bf16[384,384]{1,0:T(8,128)(2,1)S(1)}, u32[]{:S(2)}) copy-start(bf16[384,384]{1,0:T(8,128)(2,1)S(1)} %collective-permute-done.15.refs_6_) | copy-start | bytes 884740
  135.9 10.5 %collective-permute-start.16 = (bf16[384,384]{1,0:T(8,128)(2,1)S(1)}, bf16[384,384]{1,0:T(8,128)(2,1)S(1)}, u32[]{:S(2)}, u32[]{:S(2)}) collective-permute-start(bf16[384,384]{1,0:T(8,128)(2,1)S(1)} %collective-permute-done.15.refs_6_), channel_id=1, source_target_pairs={{0,1},{1,2},{2,3},{3,0},{4,5},{5,6},{6,7},{7,4},{8,9},{9,10},{10,1... | collective-permute-start | bytes 884744 | tf_op jit(solution)/shard_map/ppermute | solution.py:237
  135.9 10.4 %copy-start.16 = (bf16[384,384]{1,0:T(8,128)(2,1)}, bf16[384,384]{1,0:T(8,128)(2,1)S(1)}, u32[]{:S(2)}) copy-start(bf16[384,384]{1,0:T(8,128)(2,1)S(1)} %collective-permute-done.14.refs_3_) | copy-start | bytes 884740
  136.0 10.4 %collective-permute-start.17 = (bf16[384,384]{1,0:T(8,128)(2,1)S(1)}, bf16[384,384]{1,0:T(8,128)(2,1)S(1)}, u32[]{:S(2)}, u32[]{:S(2)}) collective-permute-start(bf16[384,384]{1,0:T(8,128)(2,1)S(1)} %collective-permute-done.14.refs_3_), channel_id=1, source_target_pairs={{0,3},{1,0},{2,1},{3,2},{4,7},{5,4},{6,5},{7,6},{8,11},{9,8},{10,9... | collective-permute-start | bytes 884744 | tf_op jit(solution)/shard_map/ppermute | solution.py:237
  155.2 10.8 %copy-start.36 = (s32[1,768]{1,0:T(1,128)S(1)}, s32[1,768]{1,0:T(1,128)}, u32[]{:S(2)}) copy-start(s32[1,768]{1,0:T(1,128)} %get-tuple-element.30.slot_ref) | copy-start | bytes 9220
  155.2 39.2 %all-to-all-start.2 = ((bf16[32,72,384]{2,1,0:T(8,128)(2,1)}), bf16[32,72,384]{2,1,0:T(8,128)(2,1)S(1)}, u32[]{:S(2)}, u32[]{:S(2)}) async-start(bf16[32,72,384]{2,1,0:T(8,128)(2,1)} %bitcast.41), calls=%async_computation.2 | async-start | bytes 3538944 | tf_op jit(solution)/shard_map/all_to_all | solution.py:622
  165.7 3.4 %collective-permute-start.26 = (f32[16,24,512]{2,1,0:T(8,128)}, f32[16,24,512]{2,1,0:T(8,128)S(1)}, u32[]{:S(2)}, u32[]{:S(2)}) collective-permute-start(f32[16,24,512]{2,1,0:T(8,128)} %get-tuple-element.48), channel_id=1, source_target_pairs={{0,4},{4,0},{1,5},{5,1},{2,6},{6,2},{3,7},{7,3},{8,12},{12,8},{9,1... | collective-permute-start | bytes 2359304 | tf_op jit(solution)/shard_map/ppermute | solution.py:641
  167.6 1.5 copy-start.9
  167.6 1.5 collective-permute-start.25
  177.2 10.2 %collective-permute-start.27 = (bf16[16,64,128]{2,1,0:T(8,128)(2,1)}, bf16[16,64,128]{2,1,0:T(8,128)(2,1)S(1)}, u32[]{:S(2)}, u32[]{:S(2)}) collective-permute-start(bf16[16,64,128]{2,1,0:T(8,128)(2,1)} %get-tuple-element.50), channel_id=1, source_target_pairs={{0,1},{1,2},{2,3},{3,0},{4,5},{5,6},{6,7},{7,4},{8,9},{9,10},{10,1... | collective-permute-start | bytes 786440 | tf_op jit(solution)/shard_map/ppermute | solution.py:237
  177.3 15.9 %collective-permute-start.28 = (bf16[16,64,128]{2,1,0:T(8,128)(2,1)}, bf16[16,64,128]{2,1,0:T(8,128)(2,1)S(1)}, u32[]{:S(2)}, u32[]{:S(2)}) collective-permute-start(bf16[16,64,128]{2,1,0:T(8,128)(2,1)} %get-tuple-element.51), channel_id=1, source_target_pairs={{0,2},{1,3},{2,0},{3,1},{4,6},{5,7},{6,4},{7,5},{8,10},{9,11},{10,... | collective-permute-start | bytes 786440 | tf_op jit(solution)/shard_map/ppermute | solution.py:237
  180.9 12.4 %collective-permute-start.29 = (bf16[16,64,128]{2,1,0:T(8,128)(2,1)}, bf16[16,64,128]{2,1,0:T(8,128)(2,1)S(1)}, u32[]{:S(2)}, u32[]{:S(2)}) collective-permute-start(bf16[16,64,128]{2,1,0:T(8,128)(2,1)} %get-tuple-element.52), channel_id=1, source_target_pairs={{0,3},{1,0},{2,1},{3,2},{4,7},{5,4},{6,5},{7,6},{8,11},{9,8},{10,9... | collective-permute-start | bytes 786440 | tf_op jit(solution)/shard_map/ppermute | solution.py:237
  194.4 2.3 copy-start
  196.7 2.1 copy-start.3
  196.7 2.1 collective-permute-start.30
  245.5 6.2 %collective-permute-start.31 = (bf16[544,128]{1,0:T(8,128)(2,1)S(1)}, bf16[544,128]{1,0:T(8,128)(2,1)S(1)}, u32[]{:S(2)}, u32[]{:S(2)}) collective-permute-start(bf16[544,128]{1,0:T(8,128)(2,1)S(1)} %shard_map.125.refs_0_), channel_id=1, source_target_pairs={{0,1},{1,0},{2,3},{3,2},{4,5},{5,4},{6,7},{7,6},{8,9},{9,8},{10,11... | collective-permute-start | bytes 417800 | tf_op jit(solution)/shard_map/ppermute | solution.py:684
  245.8 9.5 %collective-permute-start.32 = (bf16[544,128]{1,0:T(8,128)(2,1)S(1)}, bf16[544,128]{1,0:T(8,128)(2,1)S(1)}, u32[]{:S(2)}, u32[]{:S(2)}) collective-permute-start(bf16[544,128]{1,0:T(8,128)(2,1)S(1)} %shard_map.125.refs_0_), channel_id=1, source_target_pairs={{0,2},{1,3},{2,0},{3,1},{4,6},{5,7},{6,4},{7,5},{8,10},{9,11},{10,... | collective-permute-start | bytes 417800 | tf_op jit(solution)/shard_map/ppermute | solution.py:684
  249.7 7.4 %collective-permute-start.33 = (bf16[544,128]{1,0:T(8,128)(2,1)S(1)}, bf16[544,128]{1,0:T(8,128)(2,1)S(1)}, u32[]{:S(2)}, u32[]{:S(2)}) collective-permute-start(bf16[544,128]{1,0:T(8,128)(2,1)S(1)} %shard_map.125.refs_0_), channel_id=1, source_target_pairs={{0,3},{1,2},{2,1},{3,0},{4,7},{5,6},{6,5},{7,4},{8,11},{9,10},{10,... | collective-permute-start | bytes 417800 | tf_op jit(solution)/shard_map/ppermute | solution.py:684
  (12 other events, 9.5 us)

commit v3 on v2

--- a/solution.py
+++ b/solution.py
@@ -39,21 +39,39 @@
     return jax.ShapeDtypeStruct(shape, BF16)
 
 
-def pool_tiles(pick, x_ref, pooled_ref):
+def pool_tiles(pick, x_ref, pooled_ref, together):
     tiles = x_ref.shape[1] // 16
-    for group in range(x_ref.shape[0] // 16):
-        docs = pl.ds(group * 16, 16)
+    for group in range(0, x_ref.shape[0] // 16, together):
         block = jnp.concatenate(
-            [x_ref[docs, t * 16:(t + 1) * 16, :].reshape(256, 128) for t in range(tiles)], axis=1
+            [
+                x_ref[(group + g) * 16:(group + g + 1) * 16, t * 16:(t + 1) * 16, :].reshape(256, 128)
+                for g in range(together)
+                for t in range(tiles)
+            ],
+            axis=1,
         )
         mean = jnp.dot(pick[...], block, preferred_element_type=F32).astype(BF16)
-        for j in range(8):
-            for t in range(tiles):
-                at = (t * 8 + j) * 128
-                pooled_ref[docs, at:at + 128] = mean[j * 16:(j + 1) * 16, t * 128:(t + 1) * 128]
-
-
-def project_block(x_ref, w_hbm, first, pick, pooled, side, w_ref, w_sem):
+        for g in range(together):
+            docs = slice((group + g) * 16, (group + g + 1) * 16)
+            for j in range(8):
+                for t in range(tiles):
+                    at, lane = (t * 8 + j) * 128, (g * tiles + t) * 128
+                    pooled_ref[docs, at:at + 128] = mean[j * 16:(j + 1) * 16, lane:lane + 128]
+
+
+def pool_tiles_mixed(pick, wide_rows, x_ref, pooled_ref):
+    rows = x_ref.shape[1]
+    for group in range(0, x_ref.shape[0] // 16, 2):
+        pool_tiles(pick, x_ref.at[group * 16:(group + 1) * 16], pooled_ref.at[group * 16:(group + 1) * 16], 1)
+        docs = slice((group + 1) * 16, (group + 2) * 16)
+        wide_rows[...] = x_ref[docs].reshape(16 * rows, 128).astype(F32)
+        for tile in range(rows // 2):
+            first = wide_rows[pl.ds(2 * tile, 16, stride=rows), :]
+            second = wide_rows[pl.ds(2 * tile + 1, 16, stride=rows), :]
+            pooled_ref[docs, tile * 128:(tile + 1) * 128] = ((first + second) * 0.5).astype(BF16)
+
+
+def project_block(x_ref, w_hbm, first, pick, pooled, side, w_ref, w_sem, wide_rows=None):
     at = pl.program_id(0)
     step = x_ref.shape[0]
     load = pltpu.make_async_copy(w_hbm.at[:, pl.ds(first, w_ref.shape[1])], w_ref, w_sem)
@@ -66,7 +84,10 @@
         same_tile = out_row // 16 == (in_row % 16) // 2
         pick[...] = jnp.where(same_doc & same_tile, 0.5, 0.0).astype(BF16)
 
-    pool_tiles(pick, x_ref, pooled)
+    if wide_rows is None:
+        pool_tiles(pick, x_ref, pooled, 4)
+    else:
+        pool_tiles_mixed(pick, wide_rows, x_ref, pooled)
 
     @pl.when(at == 0)
     def _():
@@ -107,9 +128,9 @@
 
 
 def turn_kernel(slot_ref, x_ref, w_hbm, out_ref, mine_ref, theirs_ref,
-                pick, pooled, side, w_ref, w_sem):
+                pick, pooled, side, w_ref, w_sem, wide_rows):
     first = w_hbm.shape[1] - w_ref.shape[1]
-    project_block(x_ref, w_hbm, first, pick, pooled, side, w_ref, w_sem)
+    project_block(x_ref, w_hbm, first, pick, pooled, side, w_ref, w_sem, wide_rows)
     rows = mine_ref.shape[1]
     core = lax.axis_index("core")
     for pair in range(mine_ref.shape[0] // 2):
@@ -185,7 +206,8 @@
         ],
         out_specs=[whole(slots, wide), turned, turned],
         out_shape=[bf16(slots, wide), shape, shape],
-        scratch_shapes=pool_scratch(step, docs, depth, wide),
+        scratch_shapes=pool_scratch(step, docs, depth, wide)
+        + [pltpu.VMEM((16 * rows, 128), F32)],
         compiler_params=params(),
         cost_estimate=cost(6e9, 28e6),
     )(slot, taps, w_down)
@@ -252,13 +274,11 @@
 
 
 def block_row(index_ref, values_ref, table, row, per_row):
-    total = None
-    for k in range(per_row):
-        entry = row * per_row + k
-        at = pl.multiple_of(index_ref[entry] * 128, 128)
-        term = jnp.dot(values_ref[entry], table[pl.ds(at, 128), :], preferred_element_type=F32)
-        total = term if total is None else total + term
-    return total
+    entries = [row * per_row + k for k in range(per_row)]
+    at = [pl.multiple_of(index_ref[entry] * 128, 128) for entry in entries]
+    blocks = jnp.concatenate([values_ref[entry] for entry in entries], axis=1)
+    picked = jnp.concatenate([table[pl.ds(first, 128), :] for first in at], axis=0)
+    return jnp.dot(blocks, picked, preferred_element_type=F32)
 
 
 def product_kernel(index_ref, values_ref, *refs):
@@ -289,8 +309,7 @@
 def layer_kernel(index_ref, values_ref, *refs):
     parts = refs[:8]
     (first_ref, low_in_ref, high_in_ref, cot_ref, w_ref, wt_ref, gate_ref) = refs[8:15]
-    (side_out_ref, agg_ref, mgrad_ref, low_ref, high_ref, next_low_ref, next_high_ref,
-     gpart_ref, table) = refs[15:]
+    (side_out_ref, agg_ref, mgrad_ref, low_ref, high_ref, gpart_ref, table) = refs[15:]
     at = pl.program_id(0)
 
     @pl.when(at == 0)
@@ -299,7 +318,6 @@
 
     step = cot_ref.shape[0]
     wide = first_ref.shape[1]
-    lead = low_ref.shape[1]
     nodes = step * pl.num_programs(0)
     per_row = values_ref.shape[0] * 128 // nodes
     rows = step // 128
@@ -329,18 +347,16 @@
 
     @pl.when(at == 0)
     def _():
-        low_ref[...] = agrad[:, :lead]
-        next_low_ref[...] = agrad[:, lead:]
+        low_ref[...] = agrad
         gpart_ref[...] = part
 
     @pl.when(at == 1)
     def _():
-        high_ref[...] = agrad[:, :lead]
-        next_high_ref[...] = agrad[:, lead:]
+        high_ref[...] = agrad
         gpart_ref[...] += part
 
 
-def layer(index, values, parts, first, owned, cotangent, w_msg, gate, lead):
+def layer(index, values, parts, first, owned, cotangent, w_msg, gate):
     nodes, width = cotangent.shape
     wide = first.shape[1]
     step = nodes // 2
@@ -352,10 +368,10 @@
         + [whole(*part.shape) for part in parts]
         + [rows(wide), whole(step, wide), whole(step, wide), rows(width), whole(width, width), whole(width, width),
            whole(1, width)],
-        out_specs=[rows(width), rows(width), rows(width), whole(step, lead), whole(step, lead),
-                   whole(step, width - lead), whole(step, width - lead), whole(1, width)],
-        out_shape=[bf16(nodes, width), bf16(nodes, width), bf16(nodes, width), bf16(step, lead),
-                   bf16(step, lead), bf16(step, width - lead), bf16(step, width - lead),
+        out_specs=[rows(width), rows(width), rows(width), whole(step, width), whole(step, width),
+                   whole(1, width)],
+        out_shape=[bf16(nodes, width), bf16(nodes, width), bf16(nodes, width), bf16(step, width),
+                   bf16(step, width),
                    jax.ShapeDtypeStruct((1, width), F32)],
         scratch_shapes=[pltpu.VMEM((4 * nodes, width - wide), BF16)],
         compiler_params=params(),
@@ -363,7 +379,7 @@
     )(index, values, *parts, first, *owned, cotangent, w_msg, w_msg.T, gate)
 
 
-def back_kernel(first, index_ref, values_ref, *refs):
+def back_kernel(index_ref, values_ref, *refs):
     parts, (cot_ref, place_ref), (out_ref, table, grad) = refs[:8], refs[8:10], refs[-3:]
     nodes = cot_ref.shape[0]
     per_row = values_ref.shape[0] * 128 // nodes
@@ -374,30 +390,29 @@
         for row in range(nodes // 128):
             at = slice(row * 128, (row + 1) * 128)
             total = block_row(index_ref, values_ref, table, row, per_row)
-            upstream = cot_ref[at, first:first + total.shape[1]].astype(F32)
+            upstream = cot_ref[at, :].astype(F32)
             grad[at, :] = (upstream + total).astype(BF16)
 
     mask = iota((out_ref.shape[0], nodes), 1) == place_ref[...]
     out_ref[...] = jnp.dot(one_hot(mask), grad[...], preferred_element_type=F32).astype(BF16)
 
 
-def back(index, values, parts, cotangent, first, place, slots, after=()):
+def back(index, values, parts, cotangent, place, slots):
     nodes = cotangent.shape[0]
     wide = parts[0].shape[1]
     step = slots // 4
     return pl.pallas_call(
-        functools.partial(back_kernel, first),
+        back_kernel,
         grid=(4,),
         in_specs=[pl.BlockSpec(memory_space=pltpu.SMEM), whole(*values.shape)]
         + [whole(*part.shape) for part in parts]
-        + [whole(*cotangent.shape), pl.BlockSpec((step, 1), lambda i: (i, 0))]
-        + [pl.BlockSpec(memory_space=pl.ANY) for _ in after],
+        + [whole(*cotangent.shape), pl.BlockSpec((step, 1), lambda i: (i, 0))],
         out_specs=pl.BlockSpec((step, wide), lambda i: (i, 0)),
         out_shape=bf16(slots, wide),
         scratch_shapes=[pltpu.VMEM((4 * nodes, wide), BF16), pltpu.VMEM((nodes, wide), BF16)],
         compiler_params=params(),
         cost_estimate=cost(2 * slots * nodes * wide, 5e6),
-    )(index, values, *parts, cotangent, place, *after)
+    )(index, values, *parts, cotangent, place)
 
 
 def small_kernel(agg_ref, mgrad_ref, gate_ref, after_ref, mine_ref, theirs_ref):
@@ -435,11 +450,11 @@
 def down_rows(mine_ref, other_ref, grad_ref, other_grad_ref):
     docs = mine_ref.shape[2]
     rows = mine_ref.shape[0] * mine_ref.shape[1]
-    return jnp.dot(
-        mine_ref[...].reshape(rows, docs), grad_ref[...], preferred_element_type=F32
-    ) + jnp.dot(
-        other_ref[...].reshape(rows, docs), other_grad_ref[...], preferred_element_type=F32
+    left = jnp.concatenate(
+        [mine_ref[...].reshape(rows, docs), other_ref[...].reshape(rows, docs)], axis=1
     )
+    right = jnp.concatenate([grad_ref[...], other_grad_ref[...]], axis=0)
+    return jnp.dot(left, right, preferred_element_type=F32)
 
 
 def tiles_of(array):
@@ -448,26 +463,18 @@
 
 def two_terms(row):
     high = row.astype(BF16).astype(F32)
-    return [high, row - high, jnp.zeros((6, 128), F32)]
-
-
-def down_by_col_kernel(mine_ref, other_ref, grad_ref, other_grad_ref, small_ref,
-                       other_small_ref, *out_refs):
-    total = down_rows(mine_ref, other_ref, grad_ref, other_grad_ref)
+    return [high, row - high, jnp.zeros((14, 128), F32)]
+
+
+def small_by_col_kernel(small_ref, other_small_ref, *out_refs):
     small = small_ref[...] + other_small_ref[...]
     chips = small.shape[0]
     msg = (small.shape[1] - 8) // 4
-    piece = total.shape[0] // (4 * chips)
     blocks = []
     for chip in range(chips):
         for col in range(4):
-            at = (chip * 4 + col) * piece
             gate = small[chip, 4 * msg:4 * msg + 1, col * 128:(col + 1) * 128]
-            cells = (
-                tiles_of(total[at:at + piece, :])
-                + tiles_of(small[chip, col * msg:(col + 1) * msg, :])
-                + two_terms(gate)
-            )
+            cells = tiles_of(small[chip, col * msg:(col + 1) * msg, :]) + two_terms(gate)
             blocks.append(jnp.concatenate(cells, axis=0).astype(BF16))
     my_col = lax.axis_index("col")
     for first in range(4):
@@ -478,10 +485,22 @@
                     out_ref[chip] = blocks[chip * 4 + (first + k) % 4]
 
 
+def small_by_col(small, other_small, cols):
+    vmem = pl.BlockSpec(memory_space=pltpu.VMEM)
+    return pl.pallas_call(
+        small_by_col_kernel,
+        in_specs=[vmem] * 2,
+        out_specs=[vmem] * cols,
+        out_shape=[bf16(small.shape[0], 32, 128)] * cols,
+        compiler_params=params(),
+        cost_estimate=cost(1e6, 2e6),
+    )(small, other_small)
+
+
 def lead_kernel(*refs):
     total = sum([ref[...].astype(F32) for ref in refs[1:4]], refs[0][...].astype(F32))
     out_ref = refs[4]
-    at = total.shape[1] - 8
+    at = total.shape[1] - 16
     for chip in range(total.shape[0]):
         gate = total[chip, at:at + 1, :] + total[chip, at + 1:at + 2, :]
         cells = [total[chip, :at, :]] + two_terms(gate)
@@ -516,21 +535,6 @@
     return [rows, rows, whole(*grad.shape), whole(*grad.shape)]
 
 
-def down_by_col(mine, other, grad, other_grad, small, other_small, cols):
-    chips, share, docs = mine.shape
-    rows = share // cols * grad.shape[1] // 128 + 24
-    by_chip = pl.BlockSpec((chips // 4,) + small.shape[1:], lambda i: (i, 0, 0))
-    return pl.pallas_call(
-        down_by_col_kernel,
-        grid=(4,),
-        in_specs=down_specs(mine, grad) + [by_chip, by_chip],
-        out_specs=[pl.BlockSpec((chips // 4, rows, 128), lambda i: (i, 0, 0))] * cols,
-        out_shape=[bf16(chips, rows, 128)] * cols,
-        compiler_params=params(),
-        cost_estimate=cost(2e9, 10e6),
-    )(mine, other, grad, other_grad, small, other_small)
-
-
 def down_by_chip(mine, other, grad, other_grad, led):
     chips, share, docs = mine.shape
     rows = share * grad.shape[1] // 128 + led.shape[1]
@@ -548,7 +552,7 @@
 
 def fold_kernel(parts_ref, out_ref):
     total = jnp.sum(parts_ref[...].astype(F32), axis=0)
-    at = total.shape[0] - 8
+    at = total.shape[0] - 16
     gate = total[at:at + 1, :] + total[at + 1:at + 2, :]
     out_ref[...] = jnp.concatenate([total[:at, :]] + two_terms(gate), axis=0).astype(BF16)
 
@@ -566,16 +570,15 @@
     )(parts)
 
 
-def finish_kernel(lead, *refs):
+def finish_kernel(*refs):
     found, (down_ref, msg_ref, gate_ref) = refs[:4], refs[4:]
     share, width = down_ref.shape
     msg = msg_ref.shape[0]
-    piece = share // 4
     my_col = lax.axis_index("col")
     own, near, far, cross = (ref[...].astype(F32) for ref in found)
     total = (own + near) + (far + cross)
     at = 0
-    for lane in range(lead, width, 128):
+    for lane in range(0, width, 128):
         down_ref[:, lane:lane + 128] = total[at:at + share, :]
         at += share
 
@@ -589,25 +592,22 @@
     for col in range(4):
         part = from_col(col)
         row = 0
-        for lane in range(0, lead, 128):
-            down_ref[col * piece:(col + 1) * piece, lane:lane + 128] = part[row:row + piece, :]
-            row += piece
         for lane in range(0, width, 128):
             msg_ref[col * msg // 4:(col + 1) * msg // 4, lane:lane + 128] = (
                 part[row:row + msg // 4, :]
             )
             row += msg // 4
     first = lax.axis_index(ROWS) * msg
-    gate = from_col(first // 128)[-8:, :]
+    gate = from_col(first // 128)[-16:, :]
     spread = jnp.broadcast_to(gate[0:1, :] + gate[1:2, :], (8, 128))
     gate_ref[...] = pltpu.roll(spread, (128 - first % 128) % 128, 1)[:1, :msg]
 
 
-def finish(found, share, msg, width, lead):
+def finish(found, share, msg, width):
     vmem = pl.BlockSpec(memory_space=pltpu.VMEM)
     shape = lambda *dims: jax.ShapeDtypeStruct(dims, F32)
     return pl.pallas_call(
-        functools.partial(finish_kernel, lead),
+        finish_kernel,
         in_specs=[vmem] * 4,
         out_specs=[vmem] * 3,
         out_shape=[shape(share, width), shape(msg, width), shape(1, msg)],
@@ -629,7 +629,6 @@
     docs = doc_taps.shape[0]
     depth, width = w_down.shape
     wide = width // 2
-    lead = width // 4
     row_size, cols = lax.axis_size(ROWS), lax.axis_size("col")
     my_row, my_col = lax.axis_index(ROWS), lax.axis_index("col")
     slots = row_size * SLOTS
@@ -659,33 +658,24 @@
     parts0 = gather_ring(*owned0)
     owned1 = take(pos_row, incoming1, docs, halves=True, after=parts0[4:6])
     first = product(index, values, parts0, docs)
-    side_out, aggregate, message_grad, low, high, next_low, next_high, gate_part = layer(
-        index, values, gather_ring(*owned1), first, owned0, cotangent, w_msg, gate, lead
+    side_out, aggregate, message_grad, low, high, gate_part = layer(
+        index, values, gather_ring(*owned1), first, owned0, cotangent, w_msg, gate
     )
 
-    slot_col = slot.reshape(docs, 1)
-    next_parts = gather_ring(next_low, next_high)
-    packed_back0 = back(index, values, gather_ring(low, high), cotangent, 0, pos_col, slots,
-                        after=(next_parts[2], next_parts[7]))
-    returned0 = relay(packed_back0)
-    packed_back1 = back(index, values, next_parts, cotangent, lead, pos_col, slots)
-    returned1 = relay(packed_back1)
-
-    small, other_small = small_sums(aggregate, message_grad, gate_part, chips, packed_back0)
-    other_small = swap(other_small)
-    grad0 = take(slot_col, returned0, docs)
-    pieces = down_by_col(mine, other, grad0, swap(grad0), small, other_small, cols)
+    packed_back = back(index, values, gather_ring(low, high), cotangent, pos_col, slots)
+    returned = relay(packed_back)
+
+    small, other_small = small_sums(aggregate, message_grad, gate_part, chips, packed_back)
+    pieces = small_by_col(small, swap(other_small), cols)
     led = lead_sum([pieces[0]] + [shift(pieces[k], k) for k in range(1, cols)])
-    grad1 = take(slot_col, returned1, docs, after=(led,))
-    down = down_by_chip(mine, other, grad1, swap(grad1), led)
+    grad = take(slot.reshape(docs, 1), returned, docs, after=(led,))
+    down = down_by_chip(mine, other, grad, swap(grad), led)
     down = lax.all_to_all(down, ("z", "x"), split_axis=0, concat_axis=0, tiled=True)
     own = fold(down)
     found = [own] + [
         lax.ppermute(own, "col", [(c, c ^ step) for c in range(4)]) for step in (1, 2, 3)
     ]
-    grad_down, grad_msg, grad_gate = finish(
-        found, depth // row_size, width // row_size, width, lead
-    )
+    grad_down, grad_msg, grad_gate = finish(found, depth // row_size, width // row_size, width)
     return side_out, grad_down, grad_msg, grad_gate.reshape(width // row_size)
 
 

time: 259 us -> 247 us (0.954)
  starting transfers between devices: 75 us -> 58.5 us
  waiting for transfers between devices: 50 us -> 62.3 us
  Pallas kernels: 84.2 us -> 73.6 us
  blocking collectives: 37.2 us -> 39.9 us
    all_to_all x4 -> x3, waiting for transfers between devices: 2.9 us -> 17.2 us  [relay(): lax.all_to_all(rows.reshape(size, slots // size, width), ROWS, split_axis...]
    pallas_call x4 -> x3, Pallas kernels: 20.8 us -> 10.7 us  [the longest x1 7.49 us: back(): pl.pallas_call(back_kernel, grid=(4,), in_specs=[pl.BlockSpec(memory_spac...]
    ppermute x27 -> x21, starting transfers between devices: 38.9 us -> 30.4 us  [shift(): return lax.ppermute(part, 'col', [(c, (c + by) % 4) for c in range(4)])]
    all_to_all x4 -> x3, starting transfers between devices: 30.3 us -> 22.9 us  [relay(): lax.all_to_all(rows.reshape(size, slots // size, width), ROWS, split_axis...]
    ppermute x27 -> x21, waiting for transfers between devices: 37 us -> 32.1 us  [shift(): return lax.ppermute(part, 'col', [(c, (c + by) % 4) for c in range(4)])]
    all_to_all x1, blocking collectives: 37.2 us -> 39.9 us  [shards(): lax.all_to_all(down, ('z', 'x'), split_axis=0, concat_axis=0, tiled=True)]
    pallas_call x4 -> x3, Pallas kernels: 6.3 us -> 4.88 us  [take(): pl.pallas_call(functools.partial(take_kernel, len(after)), grid=(2,), in_...]
    unnamed x77 -> x63, local copies, waits for them, and re-layouts: 7.54 us -> 7.71 us
  transfers between devices with their start and end apart: 38 -> 30, of which waited for: 18 -> 20; matrix products, arithmetic and copies ran while one was open for 1% -> 2% of each run, Pallas kernels for 22% -> 17%
where the time goes in v3:
time: 247 us
  Pallas kernels  73.6 us (30%)
  waiting for transfers between devices  62.3 us (25%)
  starting transfers between devices  58.5 us (24%)
  blocking collectives  39.9 us (16%)
  local copies, waits for them, and re-layouts  10.2 us (4%)
    all_to_all x1, blocking collectives, shards(): lax.all_to_all(down, ('z', 'x'), split_axis=0, concat_axis=0, tiled=True)  39.9 us
    ppermute x21, waiting for transfers between devices, shift(): return lax.ppermute(part, 'col', [(c, (c + by) % 4) for c in range(4)])  32.1 us
    ppermute x21, starting transfers between devices, shift(): return lax.ppermute(part, 'col', [(c, (c + by) % 4) for c in range(4)])  30.4 us
    all_to_all x3, starting transfers between devices, relay(): lax.all_to_all(rows.reshape(size, slots // size, width), ROWS, split_axis...  22.9 us
    pallas_call x1, Pallas kernels, pool_and_turn(): pl.pallas_call(turn_kernel, grid=(6,), in_specs=[whole(1, docs), pl.Block...  21.1 us
    all_to_all x3, waiting for transfers between devices, relay(): lax.all_to_all(rows.reshape(size, slots // size, width), ROWS, split_axis...  17.2 us
    pallas_call x1, Pallas kernels, pool_and_pack(): pl.pallas_call(pool_kernel, grid=(6,), in_specs=[whole(*owner_of.shape),...  15.7 us
    pallas_call x1, Pallas kernels, down_by_chip(): pl.pallas_call(down_by_chip_kernel, grid=(4,), in_specs=down_specs(mine,...  8.59 us
  transfers between devices with their start and end apart: 30, of which 20 were waited for; matrix products, arithmetic and copies ran while one was open for 2% of the time, Pallas kernels for 17%

profile of v3, /device:TPU:0, one launch (start us, length us, event | category | flops | bytes accessed | tf_op | source)
XLA Modules:
  0.0 246.5 jit_solution(1187347760646401501)
XLA Ops:
  0.6 15.7 %shard_map.111 = (bf16[2304,256]{1,0:T(8,128)(2,1)}, s32[1,768]{1,0:T(1,128)}) custom-call(s32[1,24576]{1,0:T(1,128)} %owner_ref.1, bf16[768,80,128]{2,1,0:T(8,128)(2,1)} %bitcast.43, bf16[5120,512]{1,0:T(8,128)(2,1)} %w_hbm.3), custom_call_target="tpu_custom_call" | custom-call | flops 6000000000 | bytes 20000000 | tf_op jit(solution)/shard_map/pallas_call | solution.py:176
  16.4 8.3 %all-to-all-start.1 = ((bf16[32,72,256]{2,1,0:T(8,128)(2,1)}), bf16[32,72,256]{2,1,0:T(8,128)(2,1)S(1)}, u32[]{:S(2)}, u32[]{:S(2)}) async-start(bf16[32,72,256]{2,1,0:T(8,128)(2,1)} %bitcast.40), calls=%async_computation.1 | async-start | bytes 2359296 | tf_op jit(solution)/shard_map/all_to_all | solution.py:622
  24.7 21.1 %shard_map.112 = (bf16[2304,256]{1,0:T(8,128)(2,1)}, bf16[16,160,768]{2,1,0:T(8,128)(2,1)}, bf16[16,160,768]{2,1,0:T(8,128)(2,1)}) custom-call(s32[1,768]{1,0:T(1,128)} %get-tuple-element.28.slot_ref, bf16[768,80,128]{2,1,0:T(8,128)(2,1)} %bitcast.44, bf16[5120,512]{1,0:T(8,128)(2,1)} %w_hbm.3), custom_call_target="tpu_custom_call" | custom-call | flops 6000000000 | bytes 28000000 | tf_op jit(solution)/shard_map/pallas_call | solution.py:199
  45.8 8.1 %all-to-all-start = ((bf16[32,72,256]{2,1,0:T(8,128)(2,1)}), bf16[32,72,256]{2,1,0:T(8,128)(2,1)S(1)}, u32[]{:S(2)}, u32[]{:S(2)}) async-start(bf16[32,72,256]{2,1,0:T(8,128)(2,1)} %bitcast.39), calls=%async_computation | async-start | bytes 2359296 | tf_op jit(solution)/shard_map/all_to_all | solution.py:622
  54.7 1.3 shard_map.113
  56.0 1.6 collective-permute-start
  57.7 1.7 collective-permute-start.2
  59.3 5.1 %collective-permute-done.refs_6_ = bf16[384,256]{1,0:T(8,128)(2,1)S(1)} collective-permute-done((bf16[384,256]{1,0:T(8,128)(2,1)S(1)}, bf16[384,256]{1,0:T(8,128)(2,1)S(1)}, u32[]{:S(2)}, u32[]{:S(2)}) %collective-permute-start) | collective-permute-done | bytes 196640 | tf_op jit(solution)/shard_map/ppermute | solution.py:259
  64.5 0.3 collective-permute-start.1
  64.8 2.9 %collective-permute-start.3 = (bf16[384,256]{1,0:T(8,128)(2,1)S(1)}, bf16[384,256]{1,0:T(8,128)(2,1)S(1)}, u32[]{:S(2)}, u32[]{:S(2)}) collective-permute-start(bf16[384,256]{1,0:T(8,128)(2,1)S(1)} %collective-permute-done.2.refs_3_), channel_id=1, source_target_pairs={{0,3},{1,0},{2,1},{3,2},{4,7},{5,4},{6,5},{7,6},{8,11},{9,8},{10,9... | collective-permute-start | bytes 589832 | tf_op jit(solution)/shard_map/ppermute | solution.py:259
  67.7 0.5 collective-permute-start.10
  68.2 4.7 %all-to-all-done = bf16[32,72,256]{2,1,0:T(8,128)(2,1)S(1)} async-done(((bf16[32,72,256]{2,1,0:T(8,128)(2,1)}), bf16[32,72,256]{2,1,0:T(8,128)(2,1)S(1)}, u32[]{:S(2)}, u32[]{:S(2)}) %all-to-all-start) | async-done | bytes 1179680 | tf_op jit(solution)/shard_map/all_to_all | solution.py:622
  73.1 1.3 shard_map.114
  74.4 1.5 collective-permute-start.6
  75.9 2.3 collective-permute-start.5
  78.2 1.1 copy.19
  79.3 3.2 %collective-permute-start.4 = (bf16[384,256]{1,0:T(8,128)(2,1)S(1)}, bf16[384,256]{1,0:T(8,128)(2,1)S(1)}, u32[]{:S(2)}, u32[]{:S(2)}) collective-permute-start(bf16[384,256]{1,0:T(8,128)(2,1)S(1)} %get-tuple-element.33.refs_0_), channel_id=1, source_target_pairs={{0,3},{1,0},{2,1},{3,2},{4,7},{5,4},{6,5},{7,6},{8,11},{9,8},{10,9... | collective-permute-start | bytes 589832 | tf_op jit(solution)/shard_map/ppermute | solution.py:259
  82.6 0.8 collective-permute-start.7
  83.4 2.9 %collective-permute-start.8 = (bf16[384,256]{1,0:T(8,128)(2,1)S(1)}, bf16[384,256]{1,0:T(8,128)(2,1)S(1)}, u32[]{:S(2)}, u32[]{:S(2)}) collective-permute-start(bf16[384,256]{1,0:T(8,128)(2,1)S(1)} %collective-permute-done.5.refs_3_), channel_id=1, source_target_pairs={{0,3},{1,0},{2,1},{3,2},{4,7},{5,4},{6,5},{7,6},{8,11},{9,8},{10,9... | collective-permute-start | bytes 589832 | tf_op jit(solution)/shard_map/ppermute | solution.py:259
  86.3 0.5 fusion.2.index_ref
  86.8 1.6 collective-permute-done.11.refs_7_
  88.4 0.6 copy-done.27
  89.0 2.9 %shard_map.115.refs_8_ = bf16[768,256]{1,0:T(8,128)(2,1)} custom-call(s32[24]{0:T(128)} %fusion.2.index_ref, bf16[24,128,128]{2,1,0:T(8,128)(2,1)} %bitcast.35, bf16[384,256]{1,0:T(8,128)(2,1)} %copy-done, bf16[384,256]{1,0:T(8,128)(2,1)} %copy-done.1, bf16[384,256]{1,0:T(8,128)(2,1)} %collective-permute-done.10.refs_2_, bf16[384,256]{1,0:T(8,128)(2,1)} %copy-done.26, ...), custom_call_target="tpu_custom_call" | custom-call | flops 200000000 | bytes 3000000 | tf_op jit(solution)/shard_map/pallas_call | solution.py:298
  92.0 0.4 collective-permute-done.9.refs_7_
  92.3 2.1 collective-permute-done.7.refs_4_
  94.5 0.6 copy-done.23
  95.2 6.0 %shard_map.116 = (bf16[768,512]{1,0:T(8,128)(2,1)}, bf16[768,512]{1,0:T(8,128)(2,1)}, bf16[768,512]{1,0:T(8,128)(2,1)}, bf16[384,512]{1,0:T(8,128)(2,1)}, bf16[384,512]{1,0:T(8,128)(2,1)}, /*index=5*/f32[1,512]{1,0:T(1,128)}) custom-call(s32[24]{0:T(128)} %fusion.2.index_ref, bf16[24,128,128]{2,1,0:T(8,128)(2,1)} %bitcast.36, bf16[384,256]{1,0:T(8,128)(2,1)} %copy-done.5, ...), custom_call_target="tpu_custom_call" | custom-call | flops 1200000000 | bytes 8000000 | tf_op jit(solution)/shard_map/pallas_call | solution.py:364
  101.3 3.2 %collective-permute-start.14 = (bf16[384,512]{1,0:T(8,128)(2,1)}, bf16[384,512]{1,0:T(8,128)(2,1)S(1)}, u32[]{:S(2)}, u32[]{:S(2)}) collective-permute-start(bf16[384,512]{1,0:T(8,128)(2,1)} %get-tuple-element.39.refs_1_), channel_id=1, source_target_pairs={{0,3},{1,0},{2,1},{3,2},{4,7},{5,4},{6,5},{7,6},{8,11},{9,8},{10,9... | collective-permute-start | bytes 1179656 | tf_op jit(solution)/shard_map/ppermute | solution.py:259
  104.5 0.6 collective-permute-start.13
  105.1 1.5 collective-permute-start.18
  106.5 7.0 %collective-permute-done.15.refs_6_ = bf16[384,512]{1,0:T(8,128)(2,1)S(1)} collective-permute-done((bf16[384,512]{1,0:T(8,128)(2,1)}, bf16[384,512]{1,0:T(8,128)(2,1)S(1)}, u32[]{:S(2)}, u32[]{:S(2)}) %collective-permute-start.15) | collective-permute-done | bytes 393248 | tf_op jit(solution)/shard_map/ppermute | solution.py:259
  113.6 0.8 collective-permute-done.14.refs_3_
  114.4 3.6 %collective-permute-start.17 = (bf16[384,512]{1,0:T(8,128)(2,1)S(1)}, bf16[384,512]{1,0:T(8,128)(2,1)S(1)}, u32[]{:S(2)}, u32[]{:S(2)}) collective-permute-start(bf16[384,512]{1,0:T(8,128)(2,1)S(1)} %collective-permute-done.14.refs_3_), channel_id=1, source_target_pairs={{0,3},{1,0},{2,1},{3,2},{4,7},{5,4},{6,5},{7,6},{8,11},{9,8},{10,9... | collective-permute-start | bytes 1179656 | tf_op jit(solution)/shard_map/ppermute | solution.py:259
  118.0 1.4 select_n.51.refs_9_
  119.4 3.4 %collective-permute-done.13.refs_2_ = bf16[384,512]{1,0:T(8,128)(2,1)S(1)} collective-permute-done((bf16[384,512]{1,0:T(8,128)(2,1)}, bf16[384,512]{1,0:T(8,128)(2,1)S(1)}, u32[]{:S(2)}, u32[]{:S(2)}) %collective-permute-start.13) | collective-permute-done | bytes 393248 | tf_op jit(solution)/shard_map/ppermute | solution.py:259
  122.8 5.5 %collective-permute-done.16.refs_4_ = bf16[384,512]{1,0:T(8,128)(2,1)S(1)} collective-permute-done((bf16[384,512]{1,0:T(8,128)(2,1)S(1)}, bf16[384,512]{1,0:T(8,128)(2,1)S(1)}, u32[]{:S(2)}, u32[]{:S(2)}) %collective-permute-start.16) | collective-permute-done | bytes 393248 | tf_op jit(solution)/shard_map/ppermute | solution.py:259
  128.4 0.7 copy-done.17
  129.1 0.7 copy-done.18
  129.8 7.5 %shard_map.117.after_ref = bf16[2304,512]{1,0:T(8,128)(2,1)} custom-call(s32[24]{0:T(128)} %fusion.2.index_ref, bf16[24,128,128]{2,1,0:T(8,128)(2,1)} %bitcast.37, bf16[384,512]{1,0:T(8,128)(2,1)} %get-tuple-element.38.refs_0_, bf16[384,512]{1,0:T(8,128)(2,1)} %get-tuple-element.39.refs_1_, bf16[384,512]{1,0:T(8,128)(2,1)} %copy-done.15, ...), custom_call_target="tpu_custom_call" | custom-call | flops 1811939328 | bytes 5000000 | tf_op jit(solution)/shard_map/pallas_call | solution.py:404
  137.3 6.6 %all-to-all-start.2 = ((bf16[32,72,512]{2,1,0:T(8,128)(2,1)}), bf16[32,72,512]{2,1,0:T(8,128)(2,1)S(1)}, u32[]{:S(2)}, u32[]{:S(2)}) async-start(bf16[32,72,512]{2,1,0:T(8,128)(2,1)} %bitcast.34), calls=%async_computation.2 | async-start | bytes 4718592 | tf_op jit(solution)/shard_map/all_to_all | solution.py:622
  143.9 3.2 %shard_map.118 = (f32[16,24,512]{2,1,0:T(8,128)}, f32[16,24,512]{2,1,0:T(8,128)}) custom-call(bf16[768,512]{1,0:T(8,128)(2,1)} %get-tuple-element.40.agg_ref, bf16[768,512]{1,0:T(8,128)(2,1)} %get-tuple-element.41.mgrad_ref, f32[1,512]{1,0:T(1,128)} %get-tuple-element.42.gate_ref, bf16[2304,512]{1,0:T(8,128)(2,1)} %shard_map.117.after_ref), custom_call_target="tpu_custom_call" | custom-call | flops 400000000 | bytes 4000000 | tf_op jit(solution)/shard_map/pallas_call | solution.py:440
  147.1 0.3 collective-permute-start.19
  147.4 2.2 collective-permute-done.19.other_small_ref
  149.6 0.9 copy-done.12
  150.5 2.4 shard_map.119
  152.9 3.7 %collective-permute-start.21 = (bf16[16,32,128]{2,1,0:T(8,128)(2,1)}, bf16[16,32,128]{2,1,0:T(8,128)(2,1)S(1)}, u32[]{:S(2)}, u32[]{:S(2)}) collective-permute-start(bf16[16,32,128]{2,1,0:T(8,128)(2,1)} %get-tuple-element.47), channel_id=1, source_target_pairs={{0,2},{1,3},{2,0},{3,1},{4,6},{5,7},{6,4},{7,5},{8,10},{9,11},{10,... | collective-permute-start | bytes 393224 | tf_op jit(solution)/shard_map/ppermute | solution.py:259
  156.6 0.9 copy.21.place_ref
  157.5 2.6 %collective-permute-done.20.refs_1_ = bf16[16,32,128]{2,1,0:T(8,128)(2,1)S(1)} collective-permute-done((bf16[16,32,128]{2,1,0:T(8,128)(2,1)}, bf16[16,32,128]{2,1,0:T(8,128)(2,1)S(1)}, u32[]{:S(2)}, u32[]{:S(2)}) %collective-permute-start.20) | collective-permute-done | bytes 131104 | tf_op jit(solution)/shard_map/ppermute | solution.py:259
  160.1 3.1 %collective-permute-done.21.refs_2_ = bf16[16,32,128]{2,1,0:T(8,128)(2,1)S(1)} collective-permute-done((bf16[16,32,128]{2,1,0:T(8,128)(2,1)}, bf16[16,32,128]{2,1,0:T(8,128)(2,1)S(1)}, u32[]{:S(2)}, u32[]{:S(2)}) %collective-permute-start.21) | collective-permute-done | bytes 131104 | tf_op jit(solution)/shard_map/ppermute | solution.py:259
  163.4 0.9 copy-done.9
  164.4 12.5 %all-to-all-done.2 = bf16[32,72,512]{2,1,0:T(8,128)(2,1)S(1)} async-done(((bf16[32,72,512]{2,1,0:T(8,128)(2,1)}), bf16[32,72,512]{2,1,0:T(8,128)(2,1)S(1)}, u32[]{:S(2)}, u32[]{:S(2)}) %all-to-all-start.2) | async-done | bytes 2359328 | tf_op jit(solution)/shard_map/all_to_all | solution.py:622
  177.0 1.0 copy-done.4
  178.0 2.3 shard_map.121.grad_ref
  180.3 2.3 collective-permute-done.23.other_grad_ref
  182.6 0.9 copy-done.11
  183.5 8.6 %shard_map.122 = bf16[16,672,128]{2,1,0:T(8,128)(2,1)} custom-call(bf16[16,160,768]{2,1,0:T(8,128)(2,1)} %get-tuple-element.36.mine_ref, bf16[16,160,768]{2,1,0:T(8,128)(2,1)} %collective-permute-done.12.other_ref, bf16[768,512]{1,0:T(8,128)(2,1)} %copy-done.2, bf16[768,512]{1,0:T(8,128)(2,1)} %copy-done.11, bf16[16,32,128]{2,1,0:T(8,128)(2,1)} %copy-done.3), custom_call_target="tpu_custom_call" | custom-call | flops 2000000000 | bytes 12000000 | tf_op jit(solution)/shard_map/pallas_call | solution.py:542
  192.1 39.9 %all_to_all.20.parts_ref = bf16[16,672,128]{2,1,0:T(8,128)(2,1)S(1)} all-to-all(bf16[16,672,128]{2,1,0:T(8,128)(2,1)} %shard_map.122), channel_id=1, replica_groups=mesh['z'=4,'x'=4,'core'=2,'col'=4] {'z','x'}, dimensions={0} | all-to-all | bytes 5505024 | tf_op jit(solution)/shard_map/all_to_all | solution.py:673
  232.0 0.4 shard_map.123.refs_0_
  232.4 3.7 %collective-permute-start.25 = (bf16[672,128]{1,0:T(8,128)(2,1)S(1)}, bf16[672,128]{1,0:T(8,128)(2,1)S(1)}, u32[]{:S(2)}, u32[]{:S(2)}) collective-permute-start(bf16[672,128]{1,0:T(8,128)(2,1)S(1)} %shard_map.123.refs_0_), channel_id=1, source_target_pairs={{0,2},{1,3},{2,0},{3,1},{4,6},{5,7},{6,4},{7,5},{8,10},{9,11},{10,... | collective-permute-start | bytes 516104 | tf_op jit(solution)/shard_map/ppermute | solution.py:676
  236.1 1.0 collective-permute-start.26
  237.1 2.6 %collective-permute-done.24.refs_1_ = bf16[672,128]{1,0:T(8,128)(2,1)S(1)} collective-permute-done((bf16[672,128]{1,0:T(8,128)(2,1)S(1)}, bf16[672,128]{1,0:T(8,128)(2,1)S(1)}, u32[]{:S(2)}, u32[]{:S(2)}) %collective-permute-start.24) | collective-permute-done | bytes 172064 | tf_op jit(solution)/shard_map/ppermute | solution.py:676
  239.7 3.7 %collective-permute-done.25.refs_2_ = bf16[672,128]{1,0:T(8,128)(2,1)S(1)} collective-permute-done((bf16[672,128]{1,0:T(8,128)(2,1)S(1)}, bf16[672,128]{1,0:T(8,128)(2,1)S(1)}, u32[]{:S(2)}, u32[]{:S(2)}) %collective-permute-start.25) | collective-permute-done | bytes 172064 | tf_op jit(solution)/shard_map/ppermute | solution.py:676
  243.4 2.2 collective-permute-done.26.refs_3_
  245.7 0.9 shard_map.124
  (83 shorter events, 1.6 us)
Async XLA Ops:
  16.4 29.4 %all-to-all-start.1 = ((bf16[32,72,256]{2,1,0:T(8,128)(2,1)}), bf16[32,72,256]{2,1,0:T(8,128)(2,1)S(1)}, u32[]{:S(2)}, u32[]{:S(2)}) async-start(bf16[32,72,256]{2,1,0:T(8,128)(2,1)} %bitcast.40), calls=%async_computation.1 | async-start | bytes 2359296 | tf_op jit(solution)/shard_map/all_to_all | solution.py:622
  24.6 29.3 %copy-start.28 = (s32[1,24576]{1,0:T(1,128)S(1)}, s32[1,24576]{1,0:T(1,128)}, u32[]{:S(2)}) copy-start(s32[1,24576]{1,0:T(1,128)} %owner_ref.1) | copy-start | bytes 294916
  45.8 27.1 %all-to-all-start = ((bf16[32,72,256]{2,1,0:T(8,128)(2,1)}), bf16[32,72,256]{2,1,0:T(8,128)(2,1)S(1)}, u32[]{:S(2)}, u32[]{:S(2)}) async-start(bf16[32,72,256]{2,1,0:T(8,128)(2,1)} %bitcast.39), calls=%async_computation | async-start | bytes 2359296 | tf_op jit(solution)/shard_map/all_to_all | solution.py:622
  54.7 23.6 %copy-start.10 = (bf16[512,512]{1,0:T(8,128)(2,1)S(1)}, bf16[512,512]{1,0:T(8,128)(2,1)}, u32[]{:S(2)}) copy-start(bf16[512,512]{1,0:T(8,128)(2,1)} %refs_12_.1) | copy-start | bytes 1572868
  56.0 32.4 %copy-start = (bf16[384,256]{1,0:T(8,128)(2,1)}, bf16[384,256]{1,0:T(8,128)(2,1)S(1)}, u32[]{:S(2)}) copy-start(bf16[384,256]{1,0:T(8,128)(2,1)S(1)} %get-tuple-element.31.refs_0_.refs_9_) | copy-start | bytes 589828
  56.0 32.4 %copy-start.1 = (bf16[384,256]{1,0:T(8,128)(2,1)}, bf16[384,256]{1,0:T(8,128)(2,1)S(1)}, u32[]{:S(2)}) copy-start(bf16[384,256]{1,0:T(8,128)(2,1)S(1)} %get-tuple-element.32.refs_1_.refs_10_) | copy-start | bytes 589828
  56.0 30.3 %copy-start.30 = (s32[1,24]{1,0:T(1,128)S(1)}, s32[1,24]{1,0:T(1,128)}, u32[]{:S(2)}) copy-start(s32[1,24]{1,0:T(1,128)} %param.12) | copy-start | bytes 292
  56.0 8.4 %collective-permute-start = (bf16[384,256]{1,0:T(8,128)(2,1)S(1)}, bf16[384,256]{1,0:T(8,128)(2,1)S(1)}, u32[]{:S(2)}, u32[]{:S(2)}) collective-permute-start(bf16[384,256]{1,0:T(8,128)(2,1)S(1)} %get-tuple-element.31.refs_0_.refs_9_), channel_id=1, source_target_pairs={{0,1},{1,2},{2,3},{3,0},{4,5},{5,6},{6,7},{7,4},{8,9},{9,10},{10,1... | collective-permute-start | bytes 589832 | tf_op jit(solution)/shard_map/ppermute | solution.py:259
  57.7 7.1 %collective-permute-start.2 = (bf16[384,256]{1,0:T(8,128)(2,1)S(1)}, bf16[384,256]{1,0:T(8,128)(2,1)S(1)}, u32[]{:S(2)}, u32[]{:S(2)}) collective-permute-start(bf16[384,256]{1,0:T(8,128)(2,1)S(1)} %get-tuple-element.32.refs_1_.refs_10_), channel_id=1, source_target_pairs={{0,3},{1,0},{2,1},{3,2},{4,7},{5,4},{6,5},{7,6},{8,11},{9,8},{10,9... | collective-permute-start | bytes 589832 | tf_op jit(solution)/shard_map/ppermute | solution.py:259
  64.5 23.9 %copy-start.25 = (bf16[384,256]{1,0:T(8,128)(2,1)}, bf16[384,256]{1,0:T(8,128)(2,1)S(1)}, u32[]{:S(2)}) copy-start(bf16[384,256]{1,0:T(8,128)(2,1)S(1)} %collective-permute-done.refs_6_) | copy-start | bytes 589828
  64.5 8.5 %collective-permute-start.1 = (bf16[384,256]{1,0:T(8,128)(2,1)S(1)}, bf16[384,256]{1,0:T(8,128)(2,1)S(1)}, u32[]{:S(2)}, u32[]{:S(2)}) collective-permute-start(bf16[384,256]{1,0:T(8,128)(2,1)S(1)} %collective-permute-done.refs_6_), channel_id=1, source_target_pairs={{0,1},{1,2},{2,3},{3,0},{4,5},{5,6},{6,7},{7,4},{8,9},{9,10},{10,1... | collective-permute-start | bytes 589832 | tf_op jit(solution)/shard_map/ppermute | solution.py:259
  64.8 8.3 %copy-start.26 = (bf16[384,256]{1,0:T(8,128)(2,1)}, bf16[384,256]{1,0:T(8,128)(2,1)S(1)}, u32[]{:S(2)}) copy-start(bf16[384,256]{1,0:T(8,128)(2,1)S(1)} %collective-permute-done.2.refs_3_) | copy-start | bytes 589828
  64.8 8.3 %collective-permute-start.3 = (bf16[384,256]{1,0:T(8,128)(2,1)S(1)}, bf16[384,256]{1,0:T(8,128)(2,1)S(1)}, u32[]{:S(2)}, u32[]{:S(2)}) collective-permute-start(bf16[384,256]{1,0:T(8,128)(2,1)S(1)} %collective-permute-done.2.refs_3_), channel_id=1, source_target_pairs={{0,3},{1,0},{2,1},{3,2},{4,7},{5,4},{6,5},{7,6},{8,11},{9,8},{10,9... | collective-permute-start | bytes 589832 | tf_op jit(solution)/shard_map/ppermute | solution.py:259
  67.7 14.9 %collective-permute-start.10 = (bf16[384,256]{1,0:T(8,128)(2,1)S(1)}, bf16[384,256]{1,0:T(8,128)(2,1)}, u32[]{:S(2)}, u32[]{:S(2)}) collective-permute-start(bf16[384,256]{1,0:T(8,128)(2,1)S(1)} %get-tuple-element.31.refs_0_.refs_9_), channel_id=1, source_target_pairs={{0,3},{1,0},{2,1},{3,2},{4,7},{5,4},{6,5},{7,6},{8,11},{9,8},{10,9... | collective-permute-start | bytes 589832 | tf_op jit(solution)/shard_map/ppermute | solution.py:259
  72.9 15.5 %copy-start.7 = (bf16[384,256]{1,0:T(8,128)(2,1)}, bf16[384,256]{1,0:T(8,128)(2,1)S(1)}, u32[]{:S(2)}) copy-start(bf16[384,256]{1,0:T(8,128)(2,1)S(1)} %collective-permute-done.1.out_refs_0_.refs_4_) | copy-start | bytes 589828
  73.1 15.3 %copy-start.8 = (bf16[384,256]{1,0:T(8,128)(2,1)}, bf16[384,256]{1,0:T(8,128)(2,1)S(1)}, u32[]{:S(2)}) copy-start(bf16[384,256]{1,0:T(8,128)(2,1)S(1)} %collective-permute-done.3.out_refs_1_.refs_5_) | copy-start | bytes 589828
  74.4 20.1 %copy-start.5 = (bf16[384,256]{1,0:T(8,128)(2,1)}, bf16[384,256]{1,0:T(8,128)(2,1)S(1)}, u32[]{:S(2)}) copy-start(bf16[384,256]{1,0:T(8,128)(2,1)S(1)} %get-tuple-element.33.refs_0_) | copy-start | bytes 589828
  74.4 20.1 %copy-start.6 = (bf16[384,256]{1,0:T(8,128)(2,1)}, bf16[384,256]{1,0:T(8,128)(2,1)S(1)}, u32[]{:S(2)}) copy-start(bf16[384,256]{1,0:T(8,128)(2,1)S(1)} %get-tuple-element.34.refs_1_) | copy-start | bytes 589828
  74.4 8.2 %collective-permute-start.6 = (bf16[384,256]{1,0:T(8,128)(2,1)S(1)}, bf16[384,256]{1,0:T(8,128)(2,1)S(1)}, u32[]{:S(2)}, u32[]{:S(2)}) collective-permute-start(bf16[384,256]{1,0:T(8,128)(2,1)S(1)} %get-tuple-element.33.refs_0_), channel_id=1, source_target_pairs={{0,1},{1,2},{2,3},{3,0},{4,5},{5,6},{6,7},{7,4},{8,9},{9,10},{10,1... | collective-permute-start | bytes 589832 | tf_op jit(solution)/shard_map/ppermute | solution.py:259
  75.9 7.5 %collective-permute-start.5 = (bf16[384,256]{1,0:T(8,128)(2,1)S(1)}, bf16[384,256]{1,0:T(8,128)(2,1)S(1)}, u32[]{:S(2)}, u32[]{:S(2)}) collective-permute-start(bf16[384,256]{1,0:T(8,128)(2,1)S(1)} %get-tuple-element.34.refs_1_), channel_id=1, source_target_pairs={{0,3},{1,0},{2,1},{3,2},{4,7},{5,4},{6,5},{7,6},{8,11},{9,8},{10,9... | collective-permute-start | bytes 589832 | tf_op jit(solution)/shard_map/ppermute | solution.py:259
  79.3 9.1 %collective-permute-start.11 = (bf16[384,256]{1,0:T(8,128)(2,1)S(1)}, bf16[384,256]{1,0:T(8,128)(2,1)S(1)}, u32[]{:S(2)}, u32[]{:S(2)}) collective-permute-start(bf16[384,256]{1,0:T(8,128)(2,1)S(1)} %get-tuple-element.32.refs_1_.refs_10_), channel_id=1, source_target_pairs={{0,1},{1,2},{2,3},{3,0},{4,5},{5,6},{6,7},{7,4},{8,9},{9,10},{10,1... | collective-permute-start | bytes 589832 | tf_op jit(solution)/shard_map/ppermute | solution.py:259
  79.3 12.6 %collective-permute-start.4 = (bf16[384,256]{1,0:T(8,128)(2,1)S(1)}, bf16[384,256]{1,0:T(8,128)(2,1)S(1)}, u32[]{:S(2)}, u32[]{:S(2)}) collective-permute-start(bf16[384,256]{1,0:T(8,128)(2,1)S(1)} %get-tuple-element.33.refs_0_), channel_id=1, source_target_pairs={{0,3},{1,0},{2,1},{3,2},{4,7},{5,4},{6,5},{7,6},{8,11},{9,8},{10,9... | collective-permute-start | bytes 589832 | tf_op jit(solution)/shard_map/ppermute | solution.py:259
  82.6 9.8 %collective-permute-start.9 = (bf16[384,256]{1,0:T(8,128)(2,1)S(1)}, bf16[384,256]{1,0:T(8,128)(2,1)S(1)}, u32[]{:S(2)}, u32[]{:S(2)}) collective-permute-start(bf16[384,256]{1,0:T(8,128)(2,1)S(1)} %get-tuple-element.34.refs_1_), channel_id=1, source_target_pairs={{0,1},{1,2},{2,3},{3,0},{4,5},{5,6},{6,7},{7,4},{8,9},{9,10},{10,1... | collective-permute-start | bytes 589832 | tf_op jit(solution)/shard_map/ppermute | solution.py:259
  82.6 11.9 %copy-start.19 = (bf16[384,256]{1,0:T(8,128)(2,1)}, bf16[384,256]{1,0:T(8,128)(2,1)S(1)}, u32[]{:S(2)}) copy-start(bf16[384,256]{1,0:T(8,128)(2,1)S(1)} %collective-permute-done.6.refs_6_) | copy-start | bytes 589828
  82.6 11.9 %collective-permute-start.7 = (bf16[384,256]{1,0:T(8,128)(2,1)S(1)}, bf16[384,256]{1,0:T(8,128)(2,1)S(1)}, u32[]{:S(2)}, u32[]{:S(2)}) collective-permute-start(bf16[384,256]{1,0:T(8,128)(2,1)S(1)} %collective-permute-done.6.refs_6_), channel_id=1, source_target_pairs={{0,1},{1,2},{2,3},{3,0},{4,5},{5,6},{6,7},{7,4},{8,9},{9,10},{10,1... | collective-permute-start | bytes 589832 | tf_op jit(solution)/shard_map/ppermute | solution.py:259
  83.4 11.1 %copy-start.20 = (bf16[384,256]{1,0:T(8,128)(2,1)}, bf16[384,256]{1,0:T(8,128)(2,1)S(1)}, u32[]{:S(2)}) copy-start(bf16[384,256]{1,0:T(8,128)(2,1)S(1)} %collective-permute-done.5.refs_3_) | copy-start | bytes 589828
  83.4 11.0 %collective-permute-start.8 = (bf16[384,256]{1,0:T(8,128)(2,1)S(1)}, bf16[384,256]{1,0:T(8,128)(2,1)S(1)}, u32[]{:S(2)}, u32[]{:S(2)}) collective-permute-start(bf16[384,256]{1,0:T(8,128)(2,1)S(1)} %collective-permute-done.5.refs_3_), channel_id=1, source_target_pairs={{0,3},{1,0},{2,1},{3,2},{4,7},{5,4},{6,5},{7,6},{8,11},{9,8},{10,9... | collective-permute-start | bytes 589832 | tf_op jit(solution)/shard_map/ppermute | solution.py:259
  88.4 0.7 copy-start.27
  92.0 2.5 %copy-start.21 = (bf16[384,256]{1,0:T(8,128)(2,1)}, bf16[384,256]{1,0:T(8,128)(2,1)S(1)}, u32[]{:S(2)}) copy-start(bf16[384,256]{1,0:T(8,128)(2,1)S(1)} %collective-permute-done.4.refs_2_) | copy-start | bytes 589828
  92.3 2.2 copy-start.22
  94.4 0.7 copy-start.23
  94.5 0.8 copy-start.24
  101.2 12.4 %collective-permute-start.15 = (bf16[384,512]{1,0:T(8,128)(2,1)}, bf16[384,512]{1,0:T(8,128)(2,1)S(1)}, u32[]{:S(2)}, u32[]{:S(2)}) collective-permute-start(bf16[384,512]{1,0:T(8,128)(2,1)} %get-tuple-element.38.refs_0_), channel_id=1, source_target_pairs={{0,1},{1,2},{2,3},{3,0},{4,5},{5,6},{6,7},{7,4},{8,9},{9,10},{10,1... | collective-permute-start | bytes 1179656 | tf_op jit(solution)/shard_map/ppermute | solution.py:259
  101.3 13.1 %collective-permute-start.14 = (bf16[384,512]{1,0:T(8,128)(2,1)}, bf16[384,512]{1,0:T(8,128)(2,1)S(1)}, u32[]{:S(2)}, u32[]{:S(2)}) collective-permute-start(bf16[384,512]{1,0:T(8,128)(2,1)} %get-tuple-element.39.refs_1_), channel_id=1, source_target_pairs={{0,3},{1,0},{2,1},{3,2},{4,7},{5,4},{6,5},{7,6},{8,11},{9,8},{10,9... | collective-permute-start | bytes 1179656 | tf_op jit(solution)/shard_map/ppermute | solution.py:259
  104.5 75.8 %collective-permute-start.12 = (bf16[16,160,768]{2,1,0:T(8,128)(2,1)}, bf16[16,160,768]{2,1,0:T(8,128)(2,1)}, u32[]{:S(2)}, u32[]{:S(2)}) collective-permute-start(bf16[16,160,768]{2,1,0:T(8,128)(2,1)} %get-tuple-element.37), channel_id=1, source_target_pairs={{0,4},{4,0},{1,5},{5,1},{2,6},{6,2},{3,7},{7,3},{8,12},{12,8},{9,1... | collective-permute-start | bytes 11796488 | tf_op jit(solution)/shard_map/ppermute | solution.py:640
  104.5 18.3 %collective-permute-start.13 = (bf16[384,512]{1,0:T(8,128)(2,1)}, bf16[384,512]{1,0:T(8,128)(2,1)S(1)}, u32[]{:S(2)}, u32[]{:S(2)}) collective-permute-start(bf16[384,512]{1,0:T(8,128)(2,1)} %get-tuple-element.38.refs_0_), channel_id=1, source_target_pairs={{0,3},{1,0},{2,1},{3,2},{4,7},{5,4},{6,5},{7,6},{8,11},{9,8},{10,9... | collective-permute-start | bytes 1179656 | tf_op jit(solution)/shard_map/ppermute | solution.py:259
  105.1 17.8 %collective-permute-start.18 = (bf16[384,512]{1,0:T(8,128)(2,1)}, bf16[384,512]{1,0:T(8,128)(2,1)S(1)}, u32[]{:S(2)}, u32[]{:S(2)}) collective-permute-start(bf16[384,512]{1,0:T(8,128)(2,1)} %get-tuple-element.39.refs_1_), channel_id=1, source_target_pairs={{0,1},{1,2},{2,3},{3,0},{4,5},{5,6},{6,7},{7,4},{8,9},{9,10},{10,1... | collective-permute-start | bytes 1179656 | tf_op jit(solution)/shard_map/ppermute | solution.py:259
  113.5 14.8 %copy-start.13 = (bf16[384,512]{1,0:T(8,128)(2,1)}, bf16[384,512]{1,0:T(8,128)(2,1)S(1)}, u32[]{:S(2)}) copy-start(bf16[384,512]{1,0:T(8,128)(2,1)S(1)} %collective-permute-done.15.refs_6_) | copy-start | bytes 1179652
  113.6 14.8 %collective-permute-start.16 = (bf16[384,512]{1,0:T(8,128)(2,1)S(1)}, bf16[384,512]{1,0:T(8,128)(2,1)S(1)}, u32[]{:S(2)}, u32[]{:S(2)}) collective-permute-start(bf16[384,512]{1,0:T(8,128)(2,1)S(1)} %collective-permute-done.15.refs_6_), channel_id=1, source_target_pairs={{0,1},{1,2},{2,3},{3,0},{4,5},{5,6},{6,7},{7,4},{8,9},{9,10},{10,1... | collective-permute-start | bytes 1179656 | tf_op jit(solution)/shard_map/ppermute | solution.py:259
  114.4 13.9 %copy-start.14 = (bf16[384,512]{1,0:T(8,128)(2,1)}, bf16[384,512]{1,0:T(8,128)(2,1)S(1)}, u32[]{:S(2)}) copy-start(bf16[384,512]{1,0:T(8,128)(2,1)S(1)} %collective-permute-done.14.refs_3_) | copy-start | bytes 1179652
  114.4 13.9 %collective-permute-start.17 = (bf16[384,512]{1,0:T(8,128)(2,1)S(1)}, bf16[384,512]{1,0:T(8,128)(2,1)S(1)}, u32[]{:S(2)}, u32[]{:S(2)}) collective-permute-start(bf16[384,512]{1,0:T(8,128)(2,1)S(1)} %collective-permute-done.14.refs_3_), channel_id=1, source_target_pairs={{0,3},{1,0},{2,1},{3,2},{4,7},{5,4},{6,5},{7,6},{8,11},{9,8},{10,9... | collective-permute-start | bytes 1179656 | tf_op jit(solution)/shard_map/ppermute | solution.py:259
  122.8 5.5 %copy-start.15 = (bf16[384,512]{1,0:T(8,128)(2,1)}, bf16[384,512]{1,0:T(8,128)(2,1)S(1)}, u32[]{:S(2)}) copy-start(bf16[384,512]{1,0:T(8,128)(2,1)S(1)} %collective-permute-done.13.refs_2_) | copy-start | bytes 1179652
  122.8 5.5 %copy-start.16 = (bf16[384,512]{1,0:T(8,128)(2,1)}, bf16[384,512]{1,0:T(8,128)(2,1)S(1)}, u32[]{:S(2)}) copy-start(bf16[384,512]{1,0:T(8,128)(2,1)S(1)} %collective-permute-done.18.refs_7_) | copy-start | bytes 1179652
  128.3 0.8 copy-start.17
  129.1 0.7 copy-start.18
  137.3 39.7 %all-to-all-start.2 = ((bf16[32,72,512]{2,1,0:T(8,128)(2,1)}), bf16[32,72,512]{2,1,0:T(8,128)(2,1)S(1)}, u32[]{:S(2)}, u32[]{:S(2)}) async-start(bf16[32,72,512]{2,1,0:T(8,128)(2,1)} %bitcast.34), calls=%async_computation.2 | async-start | bytes 4718592 | tf_op jit(solution)/shard_map/all_to_all | solution.py:622
  143.9 12.7 %copy-start.29 = (s32[1,768]{1,0:T(1,128)S(1)}, s32[1,768]{1,0:T(1,128)}, u32[]{:S(2)}) copy-start(s32[1,768]{1,0:T(1,128)} %get-tuple-element.28.slot_ref) | copy-start | bytes 9220
  147.1 2.5 %collective-permute-start.19 = (f32[16,24,512]{2,1,0:T(8,128)}, f32[16,24,512]{2,1,0:T(8,128)S(1)}, u32[]{:S(2)}, u32[]{:S(2)}) collective-permute-start(f32[16,24,512]{2,1,0:T(8,128)} %get-tuple-element.44), channel_id=1, source_target_pairs={{0,4},{4,0},{1,5},{5,1},{2,6},{6,2},{3,7},{7,3},{8,12},{12,8},{9,1... | collective-permute-start | bytes 2359304 | tf_op jit(solution)/shard_map/ppermute | solution.py:640
  149.6 0.9 copy-start.12
  152.9 7.3 %collective-permute-start.20 = (bf16[16,32,128]{2,1,0:T(8,128)(2,1)}, bf16[16,32,128]{2,1,0:T(8,128)(2,1)S(1)}, u32[]{:S(2)}, u32[]{:S(2)}) collective-permute-start(bf16[16,32,128]{2,1,0:T(8,128)(2,1)} %get-tuple-element.46), channel_id=1, source_target_pairs={{0,1},{1,2},{2,3},{3,0},{4,5},{5,6},{6,7},{7,4},{8,9},{9,10},{10,1... | collective-permute-start | bytes 393224 | tf_op jit(solution)/shard_map/ppermute | solution.py:259
  152.9 10.4 %collective-permute-start.21 = (bf16[16,32,128]{2,1,0:T(8,128)(2,1)}, bf16[16,32,128]{2,1,0:T(8,128)(2,1)S(1)}, u32[]{:S(2)}, u32[]{:S(2)}) collective-permute-start(bf16[16,32,128]{2,1,0:T(8,128)(2,1)} %get-tuple-element.47), channel_id=1, source_target_pairs={{0,2},{1,3},{2,0},{3,1},{4,6},{5,7},{6,4},{7,5},{8,10},{9,11},{10,... | collective-permute-start | bytes 393224 | tf_op jit(solution)/shard_map/ppermute | solution.py:259
  156.6 6.9 %collective-permute-start.22 = (bf16[16,32,128]{2,1,0:T(8,128)(2,1)}, bf16[16,32,128]{2,1,0:T(8,128)(2,1)S(1)}, u32[]{:S(2)}, u32[]{:S(2)}) collective-permute-start(bf16[16,32,128]{2,1,0:T(8,128)(2,1)} %get-tuple-element.48), channel_id=1, source_target_pairs={{0,3},{1,0},{2,1},{3,2},{4,7},{5,4},{6,5},{7,6},{8,11},{9,8},{10,9... | collective-permute-start | bytes 393224 | tf_op jit(solution)/shard_map/ppermute | solution.py:259
  163.4 0.9 copy-start.9
  164.4 15.8 %copy-start.3 = (bf16[16,32,128]{2,1,0:T(8,128)(2,1)}, bf16[16,32,128]{2,1,0:T(8,128)(2,1)S(1)}, u32[]{:S(2)}) copy-start(bf16[16,32,128]{2,1,0:T(8,128)(2,1)S(1)} %shard_map.120.out_refs_0_.led_ref) | copy-start | bytes 393220
  177.0 1.0 copy-start.4
  180.2 2.4 copy-start.2
  180.2 2.4 collective-permute-start.23
  182.6 0.9 copy-start.11
  232.3 7.4 %collective-permute-start.24 = (bf16[672,128]{1,0:T(8,128)(2,1)S(1)}, bf16[672,128]{1,0:T(8,128)(2,1)S(1)}, u32[]{:S(2)}, u32[]{:S(2)}) collective-permute-start(bf16[672,128]{1,0:T(8,128)(2,1)S(1)} %shard_map.123.refs_0_), channel_id=1, source_target_pairs={{0,1},{1,0},{2,3},{3,2},{4,5},{5,4},{6,7},{7,6},{8,9},{9,8},{10,11... | collective-permute-start | bytes 516104 | tf_op jit(solution)/shard_map/ppermute | solution.py:676
  232.4 11.0 %collective-permute-start.25 = (bf16[672,128]{1,0:T(8,128)(2,1)S(1)}, bf16[672,128]{1,0:T(8,128)(2,1)S(1)}, u32[]{:S(2)}, u32[]{:S(2)}) collective-permute-start(bf16[672,128]{1,0:T(8,128)(2,1)S(1)} %shard_map.123.refs_0_), channel_id=1, source_target_pairs={{0,2},{1,3},{2,0},{3,1},{4,6},{5,7},{6,4},{7,5},{8,10},{9,11},{10,... | collective-permute-start | bytes 516104 | tf_op jit(solution)/shard_map/ppermute | solution.py:676
  236.1 9.6 %collective-permute-start.26 = (bf16[672,128]{1,0:T(8,128)(2,1)S(1)}, bf16[672,128]{1,0:T(8,128)(2,1)S(1)}, u32[]{:S(2)}, u32[]{:S(2)}) collective-permute-start(bf16[672,128]{1,0:T(8,128)(2,1)S(1)} %shard_map.123.refs_0_), channel_id=1, source_target_pairs={{0,3},{1,2},{2,1},{3,0},{4,7},{5,6},{6,5},{7,4},{8,11},{9,10},{10,... | collective-permute-start | bytes 516104 | tf_op jit(solution)/shard_map/ppermute | solution.py:676

commit v4 on v3

--- a/solution.py
+++ b/solution.py
@@ -39,73 +39,53 @@
     return jax.ShapeDtypeStruct(shape, BF16)
 
 
-def pool_tiles(pick, x_ref, pooled_ref, together):
-    tiles = x_ref.shape[1] // 16
-    for group in range(0, x_ref.shape[0] // 16, together):
+STREAMS = 4
+
+
+def pool_tiles(pick, x_refs, pooled_ref):
+    tiles = x_refs[0].shape[1] // 16
+    docs = x_refs[0].shape[0]
+    for stream, x_ref in enumerate(x_refs):
         block = jnp.concatenate(
             [
-                x_ref[(group + g) * 16:(group + g + 1) * 16, t * 16:(t + 1) * 16, :].reshape(256, 128)
-                for g in range(together)
+                x_ref[at:at + 16, t * 16:(t + 1) * 16, :].reshape(256, 128)
+                for at in range(0, docs, 16)
                 for t in range(tiles)
             ],
             axis=1,
         )
         mean = jnp.dot(pick[...], block, preferred_element_type=F32).astype(BF16)
-        for g in range(together):
-            docs = slice((group + g) * 16, (group + g + 1) * 16)
+        for group in range(docs // 16):
+            first = stream * docs + group * 16
             for j in range(8):
                 for t in range(tiles):
-                    at, lane = (t * 8 + j) * 128, (g * tiles + t) * 128
-                    pooled_ref[docs, at:at + 128] = mean[j * 16:(j + 1) * 16, lane:lane + 128]
-
-
-def pool_tiles_mixed(pick, wide_rows, x_ref, pooled_ref):
-    rows = x_ref.shape[1]
-    for group in range(0, x_ref.shape[0] // 16, 2):
-        pool_tiles(pick, x_ref.at[group * 16:(group + 1) * 16], pooled_ref.at[group * 16:(group + 1) * 16], 1)
-        docs = slice((group + 1) * 16, (group + 2) * 16)
-        wide_rows[...] = x_ref[docs].reshape(16 * rows, 128).astype(F32)
-        for tile in range(rows // 2):
-            first = wide_rows[pl.ds(2 * tile, 16, stride=rows), :]
-            second = wide_rows[pl.ds(2 * tile + 1, 16, stride=rows), :]
-            pooled_ref[docs, tile * 128:(tile + 1) * 128] = ((first + second) * 0.5).astype(BF16)
-
-
-def project_block(x_ref, w_hbm, first, pick, pooled, side, w_ref, w_sem, wide_rows=None):
+                    at, lane = (t * 8 + j) * 128, (group * tiles + t) * 128
+                    pooled_ref[first:first + 16, at:at + 128] = (
+                        mean[j * 16:(j + 1) * 16, lane:lane + 128]
+                    )
+
+
+def set_pick(pick):
+    out_row, in_row = iota((128, 256), 0), iota((128, 256), 1)
+    same_doc = out_row % 16 == in_row // 16
+    same_tile = out_row // 16 == (in_row % 16) // 2
+    pick[...] = jnp.where(same_doc & same_tile, 0.5, 0.0).astype(BF16)
+
+
+def pool_kernel(owner_ref, *refs):
+    x_refs, (w_hbm, out_ref, slot_ref) = refs[:STREAMS], refs[STREAMS:STREAMS + 3]
+    pick, pooled, side, w_ref, w_sem, chosen = refs[STREAMS + 3:]
     at = pl.program_id(0)
-    step = x_ref.shape[0]
-    load = pltpu.make_async_copy(w_hbm.at[:, pl.ds(first, w_ref.shape[1])], w_ref, w_sem)
+    steps = pl.num_programs(0)
+    docs = side.shape[0]
+    step = STREAMS * x_refs[0].shape[0]
+    share = out_ref.shape[0] // 6
+    load = pltpu.make_async_copy(w_hbm, w_ref, w_sem)
 
     @pl.when(at == 0)
     def _():
         load.start()
-        out_row, in_row = iota((128, 256), 0), iota((128, 256), 1)
-        same_doc = out_row % 16 == in_row // 16
-        same_tile = out_row // 16 == (in_row % 16) // 2
-        pick[...] = jnp.where(same_doc & same_tile, 0.5, 0.0).astype(BF16)
-
-    if wide_rows is None:
-        pool_tiles(pick, x_ref, pooled, 4)
-    else:
-        pool_tiles_mixed(pick, wide_rows, x_ref, pooled)
-
-    @pl.when(at == 0)
-    def _():
-        load.wait()
-
-    side[pl.ds(pl.multiple_of(at * step, step), step), :] = jnp.dot(
-        pooled[...], w_ref[...], preferred_element_type=F32
-    ).astype(BF16)
-
-
-def pool_kernel(owner_ref, x_ref, w_hbm, out_ref, slot_ref,
-                pick, pooled, side, w_ref, w_sem, chosen):
-    at = pl.program_id(0)
-    docs = side.shape[0]
-    share = out_ref.shape[0] // 6
-
-    @pl.when(at == 0)
-    def _():
+        set_pick(pick)
         first = pl.multiple_of(lax.axis_index(ROWS) * docs, 128)
         dest = owner_ref[:, pl.ds(first, docs)]
         hit = iota((32, docs), 0) == dest
@@ -114,12 +94,18 @@
         rank = jnp.sum(jnp.where(hit, before, 0.0), axis=0, keepdims=True)
         slot_ref[...] = dest * SLOTS + rank.astype(jnp.int32)
 
-    project_block(x_ref, w_hbm, 0, pick, pooled, side, w_ref, w_sem)
+    pool_tiles(pick, x_refs, pooled.at[pl.ds(pl.multiple_of(at * step, step), step)])
     rows = iota((share, docs), 0) + at * share
     chosen[pl.ds(pl.multiple_of(at * share, 16), share), :] = one_hot(rows == slot_ref[...])
 
-    @pl.when(at == pl.num_programs(0) - 1)
+    @pl.when(at == steps - 1)
     def _():
+        load.wait()
+        for part in range(2):
+            rows = slice(part * docs // 2, (part + 1) * docs // 2)
+            side[rows, :] = jnp.dot(
+                pooled[rows, :], w_ref[...], preferred_element_type=F32
+            ).astype(BF16)
         for part in range(6):
             rows = slice(part * share, (part + 1) * share)
             out_ref[rows, :] = jnp.dot(
@@ -127,10 +113,15 @@
             ).astype(BF16)
 
 
-def turn_kernel(slot_ref, x_ref, w_hbm, out_ref, mine_ref, theirs_ref,
-                pick, pooled, side, w_ref, w_sem, wide_rows):
-    first = w_hbm.shape[1] - w_ref.shape[1]
-    project_block(x_ref, w_hbm, first, pick, pooled, side, w_ref, w_sem, wide_rows)
+def turn_kernel(*refs):
+    x_refs, (mine_ref, theirs_ref, done_ref, pick, pooled) = refs[:STREAMS], refs[STREAMS + 1:]
+
+    @pl.when(pl.program_id(0) == 0)
+    def _():
+        set_pick(pick)
+        done_ref[...] = jnp.zeros_like(done_ref)
+
+    pool_tiles(pick, x_refs, pooled)
     rows = mine_ref.shape[1]
     core = lax.axis_index("core")
     for pair in range(mine_ref.shape[0] // 2):
@@ -143,15 +134,6 @@
                         at = (chip * 2 + which) * rows
                         turned_ref[pair * 2 + chip] = turned[at:at + rows, :]
 
-    @pl.when(pl.program_id(0) == pl.num_programs(0) - 1)
-    def _():
-        step = out_ref.shape[0] // 6
-        for part in range(6):
-            rows = iota((step, side.shape[0]), 0) + part * step
-            out_ref[part * step:(part + 1) * step, :] = jnp.dot(
-                one_hot(rows == slot_ref[...]), side[...], preferred_element_type=F32
-            ).astype(BF16)
-
 
 def taps_by_tile(doc_taps):
     docs, tokens, depth = doc_taps.shape
@@ -160,57 +142,54 @@
     return taps.reshape(docs, tokens * tiles, 128)
 
 
-def pool_scratch(step, docs, depth, wide):
-    return [
-        pltpu.VMEM((128, 256), BF16),
-        pltpu.VMEM((step, depth), BF16),
-        pltpu.VMEM((docs, wide), BF16),
-        pltpu.VMEM((depth, wide), BF16),
-        pltpu.SemaphoreType.DMA,
-    ]
-
-
-def pool_and_pack(owner_of, taps, w_down, wide, slots):
+def streams(step, rows):
+    def spec(stream):
+        return pl.BlockSpec((step // STREAMS, rows, 128), lambda i: (i * STREAMS + stream, 0, 0))
+
+    return [spec(stream) for stream in range(STREAMS)]
+
+
+def pool_and_pack(owner_of, taps, w_down, slots):
     docs, rows, _ = taps.shape
-    step = docs // 6
+    depth, width = w_down.shape
     return pl.pallas_call(
         pool_kernel,
         grid=(6,),
         in_specs=[
             whole(*owner_of.shape),
-            pl.BlockSpec((step, rows, 128), lambda i: (i, 0, 0)),
+            *streams(docs // 6, rows),
             pl.BlockSpec(memory_space=pl.ANY),
         ],
-        out_specs=[whole(slots, wide), whole(1, docs)],
-        out_shape=[bf16(slots, wide), jax.ShapeDtypeStruct((1, docs), jnp.int32)],
-        scratch_shapes=pool_scratch(step, docs, w_down.shape[0], wide)
-        + [pltpu.VMEM((slots, docs), BF16)],
+        out_specs=[whole(slots, width), whole(1, docs)],
+        out_shape=[bf16(slots, width), jax.ShapeDtypeStruct((1, docs), jnp.int32)],
+        scratch_shapes=[
+            pltpu.VMEM((128, 256), BF16),
+            pltpu.VMEM((docs, depth), BF16),
+            pltpu.VMEM((docs, width), BF16),
+            pltpu.VMEM((depth, width), BF16),
+            pltpu.SemaphoreType.DMA,
+            pltpu.VMEM((slots, docs), BF16),
+        ],
         compiler_params=params(),
-        cost_estimate=cost(6e9, 20e6),
-    )(owner_of, taps, w_down)
-
-
-def pool_and_turn(slot, taps, w_down, wide, slots, chips):
+        cost_estimate=cost(8e9, 23e6),
+    )(owner_of, *[taps] * STREAMS, w_down)
+
+
+def pool_and_turn(taps, depth, chips, after):
     docs, rows, _ = taps.shape
-    depth = w_down.shape[0]
     step = docs // 6
     turned = pl.BlockSpec((chips, depth // (2 * chips), step), lambda i: (0, 0, i))
-    shape = bf16(chips, depth // (2 * chips), docs)
     return pl.pallas_call(
         turn_kernel,
         grid=(6,),
-        in_specs=[
-            whole(1, docs),
-            pl.BlockSpec((step, rows, 128), lambda i: (i, 0, 0)),
-            pl.BlockSpec(memory_space=pl.ANY),
-        ],
-        out_specs=[whole(slots, wide), turned, turned],
-        out_shape=[bf16(slots, wide), shape, shape],
-        scratch_shapes=pool_scratch(step, docs, depth, wide)
-        + [pltpu.VMEM((16 * rows, 128), F32)],
+        in_specs=streams(step, rows) + [pl.BlockSpec(memory_space=pl.ANY)],
+        out_specs=[turned, turned, whole(8, 128)],
+        out_shape=[bf16(chips, depth // (2 * chips), docs)] * 2
+        + [jax.ShapeDtypeStruct((8, 128), F32)],
+        scratch_shapes=[pltpu.VMEM((128, 256), BF16), pltpu.VMEM((step, depth), BF16)],
         compiler_params=params(),
-        cost_estimate=cost(6e9, 28e6),
-    )(slot, taps, w_down)
+        cost_estimate=cost(2e9, 24e6),
+    )(*[taps] * STREAMS, after)
 
 
 def take_kernel(waited, place_ref, table_ref, *out_refs):
@@ -281,35 +260,10 @@
     return jnp.dot(blocks, picked, preferred_element_type=F32)
 
 
-def product_kernel(index_ref, values_ref, *refs):
-    parts, (out_ref, table) = refs[:-2], refs[-2:]
-    stage(parts, table)
-    rows = out_ref.shape[0] // 128
-    per_row = values_ref.shape[0] // rows
-    for row in range(rows):
-        out_ref[row * 128:(row + 1) * 128, :] = block_row(
-            index_ref, values_ref, table, row, per_row
-        ).astype(BF16)
-
-
-def product(index, values, parts, nodes):
-    width = parts[0].shape[1]
-    vmem = pl.BlockSpec(memory_space=pltpu.VMEM)
-    return pl.pallas_call(
-        product_kernel,
-        in_specs=[pl.BlockSpec(memory_space=pltpu.SMEM), vmem] + [vmem] * len(parts),
-        out_specs=vmem,
-        out_shape=bf16(nodes, width),
-        scratch_shapes=[pltpu.VMEM((4 * nodes, width), BF16)],
-        compiler_params=params(),
-        cost_estimate=cost(2e8, 3e6),
-    )(index, values, *parts)
-
-
 def layer_kernel(index_ref, values_ref, *refs):
     parts = refs[:8]
-    (first_ref, low_in_ref, high_in_ref, cot_ref, w_ref, wt_ref, gate_ref) = refs[8:15]
-    (side_out_ref, agg_ref, mgrad_ref, low_ref, high_ref, gpart_ref, table) = refs[15:]
+    (cot_ref, w_ref, gate_ref) = refs[8:11]
+    (side_out_ref, agg_ref, mgrad_ref, low_ref, high_ref, gpart_ref, table) = refs[11:]
     at = pl.program_id(0)
 
     @pl.when(at == 0)
@@ -317,13 +271,11 @@
         stage(parts, table)
 
     step = cot_ref.shape[0]
-    wide = first_ref.shape[1]
     nodes = step * pl.num_programs(0)
     per_row = values_ref.shape[0] * 128 // nodes
     rows = step // 128
-    agg_ref[:, :wide] = first_ref[...]
     for row in range(rows):
-        agg_ref[row * 128:(row + 1) * 128, wide:] = block_row(
+        agg_ref[row * 128:(row + 1) * 128, :] = block_row(
             index_ref, values_ref, table, at * rows + row, per_row
         ).astype(BF16)
     gate = gate_ref[...]
@@ -335,15 +287,16 @@
         activated = message * squash
         upstream = cot_ref[here, :].astype(F32)
         at_row = pl.multiple_of(at * step + third * 128, 128)
-        lead_in = jnp.where(at == 0, low_in_ref[here, :], high_in_ref[here, :])
-        owned = jnp.concatenate([lead_in, table[pl.ds(at_row, 128), :]], axis=1)
+        owned = table[pl.ds(at_row, 128), :]
         side_out_ref[here, :] = (owned.astype(F32) + gate * activated).astype(BF16)
         mgrad_ref[here, :] = (
             upstream * gate * squash * (1.0 + message * (1.0 - squash))
         ).astype(BF16)
         term = jnp.sum(upstream * activated, axis=0, keepdims=True)
         part = term if part is None else part + term
-    agrad = jnp.dot(mgrad_ref[...], wt_ref[...], preferred_element_type=F32).astype(BF16)
+    agrad = lax.dot_general(
+        mgrad_ref[...], w_ref[...], (((1,), (1,)), ((), ())), preferred_element_type=F32
+    ).astype(BF16)
 
     @pl.when(at == 0)
     def _():
@@ -356,9 +309,8 @@
         gpart_ref[...] += part
 
 
-def layer(index, values, parts, first, owned, cotangent, w_msg, gate):
+def layer(index, values, parts, cotangent, w_msg, gate):
     nodes, width = cotangent.shape
-    wide = first.shape[1]
     step = nodes // 2
     rows = lambda size: pl.BlockSpec((step, size), lambda i: (i, 0))
     return pl.pallas_call(
@@ -366,17 +318,16 @@
         grid=(2,),
         in_specs=[pl.BlockSpec(memory_space=pltpu.SMEM), whole(*values.shape)]
         + [whole(*part.shape) for part in parts]
-        + [rows(wide), whole(step, wide), whole(step, wide), rows(width), whole(width, width), whole(width, width),
-           whole(1, width)],
+        + [rows(width), whole(width, width), whole(1, width)],
         out_specs=[rows(width), rows(width), rows(width), whole(step, width), whole(step, width),
                    whole(1, width)],
         out_shape=[bf16(nodes, width), bf16(nodes, width), bf16(nodes, width), bf16(step, width),
                    bf16(step, width),
                    jax.ShapeDtypeStruct((1, width), F32)],
-        scratch_shapes=[pltpu.VMEM((4 * nodes, width - wide), BF16)],
+        scratch_shapes=[pltpu.VMEM((4 * nodes, width), BF16)],
         compiler_params=params(),
         cost_estimate=cost(12e8, 8e6, nodes * width),
-    )(index, values, *parts, first, *owned, cotangent, w_msg, w_msg.T, gate)
+    )(index, values, *parts, cotangent, w_msg, gate)
 
 
 def back_kernel(index_ref, values_ref, *refs):
@@ -442,7 +393,7 @@
         in_specs=[vmem] * 3 + [pl.BlockSpec(memory_space=pl.ANY)],
         out_specs=[vmem] * 2,
         out_shape=[out, out],
-        compiler_params=params(),
+        compiler_params=params(24),
         cost_estimate=cost(4e8, 4e6),
     )(aggregate, message_grad, gate_part, after)
 
@@ -492,7 +443,7 @@
         in_specs=[vmem] * 2,
         out_specs=[vmem] * cols,
         out_shape=[bf16(small.shape[0], 32, 128)] * cols,
-        compiler_params=params(),
+        compiler_params=params(24),
         cost_estimate=cost(1e6, 2e6),
     )(small, other_small)
 
@@ -545,7 +496,7 @@
         in_specs=down_specs(mine, grad) + [by_chip(led.shape[1])],
         out_specs=by_chip(rows),
         out_shape=bf16(chips, rows, 128),
-        compiler_params=params(),
+        compiler_params=params(40),
         cost_estimate=cost(2e9, 12e6),
     )(mine, other, grad, other_grad, led)
 
@@ -628,7 +579,6 @@
 def shards(doc_taps, w_down, owner_of, adj_values, adj_index, w_msg, gate_scale, cotangent):
     docs = doc_taps.shape[0]
     depth, width = w_down.shape
-    wide = width // 2
     row_size, cols = lax.axis_size(ROWS), lax.axis_size("col")
     my_row, my_col = lax.axis_index(ROWS), lax.axis_index("col")
     slots = row_size * SLOTS
@@ -640,11 +590,10 @@
     swap = lambda array: lax.ppermute(array, "core", [(0, 1), (1, 0)])
 
     taps = taps_by_tile(doc_taps)
-    packed0, slot = pool_and_pack(owner_of, taps, w_down, wide, slots)
-    incoming0 = relay(packed0)
-    packed1, mine, theirs = pool_and_turn(slot, taps, w_down, width - wide, slots, chips)
+    packed, slot = pool_and_pack(owner_of, taps, w_down, slots)
+    incoming = relay(packed)
+    mine, theirs, turned = pool_and_turn(taps, depth, chips, slot)
     other = swap(theirs)
-    incoming1 = relay(packed1)
 
     owners = owner_of[0]
     counts = jnp.sum((owners.reshape(row_size, docs) == my_row).astype(jnp.int32), axis=1)
@@ -654,12 +603,9 @@
     position = jnp.where(in_slot < counts[:, None], starts[:, None] + in_slot, -1).reshape(slots)
     pos_row, pos_col = position.reshape(1, slots), position.reshape(slots, 1)
 
-    owned0 = take(pos_row, incoming0, docs, halves=True)
-    parts0 = gather_ring(*owned0)
-    owned1 = take(pos_row, incoming1, docs, halves=True, after=parts0[4:6])
-    first = product(index, values, parts0, docs)
+    owned = take(pos_row, incoming, docs, halves=True, after=(turned,))
     side_out, aggregate, message_grad, low, high, gate_part = layer(
-        index, values, gather_ring(*owned1), first, owned0, cotangent, w_msg, gate
+        index, values, gather_ring(*owned), cotangent, w_msg, gate
     )
 
     packed_back = back(index, values, gather_ring(low, high), cotangent, pos_col, slots)

time: 247 us -> 240 us (0.972)
  waiting for transfers between devices: 62.3 us -> 89.6 us
  Pallas kernels: 73.6 us -> 58 us
  starting transfers between devices: 58.5 us -> 44.8 us
  local copies, waits for them, and re-layouts: 10.2 us -> 5.89 us
    all_to_all x3 -> x2, waiting for transfers between devices: 17.2 us -> 37.7 us  [relay(): lax.all_to_all(rows.reshape(size, slots // size, width), ROWS, split_axis...]
    pallas_call x2 -> x1, Pallas kernels: 24 us -> 12.9 us  [pool_and_turn(): pl.pallas_call(turn_kernel, grid=(6,), in_specs=streams(step, rows) + [pl...]
    ppermute x21 -> x15, starting transfers between devices: 30.4 us -> 22.7 us  [shift(): return lax.ppermute(part, 'col', [(c, (c + by) % 4) for c in range(4)])]
    ppermute x21 -> x15, waiting for transfers between devices: 32.1 us -> 39 us  [shift(): return lax.ppermute(part, 'col', [(c, (c + by) % 4) for c in range(4)])]
    all_to_all x3 -> x2, starting transfers between devices: 22.9 us -> 16.9 us  [relay(): lax.all_to_all(rows.reshape(size, slots // size, width), ROWS, split_axis...]
    unnamed x63 -> x46, local copies, waits for them, and re-layouts: 7.71 us -> 4.18 us
    pallas_call x1, Pallas kernels: 8.59 us -> 5.98 us  [down_by_chip(): pl.pallas_call(down_by_chip_kernel, grid=(4,), in_specs=down_specs(mine,...]
    pallas_call x1, Pallas kernels: 3.2 us -> 0.67 us  [small_sums(): pl.pallas_call(small_kernel, in_specs=[vmem] * 3 + [pl.BlockSpec(memory_s...]
  transfers between devices with their start and end apart: 30 -> 23, of which waited for: 20 -> 18; matrix products, arithmetic and copies ran while one was open for 2% -> 1% of each run, Pallas kernels for 17% -> 11%
where the time goes in v4:
time: 240 us; the launch traced here: 239 us
  waiting for transfers between devices  89.6 us (37%)
  Pallas kernels  58 us (24%)
  starting transfers between devices  44.8 us (19%)
  blocking collectives  38.8 us (16%)
  local copies, waits for them, and re-layouts  5.89 us (2%)
    ppermute x15, waiting for transfers between devices, shift(): return lax.ppermute(part, 'col', [(c, (c + by) % 4) for c in range(4)])  39 us
    all_to_all x1, blocking collectives, shards(): lax.all_to_all(down, ('z', 'x'), split_axis=0, concat_axis=0, tiled=True)  38.8 us
    all_to_all x2, waiting for transfers between devices, relay(): lax.all_to_all(rows.reshape(size, slots // size, width), ROWS, split_axis...  37.7 us
    ppermute x15, starting transfers between devices, shift(): return lax.ppermute(part, 'col', [(c, (c + by) % 4) for c in range(4)])  22.7 us
    all_to_all x2, starting transfers between devices, relay(): lax.all_to_all(rows.reshape(size, slots // size, width), ROWS, split_axis...  16.9 us
    pallas_call x1, Pallas kernels, pool_and_pack(): pl.pallas_call(pool_kernel, grid=(6,), in_specs=[whole(*owner_of.shape),...  16.8 us
    pallas_call x1, Pallas kernels, pool_and_turn(): pl.pallas_call(turn_kernel, grid=(6,), in_specs=streams(step, rows) + [pl...  12.9 us
    ppermute x3, waiting for transfers between devices, shards(): lax.ppermute(own, 'col', [(c, c ^ step) for c in range(4)])  8.58 us
  transfers between devices with their start and end apart: 23, of which 18 were waited for; matrix products, arithmetic and copies ran while one was open for 1% of the time, Pallas kernels for 11%

profile of v4, /device:TPU:0, one launch (start us, length us, event | category | flops | bytes accessed | tf_op | source)
XLA Modules:
  0.0 239.1 jit_solution(14210818730448042908)
XLA Ops:
  0.6 16.8 %shard_map.111 = (bf16[2304,512]{1,0:T(8,128)(2,1)}, s32[1,768]{1,0:T(1,128)}) custom-call(s32[1,24576]{1,0:T(1,128)} %owner_ref.1, bf16[768,80,128]{2,1,0:T(8,128)(2,1)} %bitcast.30, bf16[768,80,128]{2,1,0:T(8,128)(2,1)} %bitcast.31, bf16[768,80,128]{2,1,0:T(8,128)(2,1)} %bitcast.32, bf16[768,80,128]{2,1,0:T(8,128)(2,1)} %bitcast.33, bf16[5120,512]{1,0:T(8,128)(2,1)} %refs_4_.1), custom_call_target="tpu_custom_call" | custom-call | flops 8000000000 | bytes 23000000 | tf_op jit(solution)/shard_map/pallas_call | solution.py:155
  17.5 8.4 %all-to-all-start = ((bf16[32,72,512]{2,1,0:T(8,128)(2,1)}), bf16[32,72,512]{2,1,0:T(8,128)(2,1)S(1)}, u32[]{:S(2)}, u32[]{:S(2)}) async-start(bf16[32,72,512]{2,1,0:T(8,128)(2,1)} %bitcast.40), calls=%async_computation | async-start | bytes 4718592 | tf_op jit(solution)/shard_map/all_to_all | solution.py:573
  25.9 0.3 fusion
  26.2 0.1 reduce_sum.18
  26.3 0.1 select_reduce_fusion
  26.5 0.1 select_n.49.place_ref
  26.6 12.9 %shard_map.112 = (bf16[16,160,768]{2,1,0:T(8,128)(2,1)}, bf16[16,160,768]{2,1,0:T(8,128)(2,1)}, f32[8,128]{1,0:T(8,128)}) custom-call(bf16[768,80,128]{2,1,0:T(8,128)(2,1)} %bitcast.34, bf16[768,80,128]{2,1,0:T(8,128)(2,1)} %bitcast.35, bf16[768,80,128]{2,1,0:T(8,128)(2,1)} %bitcast.36, bf16[768,80,128]{2,1,0:T(8,128)(2,1)} %bitcast.37, ...), custom_call_target="tpu_custom_call" | custom-call | flops 2000000000 | bytes 24000000 | tf_op jit(solution)/shard_map/pallas_call | solution.py:182
  39.6 19.4 %all-to-all-done = bf16[32,72,512]{2,1,0:T(8,128)(2,1)S(1)} async-done(((bf16[32,72,512]{2,1,0:T(8,128)(2,1)}), bf16[32,72,512]{2,1,0:T(8,128)(2,1)S(1)}, u32[]{:S(2)}, u32[]{:S(2)}) %all-to-all-start) | async-done | bytes 2359328 | tf_op jit(solution)/shard_map/all_to_all | solution.py:573
  59.0 0.7 copy-done.7
  59.6 2.2 shard_map.113
  61.9 1.6 collective-permute-start.2
  63.6 1.7 collective-permute-start.1
  65.2 1.8 collective-permute-start
  67.0 0.2 collective-permute-start.5
  67.3 8.0 %collective-permute-done.2.refs_6_ = bf16[384,512]{1,0:T(8,128)(2,1)S(1)} collective-permute-done((bf16[384,512]{1,0:T(8,128)(2,1)S(1)}, bf16[384,512]{1,0:T(8,128)(2,1)S(1)}, u32[]{:S(2)}, u32[]{:S(2)}) %collective-permute-start.2) | collective-permute-done | bytes 393248 | tf_op jit(solution)/shard_map/ppermute | solution.py:238
  75.3 0.4 collective-permute-start.3
  75.6 2.9 %collective-permute-start.4 = (bf16[384,512]{1,0:T(8,128)(2,1)S(1)}, bf16[384,512]{1,0:T(8,128)(2,1)S(1)}, u32[]{:S(2)}, u32[]{:S(2)}) collective-permute-start(bf16[384,512]{1,0:T(8,128)(2,1)S(1)} %collective-permute-done.1.refs_3_), channel_id=1, source_target_pairs={{0,3},{1,0},{2,1},{3,2},{4,7},{5,4},{6,5},{7,6},{8,11},{9,8},{10,9... | collective-permute-start | bytes 1179656 | tf_op jit(solution)/shard_map/ppermute | solution.py:238
  78.5 0.5 fusion.2.index_ref
  79.0 5.0 %collective-permute-done.refs_2_ = bf16[384,512]{1,0:T(8,128)(2,1)S(1)} collective-permute-done((bf16[384,512]{1,0:T(8,128)(2,1)S(1)}, bf16[384,512]{1,0:T(8,128)(2,1)S(1)}, u32[]{:S(2)}, u32[]{:S(2)}) %collective-permute-start) | collective-permute-done | bytes 393248 | tf_op jit(solution)/shard_map/ppermute | solution.py:238
  84.1 5.0 %collective-permute-done.3.refs_4_ = bf16[384,512]{1,0:T(8,128)(2,1)S(1)} collective-permute-done((bf16[384,512]{1,0:T(8,128)(2,1)S(1)}, bf16[384,512]{1,0:T(8,128)(2,1)S(1)}, u32[]{:S(2)}, u32[]{:S(2)}) %collective-permute-start.3) | collective-permute-done | bytes 393248 | tf_op jit(solution)/shard_map/ppermute | solution.py:238
  89.1 0.7 copy-done.19
  89.8 0.1 copy-done.20
  90.0 6.3 %shard_map.114 = (bf16[768,512]{1,0:T(8,128)(2,1)}, bf16[768,512]{1,0:T(8,128)(2,1)}, bf16[768,512]{1,0:T(8,128)(2,1)}, bf16[384,512]{1,0:T(8,128)(2,1)}, bf16[384,512]{1,0:T(8,128)(2,1)}, /*index=5*/f32[1,512]{1,0:T(1,128)}) custom-call(s32[24]{0:T(128)} %fusion.2.index_ref, bf16[24,128,128]{2,1,0:T(8,128)(2,1)} %bitcast.38, bf16[384,512]{1,0:T(8,128)(2,1)} %copy-done.4, ...), custom_call_target="tpu_custom_call" | custom-call | flops 1200000000 | bytes 8000000 | tf_op jit(solution)/shard_map/pallas_call | solution.py:316
  96.3 1.5 collective-permute-start.9
  97.8 1.8 collective-permute-start.8
  99.6 0.2 collective-permute-start.12
  99.8 3.0 %collective-permute-start.7 = (bf16[384,512]{1,0:T(8,128)(2,1)}, bf16[384,512]{1,0:T(8,128)(2,1)S(1)}, u32[]{:S(2)}, u32[]{:S(2)}) collective-permute-start(bf16[384,512]{1,0:T(8,128)(2,1)} %get-tuple-element.34.refs_0_), channel_id=1, source_target_pairs={{0,3},{1,0},{2,1},{3,2},{4,7},{5,4},{6,5},{7,6},{8,11},{9,8},{10,9... | collective-permute-start | bytes 1179656 | tf_op jit(solution)/shard_map/ppermute | solution.py:238
  102.8 4.7 %collective-permute-done.9.refs_6_ = bf16[384,512]{1,0:T(8,128)(2,1)S(1)} collective-permute-done((bf16[384,512]{1,0:T(8,128)(2,1)}, bf16[384,512]{1,0:T(8,128)(2,1)S(1)}, u32[]{:S(2)}, u32[]{:S(2)}) %collective-permute-start.9) | collective-permute-done | bytes 393248 | tf_op jit(solution)/shard_map/ppermute | solution.py:238
  107.5 0.8 collective-permute-start.10
  108.3 0.3 collective-permute-done.8.refs_3_
  108.6 2.2 collective-permute-start.11
  110.8 1.4 select_n.51.refs_9_
  112.2 3.8 %collective-permute-done.12.refs_7_ = bf16[384,512]{1,0:T(8,128)(2,1)S(1)} collective-permute-done((bf16[384,512]{1,0:T(8,128)(2,1)}, bf16[384,512]{1,0:T(8,128)(2,1)S(1)}, u32[]{:S(2)}, u32[]{:S(2)}) %collective-permute-start.12) | collective-permute-done | bytes 393248 | tf_op jit(solution)/shard_map/ppermute | solution.py:238
  116.0 1.1 collective-permute-done.7.refs_2_
  117.0 5.7 %collective-permute-done.10.refs_4_ = bf16[384,512]{1,0:T(8,128)(2,1)S(1)} collective-permute-done((bf16[384,512]{1,0:T(8,128)(2,1)S(1)}, bf16[384,512]{1,0:T(8,128)(2,1)S(1)}, u32[]{:S(2)}, u32[]{:S(2)}) %collective-permute-start.10) | collective-permute-done | bytes 393248 | tf_op jit(solution)/shard_map/ppermute | solution.py:238
  122.7 0.7 copy-done.13
  123.5 0.8 copy-done.14
  124.2 7.5 %shard_map.115.after_ref = bf16[2304,512]{1,0:T(8,128)(2,1)} custom-call(s32[24]{0:T(128)} %fusion.2.index_ref, bf16[24,128,128]{2,1,0:T(8,128)(2,1)} %bitcast.39, bf16[384,512]{1,0:T(8,128)(2,1)} %get-tuple-element.34.refs_0_, bf16[384,512]{1,0:T(8,128)(2,1)} %get-tuple-element.35.refs_1_, bf16[384,512]{1,0:T(8,128)(2,1)} %copy-done.12, ...), custom_call_target="tpu_custom_call" | custom-call | flops 1811939328 | bytes 5000000 | tf_op jit(solution)/shard_map/pallas_call | solution.py:355
  131.7 8.5 %all-to-all-start.1 = ((bf16[32,72,512]{2,1,0:T(8,128)(2,1)}), bf16[32,72,512]{2,1,0:T(8,128)(2,1)}, u32[]{:S(2)}, u32[]{:S(2)}) async-start(bf16[32,72,512]{2,1,0:T(8,128)(2,1)} %bitcast.28), calls=%async_computation.1 | async-start | bytes 4718592 | tf_op jit(solution)/shard_map/all_to_all | solution.py:573
  140.3 1.1 copy-done.3
  141.4 0.7 shard_map.116
  142.1 0.3 collective-permute-start.13
  142.4 2.0 collective-permute-done.13.other_small_ref
  144.4 0.2 shard_map.117
  144.7 0.7 collective-permute-start.14
  145.4 3.0 %collective-permute-start.15 = (bf16[16,32,128]{2,1,0:T(8,128)(2,1)S(1)}, bf16[16,32,128]{2,1,0:T(8,128)(2,1)S(1)}, u32[]{:S(2)}, u32[]{:S(2)}) collective-permute-start(bf16[16,32,128]{2,1,0:T(8,128)(2,1)S(1)} %get-tuple-element.43), channel_id=1, source_target_pairs={{0,2},{1,3},{2,0},{3,1},{4,6},{5,7},{6,4},{7,5},{8,10},{9,11},{10,... | collective-permute-start | bytes 393224 | tf_op jit(solution)/shard_map/ppermute | solution.py:238
  148.4 0.9 collective-permute-start.16
  149.4 0.2 copy.18.place_ref
  149.5 2.3 collective-permute-done.14.refs_1_
  151.8 3.0 %collective-permute-done.15.refs_2_ = bf16[16,32,128]{2,1,0:T(8,128)(2,1)S(1)} collective-permute-done((bf16[16,32,128]{2,1,0:T(8,128)(2,1)S(1)}, bf16[16,32,128]{2,1,0:T(8,128)(2,1)S(1)}, u32[]{:S(2)}, u32[]{:S(2)}) %collective-permute-start.15) | collective-permute-done | bytes 131104 | tf_op jit(solution)/shard_map/ppermute | solution.py:238
  154.8 0.1 collective-permute-done.16.refs_3_
  155.0 18.3 %all-to-all-done.1 = bf16[32,72,512]{2,1,0:T(8,128)(2,1)} async-done(((bf16[32,72,512]{2,1,0:T(8,128)(2,1)}), bf16[32,72,512]{2,1,0:T(8,128)(2,1)}, u32[]{:S(2)}, u32[]{:S(2)}) %all-to-all-start.1) | async-done | bytes 2359328 | tf_op jit(solution)/shard_map/all_to_all | solution.py:573
  173.3 4.1 %shard_map.119.grad_ref = bf16[768,512]{1,0:T(8,128)(2,1)S(1)} custom-call(s32[768,1]{1,0:T(8,128)S(1)} %copy.18.place_ref, bf16[2304,512]{1,0:T(8,128)(2,1)} %bitcast.14.table_ref, bf16[16,32,128]{2,1,0:T(8,128)(2,1)S(1)} %shard_map.118.out_refs_0_.led_ref), custom_call_target="tpu_custom_call" | custom-call | flops 1811939328 | bytes 2000000 | tf_op jit(solution)/shard_map/pallas_call | solution.py:225
  177.5 2.3 collective-permute-done.17.other_grad_ref
  179.8 6.0 %shard_map.120 = bf16[16,672,128]{2,1,0:T(8,128)(2,1)S(1)} custom-call(bf16[16,160,768]{2,1,0:T(8,128)(2,1)S(1)} %copy-done.1, bf16[16,160,768]{2,1,0:T(8,128)(2,1)} %collective-permute-done.6.other_ref, bf16[768,512]{1,0:T(8,128)(2,1)S(1)} %shard_map.119.grad_ref, bf16[768,512]{1,0:T(8,128)(2,1)S(1)} %collective-permute-done.17.other_grad_ref, ...), custom_call_target="tpu_custom_call" | custom-call | flops 2000000000 | bytes 12000000 | tf_op jit(solution)/shard_map/pallas_call | solution.py:493
  185.8 38.8 %all_to_all.15.parts_ref = bf16[16,672,128]{2,1,0:T(8,128)(2,1)S(1)} all-to-all(bf16[16,672,128]{2,1,0:T(8,128)(2,1)S(1)} %shard_map.120), channel_id=1, replica_groups=mesh['z'=4,'x'=4,'core'=2,'col'=4] {'z','x'}, dimensions={0} | all-to-all | bytes 5505024 | tf_op jit(solution)/shard_map/all_to_all | solution.py:619
  224.5 0.4 shard_map.121.refs_0_
  224.9 0.7 collective-permute-start.18
  225.6 3.0 %collective-permute-start.19 = (bf16[672,128]{1,0:T(8,128)(2,1)S(1)}, bf16[672,128]{1,0:T(8,128)(2,1)S(1)}, u32[]{:S(2)}, u32[]{:S(2)}) collective-permute-start(bf16[672,128]{1,0:T(8,128)(2,1)S(1)} %shard_map.121.refs_0_), channel_id=1, source_target_pairs={{0,2},{1,3},{2,0},{3,1},{4,6},{5,7},{6,4},{7,5},{8,10},{9,11},{10,... | collective-permute-start | bytes 516104 | tf_op jit(solution)/shard_map/ppermute | solution.py:622
  228.7 1.0 collective-permute-start.20
  229.7 2.6 %collective-permute-done.18.refs_1_ = bf16[672,128]{1,0:T(8,128)(2,1)S(1)} collective-permute-done((bf16[672,128]{1,0:T(8,128)(2,1)S(1)}, bf16[672,128]{1,0:T(8,128)(2,1)S(1)}, u32[]{:S(2)}, u32[]{:S(2)}) %collective-permute-start.18) | collective-permute-done | bytes 172064 | tf_op jit(solution)/shard_map/ppermute | solution.py:622
  232.3 3.7 %collective-permute-done.19.refs_2_ = bf16[672,128]{1,0:T(8,128)(2,1)S(1)} collective-permute-done((bf16[672,128]{1,0:T(8,128)(2,1)S(1)}, bf16[672,128]{1,0:T(8,128)(2,1)S(1)}, u32[]{:S(2)}, u32[]{:S(2)}) %collective-permute-start.19) | collective-permute-done | bytes 172064 | tf_op jit(solution)/shard_map/ppermute | solution.py:622
  236.0 2.2 collective-permute-done.20.refs_3_
  238.3 0.9 shard_map.122
  (50 shorter events, 0.4 us)
Async XLA Ops:
  17.5 8.4 %copy-start.8 = (s32[1,24576]{1,0:T(1,128)S(1)}, s32[1,24576]{1,0:T(1,128)}, u32[]{:S(2)}) copy-start(s32[1,24576]{1,0:T(1,128)} %owner_ref.1) | copy-start | bytes 294916
  17.5 41.5 %all-to-all-start = ((bf16[32,72,512]{2,1,0:T(8,128)(2,1)}), bf16[32,72,512]{2,1,0:T(8,128)(2,1)S(1)}, u32[]{:S(2)}, u32[]{:S(2)}) async-start(bf16[32,72,512]{2,1,0:T(8,128)(2,1)} %bitcast.40), calls=%async_computation | async-start | bytes 4718592 | tf_op jit(solution)/shard_map/all_to_all | solution.py:573
  59.0 0.7 copy-start.7
  59.6 18.9 %copy-start.22 = (s32[1,24]{1,0:T(1,128)S(1)}, s32[1,24]{1,0:T(1,128)}, u32[]{:S(2)}) copy-start(s32[1,24]{1,0:T(1,128)} %param.12) | copy-start | bytes 292
  61.9 27.2 %copy-start.4 = (bf16[384,512]{1,0:T(8,128)(2,1)}, bf16[384,512]{1,0:T(8,128)(2,1)S(1)}, u32[]{:S(2)}) copy-start(bf16[384,512]{1,0:T(8,128)(2,1)S(1)} %get-tuple-element.29.refs_0_) | copy-start | bytes 1179652
  61.9 27.2 %copy-start.5 = (bf16[384,512]{1,0:T(8,128)(2,1)}, bf16[384,512]{1,0:T(8,128)(2,1)S(1)}, u32[]{:S(2)}) copy-start(bf16[384,512]{1,0:T(8,128)(2,1)S(1)} %get-tuple-element.30.refs_1_) | copy-start | bytes 1179652
  61.9 13.3 %collective-permute-start.2 = (bf16[384,512]{1,0:T(8,128)(2,1)S(1)}, bf16[384,512]{1,0:T(8,128)(2,1)S(1)}, u32[]{:S(2)}, u32[]{:S(2)}) collective-permute-start(bf16[384,512]{1,0:T(8,128)(2,1)S(1)} %get-tuple-element.29.refs_0_), channel_id=1, source_target_pairs={{0,1},{1,2},{2,3},{3,0},{4,5},{5,6},{6,7},{7,4},{8,9},{9,10},{10,1... | collective-permute-start | bytes 1179656 | tf_op jit(solution)/shard_map/ppermute | solution.py:238
  63.6 12.1 %collective-permute-start.1 = (bf16[384,512]{1,0:T(8,128)(2,1)S(1)}, bf16[384,512]{1,0:T(8,128)(2,1)S(1)}, u32[]{:S(2)}, u32[]{:S(2)}) collective-permute-start(bf16[384,512]{1,0:T(8,128)(2,1)S(1)} %get-tuple-element.30.refs_1_), channel_id=1, source_target_pairs={{0,3},{1,0},{2,1},{3,2},{4,7},{5,4},{6,5},{7,6},{8,11},{9,8},{10,9... | collective-permute-start | bytes 1179656 | tf_op jit(solution)/shard_map/ppermute | solution.py:238
  65.2 18.8 %collective-permute-start = (bf16[384,512]{1,0:T(8,128)(2,1)S(1)}, bf16[384,512]{1,0:T(8,128)(2,1)S(1)}, u32[]{:S(2)}, u32[]{:S(2)}) collective-permute-start(bf16[384,512]{1,0:T(8,128)(2,1)S(1)} %get-tuple-element.29.refs_0_), channel_id=1, source_target_pairs={{0,3},{1,0},{2,1},{3,2},{4,7},{5,4},{6,5},{7,6},{8,11},{9,8},{10,9... | collective-permute-start | bytes 1179656 | tf_op jit(solution)/shard_map/ppermute | solution.py:238
  67.0 17.0 %collective-permute-start.5 = (bf16[384,512]{1,0:T(8,128)(2,1)S(1)}, bf16[384,512]{1,0:T(8,128)(2,1)S(1)}, u32[]{:S(2)}, u32[]{:S(2)}) collective-permute-start(bf16[384,512]{1,0:T(8,128)(2,1)S(1)} %get-tuple-element.30.refs_1_), channel_id=1, source_target_pairs={{0,1},{1,2},{2,3},{3,0},{4,5},{5,6},{6,7},{7,4},{8,9},{9,10},{10,1... | collective-permute-start | bytes 1179656 | tf_op jit(solution)/shard_map/ppermute | solution.py:238
  75.3 13.9 %copy-start.15 = (bf16[384,512]{1,0:T(8,128)(2,1)}, bf16[384,512]{1,0:T(8,128)(2,1)S(1)}, u32[]{:S(2)}) copy-start(bf16[384,512]{1,0:T(8,128)(2,1)S(1)} %collective-permute-done.2.refs_6_) | copy-start | bytes 1179652
  75.3 13.8 %collective-permute-start.3 = (bf16[384,512]{1,0:T(8,128)(2,1)S(1)}, bf16[384,512]{1,0:T(8,128)(2,1)S(1)}, u32[]{:S(2)}, u32[]{:S(2)}) collective-permute-start(bf16[384,512]{1,0:T(8,128)(2,1)S(1)} %collective-permute-done.2.refs_6_), channel_id=1, source_target_pairs={{0,1},{1,2},{2,3},{3,0},{4,5},{5,6},{6,7},{7,4},{8,9},{9,10},{10,1... | collective-permute-start | bytes 1179656 | tf_op jit(solution)/shard_map/ppermute | solution.py:238
  75.6 13.5 %copy-start.16 = (bf16[384,512]{1,0:T(8,128)(2,1)}, bf16[384,512]{1,0:T(8,128)(2,1)S(1)}, u32[]{:S(2)}) copy-start(bf16[384,512]{1,0:T(8,128)(2,1)S(1)} %collective-permute-done.1.refs_3_) | copy-start | bytes 1179652
  75.6 13.5 %collective-permute-start.4 = (bf16[384,512]{1,0:T(8,128)(2,1)S(1)}, bf16[384,512]{1,0:T(8,128)(2,1)S(1)}, u32[]{:S(2)}, u32[]{:S(2)}) collective-permute-start(bf16[384,512]{1,0:T(8,128)(2,1)S(1)} %collective-permute-done.1.refs_3_), channel_id=1, source_target_pairs={{0,3},{1,0},{2,1},{3,2},{4,7},{5,4},{6,5},{7,6},{8,11},{9,8},{10,9... | collective-permute-start | bytes 1179656 | tf_op jit(solution)/shard_map/ppermute | solution.py:238
  84.0 5.1 %copy-start.17 = (bf16[384,512]{1,0:T(8,128)(2,1)}, bf16[384,512]{1,0:T(8,128)(2,1)S(1)}, u32[]{:S(2)}) copy-start(bf16[384,512]{1,0:T(8,128)(2,1)S(1)} %collective-permute-done.refs_2_) | copy-start | bytes 1179652
  84.1 5.1 %copy-start.18 = (bf16[384,512]{1,0:T(8,128)(2,1)}, bf16[384,512]{1,0:T(8,128)(2,1)S(1)}, u32[]{:S(2)}) copy-start(bf16[384,512]{1,0:T(8,128)(2,1)S(1)} %collective-permute-done.5.refs_7_) | copy-start | bytes 1179652
  89.1 0.8 copy-start.19
  89.1 0.9 copy-start.20
  96.3 11.3 %collective-permute-start.9 = (bf16[384,512]{1,0:T(8,128)(2,1)}, bf16[384,512]{1,0:T(8,128)(2,1)S(1)}, u32[]{:S(2)}, u32[]{:S(2)}) collective-permute-start(bf16[384,512]{1,0:T(8,128)(2,1)} %get-tuple-element.34.refs_0_), channel_id=1, source_target_pairs={{0,1},{1,2},{2,3},{3,0},{4,5},{5,6},{6,7},{7,4},{8,9},{9,10},{10,1... | collective-permute-start | bytes 1179656 | tf_op jit(solution)/shard_map/ppermute | solution.py:238
  97.8 10.8 %collective-permute-start.8 = (bf16[384,512]{1,0:T(8,128)(2,1)}, bf16[384,512]{1,0:T(8,128)(2,1)S(1)}, u32[]{:S(2)}, u32[]{:S(2)}) collective-permute-start(bf16[384,512]{1,0:T(8,128)(2,1)} %get-tuple-element.35.refs_1_), channel_id=1, source_target_pairs={{0,3},{1,0},{2,1},{3,2},{4,7},{5,4},{6,5},{7,6},{8,11},{9,8},{10,9... | collective-permute-start | bytes 1179656 | tf_op jit(solution)/shard_map/ppermute | solution.py:238
  99.6 77.9 %collective-permute-start.6 = (bf16[16,160,768]{2,1,0:T(8,128)(2,1)}, bf16[16,160,768]{2,1,0:T(8,128)(2,1)}, u32[]{:S(2)}, u32[]{:S(2)}) collective-permute-start(bf16[16,160,768]{2,1,0:T(8,128)(2,1)} %get-tuple-element.33), channel_id=1, source_target_pairs={{0,4},{4,0},{1,5},{5,1},{2,6},{6,2},{3,7},{7,3},{8,12},{12,8},{9,1... | collective-permute-start | bytes 11796488 | tf_op jit(solution)/shard_map/ppermute | solution.py:590
  99.6 16.4 %collective-permute-start.12 = (bf16[384,512]{1,0:T(8,128)(2,1)}, bf16[384,512]{1,0:T(8,128)(2,1)S(1)}, u32[]{:S(2)}, u32[]{:S(2)}) collective-permute-start(bf16[384,512]{1,0:T(8,128)(2,1)} %get-tuple-element.35.refs_1_), channel_id=1, source_target_pairs={{0,1},{1,2},{2,3},{3,0},{4,5},{5,6},{6,7},{7,4},{8,9},{9,10},{10,1... | collective-permute-start | bytes 1179656 | tf_op jit(solution)/shard_map/ppermute | solution.py:238
  99.8 17.2 %collective-permute-start.7 = (bf16[384,512]{1,0:T(8,128)(2,1)}, bf16[384,512]{1,0:T(8,128)(2,1)S(1)}, u32[]{:S(2)}, u32[]{:S(2)}) collective-permute-start(bf16[384,512]{1,0:T(8,128)(2,1)} %get-tuple-element.34.refs_0_), channel_id=1, source_target_pairs={{0,3},{1,0},{2,1},{3,2},{4,7},{5,4},{6,5},{7,6},{8,11},{9,8},{10,9... | collective-permute-start | bytes 1179656 | tf_op jit(solution)/shard_map/ppermute | solution.py:238
  107.5 15.2 %copy-start.9 = (bf16[384,512]{1,0:T(8,128)(2,1)}, bf16[384,512]{1,0:T(8,128)(2,1)S(1)}, u32[]{:S(2)}) copy-start(bf16[384,512]{1,0:T(8,128)(2,1)S(1)} %collective-permute-done.9.refs_6_) | copy-start | bytes 1179652
  107.5 15.2 %collective-permute-start.10 = (bf16[384,512]{1,0:T(8,128)(2,1)S(1)}, bf16[384,512]{1,0:T(8,128)(2,1)S(1)}, u32[]{:S(2)}, u32[]{:S(2)}) collective-permute-start(bf16[384,512]{1,0:T(8,128)(2,1)S(1)} %collective-permute-done.9.refs_6_), channel_id=1, source_target_pairs={{0,1},{1,2},{2,3},{3,0},{4,5},{5,6},{6,7},{7,4},{8,9},{9,10},{10,1... | collective-permute-start | bytes 1179656 | tf_op jit(solution)/shard_map/ppermute | solution.py:238
  108.6 14.1 %copy-start.10 = (bf16[384,512]{1,0:T(8,128)(2,1)}, bf16[384,512]{1,0:T(8,128)(2,1)S(1)}, u32[]{:S(2)}) copy-start(bf16[384,512]{1,0:T(8,128)(2,1)S(1)} %collective-permute-done.8.refs_3_) | copy-start | bytes 1179652
  108.6 14.1 %collective-permute-start.11 = (bf16[384,512]{1,0:T(8,128)(2,1)S(1)}, bf16[384,512]{1,0:T(8,128)(2,1)S(1)}, u32[]{:S(2)}, u32[]{:S(2)}) collective-permute-start(bf16[384,512]{1,0:T(8,128)(2,1)S(1)} %collective-permute-done.8.refs_3_), channel_id=1, source_target_pairs={{0,3},{1,0},{2,1},{3,2},{4,7},{5,4},{6,5},{7,6},{8,11},{9,8},{10,9... | collective-permute-start | bytes 1179656 | tf_op jit(solution)/shard_map/ppermute | solution.py:238
  116.0 6.8 %copy-start.11 = (bf16[384,512]{1,0:T(8,128)(2,1)}, bf16[384,512]{1,0:T(8,128)(2,1)S(1)}, u32[]{:S(2)}) copy-start(bf16[384,512]{1,0:T(8,128)(2,1)S(1)} %collective-permute-done.12.refs_7_) | copy-start | bytes 1179652
  117.0 5.7 %copy-start.12 = (bf16[384,512]{1,0:T(8,128)(2,1)}, bf16[384,512]{1,0:T(8,128)(2,1)S(1)}, u32[]{:S(2)}) copy-start(bf16[384,512]{1,0:T(8,128)(2,1)S(1)} %collective-permute-done.7.refs_2_) | copy-start | bytes 1179652
  122.7 0.8 copy-start.13
  123.5 0.8 copy-start.14
  131.7 8.5 %copy-start = (bf16[2304,512]{1,0:T(8,128)(2,1)S(1)}, bf16[2304,512]{1,0:T(8,128)(2,1)}, u32[]{:S(2)}) copy-start(bf16[2304,512]{1,0:T(8,128)(2,1)} %shard_map.115.after_ref) | copy-start | bytes 7077892
  131.7 8.5 %copy-start.2 = (bf16[768,512]{1,0:T(8,128)(2,1)S(1)}, bf16[768,512]{1,0:T(8,128)(2,1)}, u32[]{:S(2)}) copy-start(bf16[768,512]{1,0:T(8,128)(2,1)} %get-tuple-element.36.agg_ref) | copy-start | bytes 2359300
  131.7 8.5 %copy-start.6 = (f32[1,512]{1,0:T(1,128)S(1)}, f32[1,512]{1,0:T(1,128)}, u32[]{:S(2)}) copy-start(f32[1,512]{1,0:T(1,128)} %get-tuple-element.38.gate_ref) | copy-start | bytes 6148
  131.7 41.6 %all-to-all-start.1 = ((bf16[32,72,512]{2,1,0:T(8,128)(2,1)}), bf16[32,72,512]{2,1,0:T(8,128)(2,1)}, u32[]{:S(2)}, u32[]{:S(2)}) async-start(bf16[32,72,512]{2,1,0:T(8,128)(2,1)} %bitcast.28), calls=%async_computation.1 | async-start | bytes 4718592 | tf_op jit(solution)/shard_map/all_to_all | solution.py:573
  140.3 1.1 copy-start.3
  141.4 8.0 %copy-start.21 = (s32[1,768]{1,0:T(1,128)S(1)}, s32[1,768]{1,0:T(1,128)}, u32[]{:S(2)}) copy-start(s32[1,768]{1,0:T(1,128)} %get-tuple-element.27.refs_4_) | copy-start | bytes 9220
  142.1 2.4 collective-permute-start.13
  144.7 7.2 %collective-permute-start.14 = (bf16[16,32,128]{2,1,0:T(8,128)(2,1)S(1)}, bf16[16,32,128]{2,1,0:T(8,128)(2,1)S(1)}, u32[]{:S(2)}, u32[]{:S(2)}) collective-permute-start(bf16[16,32,128]{2,1,0:T(8,128)(2,1)S(1)} %get-tuple-element.42), channel_id=1, source_target_pairs={{0,1},{1,2},{2,3},{3,0},{4,5},{5,6},{6,7},{7,4},{8,9},{9,10},{10,1... | collective-permute-start | bytes 393224 | tf_op jit(solution)/shard_map/ppermute | solution.py:238
  145.4 9.5 %collective-permute-start.15 = (bf16[16,32,128]{2,1,0:T(8,128)(2,1)S(1)}, bf16[16,32,128]{2,1,0:T(8,128)(2,1)S(1)}, u32[]{:S(2)}, u32[]{:S(2)}) collective-permute-start(bf16[16,32,128]{2,1,0:T(8,128)(2,1)S(1)} %get-tuple-element.43), channel_id=1, source_target_pairs={{0,2},{1,3},{2,0},{3,1},{4,6},{5,7},{6,4},{7,5},{8,10},{9,11},{10,... | collective-permute-start | bytes 393224 | tf_op jit(solution)/shard_map/ppermute | solution.py:238
  148.4 6.6 %collective-permute-start.16 = (bf16[16,32,128]{2,1,0:T(8,128)(2,1)S(1)}, bf16[16,32,128]{2,1,0:T(8,128)(2,1)S(1)}, u32[]{:S(2)}, u32[]{:S(2)}) collective-permute-start(bf16[16,32,128]{2,1,0:T(8,128)(2,1)S(1)} %get-tuple-element.44), channel_id=1, source_target_pairs={{0,3},{1,0},{2,1},{3,2},{4,7},{5,4},{6,5},{7,6},{8,11},{9,8},{10,9... | collective-permute-start | bytes 393224 | tf_op jit(solution)/shard_map/ppermute | solution.py:238
  173.3 6.5 %copy-start.1 = (bf16[16,160,768]{2,1,0:T(8,128)(2,1)S(1)}, bf16[16,160,768]{2,1,0:T(8,128)(2,1)}, u32[]{:S(2)}) copy-start(bf16[16,160,768]{2,1,0:T(8,128)(2,1)} %get-tuple-element.32.mine_ref) | copy-start | bytes 11796484
  177.4 2.4 collective-permute-start.17
  224.9 7.4 %collective-permute-start.18 = (bf16[672,128]{1,0:T(8,128)(2,1)S(1)}, bf16[672,128]{1,0:T(8,128)(2,1)S(1)}, u32[]{:S(2)}, u32[]{:S(2)}) collective-permute-start(bf16[672,128]{1,0:T(8,128)(2,1)S(1)} %shard_map.121.refs_0_), channel_id=1, source_target_pairs={{0,1},{1,0},{2,3},{3,2},{4,5},{5,4},{6,7},{7,6},{8,9},{9,8},{10,11... | collective-permute-start | bytes 516104 | tf_op jit(solution)/shard_map/ppermute | solution.py:622
  225.6 10.4 %collective-permute-start.19 = (bf16[672,128]{1,0:T(8,128)(2,1)S(1)}, bf16[672,128]{1,0:T(8,128)(2,1)S(1)}, u32[]{:S(2)}, u32[]{:S(2)}) collective-permute-start(bf16[672,128]{1,0:T(8,128)(2,1)S(1)} %shard_map.121.refs_0_), channel_id=1, source_target_pairs={{0,2},{1,3},{2,0},{3,1},{4,6},{5,7},{6,4},{7,5},{8,10},{9,11},{10,... | collective-permute-start | bytes 516104 | tf_op jit(solution)/shard_map/ppermute | solution.py:622
  228.7 9.6 %collective-permute-start.20 = (bf16[672,128]{1,0:T(8,128)(2,1)S(1)}, bf16[672,128]{1,0:T(8,128)(2,1)S(1)}, u32[]{:S(2)}, u32[]{:S(2)}) collective-permute-start(bf16[672,128]{1,0:T(8,128)(2,1)S(1)} %shard_map.121.refs_0_), channel_id=1, source_target_pairs={{0,3},{1,2},{2,1},{3,0},{4,7},{5,6},{6,5},{7,4},{8,11},{9,10},{10,... | collective-permute-start | bytes 516104 | tf_op jit(solution)/shard_map/ppermute | solution.py:622

commit v5 on v4

--- a/solution.py
+++ b/solution.py
@@ -98,14 +98,19 @@
     rows = iota((share, docs), 0) + at * share
     chosen[pl.ds(pl.multiple_of(at * share, 16), share), :] = one_hot(rows == slot_ref[...])
 
+    @pl.when(at == 1)
+    def _():
+        load.wait()
+
+    @pl.when(at % 2 == 1)
+    def _():
+        rows = pl.ds(pl.multiple_of((at - 1) * step, step), 2 * step)
+        side[rows, :] = jnp.dot(
+            pooled[rows, :], w_ref[...], preferred_element_type=F32
+        ).astype(BF16)
+
     @pl.when(at == steps - 1)
     def _():
-        load.wait()
-        for part in range(2):
-            rows = slice(part * docs // 2, (part + 1) * docs // 2)
-            side[rows, :] = jnp.dot(
-                pooled[rows, :], w_ref[...], preferred_element_type=F32
-            ).astype(BF16)
         for part in range(6):
             rows = slice(part * share, (part + 1) * share)
             out_ref[rows, :] = jnp.dot(
@@ -325,7 +330,7 @@
                    bf16(step, width),
                    jax.ShapeDtypeStruct((1, width), F32)],
         scratch_shapes=[pltpu.VMEM((4 * nodes, width), BF16)],
-        compiler_params=params(),
+        compiler_params=params(40),
         cost_estimate=cost(12e8, 8e6, nodes * width),
     )(index, values, *parts, cotangent, w_msg, gate)
 
@@ -361,7 +366,7 @@
         out_specs=pl.BlockSpec((step, wide), lambda i: (i, 0)),
         out_shape=bf16(slots, wide),
         scratch_shapes=[pltpu.VMEM((4 * nodes, wide), BF16), pltpu.VMEM((nodes, wide), BF16)],
-        compiler_params=params(),
+        compiler_params=params(40),
         cost_estimate=cost(2 * slots * nodes * wide, 5e6),
     )(index, values, *parts, cotangent, place)
 

time: 240 us -> 241 us (level)
  local copies, waits for them, and re-layouts: 5.89 us -> 10.8 us
  Pallas kernels: 58 us -> 55.2 us
    unnamed x46 -> x36, local copies, waits for them, and re-layouts: 4.18 us -> 9.37 us
  transfers between devices with their start and end apart: 23 -> 23, of which waited for: 18 -> 17; matrix products, arithmetic and copies ran while one was open for 1% -> 1% of each run, Pallas kernels for 11% -> 10%
where the time goes in v5:
time: 241 us; the launch traced here: 240 us
  waiting for transfers between devices  88.6 us (37%)
  Pallas kernels  55.2 us (23%)
  starting transfers between devices  45.2 us (19%)
  blocking collectives  38.8 us (16%)
  local copies, waits for them, and re-layouts  10.8 us (4%)
    all_to_all x1, blocking collectives, shards(): lax.all_to_all(down, ('z', 'x'), split_axis=0, concat_axis=0, tiled=True)  38.8 us
    ppermute x15, waiting for transfers between devices, shift(): return lax.ppermute(part, 'col', [(c, (c + by) % 4) for c in range(4)])  38.8 us
    all_to_all x2, waiting for transfers between devices, relay(): lax.all_to_all(rows.reshape(size, slots // size, width), ROWS, split_axis...  36.4 us
    ppermute x15, starting transfers between devices, shift(): return lax.ppermute(part, 'col', [(c, (c + by) % 4) for c in range(4)])  23.2 us
    pallas_call x1, Pallas kernels, pool_and_pack(): pl.pallas_call(pool_kernel, grid=(6,), in_specs=[whole(*owner_of.shape),...  17.4 us
    all_to_all x2, starting transfers between devices, relay(): lax.all_to_all(rows.reshape(size, slots // size, width), ROWS, split_axis...  16.7 us
    pallas_call x1, Pallas kernels, pool_and_turn(): pl.pallas_call(turn_kernel, grid=(6,), in_specs=streams(step, rows) + [pl...  12.9 us
    unnamed x36, local copies, waits for them, and re-layouts  9.37 us
  transfers between devices with their start and end apart: 23, of which 17 were waited for; matrix products, arithmetic and copies ran while one was open for 1% of the time, Pallas kernels for 10%

profile of v5, /device:TPU:0, one launch (start us, length us, event | category | flops | bytes accessed | tf_op | source)
XLA Modules:
  0.0 240.0 jit_solution(13647817442080511755)
XLA Ops:
  0.6 17.4 %shard_map.111 = (bf16[2304,512]{1,0:T(8,128)(2,1)}, s32[1,768]{1,0:T(1,128)}) custom-call(s32[1,24576]{1,0:T(1,128)} %owner_ref.1, bf16[768,80,128]{2,1,0:T(8,128)(2,1)} %bitcast.33, bf16[768,80,128]{2,1,0:T(8,128)(2,1)} %bitcast.34, bf16[768,80,128]{2,1,0:T(8,128)(2,1)} %bitcast.35, bf16[768,80,128]{2,1,0:T(8,128)(2,1)} %bitcast.36, bf16[5120,512]{1,0:T(8,128)(2,1)} %refs_4_.1), custom_call_target="tpu_custom_call" | custom-call | flops 8000000000 | bytes 23000000 | tf_op jit(solution)/shard_map/pallas_call | solution.py:160
  18.0 8.4 %all-to-all-start = ((bf16[32,72,512]{2,1,0:T(8,128)(2,1)}), bf16[32,72,512]{2,1,0:T(8,128)(2,1)S(1)}, u32[]{:S(2)}, u32[]{:S(2)}) async-start(bf16[32,72,512]{2,1,0:T(8,128)(2,1)} %bitcast.41), calls=%async_computation | async-start | bytes 4718592 | tf_op jit(solution)/shard_map/all_to_all | solution.py:578
  26.4 0.3 fusion
  26.7 0.1 reduce_sum.18
  26.9 0.1 select_reduce_fusion
  27.2 12.9 %shard_map.112 = (bf16[16,160,768]{2,1,0:T(8,128)(2,1)}, bf16[16,160,768]{2,1,0:T(8,128)(2,1)}, f32[8,128]{1,0:T(8,128)}) custom-call(bf16[768,80,128]{2,1,0:T(8,128)(2,1)} %bitcast.37, bf16[768,80,128]{2,1,0:T(8,128)(2,1)} %bitcast.38, bf16[768,80,128]{2,1,0:T(8,128)(2,1)} %bitcast.39, bf16[768,80,128]{2,1,0:T(8,128)(2,1)} %bitcast.40, ...), custom_call_target="tpu_custom_call" | custom-call | flops 2000000000 | bytes 24000000 | tf_op jit(solution)/shard_map/pallas_call | solution.py:187
  40.1 19.4 %all-to-all-done = bf16[32,72,512]{2,1,0:T(8,128)(2,1)S(1)} async-done(((bf16[32,72,512]{2,1,0:T(8,128)(2,1)}), bf16[32,72,512]{2,1,0:T(8,128)(2,1)S(1)}, u32[]{:S(2)}, u32[]{:S(2)}) %all-to-all-start) | async-done | bytes 2359328 | tf_op jit(solution)/shard_map/all_to_all | solution.py:578
  59.5 1.5 copy-done.3
  61.0 1.7 copy-done.4
  62.6 0.7 copy-done.13
  63.4 2.3 shard_map.113
  65.6 1.6 collective-permute-start.2
  67.3 1.7 collective-permute-start.1
  68.9 1.8 collective-permute-start
  70.7 0.2 collective-permute-start.5
  71.0 0.7 copy-done.8
  71.7 7.3 %collective-permute-done.2.refs_6_ = bf16[384,512]{1,0:T(8,128)(2,1)S(1)} collective-permute-done((bf16[384,512]{1,0:T(8,128)(2,1)S(1)}, bf16[384,512]{1,0:T(8,128)(2,1)S(1)}, u32[]{:S(2)}, u32[]{:S(2)}) %collective-permute-start.2) | collective-permute-done | bytes 393248 | tf_op jit(solution)/shard_map/ppermute | solution.py:243
  79.0 0.4 collective-permute-start.3
  79.3 0.8 copy-done.10
  80.1 2.9 %collective-permute-start.4 = (bf16[384,512]{1,0:T(8,128)(2,1)}, bf16[384,512]{1,0:T(8,128)(2,1)}, u32[]{:S(2)}, u32[]{:S(2)}) collective-permute-start(bf16[384,512]{1,0:T(8,128)(2,1)} %collective-permute-done.1.refs_3_), channel_id=1, source_target_pairs={{0,3},{1,0},{2,1},{3,2},{4,7},{5,4},{6,5},{7,6},{8,11},{9,8},{10,9... | collective-permute-start | bytes 1179656 | tf_op jit(solution)/shard_map/ppermute | solution.py:243
  83.0 4.9 %collective-permute-done.refs_2_ = bf16[384,512]{1,0:T(8,128)(2,1)} collective-permute-done((bf16[384,512]{1,0:T(8,128)(2,1)S(1)}, bf16[384,512]{1,0:T(8,128)(2,1)}, u32[]{:S(2)}, u32[]{:S(2)}) %collective-permute-start) | collective-permute-done | bytes 393248 | tf_op jit(solution)/shard_map/ppermute | solution.py:243
  87.9 5.0 %collective-permute-done.3.refs_4_ = bf16[384,512]{1,0:T(8,128)(2,1)} collective-permute-done((bf16[384,512]{1,0:T(8,128)(2,1)S(1)}, bf16[384,512]{1,0:T(8,128)(2,1)}, u32[]{:S(2)}, u32[]{:S(2)}) %collective-permute-start.3) | collective-permute-done | bytes 393248 | tf_op jit(solution)/shard_map/ppermute | solution.py:243
  92.9 1.0 copy-done.9
  93.9 1.0 copy-done.11
  94.9 5.1 %shard_map.114 = (bf16[768,512]{1,0:T(8,128)(2,1)}, bf16[768,512]{1,0:T(8,128)(2,1)S(1)}, bf16[768,512]{1,0:T(8,128)(2,1)S(1)}, bf16[384,512]{1,0:T(8,128)(2,1)}...) custom-call(s32[24]{0:T(128)S(1)} %fusion.2.index_ref, bf16[24,128,128]{2,1,0:T(8,128)(2,1)S(1)} %bitcast.28, ...), custom_call_target="tpu_custom_call" | custom-call | flops 1200000000 | bytes 8000000 | tf_op jit(solution)/shard_map/pallas_call | solution.py:321
  100.1 0.9 copy-done.5
  100.9 1.6 collective-permute-start.9
  102.5 1.7 collective-permute-start.8
  104.2 0.4 collective-permute-start.12
  104.5 2.9 %collective-permute-start.7 = (bf16[384,512]{1,0:T(8,128)(2,1)}, bf16[384,512]{1,0:T(8,128)(2,1)}, u32[]{:S(2)}, u32[]{:S(2)}) collective-permute-start(bf16[384,512]{1,0:T(8,128)(2,1)} %get-tuple-element.34.refs_0_), channel_id=1, source_target_pairs={{0,3},{1,0},{2,1},{3,2},{4,7},{5,4},{6,5},{7,6},{8,11},{9,8},{10,9... | collective-permute-start | bytes 1179656 | tf_op jit(solution)/shard_map/ppermute | solution.py:243
  107.4 4.8 %collective-permute-done.9.refs_6_ = bf16[384,512]{1,0:T(8,128)(2,1)} collective-permute-done((bf16[384,512]{1,0:T(8,128)(2,1)}, bf16[384,512]{1,0:T(8,128)(2,1)}, u32[]{:S(2)}, u32[]{:S(2)}) %collective-permute-start.9) | collective-permute-done | bytes 393248 | tf_op jit(solution)/shard_map/ppermute | solution.py:243
  112.3 0.9 collective-permute-start.10
  113.2 0.3 collective-permute-done.8.refs_3_
  113.5 2.0 collective-permute-start.11
  115.5 1.1 select_n.51.refs_9_
  116.6 4.1 %collective-permute-done.12.refs_7_ = bf16[384,512]{1,0:T(8,128)(2,1)} collective-permute-done((bf16[384,512]{1,0:T(8,128)(2,1)}, bf16[384,512]{1,0:T(8,128)(2,1)}, u32[]{:S(2)}, u32[]{:S(2)}) %collective-permute-start.12) | collective-permute-done | bytes 393248 | tf_op jit(solution)/shard_map/ppermute | solution.py:243
  120.7 1.2 collective-permute-done.7.refs_2_
  121.9 5.5 %collective-permute-done.10.refs_4_ = bf16[384,512]{1,0:T(8,128)(2,1)} collective-permute-done((bf16[384,512]{1,0:T(8,128)(2,1)}, bf16[384,512]{1,0:T(8,128)(2,1)}, u32[]{:S(2)}, u32[]{:S(2)}) %collective-permute-start.10) | collective-permute-done | bytes 393248 | tf_op jit(solution)/shard_map/ppermute | solution.py:243
  127.5 6.5 %shard_map.115.after_ref = bf16[2304,512]{1,0:T(8,128)(2,1)} custom-call(s32[24]{0:T(128)S(1)} %fusion.2.index_ref, bf16[24,128,128]{2,1,0:T(8,128)(2,1)S(1)} %bitcast.29, bf16[384,512]{1,0:T(8,128)(2,1)} %get-tuple-element.34.refs_0_, bf16[384,512]{1,0:T(8,128)(2,1)} %get-tuple-element.35.refs_1_, bf16[384,512]{1,0:T(8,128)(2,1)} %collective-permute-done.7.refs_2_, ...), custom_call_target="tpu_custom_call" | custom-call | flops 1811939328 | bytes 5000000 | tf_op jit(solution)/shard_map/pallas_call | solution.py:360
  134.0 8.3 %all-to-all-start.1 = ((bf16[32,72,512]{2,1,0:T(8,128)(2,1)}), bf16[32,72,512]{2,1,0:T(8,128)(2,1)S(1)}, u32[]{:S(2)}, u32[]{:S(2)}) async-start(bf16[32,72,512]{2,1,0:T(8,128)(2,1)} %bitcast.13), calls=%async_computation.1 | async-start | bytes 4718592 | tf_op jit(solution)/shard_map/all_to_all | solution.py:578
  142.3 1.1 copy-done.6
  143.4 0.7 shard_map.116
  144.1 0.4 collective-permute-start.13
  144.5 2.0 collective-permute-done.13.other_small_ref
  146.4 0.9 shard_map.117
  147.3 1.3 collective-permute-start.14
  148.6 3.0 %collective-permute-start.15 = (bf16[16,32,128]{2,1,0:T(8,128)(2,1)S(1)}, bf16[16,32,128]{2,1,0:T(8,128)(2,1)S(1)}, u32[]{:S(2)}, u32[]{:S(2)}) collective-permute-start(bf16[16,32,128]{2,1,0:T(8,128)(2,1)S(1)} %get-tuple-element.43), channel_id=1, source_target_pairs={{0,2},{1,3},{2,0},{3,1},{4,6},{5,7},{6,4},{7,5},{8,10},{9,11},{10,... | collective-permute-start | bytes 393224 | tf_op jit(solution)/shard_map/ppermute | solution.py:243
  151.6 0.9 collective-permute-start.16
  152.6 0.2 copy.18.place_ref
  152.8 1.7 collective-permute-done.14.refs_1_
  154.4 3.9 %collective-permute-done.15.refs_2_ = bf16[16,32,128]{2,1,0:T(8,128)(2,1)S(1)} collective-permute-done((bf16[16,32,128]{2,1,0:T(8,128)(2,1)S(1)}, bf16[16,32,128]{2,1,0:T(8,128)(2,1)S(1)}, u32[]{:S(2)}, u32[]{:S(2)}) %collective-permute-start.15) | collective-permute-done | bytes 131104 | tf_op jit(solution)/shard_map/ppermute | solution.py:243
  158.4 17.0 %all-to-all-done.1 = bf16[32,72,512]{2,1,0:T(8,128)(2,1)S(1)} async-done(((bf16[32,72,512]{2,1,0:T(8,128)(2,1)}), bf16[32,72,512]{2,1,0:T(8,128)(2,1)S(1)}, u32[]{:S(2)}, u32[]{:S(2)}) %all-to-all-start.1) | async-done | bytes 2359328 | tf_op jit(solution)/shard_map/all_to_all | solution.py:578
  175.4 2.3 shard_map.119.grad_ref
  177.7 2.3 collective-permute-done.17.other_grad_ref
  180.0 6.0 %shard_map.120 = bf16[16,672,128]{2,1,0:T(8,128)(2,1)S(1)} custom-call(bf16[16,160,768]{2,1,0:T(8,128)(2,1)S(1)} %copy-done, bf16[16,160,768]{2,1,0:T(8,128)(2,1)} %collective-permute-done.6.other_ref, bf16[768,512]{1,0:T(8,128)(2,1)S(1)} %shard_map.119.grad_ref, bf16[768,512]{1,0:T(8,128)(2,1)S(1)} %collective-permute-done.17.other_grad_ref, ...), custom_call_target="tpu_custom_call" | custom-call | flops 2000000000 | bytes 12000000 | tf_op jit(solution)/shard_map/pallas_call | solution.py:498
  186.0 38.8 %all_to_all.15.parts_ref = bf16[16,672,128]{2,1,0:T(8,128)(2,1)S(1)} all-to-all(bf16[16,672,128]{2,1,0:T(8,128)(2,1)S(1)} %shard_map.120), channel_id=1, replica_groups=mesh['z'=4,'x'=4,'core'=2,'col'=4] {'z','x'}, dimensions={0} | all-to-all | bytes 5505024 | tf_op jit(solution)/shard_map/all_to_all | solution.py:624
  224.8 0.4 shard_map.121.refs_0_
  225.1 1.4 collective-permute-start.18
  226.5 3.0 %collective-permute-start.19 = (bf16[672,128]{1,0:T(8,128)(2,1)S(1)}, bf16[672,128]{1,0:T(8,128)(2,1)S(1)}, u32[]{:S(2)}, u32[]{:S(2)}) collective-permute-start(bf16[672,128]{1,0:T(8,128)(2,1)S(1)} %shard_map.121.refs_0_), channel_id=1, source_target_pairs={{0,2},{1,3},{2,0},{3,1},{4,6},{5,7},{6,4},{7,5},{8,10},{9,11},{10,... | collective-permute-start | bytes 516104 | tf_op jit(solution)/shard_map/ppermute | solution.py:627
  229.5 0.4 collective-permute-start.20
  229.9 2.6 %collective-permute-done.18.refs_1_ = bf16[672,128]{1,0:T(8,128)(2,1)S(1)} collective-permute-done((bf16[672,128]{1,0:T(8,128)(2,1)S(1)}, bf16[672,128]{1,0:T(8,128)(2,1)S(1)}, u32[]{:S(2)}, u32[]{:S(2)}) %collective-permute-start.18) | collective-permute-done | bytes 172064 | tf_op jit(solution)/shard_map/ppermute | solution.py:627
  232.5 4.4 %collective-permute-done.19.refs_2_ = bf16[672,128]{1,0:T(8,128)(2,1)S(1)} collective-permute-done((bf16[672,128]{1,0:T(8,128)(2,1)S(1)}, bf16[672,128]{1,0:T(8,128)(2,1)S(1)}, u32[]{:S(2)}, u32[]{:S(2)}) %collective-permute-start.19) | collective-permute-done | bytes 172064 | tf_op jit(solution)/shard_map/ppermute | solution.py:627
  236.9 2.2 collective-permute-done.20.refs_3_
  239.1 0.9 shard_map.122
  (40 shorter events, 0.5 us)
Async XLA Ops:
  18.0 8.4 %copy-start.14 = (s32[1,24576]{1,0:T(1,128)S(1)}, s32[1,24576]{1,0:T(1,128)}, u32[]{:S(2)}) copy-start(s32[1,24576]{1,0:T(1,128)} %owner_ref.1) | copy-start | bytes 294916
  18.0 41.5 %all-to-all-start = ((bf16[32,72,512]{2,1,0:T(8,128)(2,1)}), bf16[32,72,512]{2,1,0:T(8,128)(2,1)S(1)}, u32[]{:S(2)}, u32[]{:S(2)}) async-start(bf16[32,72,512]{2,1,0:T(8,128)(2,1)} %bitcast.41), calls=%async_computation | async-start | bytes 4718592 | tf_op jit(solution)/shard_map/all_to_all | solution.py:578
  27.0 13.0 %copy-start.15 = (s32[32,72]{1,0:T(8,128)}, s32[32,72]{1,0:T(8,128)S(1)}, u32[]{:S(2)}) copy-start(s32[32,72]{1,0:T(8,128)S(1)} %add_select_fusion) | copy-start | bytes 27652
  59.5 1.5 copy-start.3
  61.0 1.7 copy-start.4
  62.6 0.7 copy-start.13
  63.3 19.6 %copy-start.17 = (s32[1,24]{1,0:T(1,128)S(1)}, s32[1,24]{1,0:T(1,128)}, u32[]{:S(2)}) copy-start(s32[1,24]{1,0:T(1,128)} %param.12) | copy-start | bytes 292
  63.3 29.6 %copy-start.1 = (bf16[1,24,128,128]{3,2,1,0:T(8,128)(2,1)S(1)}, bf16[1,24,128,128]{3,2,1,0:T(8,128)(2,1)}, u32[]{:S(2)}) copy-start(bf16[1,24,128,128]{3,2,1,0:T(8,128)(2,1)} %param.11) | copy-start | bytes 2359300
  63.3 29.6 %copy-start.2 = (bf16[768,512]{1,0:T(8,128)(2,1)S(1)}, bf16[768,512]{1,0:T(8,128)(2,1)}, u32[]{:S(2)}) copy-start(bf16[768,512]{1,0:T(8,128)(2,1)} %refs_8_.3) | copy-start | bytes 2359300
  63.3 29.6 %copy-start.7 = (bf16[512,512]{1,0:T(8,128)(2,1)S(1)}, bf16[512,512]{1,0:T(8,128)(2,1)}, u32[]{:S(2)}) copy-start(bf16[512,512]{1,0:T(8,128)(2,1)} %refs_9_.1) | copy-start | bytes 1572868
  63.3 29.6 %copy-start.12 = (f32[512]{0:T(512)S(1)}, f32[512]{0:T(512)}, u32[]{:S(2)}) copy-start(f32[512]{0:T(512)} %param.14) | copy-start | bytes 6148
  65.6 13.3 %collective-permute-start.2 = (bf16[384,512]{1,0:T(8,128)(2,1)S(1)}, bf16[384,512]{1,0:T(8,128)(2,1)S(1)}, u32[]{:S(2)}, u32[]{:S(2)}) collective-permute-start(bf16[384,512]{1,0:T(8,128)(2,1)S(1)} %get-tuple-element.29.refs_0_), channel_id=1, source_target_pairs={{0,1},{1,2},{2,3},{3,0},{4,5},{5,6},{6,7},{7,4},{8,9},{9,10},{10,1... | collective-permute-start | bytes 1179656 | tf_op jit(solution)/shard_map/ppermute | solution.py:243
  67.3 12.8 %collective-permute-start.1 = (bf16[384,512]{1,0:T(8,128)(2,1)S(1)}, bf16[384,512]{1,0:T(8,128)(2,1)}, u32[]{:S(2)}, u32[]{:S(2)}) collective-permute-start(bf16[384,512]{1,0:T(8,128)(2,1)S(1)} %get-tuple-element.30.refs_1_), channel_id=1, source_target_pairs={{0,3},{1,0},{2,1},{3,2},{4,7},{5,4},{6,5},{7,6},{8,11},{9,8},{10,9... | collective-permute-start | bytes 1179656 | tf_op jit(solution)/shard_map/ppermute | solution.py:243
  68.9 18.9 %collective-permute-start = (bf16[384,512]{1,0:T(8,128)(2,1)S(1)}, bf16[384,512]{1,0:T(8,128)(2,1)}, u32[]{:S(2)}, u32[]{:S(2)}) collective-permute-start(bf16[384,512]{1,0:T(8,128)(2,1)S(1)} %get-tuple-element.29.refs_0_), channel_id=1, source_target_pairs={{0,3},{1,0},{2,1},{3,2},{4,7},{5,4},{6,5},{7,6},{8,11},{9,8},{10,9... | collective-permute-start | bytes 1179656 | tf_op jit(solution)/shard_map/ppermute | solution.py:243
  70.7 17.1 %collective-permute-start.5 = (bf16[384,512]{1,0:T(8,128)(2,1)S(1)}, bf16[384,512]{1,0:T(8,128)(2,1)}, u32[]{:S(2)}, u32[]{:S(2)}) collective-permute-start(bf16[384,512]{1,0:T(8,128)(2,1)S(1)} %get-tuple-element.30.refs_1_), channel_id=1, source_target_pairs={{0,1},{1,2},{2,3},{3,0},{4,5},{5,6},{6,7},{7,4},{8,9},{9,10},{10,1... | collective-permute-start | bytes 1179656 | tf_op jit(solution)/shard_map/ppermute | solution.py:243
  71.0 0.7 copy-start.8
  79.0 13.9 %collective-permute-start.3 = (bf16[384,512]{1,0:T(8,128)(2,1)S(1)}, bf16[384,512]{1,0:T(8,128)(2,1)}, u32[]{:S(2)}, u32[]{:S(2)}) collective-permute-start(bf16[384,512]{1,0:T(8,128)(2,1)S(1)} %collective-permute-done.2.refs_6_), channel_id=1, source_target_pairs={{0,1},{1,2},{2,3},{3,0},{4,5},{5,6},{6,7},{7,4},{8,9},{9,10},{10,1... | collective-permute-start | bytes 1179656 | tf_op jit(solution)/shard_map/ppermute | solution.py:243
  79.3 0.8 copy-start.10
  80.1 12.8 %collective-permute-start.4 = (bf16[384,512]{1,0:T(8,128)(2,1)}, bf16[384,512]{1,0:T(8,128)(2,1)}, u32[]{:S(2)}, u32[]{:S(2)}) collective-permute-start(bf16[384,512]{1,0:T(8,128)(2,1)} %collective-permute-done.1.refs_3_), channel_id=1, source_target_pairs={{0,3},{1,0},{2,1},{3,2},{4,7},{5,4},{6,5},{7,6},{8,11},{9,8},{10,9... | collective-permute-start | bytes 1179656 | tf_op jit(solution)/shard_map/ppermute | solution.py:243
  92.9 1.0 copy-start.9
  93.9 1.0 copy-start.11
  100.1 0.9 copy-start.5
  100.9 11.3 %collective-permute-start.9 = (bf16[384,512]{1,0:T(8,128)(2,1)}, bf16[384,512]{1,0:T(8,128)(2,1)}, u32[]{:S(2)}, u32[]{:S(2)}) collective-permute-start(bf16[384,512]{1,0:T(8,128)(2,1)} %get-tuple-element.34.refs_0_), channel_id=1, source_target_pairs={{0,1},{1,2},{2,3},{3,0},{4,5},{5,6},{6,7},{7,4},{8,9},{9,10},{10,1... | collective-permute-start | bytes 1179656 | tf_op jit(solution)/shard_map/ppermute | solution.py:243
  102.5 11.0 %collective-permute-start.8 = (bf16[384,512]{1,0:T(8,128)(2,1)}, bf16[384,512]{1,0:T(8,128)(2,1)}, u32[]{:S(2)}, u32[]{:S(2)}) collective-permute-start(bf16[384,512]{1,0:T(8,128)(2,1)} %get-tuple-element.35.refs_1_), channel_id=1, source_target_pairs={{0,3},{1,0},{2,1},{3,2},{4,7},{5,4},{6,5},{7,6},{8,11},{9,8},{10,9... | collective-permute-start | bytes 1179656 | tf_op jit(solution)/shard_map/ppermute | solution.py:243
  104.2 73.6 %collective-permute-start.6 = (bf16[16,160,768]{2,1,0:T(8,128)(2,1)}, bf16[16,160,768]{2,1,0:T(8,128)(2,1)}, u32[]{:S(2)}, u32[]{:S(2)}) collective-permute-start(bf16[16,160,768]{2,1,0:T(8,128)(2,1)} %get-tuple-element.33), channel_id=1, source_target_pairs={{0,4},{4,0},{1,5},{5,1},{2,6},{6,2},{3,7},{7,3},{8,12},{12,8},{9,1... | collective-permute-start | bytes 11796488 | tf_op jit(solution)/shard_map/ppermute | solution.py:595
  104.2 16.5 %collective-permute-start.12 = (bf16[384,512]{1,0:T(8,128)(2,1)}, bf16[384,512]{1,0:T(8,128)(2,1)}, u32[]{:S(2)}, u32[]{:S(2)}) collective-permute-start(bf16[384,512]{1,0:T(8,128)(2,1)} %get-tuple-element.35.refs_1_), channel_id=1, source_target_pairs={{0,1},{1,2},{2,3},{3,0},{4,5},{5,6},{6,7},{7,4},{8,9},{9,10},{10,1... | collective-permute-start | bytes 1179656 | tf_op jit(solution)/shard_map/ppermute | solution.py:243
  104.5 17.4 %collective-permute-start.7 = (bf16[384,512]{1,0:T(8,128)(2,1)}, bf16[384,512]{1,0:T(8,128)(2,1)}, u32[]{:S(2)}, u32[]{:S(2)}) collective-permute-start(bf16[384,512]{1,0:T(8,128)(2,1)} %get-tuple-element.34.refs_0_), channel_id=1, source_target_pairs={{0,3},{1,0},{2,1},{3,2},{4,7},{5,4},{6,5},{7,6},{8,11},{9,8},{10,9... | collective-permute-start | bytes 1179656 | tf_op jit(solution)/shard_map/ppermute | solution.py:243
  112.3 15.2 %collective-permute-start.10 = (bf16[384,512]{1,0:T(8,128)(2,1)}, bf16[384,512]{1,0:T(8,128)(2,1)}, u32[]{:S(2)}, u32[]{:S(2)}) collective-permute-start(bf16[384,512]{1,0:T(8,128)(2,1)} %collective-permute-done.9.refs_6_), channel_id=1, source_target_pairs={{0,1},{1,2},{2,3},{3,0},{4,5},{5,6},{6,7},{7,4},{8,9},{9,10},{10,1... | collective-permute-start | bytes 1179656 | tf_op jit(solution)/shard_map/ppermute | solution.py:243
  113.5 14.0 %collective-permute-start.11 = (bf16[384,512]{1,0:T(8,128)(2,1)}, bf16[384,512]{1,0:T(8,128)(2,1)}, u32[]{:S(2)}, u32[]{:S(2)}) collective-permute-start(bf16[384,512]{1,0:T(8,128)(2,1)} %collective-permute-done.8.refs_3_), channel_id=1, source_target_pairs={{0,3},{1,0},{2,1},{3,2},{4,7},{5,4},{6,5},{7,6},{8,11},{9,8},{10,9... | collective-permute-start | bytes 1179656 | tf_op jit(solution)/shard_map/ppermute | solution.py:243
  134.0 41.4 %all-to-all-start.1 = ((bf16[32,72,512]{2,1,0:T(8,128)(2,1)}), bf16[32,72,512]{2,1,0:T(8,128)(2,1)S(1)}, u32[]{:S(2)}, u32[]{:S(2)}) async-start(bf16[32,72,512]{2,1,0:T(8,128)(2,1)} %bitcast.13), calls=%async_computation.1 | async-start | bytes 4718592 | tf_op jit(solution)/shard_map/all_to_all | solution.py:578
  142.3 1.1 copy-start.6
  143.4 9.2 %copy-start.16 = (s32[1,768]{1,0:T(1,128)S(1)}, s32[1,768]{1,0:T(1,128)}, u32[]{:S(2)}) copy-start(s32[1,768]{1,0:T(1,128)} %get-tuple-element.27.refs_4_) | copy-start | bytes 9220
  144.1 2.4 collective-permute-start.13
  147.3 7.1 %collective-permute-start.14 = (bf16[16,32,128]{2,1,0:T(8,128)(2,1)}, bf16[16,32,128]{2,1,0:T(8,128)(2,1)S(1)}, u32[]{:S(2)}, u32[]{:S(2)}) collective-permute-start(bf16[16,32,128]{2,1,0:T(8,128)(2,1)} %get-tuple-element.42), channel_id=1, source_target_pairs={{0,1},{1,2},{2,3},{3,0},{4,5},{5,6},{6,7},{7,4},{8,9},{9,10},{10,1... | collective-permute-start | bytes 393224 | tf_op jit(solution)/shard_map/ppermute | solution.py:243
  148.6 9.7 %collective-permute-start.15 = (bf16[16,32,128]{2,1,0:T(8,128)(2,1)S(1)}, bf16[16,32,128]{2,1,0:T(8,128)(2,1)S(1)}, u32[]{:S(2)}, u32[]{:S(2)}) collective-permute-start(bf16[16,32,128]{2,1,0:T(8,128)(2,1)S(1)} %get-tuple-element.43), channel_id=1, source_target_pairs={{0,2},{1,3},{2,0},{3,1},{4,6},{5,7},{6,4},{7,5},{8,10},{9,11},{10,... | collective-permute-start | bytes 393224 | tf_op jit(solution)/shard_map/ppermute | solution.py:243
  151.6 6.7 %collective-permute-start.16 = (bf16[16,32,128]{2,1,0:T(8,128)(2,1)S(1)}, bf16[16,32,128]{2,1,0:T(8,128)(2,1)S(1)}, u32[]{:S(2)}, u32[]{:S(2)}) collective-permute-start(bf16[16,32,128]{2,1,0:T(8,128)(2,1)S(1)} %get-tuple-element.44), channel_id=1, source_target_pairs={{0,3},{1,0},{2,1},{3,2},{4,7},{5,4},{6,5},{7,6},{8,11},{9,8},{10,9... | collective-permute-start | bytes 393224 | tf_op jit(solution)/shard_map/ppermute | solution.py:243
  175.4 4.6 %copy-start = (bf16[16,160,768]{2,1,0:T(8,128)(2,1)S(1)}, bf16[16,160,768]{2,1,0:T(8,128)(2,1)}, u32[]{:S(2)}) copy-start(bf16[16,160,768]{2,1,0:T(8,128)(2,1)} %get-tuple-element.32.mine_ref) | copy-start | bytes 11796484
  177.6 2.4 collective-permute-start.17
  225.1 7.4 %collective-permute-start.18 = (bf16[672,128]{1,0:T(8,128)(2,1)S(1)}, bf16[672,128]{1,0:T(8,128)(2,1)S(1)}, u32[]{:S(2)}, u32[]{:S(2)}) collective-permute-start(bf16[672,128]{1,0:T(8,128)(2,1)S(1)} %shard_map.121.refs_0_), channel_id=1, source_target_pairs={{0,1},{1,0},{2,3},{3,2},{4,5},{5,4},{6,7},{7,6},{8,9},{9,8},{10,11... | collective-permute-start | bytes 516104 | tf_op jit(solution)/shard_map/ppermute | solution.py:627
  226.5 10.4 %collective-permute-start.19 = (bf16[672,128]{1,0:T(8,128)(2,1)S(1)}, bf16[672,128]{1,0:T(8,128)(2,1)S(1)}, u32[]{:S(2)}, u32[]{:S(2)}) collective-permute-start(bf16[672,128]{1,0:T(8,128)(2,1)S(1)} %shard_map.121.refs_0_), channel_id=1, source_target_pairs={{0,2},{1,3},{2,0},{3,1},{4,6},{5,7},{6,4},{7,5},{8,10},{9,11},{10,... | collective-permute-start | bytes 516104 | tf_op jit(solution)/shard_map/ppermute | solution.py:627
  229.5 9.6 %collective-permute-start.20 = (bf16[672,128]{1,0:T(8,128)(2,1)S(1)}, bf16[672,128]{1,0:T(8,128)(2,1)S(1)}, u32[]{:S(2)}, u32[]{:S(2)}) collective-permute-start(bf16[672,128]{1,0:T(8,128)(2,1)S(1)} %shard_map.121.refs_0_), channel_id=1, source_target_pairs={{0,3},{1,2},{2,1},{3,0},{4,7},{5,6},{6,5},{7,4},{8,11},{9,10},{10,... | collective-permute-start | bytes 516104 | tf_op jit(solution)/shard_map/ppermute | solution.py:627

commit v6 on v4

--- a/solution.py
+++ b/solution.py
@@ -101,11 +101,7 @@
     @pl.when(at == steps - 1)
     def _():
         load.wait()
-        for part in range(2):
-            rows = slice(part * docs // 2, (part + 1) * docs // 2)
-            side[rows, :] = jnp.dot(
-                pooled[rows, :], w_ref[...], preferred_element_type=F32
-            ).astype(BF16)
+        side[...] = jnp.dot(pooled[...], w_ref[...], preferred_element_type=F32).astype(BF16)
         for part in range(6):
             rows = slice(part * share, (part + 1) * share)
             out_ref[rows, :] = jnp.dot(
@@ -175,7 +171,7 @@
     )(owner_of, *[taps] * STREAMS, w_down)
 
 
-def pool_and_turn(taps, depth, chips, after):
+def pool_and_turn(taps, depth, chips, after, slots):
     docs, rows, _ = taps.shape
     step = docs // 6
     turned = pl.BlockSpec((chips, depth // (2 * chips), step), lambda i: (0, 0, i))
@@ -183,9 +179,9 @@
         turn_kernel,
         grid=(6,),
         in_specs=streams(step, rows) + [pl.BlockSpec(memory_space=pl.ANY)],
-        out_specs=[turned, turned, whole(8, 128)],
+        out_specs=[turned, turned, whole(1, slots)],
         out_shape=[bf16(chips, depth // (2 * chips), docs)] * 2
-        + [jax.ShapeDtypeStruct((8, 128), F32)],
+        + [jax.ShapeDtypeStruct((1, slots), jnp.int32)],
         scratch_shapes=[pltpu.VMEM((128, 256), BF16), pltpu.VMEM((step, depth), BF16)],
         compiler_params=params(),
         cost_estimate=cost(2e9, 24e6),
@@ -361,7 +357,7 @@
         out_specs=pl.BlockSpec((step, wide), lambda i: (i, 0)),
         out_shape=bf16(slots, wide),
         scratch_shapes=[pltpu.VMEM((4 * nodes, wide), BF16), pltpu.VMEM((nodes, wide), BF16)],
-        compiler_params=params(),
+        compiler_params=params(40),
         cost_estimate=cost(2 * slots * nodes * wide, 5e6),
     )(index, values, *parts, cotangent, place)
 
@@ -592,7 +588,7 @@
     taps = taps_by_tile(doc_taps)
     packed, slot = pool_and_pack(owner_of, taps, w_down, slots)
     incoming = relay(packed)
-    mine, theirs, turned = pool_and_turn(taps, depth, chips, slot)
+    mine, theirs, turned = pool_and_turn(taps, depth, chips, slot, slots)
     other = swap(theirs)
 
     owners = owner_of[0]
@@ -601,9 +597,9 @@
     starts = jnp.sum(jnp.where(lower, counts[None, :], 0), axis=1)
     in_slot = jnp.arange(SLOTS, dtype=jnp.int32)[None, :]
     position = jnp.where(in_slot < counts[:, None], starts[:, None] + in_slot, -1).reshape(slots)
-    pos_row, pos_col = position.reshape(1, slots), position.reshape(slots, 1)
-
-    owned = take(pos_row, incoming, docs, halves=True, after=(turned,))
+    pos_row, pos_col = position.reshape(1, slots) + turned, position.reshape(slots, 1)
+
+    owned = take(pos_row, incoming, docs, halves=True)
     side_out, aggregate, message_grad, low, high, gate_part = layer(
         index, values, gather_ring(*owned), cotangent, w_msg, gate
     )

time: 240 us -> 237 us (0.988)
  Pallas kernels: 58 us -> 55.5 us
  transfers between devices with their start and end apart: 23 -> 23, of which waited for: 18 -> 17; matrix products, arithmetic and copies ran while one was open for 1% -> 1% of each run, Pallas kernels for 11% -> 10%
where the time goes in v6:
time: 237 us; the launch traced here: 236 us
  waiting for transfers between devices  88.7 us (37%)
  Pallas kernels  55.5 us (23%)
  starting transfers between devices  45.2 us (19%)
  blocking collectives  38.8 us (16%)
  local copies, waits for them, and re-layouts  5.5 us (2%)
    ppermute x15, waiting for transfers between devices, shift(): return lax.ppermute(part, 'col', [(c, (c + by) % 4) for c in range(4)])  39.6 us
    all_to_all x1, blocking collectives, shards(): lax.all_to_all(down, ('z', 'x'), split_axis=0, concat_axis=0, tiled=True)  38.8 us
    all_to_all x2, waiting for transfers between devices, relay(): lax.all_to_all(rows.reshape(size, slots // size, width), ROWS, split_axis...  35.6 us
    ppermute x15, starting transfers between devices, shift(): return lax.ppermute(part, 'col', [(c, (c + by) % 4) for c in range(4)])  23.3 us
    pallas_call x1, Pallas kernels, pool_and_pack(): pl.pallas_call(pool_kernel, grid=(6,), in_specs=[whole(*owner_of.shape),...  16.8 us
    all_to_all x2, starting transfers between devices, relay(): lax.all_to_all(rows.reshape(size, slots // size, width), ROWS, split_axis...  16.7 us
    pallas_call x1, Pallas kernels, pool_and_turn(): pl.pallas_call(turn_kernel, grid=(6,), in_specs=streams(step, rows) + [pl...  12.9 us
    ppermute x3, waiting for transfers between devices, shards(): lax.ppermute(own, 'col', [(c, c ^ step) for c in range(4)])  9.19 us
  transfers between devices with their start and end apart: 23, of which 17 were waited for; matrix products, arithmetic and copies ran while one was open for 1% of the time, Pallas kernels for 10%

profile of v6, /device:TPU:0, one launch (start us, length us, event | category | flops | bytes accessed | tf_op | source)
XLA Modules:
  0.0 236.4 jit_solution(2774213370171510493)
XLA Ops:
  0.6 16.8 %shard_map.111 = (bf16[2304,512]{1,0:T(8,128)(2,1)}, s32[1,768]{1,0:T(1,128)}) custom-call(s32[1,24576]{1,0:T(1,128)} %owner_ref.1, bf16[768,80,128]{2,1,0:T(8,128)(2,1)} %bitcast.32, bf16[768,80,128]{2,1,0:T(8,128)(2,1)} %bitcast.33, bf16[768,80,128]{2,1,0:T(8,128)(2,1)} %bitcast.34, bf16[768,80,128]{2,1,0:T(8,128)(2,1)} %bitcast.35, bf16[5120,512]{1,0:T(8,128)(2,1)} %refs_4_.1), custom_call_target="tpu_custom_call" | custom-call | flops 8000000000 | bytes 23000000 | tf_op jit(solution)/shard_map/pallas_call | solution.py:151
  17.5 8.4 %all-to-all-start = ((bf16[32,72,512]{2,1,0:T(8,128)(2,1)}), bf16[32,72,512]{2,1,0:T(8,128)(2,1)S(1)}, u32[]{:S(2)}, u32[]{:S(2)}) async-start(bf16[32,72,512]{2,1,0:T(8,128)(2,1)} %bitcast.40), calls=%async_computation | async-start | bytes 4718592 | tf_op jit(solution)/shard_map/all_to_all | solution.py:569
  25.9 0.3 fusion
  26.2 0.1 reduce_sum.18
  26.3 0.1 select_reduce_fusion
  26.5 0.1 select_n.49
  26.6 12.9 %shard_map.112 = (bf16[16,160,768]{2,1,0:T(8,128)(2,1)}, bf16[16,160,768]{2,1,0:T(8,128)(2,1)}, s32[1,2304]{1,0:T(1,128)}) custom-call(bf16[768,80,128]{2,1,0:T(8,128)(2,1)} %bitcast.36, bf16[768,80,128]{2,1,0:T(8,128)(2,1)} %bitcast.37, bf16[768,80,128]{2,1,0:T(8,128)(2,1)} %bitcast.38, bf16[768,80,128]{2,1,0:T(8,128)(2,1)} %bitcast.39, ...), custom_call_target="tpu_custom_call" | custom-call | flops 2000000000 | bytes 24000000 | tf_op jit(solution)/shard_map/pallas_call | solution.py:178
  39.5 0.7 add.57.place_ref
  40.2 18.7 %all-to-all-done = bf16[32,72,512]{2,1,0:T(8,128)(2,1)S(1)} async-done(((bf16[32,72,512]{2,1,0:T(8,128)(2,1)}), bf16[32,72,512]{2,1,0:T(8,128)(2,1)S(1)}, u32[]{:S(2)}, u32[]{:S(2)}) %all-to-all-start) | async-done | bytes 2359328 | tf_op jit(solution)/shard_map/all_to_all | solution.py:569
  58.9 2.2 shard_map.113
  61.2 1.6 collective-permute-start.2
  62.9 1.7 collective-permute-start.1
  64.5 1.8 collective-permute-start
  66.3 0.2 collective-permute-start.5
  66.6 8.0 %collective-permute-done.2.refs_6_ = bf16[384,512]{1,0:T(8,128)(2,1)S(1)} collective-permute-done((bf16[384,512]{1,0:T(8,128)(2,1)S(1)}, bf16[384,512]{1,0:T(8,128)(2,1)S(1)}, u32[]{:S(2)}, u32[]{:S(2)}) %collective-permute-start.2) | collective-permute-done | bytes 393248 | tf_op jit(solution)/shard_map/ppermute | solution.py:234
  74.6 0.4 collective-permute-start.3
  74.9 2.9 %collective-permute-start.4 = (bf16[384,512]{1,0:T(8,128)(2,1)S(1)}, bf16[384,512]{1,0:T(8,128)(2,1)S(1)}, u32[]{:S(2)}, u32[]{:S(2)}) collective-permute-start(bf16[384,512]{1,0:T(8,128)(2,1)S(1)} %collective-permute-done.1.refs_3_), channel_id=1, source_target_pairs={{0,3},{1,0},{2,1},{3,2},{4,7},{5,4},{6,5},{7,6},{8,11},{9,8},{10,9... | collective-permute-start | bytes 1179656 | tf_op jit(solution)/shard_map/ppermute | solution.py:234
  77.8 0.5 fusion.2.index_ref
  78.3 5.0 %collective-permute-done.refs_2_ = bf16[384,512]{1,0:T(8,128)(2,1)S(1)} collective-permute-done((bf16[384,512]{1,0:T(8,128)(2,1)S(1)}, bf16[384,512]{1,0:T(8,128)(2,1)S(1)}, u32[]{:S(2)}, u32[]{:S(2)}) %collective-permute-start) | collective-permute-done | bytes 393248 | tf_op jit(solution)/shard_map/ppermute | solution.py:234
  83.4 5.0 %collective-permute-done.3.refs_4_ = bf16[384,512]{1,0:T(8,128)(2,1)S(1)} collective-permute-done((bf16[384,512]{1,0:T(8,128)(2,1)S(1)}, bf16[384,512]{1,0:T(8,128)(2,1)S(1)}, u32[]{:S(2)}, u32[]{:S(2)}) %collective-permute-start.3) | collective-permute-done | bytes 393248 | tf_op jit(solution)/shard_map/ppermute | solution.py:234
  88.4 0.7 copy-done.16
  89.1 0.2 copy-done.17
  89.4 6.4 %shard_map.114 = (bf16[768,512]{1,0:T(8,128)(2,1)}, bf16[768,512]{1,0:T(8,128)(2,1)}, bf16[768,512]{1,0:T(8,128)(2,1)}, bf16[384,512]{1,0:T(8,128)(2,1)}, bf16[384,512]{1,0:T(8,128)(2,1)}, /*index=5*/f32[1,512]{1,0:T(1,128)}) custom-call(s32[24]{0:T(128)} %fusion.2.index_ref, bf16[24,128,128]{2,1,0:T(8,128)(2,1)} %bitcast.28, bf16[384,512]{1,0:T(8,128)(2,1)} %copy-done.7, ...), custom_call_target="tpu_custom_call" | custom-call | flops 1200000000 | bytes 8000000 | tf_op jit(solution)/shard_map/pallas_call | solution.py:312
  95.8 1.5 collective-permute-start.9
  97.3 1.8 collective-permute-start.8
  99.1 0.2 collective-permute-start.12
  99.3 3.0 %collective-permute-start.7 = (bf16[384,512]{1,0:T(8,128)(2,1)}, bf16[384,512]{1,0:T(8,128)(2,1)}, u32[]{:S(2)}, u32[]{:S(2)}) collective-permute-start(bf16[384,512]{1,0:T(8,128)(2,1)} %get-tuple-element.34.refs_0_), channel_id=1, source_target_pairs={{0,3},{1,0},{2,1},{3,2},{4,7},{5,4},{6,5},{7,6},{8,11},{9,8},{10,9... | collective-permute-start | bytes 1179656 | tf_op jit(solution)/shard_map/ppermute | solution.py:234
  102.3 4.7 %collective-permute-done.9.refs_6_ = bf16[384,512]{1,0:T(8,128)(2,1)S(1)} collective-permute-done((bf16[384,512]{1,0:T(8,128)(2,1)}, bf16[384,512]{1,0:T(8,128)(2,1)S(1)}, u32[]{:S(2)}, u32[]{:S(2)}) %collective-permute-start.9) | collective-permute-done | bytes 393248 | tf_op jit(solution)/shard_map/ppermute | solution.py:234
  107.1 0.7 collective-permute-start.10
  107.8 0.3 collective-permute-done.8.refs_3_
  108.1 2.2 collective-permute-start.11
  110.3 1.1 select_n.51.refs_9_
  111.4 4.2 %collective-permute-done.12.refs_7_ = bf16[384,512]{1,0:T(8,128)(2,1)} collective-permute-done((bf16[384,512]{1,0:T(8,128)(2,1)}, bf16[384,512]{1,0:T(8,128)(2,1)}, u32[]{:S(2)}, u32[]{:S(2)}) %collective-permute-start.12) | collective-permute-done | bytes 393248 | tf_op jit(solution)/shard_map/ppermute | solution.py:234
  115.6 1.0 collective-permute-done.7.refs_2_
  116.6 5.7 %collective-permute-done.10.refs_4_ = bf16[384,512]{1,0:T(8,128)(2,1)} collective-permute-done((bf16[384,512]{1,0:T(8,128)(2,1)S(1)}, bf16[384,512]{1,0:T(8,128)(2,1)}, u32[]{:S(2)}, u32[]{:S(2)}) %collective-permute-start.10) | collective-permute-done | bytes 393248 | tf_op jit(solution)/shard_map/ppermute | solution.py:234
  122.4 1.0 copy-done.5
  123.4 1.0 copy-done.6
  124.4 6.1 %shard_map.115.after_ref = bf16[2304,512]{1,0:T(8,128)(2,1)} custom-call(s32[24]{0:T(128)S(1)} %copy-done.10, bf16[24,128,128]{2,1,0:T(8,128)(2,1)S(1)} %bitcast.29, bf16[384,512]{1,0:T(8,128)(2,1)S(1)} %copy-done.5, bf16[384,512]{1,0:T(8,128)(2,1)S(1)} %copy-done.6, bf16[384,512]{1,0:T(8,128)(2,1)} %collective-permute-done.7.refs_2_, ...), custom_call_target="tpu_custom_call" | custom-call | flops 1811939328 | bytes 5000000 | tf_op jit(solution)/shard_map/pallas_call | solution.py:351
  130.4 8.3 %all-to-all-start.1 = ((bf16[32,72,512]{2,1,0:T(8,128)(2,1)}), bf16[32,72,512]{2,1,0:T(8,128)(2,1)S(1)}, u32[]{:S(2)}, u32[]{:S(2)}) async-start(bf16[32,72,512]{2,1,0:T(8,128)(2,1)} %bitcast.13), calls=%async_computation.1 | async-start | bytes 4718592 | tf_op jit(solution)/shard_map/all_to_all | solution.py:569
  138.8 1.1 copy-done.4
  139.9 0.7 shard_map.116
  140.6 0.4 collective-permute-start.13
  141.0 2.0 collective-permute-done.13.other_small_ref
  142.9 0.9 shard_map.117
  143.8 1.3 collective-permute-start.14
  145.1 3.0 %collective-permute-start.15 = (bf16[16,32,128]{2,1,0:T(8,128)(2,1)S(1)}, bf16[16,32,128]{2,1,0:T(8,128)(2,1)S(1)}, u32[]{:S(2)}, u32[]{:S(2)}) collective-permute-start(bf16[16,32,128]{2,1,0:T(8,128)(2,1)S(1)} %get-tuple-element.43), channel_id=1, source_target_pairs={{0,2},{1,3},{2,0},{3,1},{4,6},{5,7},{6,4},{7,5},{8,10},{9,11},{10,... | collective-permute-start | bytes 393224 | tf_op jit(solution)/shard_map/ppermute | solution.py:234
  148.1 0.9 collective-permute-start.16
  149.1 0.2 copy.18.place_ref
  149.2 1.7 collective-permute-done.14.refs_1_
  150.9 3.9 %collective-permute-done.15.refs_2_ = bf16[16,32,128]{2,1,0:T(8,128)(2,1)S(1)} collective-permute-done((bf16[16,32,128]{2,1,0:T(8,128)(2,1)S(1)}, bf16[16,32,128]{2,1,0:T(8,128)(2,1)S(1)}, u32[]{:S(2)}, u32[]{:S(2)}) %collective-permute-start.15) | collective-permute-done | bytes 131104 | tf_op jit(solution)/shard_map/ppermute | solution.py:234
  154.9 16.9 %all-to-all-done.1 = bf16[32,72,512]{2,1,0:T(8,128)(2,1)S(1)} async-done(((bf16[32,72,512]{2,1,0:T(8,128)(2,1)}), bf16[32,72,512]{2,1,0:T(8,128)(2,1)S(1)}, u32[]{:S(2)}, u32[]{:S(2)}) %all-to-all-start.1) | async-done | bytes 2359328 | tf_op jit(solution)/shard_map/all_to_all | solution.py:569
  171.8 2.3 shard_map.119.grad_ref
  174.1 0.1 collective-permute-start.17
  174.2 2.3 collective-permute-done.17.other_grad_ref
  176.5 6.0 %shard_map.120 = bf16[16,672,128]{2,1,0:T(8,128)(2,1)S(1)} custom-call(bf16[16,160,768]{2,1,0:T(8,128)(2,1)S(1)} %copy-done, bf16[16,160,768]{2,1,0:T(8,128)(2,1)} %collective-permute-done.6.other_ref, bf16[768,512]{1,0:T(8,128)(2,1)S(1)} %shard_map.119.grad_ref, bf16[768,512]{1,0:T(8,128)(2,1)S(1)} %collective-permute-done.17.other_grad_ref, ...), custom_call_target="tpu_custom_call" | custom-call | flops 2000000000 | bytes 12000000 | tf_op jit(solution)/shard_map/pallas_call | solution.py:489
  182.4 38.8 %all_to_all.15.parts_ref = bf16[16,672,128]{2,1,0:T(8,128)(2,1)S(1)} all-to-all(bf16[16,672,128]{2,1,0:T(8,128)(2,1)S(1)} %shard_map.120), channel_id=1, replica_groups=mesh['z'=4,'x'=4,'core'=2,'col'=4] {'z','x'}, dimensions={0} | all-to-all | bytes 5505024 | tf_op jit(solution)/shard_map/all_to_all | solution.py:615
  221.2 0.4 shard_map.121.refs_0_
  221.6 1.4 collective-permute-start.18
  223.0 3.0 %collective-permute-start.19 = (bf16[672,128]{1,0:T(8,128)(2,1)S(1)}, bf16[672,128]{1,0:T(8,128)(2,1)S(1)}, u32[]{:S(2)}, u32[]{:S(2)}) collective-permute-start(bf16[672,128]{1,0:T(8,128)(2,1)S(1)} %shard_map.121.refs_0_), channel_id=1, source_target_pairs={{0,2},{1,3},{2,0},{3,1},{4,6},{5,7},{6,4},{7,5},{8,10},{9,11},{10,... | collective-permute-start | bytes 516104 | tf_op jit(solution)/shard_map/ppermute | solution.py:618
  226.0 0.4 collective-permute-start.20
  226.4 2.6 %collective-permute-done.18.refs_1_ = bf16[672,128]{1,0:T(8,128)(2,1)S(1)} collective-permute-done((bf16[672,128]{1,0:T(8,128)(2,1)S(1)}, bf16[672,128]{1,0:T(8,128)(2,1)S(1)}, u32[]{:S(2)}, u32[]{:S(2)}) %collective-permute-start.18) | collective-permute-done | bytes 172064 | tf_op jit(solution)/shard_map/ppermute | solution.py:618
  229.0 4.4 %collective-permute-done.19.refs_2_ = bf16[672,128]{1,0:T(8,128)(2,1)S(1)} collective-permute-done((bf16[672,128]{1,0:T(8,128)(2,1)S(1)}, bf16[672,128]{1,0:T(8,128)(2,1)S(1)}, u32[]{:S(2)}, u32[]{:S(2)}) %collective-permute-start.19) | collective-permute-done | bytes 172064 | tf_op jit(solution)/shard_map/ppermute | solution.py:618
  233.3 2.2 collective-permute-done.20.refs_3_
  235.6 0.9 shard_map.122
  (47 shorter events, 0.3 us)
Async XLA Ops:
  17.4 8.4 %copy-start.11 = (s32[1,24576]{1,0:T(1,128)S(1)}, s32[1,24576]{1,0:T(1,128)}, u32[]{:S(2)}) copy-start(s32[1,24576]{1,0:T(1,128)} %owner_ref.1) | copy-start | bytes 294916
  17.5 41.5 %all-to-all-start = ((bf16[32,72,512]{2,1,0:T(8,128)(2,1)}), bf16[32,72,512]{2,1,0:T(8,128)(2,1)S(1)}, u32[]{:S(2)}, u32[]{:S(2)}) async-start(bf16[32,72,512]{2,1,0:T(8,128)(2,1)} %bitcast.40), calls=%async_computation | async-start | bytes 4718592 | tf_op jit(solution)/shard_map/all_to_all | solution.py:569
  26.5 13.0 %copy-start.18 = (s32[32,72]{1,0:T(8,128)}, s32[32,72]{1,0:T(8,128)S(1)}, u32[]{:S(2)}) copy-start(s32[32,72]{1,0:T(8,128)S(1)} %add_select_fusion) | copy-start | bytes 27652
  58.9 18.9 %copy-start.20 = (s32[1,24]{1,0:T(1,128)S(1)}, s32[1,24]{1,0:T(1,128)}, u32[]{:S(2)}) copy-start(s32[1,24]{1,0:T(1,128)} %param.12) | copy-start | bytes 292
  61.2 28.1 %copy-start.7 = (bf16[384,512]{1,0:T(8,128)(2,1)}, bf16[384,512]{1,0:T(8,128)(2,1)S(1)}, u32[]{:S(2)}) copy-start(bf16[384,512]{1,0:T(8,128)(2,1)S(1)} %get-tuple-element.29.refs_0_) | copy-start | bytes 1179652
  61.2 28.1 %copy-start.8 = (bf16[384,512]{1,0:T(8,128)(2,1)}, bf16[384,512]{1,0:T(8,128)(2,1)S(1)}, u32[]{:S(2)}) copy-start(bf16[384,512]{1,0:T(8,128)(2,1)S(1)} %get-tuple-element.30.refs_1_) | copy-start | bytes 1179652
  61.2 13.3 %collective-permute-start.2 = (bf16[384,512]{1,0:T(8,128)(2,1)S(1)}, bf16[384,512]{1,0:T(8,128)(2,1)S(1)}, u32[]{:S(2)}, u32[]{:S(2)}) collective-permute-start(bf16[384,512]{1,0:T(8,128)(2,1)S(1)} %get-tuple-element.29.refs_0_), channel_id=1, source_target_pairs={{0,1},{1,2},{2,3},{3,0},{4,5},{5,6},{6,7},{7,4},{8,9},{9,10},{10,1... | collective-permute-start | bytes 1179656 | tf_op jit(solution)/shard_map/ppermute | solution.py:234
  62.9 12.1 %collective-permute-start.1 = (bf16[384,512]{1,0:T(8,128)(2,1)S(1)}, bf16[384,512]{1,0:T(8,128)(2,1)S(1)}, u32[]{:S(2)}, u32[]{:S(2)}) collective-permute-start(bf16[384,512]{1,0:T(8,128)(2,1)S(1)} %get-tuple-element.30.refs_1_), channel_id=1, source_target_pairs={{0,3},{1,0},{2,1},{3,2},{4,7},{5,4},{6,5},{7,6},{8,11},{9,8},{10,9... | collective-permute-start | bytes 1179656 | tf_op jit(solution)/shard_map/ppermute | solution.py:234
  64.5 18.8 %collective-permute-start = (bf16[384,512]{1,0:T(8,128)(2,1)S(1)}, bf16[384,512]{1,0:T(8,128)(2,1)S(1)}, u32[]{:S(2)}, u32[]{:S(2)}) collective-permute-start(bf16[384,512]{1,0:T(8,128)(2,1)S(1)} %get-tuple-element.29.refs_0_), channel_id=1, source_target_pairs={{0,3},{1,0},{2,1},{3,2},{4,7},{5,4},{6,5},{7,6},{8,11},{9,8},{10,9... | collective-permute-start | bytes 1179656 | tf_op jit(solution)/shard_map/ppermute | solution.py:234
  66.3 17.0 %collective-permute-start.5 = (bf16[384,512]{1,0:T(8,128)(2,1)S(1)}, bf16[384,512]{1,0:T(8,128)(2,1)S(1)}, u32[]{:S(2)}, u32[]{:S(2)}) collective-permute-start(bf16[384,512]{1,0:T(8,128)(2,1)S(1)} %get-tuple-element.30.refs_1_), channel_id=1, source_target_pairs={{0,1},{1,2},{2,3},{3,0},{4,5},{5,6},{6,7},{7,4},{8,9},{9,10},{10,1... | collective-permute-start | bytes 1179656 | tf_op jit(solution)/shard_map/ppermute | solution.py:234
  74.5 14.8 %copy-start.12 = (bf16[384,512]{1,0:T(8,128)(2,1)}, bf16[384,512]{1,0:T(8,128)(2,1)S(1)}, u32[]{:S(2)}) copy-start(bf16[384,512]{1,0:T(8,128)(2,1)S(1)} %collective-permute-done.2.refs_6_) | copy-start | bytes 1179652
  74.6 13.8 %collective-permute-start.3 = (bf16[384,512]{1,0:T(8,128)(2,1)S(1)}, bf16[384,512]{1,0:T(8,128)(2,1)S(1)}, u32[]{:S(2)}, u32[]{:S(2)}) collective-permute-start(bf16[384,512]{1,0:T(8,128)(2,1)S(1)} %collective-permute-done.2.refs_6_), channel_id=1, source_target_pairs={{0,1},{1,2},{2,3},{3,0},{4,5},{5,6},{6,7},{7,4},{8,9},{9,10},{10,1... | collective-permute-start | bytes 1179656 | tf_op jit(solution)/shard_map/ppermute | solution.py:234
  74.9 14.4 %copy-start.13 = (bf16[384,512]{1,0:T(8,128)(2,1)}, bf16[384,512]{1,0:T(8,128)(2,1)S(1)}, u32[]{:S(2)}) copy-start(bf16[384,512]{1,0:T(8,128)(2,1)S(1)} %collective-permute-done.1.refs_3_) | copy-start | bytes 1179652
  74.9 13.5 %collective-permute-start.4 = (bf16[384,512]{1,0:T(8,128)(2,1)S(1)}, bf16[384,512]{1,0:T(8,128)(2,1)S(1)}, u32[]{:S(2)}, u32[]{:S(2)}) collective-permute-start(bf16[384,512]{1,0:T(8,128)(2,1)S(1)} %collective-permute-done.1.refs_3_), channel_id=1, source_target_pairs={{0,3},{1,0},{2,1},{3,2},{4,7},{5,4},{6,5},{7,6},{8,11},{9,8},{10,9... | collective-permute-start | bytes 1179656 | tf_op jit(solution)/shard_map/ppermute | solution.py:234
  83.3 5.1 %copy-start.14 = (bf16[384,512]{1,0:T(8,128)(2,1)}, bf16[384,512]{1,0:T(8,128)(2,1)S(1)}, u32[]{:S(2)}) copy-start(bf16[384,512]{1,0:T(8,128)(2,1)S(1)} %collective-permute-done.refs_2_) | copy-start | bytes 1179652
  83.4 5.1 %copy-start.15 = (bf16[384,512]{1,0:T(8,128)(2,1)}, bf16[384,512]{1,0:T(8,128)(2,1)S(1)}, u32[]{:S(2)}) copy-start(bf16[384,512]{1,0:T(8,128)(2,1)S(1)} %collective-permute-done.5.refs_7_) | copy-start | bytes 1179652
  88.4 0.8 copy-start.16
  88.4 0.9 copy-start.17
  89.3 33.0 %copy-start.1 = (bf16[1,24,128,128]{3,2,1,0:T(8,128)(2,1)S(1)}, bf16[1,24,128,128]{3,2,1,0:T(8,128)(2,1)}, u32[]{:S(2)}) copy-start(bf16[1,24,128,128]{3,2,1,0:T(8,128)(2,1)} %param.11) | copy-start | bytes 2359300
  89.4 33.0 %copy-start.2 = (bf16[768,512]{1,0:T(8,128)(2,1)S(1)}, bf16[768,512]{1,0:T(8,128)(2,1)}, u32[]{:S(2)}) copy-start(bf16[768,512]{1,0:T(8,128)(2,1)} %refs_8_.3) | copy-start | bytes 2359300
  89.4 33.0 %copy-start.10 = (s32[24]{0:T(128)S(1)}, s32[24]{0:T(128)}, u32[]{:S(2)}) copy-start(s32[24]{0:T(128)} %fusion.2.index_ref) | copy-start | bytes 292
  95.8 11.3 %collective-permute-start.9 = (bf16[384,512]{1,0:T(8,128)(2,1)}, bf16[384,512]{1,0:T(8,128)(2,1)S(1)}, u32[]{:S(2)}, u32[]{:S(2)}) collective-permute-start(bf16[384,512]{1,0:T(8,128)(2,1)} %get-tuple-element.34.refs_0_), channel_id=1, source_target_pairs={{0,1},{1,2},{2,3},{3,0},{4,5},{5,6},{6,7},{7,4},{8,9},{9,10},{10,1... | collective-permute-start | bytes 1179656 | tf_op jit(solution)/shard_map/ppermute | solution.py:234
  97.3 10.8 %collective-permute-start.8 = (bf16[384,512]{1,0:T(8,128)(2,1)}, bf16[384,512]{1,0:T(8,128)(2,1)S(1)}, u32[]{:S(2)}, u32[]{:S(2)}) collective-permute-start(bf16[384,512]{1,0:T(8,128)(2,1)} %get-tuple-element.35.refs_1_), channel_id=1, source_target_pairs={{0,3},{1,0},{2,1},{3,2},{4,7},{5,4},{6,5},{7,6},{8,11},{9,8},{10,9... | collective-permute-start | bytes 1179656 | tf_op jit(solution)/shard_map/ppermute | solution.py:234
  99.1 75.1 %collective-permute-start.6 = (bf16[16,160,768]{2,1,0:T(8,128)(2,1)}, bf16[16,160,768]{2,1,0:T(8,128)(2,1)}, u32[]{:S(2)}, u32[]{:S(2)}) collective-permute-start(bf16[16,160,768]{2,1,0:T(8,128)(2,1)} %get-tuple-element.33), channel_id=1, source_target_pairs={{0,4},{4,0},{1,5},{5,1},{2,6},{6,2},{3,7},{7,3},{8,12},{12,8},{9,1... | collective-permute-start | bytes 11796488 | tf_op jit(solution)/shard_map/ppermute | solution.py:586
  99.1 16.5 %collective-permute-start.12 = (bf16[384,512]{1,0:T(8,128)(2,1)}, bf16[384,512]{1,0:T(8,128)(2,1)}, u32[]{:S(2)}, u32[]{:S(2)}) collective-permute-start(bf16[384,512]{1,0:T(8,128)(2,1)} %get-tuple-element.35.refs_1_), channel_id=1, source_target_pairs={{0,1},{1,2},{2,3},{3,0},{4,5},{5,6},{6,7},{7,4},{8,9},{9,10},{10,1... | collective-permute-start | bytes 1179656 | tf_op jit(solution)/shard_map/ppermute | solution.py:234
  99.3 17.3 %collective-permute-start.7 = (bf16[384,512]{1,0:T(8,128)(2,1)}, bf16[384,512]{1,0:T(8,128)(2,1)}, u32[]{:S(2)}, u32[]{:S(2)}) collective-permute-start(bf16[384,512]{1,0:T(8,128)(2,1)} %get-tuple-element.34.refs_0_), channel_id=1, source_target_pairs={{0,3},{1,0},{2,1},{3,2},{4,7},{5,4},{6,5},{7,6},{8,11},{9,8},{10,9... | collective-permute-start | bytes 1179656 | tf_op jit(solution)/shard_map/ppermute | solution.py:234
  107.1 15.3 %collective-permute-start.10 = (bf16[384,512]{1,0:T(8,128)(2,1)S(1)}, bf16[384,512]{1,0:T(8,128)(2,1)}, u32[]{:S(2)}, u32[]{:S(2)}) collective-permute-start(bf16[384,512]{1,0:T(8,128)(2,1)S(1)} %collective-permute-done.9.refs_6_), channel_id=1, source_target_pairs={{0,1},{1,2},{2,3},{3,0},{4,5},{5,6},{6,7},{7,4},{8,9},{9,10},{10,1... | collective-permute-start | bytes 1179656 | tf_op jit(solution)/shard_map/ppermute | solution.py:234
  108.1 14.2 %collective-permute-start.11 = (bf16[384,512]{1,0:T(8,128)(2,1)S(1)}, bf16[384,512]{1,0:T(8,128)(2,1)}, u32[]{:S(2)}, u32[]{:S(2)}) collective-permute-start(bf16[384,512]{1,0:T(8,128)(2,1)S(1)} %collective-permute-done.8.refs_3_), channel_id=1, source_target_pairs={{0,3},{1,0},{2,1},{3,2},{4,7},{5,4},{6,5},{7,6},{8,11},{9,8},{10,9... | collective-permute-start | bytes 1179656 | tf_op jit(solution)/shard_map/ppermute | solution.py:234
  122.4 1.0 copy-start.5
  123.4 1.0 copy-start.6
  130.4 8.3 %copy-start.3 = (bf16[768,512]{1,0:T(8,128)(2,1)S(1)}, bf16[768,512]{1,0:T(8,128)(2,1)}, u32[]{:S(2)}) copy-start(bf16[768,512]{1,0:T(8,128)(2,1)} %get-tuple-element.36.agg_ref) | copy-start | bytes 2359300
  130.4 8.3 %copy-start.9 = (f32[1,512]{1,0:T(1,128)S(1)}, f32[1,512]{1,0:T(1,128)}, u32[]{:S(2)}) copy-start(f32[1,512]{1,0:T(1,128)} %get-tuple-element.38.gate_ref) | copy-start | bytes 6148
  130.4 41.4 %all-to-all-start.1 = ((bf16[32,72,512]{2,1,0:T(8,128)(2,1)}), bf16[32,72,512]{2,1,0:T(8,128)(2,1)S(1)}, u32[]{:S(2)}, u32[]{:S(2)}) async-start(bf16[32,72,512]{2,1,0:T(8,128)(2,1)} %bitcast.13), calls=%async_computation.1 | async-start | bytes 4718592 | tf_op jit(solution)/shard_map/all_to_all | solution.py:569
  138.7 1.1 copy-start.4
  139.9 9.2 %copy-start.19 = (s32[1,768]{1,0:T(1,128)S(1)}, s32[1,768]{1,0:T(1,128)}, u32[]{:S(2)}) copy-start(s32[1,768]{1,0:T(1,128)} %get-tuple-element.26.refs_4_) | copy-start | bytes 9220
  140.6 2.4 %collective-permute-start.13 = (f32[16,24,512]{2,1,0:T(8,128)S(1)}, f32[16,24,512]{2,1,0:T(8,128)S(1)}, u32[]{:S(2)}, u32[]{:S(2)}) collective-permute-start(f32[16,24,512]{2,1,0:T(8,128)S(1)} %get-tuple-element.40), channel_id=1, source_target_pairs={{0,4},{4,0},{1,5},{5,1},{2,6},{6,2},{3,7},{7,3},{8,12},{12,8},{9,1... | collective-permute-start | bytes 2359304 | tf_op jit(solution)/shard_map/ppermute | solution.py:586
  143.8 7.1 %collective-permute-start.14 = (bf16[16,32,128]{2,1,0:T(8,128)(2,1)}, bf16[16,32,128]{2,1,0:T(8,128)(2,1)S(1)}, u32[]{:S(2)}, u32[]{:S(2)}) collective-permute-start(bf16[16,32,128]{2,1,0:T(8,128)(2,1)} %get-tuple-element.42), channel_id=1, source_target_pairs={{0,1},{1,2},{2,3},{3,0},{4,5},{5,6},{6,7},{7,4},{8,9},{9,10},{10,1... | collective-permute-start | bytes 393224 | tf_op jit(solution)/shard_map/ppermute | solution.py:234
  145.1 9.8 %collective-permute-start.15 = (bf16[16,32,128]{2,1,0:T(8,128)(2,1)S(1)}, bf16[16,32,128]{2,1,0:T(8,128)(2,1)S(1)}, u32[]{:S(2)}, u32[]{:S(2)}) collective-permute-start(bf16[16,32,128]{2,1,0:T(8,128)(2,1)S(1)} %get-tuple-element.43), channel_id=1, source_target_pairs={{0,2},{1,3},{2,0},{3,1},{4,6},{5,7},{6,4},{7,5},{8,10},{9,11},{10,... | collective-permute-start | bytes 393224 | tf_op jit(solution)/shard_map/ppermute | solution.py:234
  148.1 6.7 %collective-permute-start.16 = (bf16[16,32,128]{2,1,0:T(8,128)(2,1)S(1)}, bf16[16,32,128]{2,1,0:T(8,128)(2,1)S(1)}, u32[]{:S(2)}, u32[]{:S(2)}) collective-permute-start(bf16[16,32,128]{2,1,0:T(8,128)(2,1)S(1)} %get-tuple-element.44), channel_id=1, source_target_pairs={{0,3},{1,0},{2,1},{3,2},{4,7},{5,4},{6,5},{7,6},{8,11},{9,8},{10,9... | collective-permute-start | bytes 393224 | tf_op jit(solution)/shard_map/ppermute | solution.py:234
  171.8 4.6 %copy-start = (bf16[16,160,768]{2,1,0:T(8,128)(2,1)S(1)}, bf16[16,160,768]{2,1,0:T(8,128)(2,1)}, u32[]{:S(2)}) copy-start(bf16[16,160,768]{2,1,0:T(8,128)(2,1)} %get-tuple-element.32.mine_ref) | copy-start | bytes 11796484
  174.1 2.4 %collective-permute-start.17 = (bf16[768,512]{1,0:T(8,128)(2,1)S(1)}, bf16[768,512]{1,0:T(8,128)(2,1)S(1)}, u32[]{:S(2)}, u32[]{:S(2)}) collective-permute-start(bf16[768,512]{1,0:T(8,128)(2,1)S(1)} %shard_map.119.grad_ref), channel_id=1, source_target_pairs={{0,4},{4,0},{1,5},{5,1},{2,6},{6,2},{3,7},{7,3},{8,12},{12,8},{9,1... | collective-permute-start | bytes 2359304 | tf_op jit(solution)/shard_map/ppermute | solution.py:586
  221.6 7.4 %collective-permute-start.18 = (bf16[672,128]{1,0:T(8,128)(2,1)S(1)}, bf16[672,128]{1,0:T(8,128)(2,1)S(1)}, u32[]{:S(2)}, u32[]{:S(2)}) collective-permute-start(bf16[672,128]{1,0:T(8,128)(2,1)S(1)} %shard_map.121.refs_0_), channel_id=1, source_target_pairs={{0,1},{1,0},{2,3},{3,2},{4,5},{5,4},{6,7},{7,6},{8,9},{9,8},{10,11... | collective-permute-start | bytes 516104 | tf_op jit(solution)/shard_map/ppermute | solution.py:618
  223.0 10.4 %collective-permute-start.19 = (bf16[672,128]{1,0:T(8,128)(2,1)S(1)}, bf16[672,128]{1,0:T(8,128)(2,1)S(1)}, u32[]{:S(2)}, u32[]{:S(2)}) collective-permute-start(bf16[672,128]{1,0:T(8,128)(2,1)S(1)} %shard_map.121.refs_0_), channel_id=1, source_target_pairs={{0,2},{1,3},{2,0},{3,1},{4,6},{5,7},{6,4},{7,5},{8,10},{9,11},{10,... | collective-permute-start | bytes 516104 | tf_op jit(solution)/shard_map/ppermute | solution.py:618
  226.0 9.6 %collective-permute-start.20 = (bf16[672,128]{1,0:T(8,128)(2,1)S(1)}, bf16[672,128]{1,0:T(8,128)(2,1)S(1)}, u32[]{:S(2)}, u32[]{:S(2)}) collective-permute-start(bf16[672,128]{1,0:T(8,128)(2,1)S(1)} %shard_map.121.refs_0_), channel_id=1, source_target_pairs={{0,3},{1,2},{2,1},{3,0},{4,7},{5,6},{6,5},{7,4},{8,11},{9,10},{10,... | collective-permute-start | bytes 516104 | tf_op jit(solution)/shard_map/ppermute | solution.py:618

commit v7 on v6

--- a/solution.py
+++ b/solution.py
@@ -241,11 +241,16 @@
     return low, high, after_low, after_high, far_low, far_high, before_low, before_high
 
 
-def stage(parts, table):
+def stage(parts, table, sems):
     at = 0
-    for part in parts:
-        table[at:at + part.shape[0], :] = part[...]
-        at += part.shape[0]
+    loads = []
+    for i, part in enumerate(parts):
+        rows = part.shape[0]
+        loads.append(pltpu.make_async_copy(part, table.at[pl.ds(at, rows)], sems.at[i]))
+        loads[-1].start()
+        at += rows
+    for load in loads:
+        load.wait()
 
 
 def block_row(index_ref, values_ref, table, row, per_row):
@@ -259,12 +264,12 @@
 def layer_kernel(index_ref, values_ref, *refs):
     parts = refs[:8]
     (cot_ref, w_ref, gate_ref) = refs[8:11]
-    (side_out_ref, agg_ref, mgrad_ref, low_ref, high_ref, gpart_ref, table) = refs[11:]
+    (side_out_ref, agg_ref, mgrad_ref, low_ref, high_ref, gpart_ref, table, sems) = refs[11:]
     at = pl.program_id(0)
 
     @pl.when(at == 0)
     def _():
-        stage(parts, table)
+        stage(parts, table, sems)
 
     step = cot_ref.shape[0]
     nodes = step * pl.num_programs(0)
@@ -313,27 +318,27 @@
         layer_kernel,
         grid=(2,),
         in_specs=[pl.BlockSpec(memory_space=pltpu.SMEM), whole(*values.shape)]
-        + [whole(*part.shape) for part in parts]
+        + [pl.BlockSpec(memory_space=pl.ANY) for _ in parts]
         + [rows(width), whole(width, width), whole(1, width)],
         out_specs=[rows(width), rows(width), rows(width), whole(step, width), whole(step, width),
                    whole(1, width)],
         out_shape=[bf16(nodes, width), bf16(nodes, width), bf16(nodes, width), bf16(step, width),
                    bf16(step, width),
                    jax.ShapeDtypeStruct((1, width), F32)],
-        scratch_shapes=[pltpu.VMEM((4 * nodes, width), BF16)],
+        scratch_shapes=[pltpu.VMEM((4 * nodes, width), BF16), pltpu.SemaphoreType.DMA((8,))],
         compiler_params=params(),
         cost_estimate=cost(12e8, 8e6, nodes * width),
     )(index, values, *parts, cotangent, w_msg, gate)
 
 
 def back_kernel(index_ref, values_ref, *refs):
-    parts, (cot_ref, place_ref), (out_ref, table, grad) = refs[:8], refs[8:10], refs[-3:]
+    parts, (cot_ref, place_ref), (out_ref, table, grad, sems) = refs[:8], refs[8:10], refs[-4:]
     nodes = cot_ref.shape[0]
     per_row = values_ref.shape[0] * 128 // nodes
 
     @pl.when(pl.program_id(0) == 0)
     def _():
-        stage(parts, table)
+        stage(parts, table, sems)
         for row in range(nodes // 128):
             at = slice(row * 128, (row + 1) * 128)
             total = block_row(index_ref, values_ref, table, row, per_row)
@@ -352,11 +357,15 @@
         back_kernel,
         grid=(4,),
         in_specs=[pl.BlockSpec(memory_space=pltpu.SMEM), whole(*values.shape)]
-        + [whole(*part.shape) for part in parts]
+        + [pl.BlockSpec(memory_space=pltpu.HBM if i < 2 else pl.ANY) for i in range(len(parts))]
         + [whole(*cotangent.shape), pl.BlockSpec((step, 1), lambda i: (i, 0))],
         out_specs=pl.BlockSpec((step, wide), lambda i: (i, 0)),
         out_shape=bf16(slots, wide),
-        scratch_shapes=[pltpu.VMEM((4 * nodes, wide), BF16), pltpu.VMEM((nodes, wide), BF16)],
+        scratch_shapes=[
+            pltpu.VMEM((4 * nodes, wide), BF16),
+            pltpu.VMEM((nodes, wide), BF16),
+            pltpu.SemaphoreType.DMA((8,)),
+        ],
         compiler_params=params(40),
         cost_estimate=cost(2 * slots * nodes * wide, 5e6),
     )(index, values, *parts, cotangent, place)

time: 237 us -> 239 us (level)
  no operation moved by 1% of the time
where the time goes in v7:
time: 239 us; the launch traced here: 238 us
  waiting for transfers between devices  88.6 us (37%)
  Pallas kernels  57.3 us (24%)
  starting transfers between devices  45.3 us (19%)
  blocking collectives  38.8 us (16%)
  local copies, waits for them, and re-layouts  5.5 us (2%)
    ppermute x15, waiting for transfers between devices, shift(): return lax.ppermute(part, 'col', [(c, (c + by) % 4) for c in range(4)])  39.6 us
    all_to_all x1, blocking collectives, shards(): lax.all_to_all(down, ('z', 'x'), split_axis=0, concat_axis=0, tiled=True)  38.8 us
    all_to_all x2, waiting for transfers between devices, relay(): lax.all_to_all(rows.reshape(size, slots // size, width), ROWS, split_axis...  35.6 us
    ppermute x15, starting transfers between devices, shift(): return lax.ppermute(part, 'col', [(c, (c + by) % 4) for c in range(4)])  23.3 us
    pallas_call x1, Pallas kernels, pool_and_pack(): pl.pallas_call(pool_kernel, grid=(6,), in_specs=[whole(*owner_of.shape),...  16.8 us
    all_to_all x2, starting transfers between devices, relay(): lax.all_to_all(rows.reshape(size, slots // size, width), ROWS, split_axis...  16.7 us
    pallas_call x1, Pallas kernels, pool_and_turn(): pl.pallas_call(turn_kernel, grid=(6,), in_specs=streams(step, rows) + [pl...  12.9 us
    ppermute x3, waiting for transfers between devices, shards(): lax.ppermute(own, 'col', [(c, c ^ step) for c in range(4)])  9.18 us
  transfers between devices with their start and end apart: 23, of which 17 were waited for; matrix products, arithmetic and copies ran while one was open for 1% of the time, Pallas kernels for 10%

profile of v7, /device:TPU:0, one launch (start us, length us, event | category | flops | bytes accessed | tf_op | source)
XLA Modules:
  0.0 238.2 jit_solution(8572835113221385993)
XLA Ops:
  0.6 16.8 %shard_map.111 = (bf16[2304,512]{1,0:T(8,128)(2,1)}, s32[1,768]{1,0:T(1,128)}) custom-call(s32[1,24576]{1,0:T(1,128)} %owner_ref.1, bf16[768,80,128]{2,1,0:T(8,128)(2,1)} %bitcast.32, bf16[768,80,128]{2,1,0:T(8,128)(2,1)} %bitcast.33, bf16[768,80,128]{2,1,0:T(8,128)(2,1)} %bitcast.34, bf16[768,80,128]{2,1,0:T(8,128)(2,1)} %bitcast.35, bf16[5120,512]{1,0:T(8,128)(2,1)} %refs_4_.1), custom_call_target="tpu_custom_call" | custom-call | flops 8000000000 | bytes 23000000 | tf_op jit(solution)/shard_map/pallas_call | solution.py:151
  17.5 8.4 %all-to-all-start = ((bf16[32,72,512]{2,1,0:T(8,128)(2,1)}), bf16[32,72,512]{2,1,0:T(8,128)(2,1)S(1)}, u32[]{:S(2)}, u32[]{:S(2)}) async-start(bf16[32,72,512]{2,1,0:T(8,128)(2,1)} %bitcast.40), calls=%async_computation | async-start | bytes 4718592 | tf_op jit(solution)/shard_map/all_to_all | solution.py:578
  25.9 0.3 fusion
  26.2 0.1 reduce_sum.18
  26.3 0.1 select_reduce_fusion
  26.5 0.1 select_n.49
  26.6 12.9 %shard_map.112 = (bf16[16,160,768]{2,1,0:T(8,128)(2,1)}, bf16[16,160,768]{2,1,0:T(8,128)(2,1)}, s32[1,2304]{1,0:T(1,128)}) custom-call(bf16[768,80,128]{2,1,0:T(8,128)(2,1)} %bitcast.36, bf16[768,80,128]{2,1,0:T(8,128)(2,1)} %bitcast.37, bf16[768,80,128]{2,1,0:T(8,128)(2,1)} %bitcast.38, bf16[768,80,128]{2,1,0:T(8,128)(2,1)} %bitcast.39, ...), custom_call_target="tpu_custom_call" | custom-call | flops 2000000000 | bytes 24000000 | tf_op jit(solution)/shard_map/pallas_call | solution.py:178
  39.5 0.7 add.57.place_ref
  40.2 18.7 %all-to-all-done = bf16[32,72,512]{2,1,0:T(8,128)(2,1)S(1)} async-done(((bf16[32,72,512]{2,1,0:T(8,128)(2,1)}), bf16[32,72,512]{2,1,0:T(8,128)(2,1)S(1)}, u32[]{:S(2)}, u32[]{:S(2)}) %all-to-all-start) | async-done | bytes 2359328 | tf_op jit(solution)/shard_map/all_to_all | solution.py:578
  58.9 2.2 shard_map.113
  61.2 1.6 collective-permute-start.2
  62.9 1.7 collective-permute-start.1
  64.5 1.8 collective-permute-start
  66.3 0.2 collective-permute-start.5
  66.6 8.0 %collective-permute-done.2.refs_6_ = bf16[384,512]{1,0:T(8,128)(2,1)S(1)} collective-permute-done((bf16[384,512]{1,0:T(8,128)(2,1)S(1)}, bf16[384,512]{1,0:T(8,128)(2,1)S(1)}, u32[]{:S(2)}, u32[]{:S(2)}) %collective-permute-start.2) | collective-permute-done | bytes 393248 | tf_op jit(solution)/shard_map/ppermute | solution.py:234
  74.6 0.4 collective-permute-start.3
  74.9 2.9 %collective-permute-start.4 = (bf16[384,512]{1,0:T(8,128)(2,1)S(1)}, bf16[384,512]{1,0:T(8,128)(2,1)S(1)}, u32[]{:S(2)}, u32[]{:S(2)}) collective-permute-start(bf16[384,512]{1,0:T(8,128)(2,1)S(1)} %collective-permute-done.1.refs_3_), channel_id=1, source_target_pairs={{0,3},{1,0},{2,1},{3,2},{4,7},{5,4},{6,5},{7,6},{8,11},{9,8},{10,9... | collective-permute-start | bytes 1179656 | tf_op jit(solution)/shard_map/ppermute | solution.py:234
  77.8 0.5 fusion.2.index_ref
  78.3 5.0 %collective-permute-done.refs_2_ = bf16[384,512]{1,0:T(8,128)(2,1)S(1)} collective-permute-done((bf16[384,512]{1,0:T(8,128)(2,1)S(1)}, bf16[384,512]{1,0:T(8,128)(2,1)S(1)}, u32[]{:S(2)}, u32[]{:S(2)}) %collective-permute-start) | collective-permute-done | bytes 393248 | tf_op jit(solution)/shard_map/ppermute | solution.py:234
  83.4 5.0 %collective-permute-done.3.refs_4_ = bf16[384,512]{1,0:T(8,128)(2,1)S(1)} collective-permute-done((bf16[384,512]{1,0:T(8,128)(2,1)S(1)}, bf16[384,512]{1,0:T(8,128)(2,1)S(1)}, u32[]{:S(2)}, u32[]{:S(2)}) %collective-permute-start.3) | collective-permute-done | bytes 393248 | tf_op jit(solution)/shard_map/ppermute | solution.py:234
  88.4 0.7 copy-done.16
  89.1 0.2 copy-done.17
  89.4 7.2 %shard_map.114 = (bf16[768,512]{1,0:T(8,128)(2,1)}, bf16[768,512]{1,0:T(8,128)(2,1)}, bf16[768,512]{1,0:T(8,128)(2,1)}, bf16[384,512]{1,0:T(8,128)(2,1)}, bf16[384,512]{1,0:T(8,128)(2,1)}, /*index=5*/f32[1,512]{1,0:T(1,128)}) custom-call(s32[24]{0:T(128)} %fusion.2.index_ref, bf16[24,128,128]{2,1,0:T(8,128)(2,1)} %bitcast.28, bf16[384,512]{1,0:T(8,128)(2,1)} %copy-done.7, ...), custom_call_target="tpu_custom_call" | custom-call | flops 1200000000 | bytes 8000000 | tf_op jit(solution)/shard_map/pallas_call | solution.py:317
  96.6 1.5 collective-permute-start.9
  98.1 1.8 collective-permute-start.8
  99.9 0.2 collective-permute-start.12
  100.1 3.0 %collective-permute-start.7 = (bf16[384,512]{1,0:T(8,128)(2,1)}, bf16[384,512]{1,0:T(8,128)(2,1)}, u32[]{:S(2)}, u32[]{:S(2)}) collective-permute-start(bf16[384,512]{1,0:T(8,128)(2,1)} %get-tuple-element.34.refs_0_), channel_id=1, source_target_pairs={{0,3},{1,0},{2,1},{3,2},{4,7},{5,4},{6,5},{7,6},{8,11},{9,8},{10,9... | collective-permute-start | bytes 1179656 | tf_op jit(solution)/shard_map/ppermute | solution.py:234
  103.1 4.7 %collective-permute-done.9.refs_6_ = bf16[384,512]{1,0:T(8,128)(2,1)S(1)} collective-permute-done((bf16[384,512]{1,0:T(8,128)(2,1)}, bf16[384,512]{1,0:T(8,128)(2,1)S(1)}, u32[]{:S(2)}, u32[]{:S(2)}) %collective-permute-start.9) | collective-permute-done | bytes 393248 | tf_op jit(solution)/shard_map/ppermute | solution.py:234
  107.9 0.7 collective-permute-start.10
  108.6 0.3 collective-permute-done.8.refs_3_
  108.9 2.2 collective-permute-start.11
  111.1 1.1 select_n.51.refs_9_
  112.2 4.2 %collective-permute-done.12.refs_7_ = bf16[384,512]{1,0:T(8,128)(2,1)} collective-permute-done((bf16[384,512]{1,0:T(8,128)(2,1)}, bf16[384,512]{1,0:T(8,128)(2,1)}, u32[]{:S(2)}, u32[]{:S(2)}) %collective-permute-start.12) | collective-permute-done | bytes 393248 | tf_op jit(solution)/shard_map/ppermute | solution.py:234
  116.4 1.0 collective-permute-done.7.refs_2_
  117.4 5.7 %collective-permute-done.10.refs_4_ = bf16[384,512]{1,0:T(8,128)(2,1)} collective-permute-done((bf16[384,512]{1,0:T(8,128)(2,1)S(1)}, bf16[384,512]{1,0:T(8,128)(2,1)}, u32[]{:S(2)}, u32[]{:S(2)}) %collective-permute-start.10) | collective-permute-done | bytes 393248 | tf_op jit(solution)/shard_map/ppermute | solution.py:234
  123.2 1.0 copy-done.5
  124.1 1.0 copy-done.6
  125.1 7.0 %shard_map.115.after_ref = bf16[2304,512]{1,0:T(8,128)(2,1)} custom-call(s32[24]{0:T(128)S(1)} %copy-done.10, bf16[24,128,128]{2,1,0:T(8,128)(2,1)S(1)} %bitcast.29, bf16[384,512]{1,0:T(8,128)(2,1)S(1)} %copy-done.5, bf16[384,512]{1,0:T(8,128)(2,1)S(1)} %copy-done.6, bf16[384,512]{1,0:T(8,128)(2,1)} %collective-permute-done.7.refs_2_, ...), custom_call_target="tpu_custom_call" | custom-call | flops 1811939328 | bytes 5000000 | tf_op jit(solution)/shard_map/pallas_call | solution.py:356
  132.2 8.3 %all-to-all-start.1 = ((bf16[32,72,512]{2,1,0:T(8,128)(2,1)}), bf16[32,72,512]{2,1,0:T(8,128)(2,1)S(1)}, u32[]{:S(2)}, u32[]{:S(2)}) async-start(bf16[32,72,512]{2,1,0:T(8,128)(2,1)} %bitcast.13), calls=%async_computation.1 | async-start | bytes 4718592 | tf_op jit(solution)/shard_map/all_to_all | solution.py:578
  140.5 1.1 copy-done.4
  141.6 0.7 shard_map.116
  142.3 0.4 collective-permute-start.13
  142.7 2.0 collective-permute-done.13.other_small_ref
  144.7 0.9 shard_map.117
  145.5 1.3 collective-permute-start.14
  146.8 3.1 %collective-permute-start.15 = (bf16[16,32,128]{2,1,0:T(8,128)(2,1)S(1)}, bf16[16,32,128]{2,1,0:T(8,128)(2,1)S(1)}, u32[]{:S(2)}, u32[]{:S(2)}) collective-permute-start(bf16[16,32,128]{2,1,0:T(8,128)(2,1)S(1)} %get-tuple-element.43), channel_id=1, source_target_pairs={{0,2},{1,3},{2,0},{3,1},{4,6},{5,7},{6,4},{7,5},{8,10},{9,11},{10,... | collective-permute-start | bytes 393224 | tf_op jit(solution)/shard_map/ppermute | solution.py:234
  149.9 0.9 collective-permute-start.16
  150.8 0.2 copy.18.place_ref
  151.0 1.7 collective-permute-done.14.refs_1_
  152.7 3.9 %collective-permute-done.15.refs_2_ = bf16[16,32,128]{2,1,0:T(8,128)(2,1)S(1)} collective-permute-done((bf16[16,32,128]{2,1,0:T(8,128)(2,1)S(1)}, bf16[16,32,128]{2,1,0:T(8,128)(2,1)S(1)}, u32[]{:S(2)}, u32[]{:S(2)}) %collective-permute-start.15) | collective-permute-done | bytes 131104 | tf_op jit(solution)/shard_map/ppermute | solution.py:234
  156.7 16.9 %all-to-all-done.1 = bf16[32,72,512]{2,1,0:T(8,128)(2,1)S(1)} async-done(((bf16[32,72,512]{2,1,0:T(8,128)(2,1)}), bf16[32,72,512]{2,1,0:T(8,128)(2,1)S(1)}, u32[]{:S(2)}, u32[]{:S(2)}) %all-to-all-start.1) | async-done | bytes 2359328 | tf_op jit(solution)/shard_map/all_to_all | solution.py:578
  173.6 2.3 shard_map.119.grad_ref
  175.9 0.1 collective-permute-start.17
  176.0 2.3 collective-permute-done.17.other_grad_ref
  178.2 6.0 %shard_map.120 = bf16[16,672,128]{2,1,0:T(8,128)(2,1)S(1)} custom-call(bf16[16,160,768]{2,1,0:T(8,128)(2,1)S(1)} %copy-done, bf16[16,160,768]{2,1,0:T(8,128)(2,1)} %collective-permute-done.6.other_ref, bf16[768,512]{1,0:T(8,128)(2,1)S(1)} %shard_map.119.grad_ref, bf16[768,512]{1,0:T(8,128)(2,1)S(1)} %collective-permute-done.17.other_grad_ref, ...), custom_call_target="tpu_custom_call" | custom-call | flops 2000000000 | bytes 12000000 | tf_op jit(solution)/shard_map/pallas_call | solution.py:498
  184.2 38.8 %all_to_all.15.parts_ref = bf16[16,672,128]{2,1,0:T(8,128)(2,1)S(1)} all-to-all(bf16[16,672,128]{2,1,0:T(8,128)(2,1)S(1)} %shard_map.120), channel_id=1, replica_groups=mesh['z'=4,'x'=4,'core'=2,'col'=4] {'z','x'}, dimensions={0} | all-to-all | bytes 5505024 | tf_op jit(solution)/shard_map/all_to_all | solution.py:624
  223.0 0.4 shard_map.121.refs_0_
  223.3 1.4 collective-permute-start.18
  224.7 3.0 %collective-permute-start.19 = (bf16[672,128]{1,0:T(8,128)(2,1)S(1)}, bf16[672,128]{1,0:T(8,128)(2,1)S(1)}, u32[]{:S(2)}, u32[]{:S(2)}) collective-permute-start(bf16[672,128]{1,0:T(8,128)(2,1)S(1)} %shard_map.121.refs_0_), channel_id=1, source_target_pairs={{0,2},{1,3},{2,0},{3,1},{4,6},{5,7},{6,4},{7,5},{8,10},{9,11},{10,... | collective-permute-start | bytes 516104 | tf_op jit(solution)/shard_map/ppermute | solution.py:627
  227.7 0.4 collective-permute-start.20
  228.1 2.6 %collective-permute-done.18.refs_1_ = bf16[672,128]{1,0:T(8,128)(2,1)S(1)} collective-permute-done((bf16[672,128]{1,0:T(8,128)(2,1)S(1)}, bf16[672,128]{1,0:T(8,128)(2,1)S(1)}, u32[]{:S(2)}, u32[]{:S(2)}) %collective-permute-start.18) | collective-permute-done | bytes 172064 | tf_op jit(solution)/shard_map/ppermute | solution.py:627
  230.7 4.4 %collective-permute-done.19.refs_2_ = bf16[672,128]{1,0:T(8,128)(2,1)S(1)} collective-permute-done((bf16[672,128]{1,0:T(8,128)(2,1)S(1)}, bf16[672,128]{1,0:T(8,128)(2,1)S(1)}, u32[]{:S(2)}, u32[]{:S(2)}) %collective-permute-start.19) | collective-permute-done | bytes 172064 | tf_op jit(solution)/shard_map/ppermute | solution.py:627
  235.1 2.2 collective-permute-done.20.refs_3_
  237.3 0.9 shard_map.122
  (47 shorter events, 0.3 us)
Async XLA Ops:
  17.4 8.4 %copy-start.11 = (s32[1,24576]{1,0:T(1,128)S(1)}, s32[1,24576]{1,0:T(1,128)}, u32[]{:S(2)}) copy-start(s32[1,24576]{1,0:T(1,128)} %owner_ref.1) | copy-start | bytes 294916
  17.5 41.5 %all-to-all-start = ((bf16[32,72,512]{2,1,0:T(8,128)(2,1)}), bf16[32,72,512]{2,1,0:T(8,128)(2,1)S(1)}, u32[]{:S(2)}, u32[]{:S(2)}) async-start(bf16[32,72,512]{2,1,0:T(8,128)(2,1)} %bitcast.40), calls=%async_computation | async-start | bytes 4718592 | tf_op jit(solution)/shard_map/all_to_all | solution.py:578
  26.5 13.0 %copy-start.18 = (s32[32,72]{1,0:T(8,128)}, s32[32,72]{1,0:T(8,128)S(1)}, u32[]{:S(2)}) copy-start(s32[32,72]{1,0:T(8,128)S(1)} %add_select_fusion) | copy-start | bytes 27652
  58.9 18.9 %copy-start.20 = (s32[1,24]{1,0:T(1,128)S(1)}, s32[1,24]{1,0:T(1,128)}, u32[]{:S(2)}) copy-start(s32[1,24]{1,0:T(1,128)} %param.12) | copy-start | bytes 292
  61.2 28.1 %copy-start.7 = (bf16[384,512]{1,0:T(8,128)(2,1)}, bf16[384,512]{1,0:T(8,128)(2,1)S(1)}, u32[]{:S(2)}) copy-start(bf16[384,512]{1,0:T(8,128)(2,1)S(1)} %get-tuple-element.29.refs_0_) | copy-start | bytes 1179652
  61.2 28.1 %copy-start.8 = (bf16[384,512]{1,0:T(8,128)(2,1)}, bf16[384,512]{1,0:T(8,128)(2,1)S(1)}, u32[]{:S(2)}) copy-start(bf16[384,512]{1,0:T(8,128)(2,1)S(1)} %get-tuple-element.30.refs_1_) | copy-start | bytes 1179652
  61.2 13.3 %collective-permute-start.2 = (bf16[384,512]{1,0:T(8,128)(2,1)S(1)}, bf16[384,512]{1,0:T(8,128)(2,1)S(1)}, u32[]{:S(2)}, u32[]{:S(2)}) collective-permute-start(bf16[384,512]{1,0:T(8,128)(2,1)S(1)} %get-tuple-element.29.refs_0_), channel_id=1, source_target_pairs={{0,1},{1,2},{2,3},{3,0},{4,5},{5,6},{6,7},{7,4},{8,9},{9,10},{10,1... | collective-permute-start | bytes 1179656 | tf_op jit(solution)/shard_map/ppermute | solution.py:234
  62.9 12.1 %collective-permute-start.1 = (bf16[384,512]{1,0:T(8,128)(2,1)S(1)}, bf16[384,512]{1,0:T(8,128)(2,1)S(1)}, u32[]{:S(2)}, u32[]{:S(2)}) collective-permute-start(bf16[384,512]{1,0:T(8,128)(2,1)S(1)} %get-tuple-element.30.refs_1_), channel_id=1, source_target_pairs={{0,3},{1,0},{2,1},{3,2},{4,7},{5,4},{6,5},{7,6},{8,11},{9,8},{10,9... | collective-permute-start | bytes 1179656 | tf_op jit(solution)/shard_map/ppermute | solution.py:234
  64.5 18.8 %collective-permute-start = (bf16[384,512]{1,0:T(8,128)(2,1)S(1)}, bf16[384,512]{1,0:T(8,128)(2,1)S(1)}, u32[]{:S(2)}, u32[]{:S(2)}) collective-permute-start(bf16[384,512]{1,0:T(8,128)(2,1)S(1)} %get-tuple-element.29.refs_0_), channel_id=1, source_target_pairs={{0,3},{1,0},{2,1},{3,2},{4,7},{5,4},{6,5},{7,6},{8,11},{9,8},{10,9... | collective-permute-start | bytes 1179656 | tf_op jit(solution)/shard_map/ppermute | solution.py:234
  66.3 17.0 %collective-permute-start.5 = (bf16[384,512]{1,0:T(8,128)(2,1)S(1)}, bf16[384,512]{1,0:T(8,128)(2,1)S(1)}, u32[]{:S(2)}, u32[]{:S(2)}) collective-permute-start(bf16[384,512]{1,0:T(8,128)(2,1)S(1)} %get-tuple-element.30.refs_1_), channel_id=1, source_target_pairs={{0,1},{1,2},{2,3},{3,0},{4,5},{5,6},{6,7},{7,4},{8,9},{9,10},{10,1... | collective-permute-start | bytes 1179656 | tf_op jit(solution)/shard_map/ppermute | solution.py:234
  74.5 14.8 %copy-start.12 = (bf16[384,512]{1,0:T(8,128)(2,1)}, bf16[384,512]{1,0:T(8,128)(2,1)S(1)}, u32[]{:S(2)}) copy-start(bf16[384,512]{1,0:T(8,128)(2,1)S(1)} %collective-permute-done.2.refs_6_) | copy-start | bytes 1179652
  74.6 13.8 %collective-permute-start.3 = (bf16[384,512]{1,0:T(8,128)(2,1)S(1)}, bf16[384,512]{1,0:T(8,128)(2,1)S(1)}, u32[]{:S(2)}, u32[]{:S(2)}) collective-permute-start(bf16[384,512]{1,0:T(8,128)(2,1)S(1)} %collective-permute-done.2.refs_6_), channel_id=1, source_target_pairs={{0,1},{1,2},{2,3},{3,0},{4,5},{5,6},{6,7},{7,4},{8,9},{9,10},{10,1... | collective-permute-start | bytes 1179656 | tf_op jit(solution)/shard_map/ppermute | solution.py:234
  74.9 14.4 %copy-start.13 = (bf16[384,512]{1,0:T(8,128)(2,1)}, bf16[384,512]{1,0:T(8,128)(2,1)S(1)}, u32[]{:S(2)}) copy-start(bf16[384,512]{1,0:T(8,128)(2,1)S(1)} %collective-permute-done.1.refs_3_) | copy-start | bytes 1179652
  74.9 13.5 %collective-permute-start.4 = (bf16[384,512]{1,0:T(8,128)(2,1)S(1)}, bf16[384,512]{1,0:T(8,128)(2,1)S(1)}, u32[]{:S(2)}, u32[]{:S(2)}) collective-permute-start(bf16[384,512]{1,0:T(8,128)(2,1)S(1)} %collective-permute-done.1.refs_3_), channel_id=1, source_target_pairs={{0,3},{1,0},{2,1},{3,2},{4,7},{5,4},{6,5},{7,6},{8,11},{9,8},{10,9... | collective-permute-start | bytes 1179656 | tf_op jit(solution)/shard_map/ppermute | solution.py:234
  83.3 5.1 %copy-start.14 = (bf16[384,512]{1,0:T(8,128)(2,1)}, bf16[384,512]{1,0:T(8,128)(2,1)S(1)}, u32[]{:S(2)}) copy-start(bf16[384,512]{1,0:T(8,128)(2,1)S(1)} %collective-permute-done.refs_2_) | copy-start | bytes 1179652
  83.4 5.1 %copy-start.15 = (bf16[384,512]{1,0:T(8,128)(2,1)}, bf16[384,512]{1,0:T(8,128)(2,1)S(1)}, u32[]{:S(2)}) copy-start(bf16[384,512]{1,0:T(8,128)(2,1)S(1)} %collective-permute-done.5.refs_7_) | copy-start | bytes 1179652
  88.4 0.8 copy-start.16
  88.4 0.9 copy-start.17
  89.3 33.8 %copy-start.1 = (bf16[1,24,128,128]{3,2,1,0:T(8,128)(2,1)S(1)}, bf16[1,24,128,128]{3,2,1,0:T(8,128)(2,1)}, u32[]{:S(2)}) copy-start(bf16[1,24,128,128]{3,2,1,0:T(8,128)(2,1)} %param.11) | copy-start | bytes 2359300
  89.4 33.8 %copy-start.2 = (bf16[768,512]{1,0:T(8,128)(2,1)S(1)}, bf16[768,512]{1,0:T(8,128)(2,1)}, u32[]{:S(2)}) copy-start(bf16[768,512]{1,0:T(8,128)(2,1)} %refs_8_.3) | copy-start | bytes 2359300
  89.4 33.8 %copy-start.10 = (s32[24]{0:T(128)S(1)}, s32[24]{0:T(128)}, u32[]{:S(2)}) copy-start(s32[24]{0:T(128)} %fusion.2.index_ref) | copy-start | bytes 292
  96.6 11.3 %collective-permute-start.9 = (bf16[384,512]{1,0:T(8,128)(2,1)}, bf16[384,512]{1,0:T(8,128)(2,1)S(1)}, u32[]{:S(2)}, u32[]{:S(2)}) collective-permute-start(bf16[384,512]{1,0:T(8,128)(2,1)} %get-tuple-element.34.refs_0_), channel_id=1, source_target_pairs={{0,1},{1,2},{2,3},{3,0},{4,5},{5,6},{6,7},{7,4},{8,9},{9,10},{10,1... | collective-permute-start | bytes 1179656 | tf_op jit(solution)/shard_map/ppermute | solution.py:234
  98.1 10.8 %collective-permute-start.8 = (bf16[384,512]{1,0:T(8,128)(2,1)}, bf16[384,512]{1,0:T(8,128)(2,1)S(1)}, u32[]{:S(2)}, u32[]{:S(2)}) collective-permute-start(bf16[384,512]{1,0:T(8,128)(2,1)} %get-tuple-element.35.refs_1_), channel_id=1, source_target_pairs={{0,3},{1,0},{2,1},{3,2},{4,7},{5,4},{6,5},{7,6},{8,11},{9,8},{10,9... | collective-permute-start | bytes 1179656 | tf_op jit(solution)/shard_map/ppermute | solution.py:234
  99.9 76.1 %collective-permute-start.6 = (bf16[16,160,768]{2,1,0:T(8,128)(2,1)}, bf16[16,160,768]{2,1,0:T(8,128)(2,1)}, u32[]{:S(2)}, u32[]{:S(2)}) collective-permute-start(bf16[16,160,768]{2,1,0:T(8,128)(2,1)} %get-tuple-element.33), channel_id=1, source_target_pairs={{0,4},{4,0},{1,5},{5,1},{2,6},{6,2},{3,7},{7,3},{8,12},{12,8},{9,1... | collective-permute-start | bytes 11796488 | tf_op jit(solution)/shard_map/ppermute | solution.py:595
  99.9 16.5 %collective-permute-start.12 = (bf16[384,512]{1,0:T(8,128)(2,1)}, bf16[384,512]{1,0:T(8,128)(2,1)}, u32[]{:S(2)}, u32[]{:S(2)}) collective-permute-start(bf16[384,512]{1,0:T(8,128)(2,1)} %get-tuple-element.35.refs_1_), channel_id=1, source_target_pairs={{0,1},{1,2},{2,3},{3,0},{4,5},{5,6},{6,7},{7,4},{8,9},{9,10},{10,1... | collective-permute-start | bytes 1179656 | tf_op jit(solution)/shard_map/ppermute | solution.py:234
  100.1 17.3 %collective-permute-start.7 = (bf16[384,512]{1,0:T(8,128)(2,1)}, bf16[384,512]{1,0:T(8,128)(2,1)}, u32[]{:S(2)}, u32[]{:S(2)}) collective-permute-start(bf16[384,512]{1,0:T(8,128)(2,1)} %get-tuple-element.34.refs_0_), channel_id=1, source_target_pairs={{0,3},{1,0},{2,1},{3,2},{4,7},{5,4},{6,5},{7,6},{8,11},{9,8},{10,9... | collective-permute-start | bytes 1179656 | tf_op jit(solution)/shard_map/ppermute | solution.py:234
  107.9 15.3 %collective-permute-start.10 = (bf16[384,512]{1,0:T(8,128)(2,1)S(1)}, bf16[384,512]{1,0:T(8,128)(2,1)}, u32[]{:S(2)}, u32[]{:S(2)}) collective-permute-start(bf16[384,512]{1,0:T(8,128)(2,1)S(1)} %collective-permute-done.9.refs_6_), channel_id=1, source_target_pairs={{0,1},{1,2},{2,3},{3,0},{4,5},{5,6},{6,7},{7,4},{8,9},{9,10},{10,1... | collective-permute-start | bytes 1179656 | tf_op jit(solution)/shard_map/ppermute | solution.py:234
  108.9 14.3 %collective-permute-start.11 = (bf16[384,512]{1,0:T(8,128)(2,1)S(1)}, bf16[384,512]{1,0:T(8,128)(2,1)}, u32[]{:S(2)}, u32[]{:S(2)}) collective-permute-start(bf16[384,512]{1,0:T(8,128)(2,1)S(1)} %collective-permute-done.8.refs_3_), channel_id=1, source_target_pairs={{0,3},{1,0},{2,1},{3,2},{4,7},{5,4},{6,5},{7,6},{8,11},{9,8},{10,9... | collective-permute-start | bytes 1179656 | tf_op jit(solution)/shard_map/ppermute | solution.py:234
  123.1 1.0 copy-start.5
  124.1 1.0 copy-start.6
  132.1 8.3 %copy-start.3 = (bf16[768,512]{1,0:T(8,128)(2,1)S(1)}, bf16[768,512]{1,0:T(8,128)(2,1)}, u32[]{:S(2)}) copy-start(bf16[768,512]{1,0:T(8,128)(2,1)} %get-tuple-element.36.agg_ref) | copy-start | bytes 2359300
  132.2 8.3 %copy-start.9 = (f32[1,512]{1,0:T(1,128)S(1)}, f32[1,512]{1,0:T(1,128)}, u32[]{:S(2)}) copy-start(f32[1,512]{1,0:T(1,128)} %get-tuple-element.38.gate_ref) | copy-start | bytes 6148
  132.2 41.4 %all-to-all-start.1 = ((bf16[32,72,512]{2,1,0:T(8,128)(2,1)}), bf16[32,72,512]{2,1,0:T(8,128)(2,1)S(1)}, u32[]{:S(2)}, u32[]{:S(2)}) async-start(bf16[32,72,512]{2,1,0:T(8,128)(2,1)} %bitcast.13), calls=%async_computation.1 | async-start | bytes 4718592 | tf_op jit(solution)/shard_map/all_to_all | solution.py:578
  140.5 1.1 copy-start.4
  141.6 9.2 %copy-start.19 = (s32[1,768]{1,0:T(1,128)S(1)}, s32[1,768]{1,0:T(1,128)}, u32[]{:S(2)}) copy-start(s32[1,768]{1,0:T(1,128)} %get-tuple-element.26.refs_4_) | copy-start | bytes 9220
  142.3 2.4 collective-permute-start.13
  145.5 7.1 %collective-permute-start.14 = (bf16[16,32,128]{2,1,0:T(8,128)(2,1)}, bf16[16,32,128]{2,1,0:T(8,128)(2,1)S(1)}, u32[]{:S(2)}, u32[]{:S(2)}) collective-permute-start(bf16[16,32,128]{2,1,0:T(8,128)(2,1)} %get-tuple-element.42), channel_id=1, source_target_pairs={{0,1},{1,2},{2,3},{3,0},{4,5},{5,6},{6,7},{7,4},{8,9},{9,10},{10,1... | collective-permute-start | bytes 393224 | tf_op jit(solution)/shard_map/ppermute | solution.py:234
  146.8 9.8 %collective-permute-start.15 = (bf16[16,32,128]{2,1,0:T(8,128)(2,1)S(1)}, bf16[16,32,128]{2,1,0:T(8,128)(2,1)S(1)}, u32[]{:S(2)}, u32[]{:S(2)}) collective-permute-start(bf16[16,32,128]{2,1,0:T(8,128)(2,1)S(1)} %get-tuple-element.43), channel_id=1, source_target_pairs={{0,2},{1,3},{2,0},{3,1},{4,6},{5,7},{6,4},{7,5},{8,10},{9,11},{10,... | collective-permute-start | bytes 393224 | tf_op jit(solution)/shard_map/ppermute | solution.py:234
  149.9 6.7 %collective-permute-start.16 = (bf16[16,32,128]{2,1,0:T(8,128)(2,1)S(1)}, bf16[16,32,128]{2,1,0:T(8,128)(2,1)S(1)}, u32[]{:S(2)}, u32[]{:S(2)}) collective-permute-start(bf16[16,32,128]{2,1,0:T(8,128)(2,1)S(1)} %get-tuple-element.44), channel_id=1, source_target_pairs={{0,3},{1,0},{2,1},{3,2},{4,7},{5,4},{6,5},{7,6},{8,11},{9,8},{10,9... | collective-permute-start | bytes 393224 | tf_op jit(solution)/shard_map/ppermute | solution.py:234
  173.6 4.6 %copy-start = (bf16[16,160,768]{2,1,0:T(8,128)(2,1)S(1)}, bf16[16,160,768]{2,1,0:T(8,128)(2,1)}, u32[]{:S(2)}) copy-start(bf16[16,160,768]{2,1,0:T(8,128)(2,1)} %get-tuple-element.32.mine_ref) | copy-start | bytes 11796484
  175.9 2.4 collective-permute-start.17
  223.3 7.4 %collective-permute-start.18 = (bf16[672,128]{1,0:T(8,128)(2,1)S(1)}, bf16[672,128]{1,0:T(8,128)(2,1)S(1)}, u32[]{:S(2)}, u32[]{:S(2)}) collective-permute-start(bf16[672,128]{1,0:T(8,128)(2,1)S(1)} %shard_map.121.refs_0_), channel_id=1, source_target_pairs={{0,1},{1,0},{2,3},{3,2},{4,5},{5,4},{6,7},{7,6},{8,9},{9,8},{10,11... | collective-permute-start | bytes 516104 | tf_op jit(solution)/shard_map/ppermute | solution.py:627
  224.7 10.4 %collective-permute-start.19 = (bf16[672,128]{1,0:T(8,128)(2,1)S(1)}, bf16[672,128]{1,0:T(8,128)(2,1)S(1)}, u32[]{:S(2)}, u32[]{:S(2)}) collective-permute-start(bf16[672,128]{1,0:T(8,128)(2,1)S(1)} %shard_map.121.refs_0_), channel_id=1, source_target_pairs={{0,2},{1,3},{2,0},{3,1},{4,6},{5,7},{6,4},{7,5},{8,10},{9,11},{10,... | collective-permute-start | bytes 516104 | tf_op jit(solution)/shard_map/ppermute | solution.py:627
  227.7 9.6 %collective-permute-start.20 = (bf16[672,128]{1,0:T(8,128)(2,1)S(1)}, bf16[672,128]{1,0:T(8,128)(2,1)S(1)}, u32[]{:S(2)}, u32[]{:S(2)}) collective-permute-start(bf16[672,128]{1,0:T(8,128)(2,1)S(1)} %shard_map.121.refs_0_), channel_id=1, source_target_pairs={{0,3},{1,2},{2,1},{3,0},{4,7},{5,6},{6,5},{7,4},{8,11},{9,10},{10,... | collective-permute-start | bytes 516104 | tf_op jit(solution)/shard_map/ppermute | solution.py:627

commit v8 on v6

--- a/solution.py
+++ b/solution.py
@@ -326,8 +326,27 @@
     )(index, values, *parts, cotangent, w_msg, gate)
 
 
+def keep_kernel(low_ref, high_ref, after_ref, out_ref):
+    half = low_ref.shape[0]
+    out_ref[:half, :] = low_ref[...]
+    out_ref[half:, :] = high_ref[...]
+
+
+def keep(low, high, after):
+    half, width = low.shape
+    vmem = pl.BlockSpec(memory_space=pltpu.VMEM)
+    return pl.pallas_call(
+        keep_kernel,
+        in_specs=[vmem, vmem, pl.BlockSpec(memory_space=pl.ANY)],
+        out_specs=vmem,
+        out_shape=bf16(2 * half, width),
+        compiler_params=params(24),
+        cost_estimate=cost(1e6, 2e6),
+    )(low, high, after)
+
+
 def back_kernel(index_ref, values_ref, *refs):
-    parts, (cot_ref, place_ref), (out_ref, table, grad) = refs[:8], refs[8:10], refs[-3:]
+    parts, (cot_ref, place_ref), (out_ref, table, grad) = refs[:7], refs[7:9], refs[-3:]
     nodes = cot_ref.shape[0]
     per_row = values_ref.shape[0] * 128 // nodes
 
@@ -604,7 +623,9 @@
         index, values, gather_ring(*owned), cotangent, w_msg, gate
     )
 
-    packed_back = back(index, values, gather_ring(low, high), cotangent, pos_col, slots)
+    ring = gather_ring(low, high)
+    ring = (keep(low, high, ring[7]),) + ring[2:]
+    packed_back = back(index, values, ring, cotangent, pos_col, slots)
     returned = relay(packed_back)
 
     small, other_small = small_sums(aggregate, message_grad, gate_part, chips, packed_back)

time: 237 us -> 235 us (level)
  transfers between devices with their start and end apart: 23 -> 23, of which waited for: 17 -> 16; matrix products, arithmetic and copies ran while one was open for 1% -> 1% of each run, Pallas kernels for 10% -> 10%
where the time goes in v8:
time: 235 us; the launch traced here: 234 us
  waiting for transfers between devices  86.7 us (37%)
  Pallas kernels  55.6 us (24%)
  starting transfers between devices  45.2 us (19%)
  blocking collectives  38.8 us (17%)
  local copies, waits for them, and re-layouts  5.47 us (2%)
    all_to_all x1, blocking collectives, shards(): lax.all_to_all(down, ('z', 'x'), split_axis=0, concat_axis=0, tiled=True)  38.8 us
    ppermute x15, waiting for transfers between devices, shift(): return lax.ppermute(part, 'col', [(c, (c + by) % 4) for c in range(4)])  37.7 us
    all_to_all x2, waiting for transfers between devices, relay(): lax.all_to_all(rows.reshape(size, slots // size, width), ROWS, split_axis...  35.6 us
    ppermute x15, starting transfers between devices, shift(): return lax.ppermute(part, 'col', [(c, (c + by) % 4) for c in range(4)])  23.2 us
    pallas_call x1, Pallas kernels, pool_and_pack(): pl.pallas_call(pool_kernel, grid=(6,), in_specs=[whole(*owner_of.shape),...  16.8 us
    all_to_all x2, starting transfers between devices, relay(): lax.all_to_all(rows.reshape(size, slots // size, width), ROWS, split_axis...  16.7 us
    pallas_call x1, Pallas kernels, pool_and_turn(): pl.pallas_call(turn_kernel, grid=(6,), in_specs=streams(step, rows) + [pl...  12.9 us
    ppermute x3, waiting for transfers between devices, shards(): lax.ppermute(own, 'col', [(c, c ^ step) for c in range(4)])  9.19 us
  transfers between devices with their start and end apart: 23, of which 16 were waited for; matrix products, arithmetic and copies ran while one was open for 1% of the time, Pallas kernels for 10%

profile of v8, /device:TPU:0, one launch (start us, length us, event | category | flops | bytes accessed | tf_op | source)
XLA Modules:
  0.0 234.4 jit_solution(7882762202826519765)
XLA Ops:
  0.6 16.8 %shard_map.111 = (bf16[2304,512]{1,0:T(8,128)(2,1)}, s32[1,768]{1,0:T(1,128)}) custom-call(s32[1,24576]{1,0:T(1,128)} %owner_ref.1, bf16[768,80,128]{2,1,0:T(8,128)(2,1)} %bitcast.32, bf16[768,80,128]{2,1,0:T(8,128)(2,1)} %bitcast.33, bf16[768,80,128]{2,1,0:T(8,128)(2,1)} %bitcast.34, bf16[768,80,128]{2,1,0:T(8,128)(2,1)} %bitcast.35, bf16[5120,512]{1,0:T(8,128)(2,1)} %refs_4_.1), custom_call_target="tpu_custom_call" | custom-call | flops 8000000000 | bytes 23000000 | tf_op jit(solution)/shard_map/pallas_call | solution.py:151
  17.5 8.4 %all-to-all-start = ((bf16[32,72,512]{2,1,0:T(8,128)(2,1)}), bf16[32,72,512]{2,1,0:T(8,128)(2,1)S(1)}, u32[]{:S(2)}, u32[]{:S(2)}) async-start(bf16[32,72,512]{2,1,0:T(8,128)(2,1)} %bitcast.40), calls=%async_computation | async-start | bytes 4718592 | tf_op jit(solution)/shard_map/all_to_all | solution.py:588
  25.9 0.3 fusion
  26.2 0.1 reduce_sum.18
  26.3 0.1 select_reduce_fusion
  26.5 0.1 select_n.49
  26.6 12.9 %shard_map.112 = (bf16[16,160,768]{2,1,0:T(8,128)(2,1)}, bf16[16,160,768]{2,1,0:T(8,128)(2,1)}, s32[1,2304]{1,0:T(1,128)}) custom-call(bf16[768,80,128]{2,1,0:T(8,128)(2,1)} %bitcast.36, bf16[768,80,128]{2,1,0:T(8,128)(2,1)} %bitcast.37, bf16[768,80,128]{2,1,0:T(8,128)(2,1)} %bitcast.38, bf16[768,80,128]{2,1,0:T(8,128)(2,1)} %bitcast.39, ...), custom_call_target="tpu_custom_call" | custom-call | flops 2000000000 | bytes 24000000 | tf_op jit(solution)/shard_map/pallas_call | solution.py:178
  39.5 0.7 add.57.place_ref
  40.2 18.7 %all-to-all-done = bf16[32,72,512]{2,1,0:T(8,128)(2,1)S(1)} async-done(((bf16[32,72,512]{2,1,0:T(8,128)(2,1)}), bf16[32,72,512]{2,1,0:T(8,128)(2,1)S(1)}, u32[]{:S(2)}, u32[]{:S(2)}) %all-to-all-start) | async-done | bytes 2359328 | tf_op jit(solution)/shard_map/all_to_all | solution.py:588
  58.9 2.2 shard_map.113
  61.2 1.6 collective-permute-start.2
  62.9 1.7 collective-permute-start.1
  64.5 1.8 collective-permute-start
  66.3 0.2 collective-permute-start.5
  66.6 8.0 %collective-permute-done.2.refs_6_ = bf16[384,512]{1,0:T(8,128)(2,1)S(1)} collective-permute-done((bf16[384,512]{1,0:T(8,128)(2,1)S(1)}, bf16[384,512]{1,0:T(8,128)(2,1)S(1)}, u32[]{:S(2)}, u32[]{:S(2)}) %collective-permute-start.2) | collective-permute-done | bytes 393248 | tf_op jit(solution)/shard_map/ppermute | solution.py:234
  74.6 0.4 collective-permute-start.3
  74.9 2.9 %collective-permute-start.4 = (bf16[384,512]{1,0:T(8,128)(2,1)S(1)}, bf16[384,512]{1,0:T(8,128)(2,1)S(1)}, u32[]{:S(2)}, u32[]{:S(2)}) collective-permute-start(bf16[384,512]{1,0:T(8,128)(2,1)S(1)} %collective-permute-done.1.refs_3_), channel_id=1, source_target_pairs={{0,3},{1,0},{2,1},{3,2},{4,7},{5,4},{6,5},{7,6},{8,11},{9,8},{10,9... | collective-permute-start | bytes 1179656 | tf_op jit(solution)/shard_map/ppermute | solution.py:234
  77.8 0.5 fusion.2.index_ref
  78.3 5.0 %collective-permute-done.refs_2_ = bf16[384,512]{1,0:T(8,128)(2,1)S(1)} collective-permute-done((bf16[384,512]{1,0:T(8,128)(2,1)S(1)}, bf16[384,512]{1,0:T(8,128)(2,1)S(1)}, u32[]{:S(2)}, u32[]{:S(2)}) %collective-permute-start) | collective-permute-done | bytes 393248 | tf_op jit(solution)/shard_map/ppermute | solution.py:234
  83.4 5.0 %collective-permute-done.3.refs_4_ = bf16[384,512]{1,0:T(8,128)(2,1)S(1)} collective-permute-done((bf16[384,512]{1,0:T(8,128)(2,1)S(1)}, bf16[384,512]{1,0:T(8,128)(2,1)S(1)}, u32[]{:S(2)}, u32[]{:S(2)}) %collective-permute-start.3) | collective-permute-done | bytes 393248 | tf_op jit(solution)/shard_map/ppermute | solution.py:234
  88.4 0.7 copy-done.16
  89.1 0.2 copy-done.17
  89.3 6.3 %shard_map.114 = (bf16[768,512]{1,0:T(8,128)(2,1)}, bf16[768,512]{1,0:T(8,128)(2,1)}, bf16[768,512]{1,0:T(8,128)(2,1)}, bf16[384,512]{1,0:T(8,128)(2,1)}, bf16[384,512]{1,0:T(8,128)(2,1)}, /*index=5*/f32[1,512]{1,0:T(1,128)}) custom-call(s32[24]{0:T(128)} %fusion.2.index_ref, bf16[24,128,128]{2,1,0:T(8,128)(2,1)} %bitcast.28, bf16[384,512]{1,0:T(8,128)(2,1)} %copy-done.5, ...), custom_call_target="tpu_custom_call" | custom-call | flops 1200000000 | bytes 8000000 | tf_op jit(solution)/shard_map/pallas_call | solution.py:312
  95.7 1.5 collective-permute-start.10
  97.2 1.8 collective-permute-start.9
  99.0 0.2 collective-permute-start.7
  99.2 3.0 %collective-permute-start.8 = (bf16[384,512]{1,0:T(8,128)(2,1)}, bf16[384,512]{1,0:T(8,128)(2,1)}, u32[]{:S(2)}, u32[]{:S(2)}) collective-permute-start(bf16[384,512]{1,0:T(8,128)(2,1)} %get-tuple-element.34.low_ref), channel_id=1, source_target_pairs={{0,3},{1,0},{2,1},{3,2},{4,7},{5,4},{6,5},{7,6},{8,11},{9,8},{10,9... | collective-permute-start | bytes 1179656 | tf_op jit(solution)/shard_map/ppermute | solution.py:234
  102.2 4.8 %collective-permute-done.10.refs_5_ = bf16[384,512]{1,0:T(8,128)(2,1)S(1)} collective-permute-done((bf16[384,512]{1,0:T(8,128)(2,1)}, bf16[384,512]{1,0:T(8,128)(2,1)S(1)}, u32[]{:S(2)}, u32[]{:S(2)}) %collective-permute-start.10) | collective-permute-done | bytes 393248 | tf_op jit(solution)/shard_map/ppermute | solution.py:234
  107.0 0.7 collective-permute-start.11
  107.6 0.4 collective-permute-done.9.refs_2_
  108.0 2.2 collective-permute-start.12
  110.2 1.1 select_n.51.refs_8_
  111.3 4.1 %collective-permute-done.7.after_ref.refs_6_ = bf16[384,512]{1,0:T(8,128)(2,1)S(1)} collective-permute-done((bf16[384,512]{1,0:T(8,128)(2,1)}, bf16[384,512]{1,0:T(8,128)(2,1)S(1)}, u32[]{:S(2)}, u32[]{:S(2)}) %collective-permute-start.7) | collective-permute-done | bytes 393248 | tf_op jit(solution)/shard_map/ppermute | solution.py:234
  115.4 1.0 copy-done.7
  116.4 1.0 copy-done.8
  117.4 4.8 %collective-permute-done.11.refs_3_ = bf16[384,512]{1,0:T(8,128)(2,1)} collective-permute-done((bf16[384,512]{1,0:T(8,128)(2,1)S(1)}, bf16[384,512]{1,0:T(8,128)(2,1)}, u32[]{:S(2)}, u32[]{:S(2)}) %collective-permute-start.11) | collective-permute-done | bytes 393248 | tf_op jit(solution)/shard_map/ppermute | solution.py:234
  122.2 6.2 %shard_map.116.after_ref = bf16[2304,512]{1,0:T(8,128)(2,1)} custom-call(s32[24]{0:T(128)S(1)} %copy-done.10, bf16[24,128,128]{2,1,0:T(8,128)(2,1)S(1)} %bitcast.29, bf16[768,512]{1,0:T(8,128)(2,1)S(1)} %shard_map.115.refs_0_, bf16[384,512]{1,0:T(8,128)(2,1)} %collective-permute-done.8.refs_1_, bf16[384,512]{1,0:T(8,128)(2,1)} %collective-permute-done.9.refs_2_, ...), custom_call_target="tpu_custom_call" | custom-call | flops 1811939328 | bytes 5000000 | tf_op jit(solution)/shard_map/pallas_call | solution.py:370
  128.4 8.3 %all-to-all-start.1 = ((bf16[32,72,512]{2,1,0:T(8,128)(2,1)}), bf16[32,72,512]{2,1,0:T(8,128)(2,1)S(1)}, u32[]{:S(2)}, u32[]{:S(2)}) async-start(bf16[32,72,512]{2,1,0:T(8,128)(2,1)} %bitcast.13), calls=%async_computation.1 | async-start | bytes 4718592 | tf_op jit(solution)/shard_map/all_to_all | solution.py:588
  136.7 1.1 copy-done.4
  137.9 0.7 shard_map.117
  138.5 0.4 collective-permute-start.13
  138.9 2.0 collective-permute-done.13.other_small_ref
  140.9 0.9 shard_map.118
  141.8 1.3 collective-permute-start.14
  143.0 3.1 %collective-permute-start.15 = (bf16[16,32,128]{2,1,0:T(8,128)(2,1)S(1)}, bf16[16,32,128]{2,1,0:T(8,128)(2,1)S(1)}, u32[]{:S(2)}, u32[]{:S(2)}) collective-permute-start(bf16[16,32,128]{2,1,0:T(8,128)(2,1)S(1)} %get-tuple-element.43), channel_id=1, source_target_pairs={{0,2},{1,3},{2,0},{3,1},{4,6},{5,7},{6,4},{7,5},{8,10},{9,11},{10,... | collective-permute-start | bytes 393224 | tf_op jit(solution)/shard_map/ppermute | solution.py:234
  146.1 0.9 collective-permute-start.16
  147.0 0.2 copy.18.place_ref
  147.2 1.7 collective-permute-done.14.refs_1_
  148.9 3.9 %collective-permute-done.15.refs_2_ = bf16[16,32,128]{2,1,0:T(8,128)(2,1)S(1)} collective-permute-done((bf16[16,32,128]{2,1,0:T(8,128)(2,1)S(1)}, bf16[16,32,128]{2,1,0:T(8,128)(2,1)S(1)}, u32[]{:S(2)}, u32[]{:S(2)}) %collective-permute-start.15) | collective-permute-done | bytes 131104 | tf_op jit(solution)/shard_map/ppermute | solution.py:234
  152.8 0.1 shard_map.119.out_refs_0_.led_ref
  152.9 16.9 %all-to-all-done.1 = bf16[32,72,512]{2,1,0:T(8,128)(2,1)S(1)} async-done(((bf16[32,72,512]{2,1,0:T(8,128)(2,1)}), bf16[32,72,512]{2,1,0:T(8,128)(2,1)S(1)}, u32[]{:S(2)}, u32[]{:S(2)}) %all-to-all-start.1) | async-done | bytes 2359328 | tf_op jit(solution)/shard_map/all_to_all | solution.py:588
  169.8 2.3 shard_map.120.grad_ref
  172.1 0.1 collective-permute-start.17
  172.2 2.3 collective-permute-done.17.other_grad_ref
  174.4 6.0 %shard_map.121 = bf16[16,672,128]{2,1,0:T(8,128)(2,1)S(1)} custom-call(bf16[16,160,768]{2,1,0:T(8,128)(2,1)S(1)} %copy-done, bf16[16,160,768]{2,1,0:T(8,128)(2,1)} %collective-permute-done.6.other_ref, bf16[768,512]{1,0:T(8,128)(2,1)S(1)} %shard_map.120.grad_ref, bf16[768,512]{1,0:T(8,128)(2,1)S(1)} %collective-permute-done.17.other_grad_ref, ...), custom_call_target="tpu_custom_call" | custom-call | flops 2000000000 | bytes 12000000 | tf_op jit(solution)/shard_map/pallas_call | solution.py:508
  180.4 38.8 %all_to_all.15.parts_ref = bf16[16,672,128]{2,1,0:T(8,128)(2,1)S(1)} all-to-all(bf16[16,672,128]{2,1,0:T(8,128)(2,1)S(1)} %shard_map.121), channel_id=1, replica_groups=mesh['z'=4,'x'=4,'core'=2,'col'=4] {'z','x'}, dimensions={0} | all-to-all | bytes 5505024 | tf_op jit(solution)/shard_map/all_to_all | solution.py:636
  219.2 0.4 shard_map.122.refs_0_
  219.6 1.4 collective-permute-start.18
  220.9 3.1 %collective-permute-start.19 = (bf16[672,128]{1,0:T(8,128)(2,1)S(1)}, bf16[672,128]{1,0:T(8,128)(2,1)S(1)}, u32[]{:S(2)}, u32[]{:S(2)}) collective-permute-start(bf16[672,128]{1,0:T(8,128)(2,1)S(1)} %shard_map.122.refs_0_), channel_id=1, source_target_pairs={{0,2},{1,3},{2,0},{3,1},{4,6},{5,7},{6,4},{7,5},{8,10},{9,11},{10,... | collective-permute-start | bytes 516104 | tf_op jit(solution)/shard_map/ppermute | solution.py:639
  224.0 0.4 collective-permute-start.20
  224.3 2.6 %collective-permute-done.18.refs_1_ = bf16[672,128]{1,0:T(8,128)(2,1)S(1)} collective-permute-done((bf16[672,128]{1,0:T(8,128)(2,1)S(1)}, bf16[672,128]{1,0:T(8,128)(2,1)S(1)}, u32[]{:S(2)}, u32[]{:S(2)}) %collective-permute-start.18) | collective-permute-done | bytes 172064 | tf_op jit(solution)/shard_map/ppermute | solution.py:639
  227.0 4.4 %collective-permute-done.19.refs_2_ = bf16[672,128]{1,0:T(8,128)(2,1)S(1)} collective-permute-done((bf16[672,128]{1,0:T(8,128)(2,1)S(1)}, bf16[672,128]{1,0:T(8,128)(2,1)S(1)}, u32[]{:S(2)}, u32[]{:S(2)}) %collective-permute-start.19) | collective-permute-done | bytes 172064 | tf_op jit(solution)/shard_map/ppermute | solution.py:639
  231.3 2.2 collective-permute-done.20.refs_3_
  233.5 0.9 shard_map.123
  (48 shorter events, 0.3 us)
Async XLA Ops:
  17.4 8.4 %copy-start.11 = (s32[1,24576]{1,0:T(1,128)S(1)}, s32[1,24576]{1,0:T(1,128)}, u32[]{:S(2)}) copy-start(s32[1,24576]{1,0:T(1,128)} %owner_ref.1) | copy-start | bytes 294916
  17.5 41.5 %all-to-all-start = ((bf16[32,72,512]{2,1,0:T(8,128)(2,1)}), bf16[32,72,512]{2,1,0:T(8,128)(2,1)S(1)}, u32[]{:S(2)}, u32[]{:S(2)}) async-start(bf16[32,72,512]{2,1,0:T(8,128)(2,1)} %bitcast.40), calls=%async_computation | async-start | bytes 4718592 | tf_op jit(solution)/shard_map/all_to_all | solution.py:588
  26.5 13.0 %copy-start.18 = (s32[32,72]{1,0:T(8,128)}, s32[32,72]{1,0:T(8,128)S(1)}, u32[]{:S(2)}) copy-start(s32[32,72]{1,0:T(8,128)S(1)} %add_select_fusion) | copy-start | bytes 27652
  58.9 18.9 %copy-start.20 = (s32[1,24]{1,0:T(1,128)S(1)}, s32[1,24]{1,0:T(1,128)}, u32[]{:S(2)}) copy-start(s32[1,24]{1,0:T(1,128)} %param.12) | copy-start | bytes 292
  61.2 27.2 %copy-start.5 = (bf16[384,512]{1,0:T(8,128)(2,1)}, bf16[384,512]{1,0:T(8,128)(2,1)S(1)}, u32[]{:S(2)}) copy-start(bf16[384,512]{1,0:T(8,128)(2,1)S(1)} %get-tuple-element.29.refs_0_) | copy-start | bytes 1179652
  61.2 27.2 %copy-start.6 = (bf16[384,512]{1,0:T(8,128)(2,1)}, bf16[384,512]{1,0:T(8,128)(2,1)S(1)}, u32[]{:S(2)}) copy-start(bf16[384,512]{1,0:T(8,128)(2,1)S(1)} %get-tuple-element.30.refs_1_) | copy-start | bytes 1179652
  61.2 13.3 %collective-permute-start.2 = (bf16[384,512]{1,0:T(8,128)(2,1)S(1)}, bf16[384,512]{1,0:T(8,128)(2,1)S(1)}, u32[]{:S(2)}, u32[]{:S(2)}) collective-permute-start(bf16[384,512]{1,0:T(8,128)(2,1)S(1)} %get-tuple-element.29.refs_0_), channel_id=1, source_target_pairs={{0,1},{1,2},{2,3},{3,0},{4,5},{5,6},{6,7},{7,4},{8,9},{9,10},{10,1... | collective-permute-start | bytes 1179656 | tf_op jit(solution)/shard_map/ppermute | solution.py:234
  62.9 12.1 %collective-permute-start.1 = (bf16[384,512]{1,0:T(8,128)(2,1)S(1)}, bf16[384,512]{1,0:T(8,128)(2,1)S(1)}, u32[]{:S(2)}, u32[]{:S(2)}) collective-permute-start(bf16[384,512]{1,0:T(8,128)(2,1)S(1)} %get-tuple-element.30.refs_1_), channel_id=1, source_target_pairs={{0,3},{1,0},{2,1},{3,2},{4,7},{5,4},{6,5},{7,6},{8,11},{9,8},{10,9... | collective-permute-start | bytes 1179656 | tf_op jit(solution)/shard_map/ppermute | solution.py:234
  64.5 18.8 %collective-permute-start = (bf16[384,512]{1,0:T(8,128)(2,1)S(1)}, bf16[384,512]{1,0:T(8,128)(2,1)S(1)}, u32[]{:S(2)}, u32[]{:S(2)}) collective-permute-start(bf16[384,512]{1,0:T(8,128)(2,1)S(1)} %get-tuple-element.29.refs_0_), channel_id=1, source_target_pairs={{0,3},{1,0},{2,1},{3,2},{4,7},{5,4},{6,5},{7,6},{8,11},{9,8},{10,9... | collective-permute-start | bytes 1179656 | tf_op jit(solution)/shard_map/ppermute | solution.py:234
  66.3 17.0 %collective-permute-start.5 = (bf16[384,512]{1,0:T(8,128)(2,1)S(1)}, bf16[384,512]{1,0:T(8,128)(2,1)S(1)}, u32[]{:S(2)}, u32[]{:S(2)}) collective-permute-start(bf16[384,512]{1,0:T(8,128)(2,1)S(1)} %get-tuple-element.30.refs_1_), channel_id=1, source_target_pairs={{0,1},{1,2},{2,3},{3,0},{4,5},{5,6},{6,7},{7,4},{8,9},{9,10},{10,1... | collective-permute-start | bytes 1179656 | tf_op jit(solution)/shard_map/ppermute | solution.py:234
  74.5 13.9 %copy-start.12 = (bf16[384,512]{1,0:T(8,128)(2,1)}, bf16[384,512]{1,0:T(8,128)(2,1)S(1)}, u32[]{:S(2)}) copy-start(bf16[384,512]{1,0:T(8,128)(2,1)S(1)} %collective-permute-done.2.refs_6_) | copy-start | bytes 1179652
  74.6 13.8 %collective-permute-start.3 = (bf16[384,512]{1,0:T(8,128)(2,1)S(1)}, bf16[384,512]{1,0:T(8,128)(2,1)S(1)}, u32[]{:S(2)}, u32[]{:S(2)}) collective-permute-start(bf16[384,512]{1,0:T(8,128)(2,1)S(1)} %collective-permute-done.2.refs_6_), channel_id=1, source_target_pairs={{0,1},{1,2},{2,3},{3,0},{4,5},{5,6},{6,7},{7,4},{8,9},{9,10},{10,1... | collective-permute-start | bytes 1179656 | tf_op jit(solution)/shard_map/ppermute | solution.py:234
  74.9 13.5 %copy-start.13 = (bf16[384,512]{1,0:T(8,128)(2,1)}, bf16[384,512]{1,0:T(8,128)(2,1)S(1)}, u32[]{:S(2)}) copy-start(bf16[384,512]{1,0:T(8,128)(2,1)S(1)} %collective-permute-done.1.refs_3_) | copy-start | bytes 1179652
  74.9 13.5 %collective-permute-start.4 = (bf16[384,512]{1,0:T(8,128)(2,1)S(1)}, bf16[384,512]{1,0:T(8,128)(2,1)S(1)}, u32[]{:S(2)}, u32[]{:S(2)}) collective-permute-start(bf16[384,512]{1,0:T(8,128)(2,1)S(1)} %collective-permute-done.1.refs_3_), channel_id=1, source_target_pairs={{0,3},{1,0},{2,1},{3,2},{4,7},{5,4},{6,5},{7,6},{8,11},{9,8},{10,9... | collective-permute-start | bytes 1179656 | tf_op jit(solution)/shard_map/ppermute | solution.py:234
  83.3 5.1 %copy-start.14 = (bf16[384,512]{1,0:T(8,128)(2,1)}, bf16[384,512]{1,0:T(8,128)(2,1)S(1)}, u32[]{:S(2)}) copy-start(bf16[384,512]{1,0:T(8,128)(2,1)S(1)} %collective-permute-done.refs_2_) | copy-start | bytes 1179652
  83.4 5.1 %copy-start.15 = (bf16[384,512]{1,0:T(8,128)(2,1)}, bf16[384,512]{1,0:T(8,128)(2,1)S(1)}, u32[]{:S(2)}) copy-start(bf16[384,512]{1,0:T(8,128)(2,1)S(1)} %collective-permute-done.5.refs_7_) | copy-start | bytes 1179652
  88.4 0.8 copy-start.16
  88.4 0.9 copy-start.17
  89.3 32.9 %copy-start.10 = (s32[24]{0:T(128)S(1)}, s32[24]{0:T(128)}, u32[]{:S(2)}) copy-start(s32[24]{0:T(128)} %fusion.2.index_ref) | copy-start | bytes 292
  95.6 26.6 %copy-start.1 = (bf16[1,24,128,128]{3,2,1,0:T(8,128)(2,1)S(1)}, bf16[1,24,128,128]{3,2,1,0:T(8,128)(2,1)}, u32[]{:S(2)}) copy-start(bf16[1,24,128,128]{3,2,1,0:T(8,128)(2,1)} %param.11) | copy-start | bytes 2359300
  95.6 26.6 %copy-start.2 = (bf16[768,512]{1,0:T(8,128)(2,1)S(1)}, bf16[768,512]{1,0:T(8,128)(2,1)}, u32[]{:S(2)}) copy-start(bf16[768,512]{1,0:T(8,128)(2,1)} %refs_7_.1) | copy-start | bytes 2359300
  95.7 11.3 %collective-permute-start.10 = (bf16[384,512]{1,0:T(8,128)(2,1)}, bf16[384,512]{1,0:T(8,128)(2,1)S(1)}, u32[]{:S(2)}, u32[]{:S(2)}) collective-permute-start(bf16[384,512]{1,0:T(8,128)(2,1)} %get-tuple-element.34.low_ref), channel_id=1, source_target_pairs={{0,1},{1,2},{2,3},{3,0},{4,5},{5,6},{6,7},{7,4},{8,9},{9,10},{10,1... | collective-permute-start | bytes 1179656 | tf_op jit(solution)/shard_map/ppermute | solution.py:234
  97.2 10.9 %collective-permute-start.9 = (bf16[384,512]{1,0:T(8,128)(2,1)}, bf16[384,512]{1,0:T(8,128)(2,1)}, u32[]{:S(2)}, u32[]{:S(2)}) collective-permute-start(bf16[384,512]{1,0:T(8,128)(2,1)} %get-tuple-element.35.high_ref), channel_id=1, source_target_pairs={{0,3},{1,0},{2,1},{3,2},{4,7},{5,4},{6,5},{7,6},{8,11},{9,8},{10,9... | collective-permute-start | bytes 1179656 | tf_op jit(solution)/shard_map/ppermute | solution.py:234
  99.0 73.2 %collective-permute-start.6 = (bf16[16,160,768]{2,1,0:T(8,128)(2,1)}, bf16[16,160,768]{2,1,0:T(8,128)(2,1)}, u32[]{:S(2)}, u32[]{:S(2)}) collective-permute-start(bf16[16,160,768]{2,1,0:T(8,128)(2,1)} %get-tuple-element.33), channel_id=1, source_target_pairs={{0,4},{4,0},{1,5},{5,1},{2,6},{6,2},{3,7},{7,3},{8,12},{12,8},{9,1... | collective-permute-start | bytes 11796488 | tf_op jit(solution)/shard_map/ppermute | solution.py:605
  99.0 16.4 %collective-permute-start.7 = (bf16[384,512]{1,0:T(8,128)(2,1)}, bf16[384,512]{1,0:T(8,128)(2,1)S(1)}, u32[]{:S(2)}, u32[]{:S(2)}) collective-permute-start(bf16[384,512]{1,0:T(8,128)(2,1)} %get-tuple-element.35.high_ref), channel_id=1, source_target_pairs={{0,1},{1,2},{2,3},{3,0},{4,5},{5,6},{6,7},{7,4},{8,9},{9,10},{10,1... | collective-permute-start | bytes 1179656 | tf_op jit(solution)/shard_map/ppermute | solution.py:234
  99.2 18.3 %collective-permute-start.8 = (bf16[384,512]{1,0:T(8,128)(2,1)}, bf16[384,512]{1,0:T(8,128)(2,1)}, u32[]{:S(2)}, u32[]{:S(2)}) collective-permute-start(bf16[384,512]{1,0:T(8,128)(2,1)} %get-tuple-element.34.low_ref), channel_id=1, source_target_pairs={{0,3},{1,0},{2,1},{3,2},{4,7},{5,4},{6,5},{7,6},{8,11},{9,8},{10,9... | collective-permute-start | bytes 1179656 | tf_op jit(solution)/shard_map/ppermute | solution.py:234
  107.0 15.3 %collective-permute-start.11 = (bf16[384,512]{1,0:T(8,128)(2,1)S(1)}, bf16[384,512]{1,0:T(8,128)(2,1)}, u32[]{:S(2)}, u32[]{:S(2)}) collective-permute-start(bf16[384,512]{1,0:T(8,128)(2,1)S(1)} %collective-permute-done.10.refs_5_), channel_id=1, source_target_pairs={{0,1},{1,2},{2,3},{3,0},{4,5},{5,6},{6,7},{7,4},{8,9},{9,10},{10,1... | collective-permute-start | bytes 1179656 | tf_op jit(solution)/shard_map/ppermute | solution.py:234
  108.0 14.2 %collective-permute-start.12 = (bf16[384,512]{1,0:T(8,128)(2,1)}, bf16[384,512]{1,0:T(8,128)(2,1)}, u32[]{:S(2)}, u32[]{:S(2)}) collective-permute-start(bf16[384,512]{1,0:T(8,128)(2,1)} %collective-permute-done.9.refs_2_), channel_id=1, source_target_pairs={{0,3},{1,0},{2,1},{3,2},{4,7},{5,4},{6,5},{7,6},{8,11},{9,8},{10,9... | collective-permute-start | bytes 1179656 | tf_op jit(solution)/shard_map/ppermute | solution.py:234
  115.4 1.0 copy-start.7
  116.4 1.0 copy-start.8
  128.4 8.3 %copy-start.3 = (bf16[768,512]{1,0:T(8,128)(2,1)S(1)}, bf16[768,512]{1,0:T(8,128)(2,1)}, u32[]{:S(2)}) copy-start(bf16[768,512]{1,0:T(8,128)(2,1)} %get-tuple-element.36.agg_ref) | copy-start | bytes 2359300
  128.4 8.3 %copy-start.9 = (f32[1,512]{1,0:T(1,128)S(1)}, f32[1,512]{1,0:T(1,128)}, u32[]{:S(2)}) copy-start(f32[1,512]{1,0:T(1,128)} %get-tuple-element.38.gate_ref) | copy-start | bytes 6148
  128.4 41.4 %all-to-all-start.1 = ((bf16[32,72,512]{2,1,0:T(8,128)(2,1)}), bf16[32,72,512]{2,1,0:T(8,128)(2,1)S(1)}, u32[]{:S(2)}, u32[]{:S(2)}) async-start(bf16[32,72,512]{2,1,0:T(8,128)(2,1)} %bitcast.13), calls=%async_computation.1 | async-start | bytes 4718592 | tf_op jit(solution)/shard_map/all_to_all | solution.py:588
  136.7 1.1 copy-start.4
  137.9 9.2 %copy-start.19 = (s32[1,768]{1,0:T(1,128)S(1)}, s32[1,768]{1,0:T(1,128)}, u32[]{:S(2)}) copy-start(s32[1,768]{1,0:T(1,128)} %get-tuple-element.26.refs_4_) | copy-start | bytes 9220
  138.5 2.4 %collective-permute-start.13 = (f32[16,24,512]{2,1,0:T(8,128)S(1)}, f32[16,24,512]{2,1,0:T(8,128)S(1)}, u32[]{:S(2)}, u32[]{:S(2)}) collective-permute-start(f32[16,24,512]{2,1,0:T(8,128)S(1)} %get-tuple-element.40), channel_id=1, source_target_pairs={{0,4},{4,0},{1,5},{5,1},{2,6},{6,2},{3,7},{7,3},{8,12},{12,8},{9,1... | collective-permute-start | bytes 2359304 | tf_op jit(solution)/shard_map/ppermute | solution.py:605
  141.8 7.1 %collective-permute-start.14 = (bf16[16,32,128]{2,1,0:T(8,128)(2,1)}, bf16[16,32,128]{2,1,0:T(8,128)(2,1)S(1)}, u32[]{:S(2)}, u32[]{:S(2)}) collective-permute-start(bf16[16,32,128]{2,1,0:T(8,128)(2,1)} %get-tuple-element.42), channel_id=1, source_target_pairs={{0,1},{1,2},{2,3},{3,0},{4,5},{5,6},{6,7},{7,4},{8,9},{9,10},{10,1... | collective-permute-start | bytes 393224 | tf_op jit(solution)/shard_map/ppermute | solution.py:234
  143.0 9.8 %collective-permute-start.15 = (bf16[16,32,128]{2,1,0:T(8,128)(2,1)S(1)}, bf16[16,32,128]{2,1,0:T(8,128)(2,1)S(1)}, u32[]{:S(2)}, u32[]{:S(2)}) collective-permute-start(bf16[16,32,128]{2,1,0:T(8,128)(2,1)S(1)} %get-tuple-element.43), channel_id=1, source_target_pairs={{0,2},{1,3},{2,0},{3,1},{4,6},{5,7},{6,4},{7,5},{8,10},{9,11},{10,... | collective-permute-start | bytes 393224 | tf_op jit(solution)/shard_map/ppermute | solution.py:234
  146.1 6.7 %collective-permute-start.16 = (bf16[16,32,128]{2,1,0:T(8,128)(2,1)S(1)}, bf16[16,32,128]{2,1,0:T(8,128)(2,1)S(1)}, u32[]{:S(2)}, u32[]{:S(2)}) collective-permute-start(bf16[16,32,128]{2,1,0:T(8,128)(2,1)S(1)} %get-tuple-element.44), channel_id=1, source_target_pairs={{0,3},{1,0},{2,1},{3,2},{4,7},{5,4},{6,5},{7,6},{8,11},{9,8},{10,9... | collective-permute-start | bytes 393224 | tf_op jit(solution)/shard_map/ppermute | solution.py:234
  169.8 4.6 %copy-start = (bf16[16,160,768]{2,1,0:T(8,128)(2,1)S(1)}, bf16[16,160,768]{2,1,0:T(8,128)(2,1)}, u32[]{:S(2)}) copy-start(bf16[16,160,768]{2,1,0:T(8,128)(2,1)} %get-tuple-element.32.mine_ref) | copy-start | bytes 11796484
  172.1 2.4 %collective-permute-start.17 = (bf16[768,512]{1,0:T(8,128)(2,1)S(1)}, bf16[768,512]{1,0:T(8,128)(2,1)S(1)}, u32[]{:S(2)}, u32[]{:S(2)}) collective-permute-start(bf16[768,512]{1,0:T(8,128)(2,1)S(1)} %shard_map.120.grad_ref), channel_id=1, source_target_pairs={{0,4},{4,0},{1,5},{5,1},{2,6},{6,2},{3,7},{7,3},{8,12},{12,8},{9,1... | collective-permute-start | bytes 2359304 | tf_op jit(solution)/shard_map/ppermute | solution.py:605
  219.6 7.4 %collective-permute-start.18 = (bf16[672,128]{1,0:T(8,128)(2,1)S(1)}, bf16[672,128]{1,0:T(8,128)(2,1)S(1)}, u32[]{:S(2)}, u32[]{:S(2)}) collective-permute-start(bf16[672,128]{1,0:T(8,128)(2,1)S(1)} %shard_map.122.refs_0_), channel_id=1, source_target_pairs={{0,1},{1,0},{2,3},{3,2},{4,5},{5,4},{6,7},{7,6},{8,9},{9,8},{10,11... | collective-permute-start | bytes 516104 | tf_op jit(solution)/shard_map/ppermute | solution.py:639
  220.9 10.4 %collective-permute-start.19 = (bf16[672,128]{1,0:T(8,128)(2,1)S(1)}, bf16[672,128]{1,0:T(8,128)(2,1)S(1)}, u32[]{:S(2)}, u32[]{:S(2)}) collective-permute-start(bf16[672,128]{1,0:T(8,128)(2,1)S(1)} %shard_map.122.refs_0_), channel_id=1, source_target_pairs={{0,2},{1,3},{2,0},{3,1},{4,6},{5,7},{6,4},{7,5},{8,10},{9,11},{10,... | collective-permute-start | bytes 516104 | tf_op jit(solution)/shard_map/ppermute | solution.py:639
  224.0 9.6 %collective-permute-start.20 = (bf16[672,128]{1,0:T(8,128)(2,1)S(1)}, bf16[672,128]{1,0:T(8,128)(2,1)S(1)}, u32[]{:S(2)}, u32[]{:S(2)}) collective-permute-start(bf16[672,128]{1,0:T(8,128)(2,1)S(1)} %shard_map.122.refs_0_), channel_id=1, source_target_pairs={{0,3},{1,2},{2,1},{3,0},{4,7},{5,6},{6,5},{7,4},{8,11},{9,10},{10,... | collective-permute-start | bytes 516104 | tf_op jit(solution)/shard_map/ppermute | solution.py:639
